TPU v7x, 32 devices: a whole 2x2x4 slice. The times are simulated.
32 devices in a mesh: group: 4 (over y, x), member: 8 (over z, core).
Axes of the slice: x: 2, y: 2, z: 4, core: 2. Of those that a mesh axis runs over, the one named last changes fastest.
Arguments:
- mesh_vector: bfloat16 [32768, 128], P(('group', 'member')), may hold values from -6 to 6
- cluster_position: int32 [32768], P(('group', 'member')), may hold values from 0 to 32767, as said below
- cluster_sizes: int32 [32], replicated, may hold values from 256 to 1792, as said below
- block_ranks: int32 [62], replicated, may hold values from 32 to 128, as said below
- diag_block: bfloat16 [2, 57344, 1792], P(None, ('group', 'member')), may hold values from -0.09375 to 0.09375
- top_left: bfloat16 [2, 2, 57344, 128], P(None, None, ('group', 'member')), may hold values from -0.375 to 0.375
- top_right: bfloat16 [2, 2, 57344, 128], P(None, None, ('group', 'member'))
- low_left: bfloat16 [3, 2, 57344, 64], P(None, None, ('group', 'member')), may hold values from -0.5 to 0.5
- low_right: bfloat16 [3, 2, 57344, 64], P(None, None, ('group', 'member'))
Outputs:
- product: float32 [32768, 128], P(('group', 'member'))
Inputs may be any that keep to these rules, and one draw needn't show every extreme that they name: `cluster_position`: A permutation of the unknowns. In cluster order every aligned run of 32 positions holds exactly one row of each device, so each device holds exactly size / 32 rows of every cluster. `cluster_sizes`: multiples of 32 that sum to 32768; one is exactly 1792. `block_ranks`: entries 0 .. 5 lie in 64 .. 128, the others in 32 .. 64; entry 0 is 128.
All inputs are finite; a program needn't handle non-finite values.
Results may differ from a plain program's by a relative error of at most 0.0027.
Values may be sent and summed in bfloat16 or wider, within the bound.
No kernel may reach another device: no remote copies, remote signals or barrier semaphores. Data moves between devices by JAX's collectives and lax.ppermute only.
A program may use at most 64 MiB of HBM per device.

v0:
```python
import jax
import jax.numpy as jnp
from jax import lax
from jax.sharding import PartitionSpec as P


def partner(block, axis, apart):
    count = lax.axis_size(axis)
    route = []
    for low in range(count):
        high = low | 1 << apart
        if high != low and high < count:
            route += [(low, high), (high, low)]
    return lax.ppermute(block, axis, route)


def rotate(values):
    middle = values.shape[-1] // 2
    return jnp.concatenate([-values[..., middle:], values[..., :middle]], axis=-1)


def level_ranks(block_ranks, device, first_level, count, levels):
    picks = []
    for position in range(count):
        tree_level = first_level + position
        node_index = jnp.right_shift(device, levels - tree_level)
        picks.append(block_ranks[2**tree_level - 2 + node_index])
    return jnp.stack(picks)


def masked_pairs(coefficient, ranks):
    rank_cap = coefficient.shape[1]
    keep_mask = jnp.arange(rank_cap, dtype=jnp.int32)[None, :] < ranks[:, None]
    rounded = jnp.where(keep_mask[:, :, None], coefficient, 0.0).astype(jnp.bfloat16)
    return jnp.stack([rounded, rotate(rounded)], axis=1)


def on_device(
    mesh_vector,
    cluster_position,
    cluster_sizes,
    block_ranks,
    diag_block,
    top_left,
    top_right,
    low_left,
    low_right,
):
    groups = lax.axis_size("group")
    members = lax.axis_size("member")
    leaves = groups * members
    group_levels = groups.bit_length() - 1
    member_levels = members.bit_length() - 1
    levels = group_levels + member_levels
    device = lax.axis_index("group") * members + lax.axis_index("member")
    capacity = diag_block.shape[1]
    bucket = capacity // leaves
    columns = mesh_vector.shape[1]
    cluster_ends = jnp.cumsum(cluster_sizes)
    starts = cluster_ends - cluster_sizes
    owners = jnp.sum((cluster_position[:, None] >= cluster_ends[None, :]).astype(jnp.int32), axis=1)
    picked = owners[:, None] == jnp.arange(leaves, dtype=jnp.int32)[None, :]
    first_row = jnp.sum(jnp.where(picked, starts[None, :], 0), axis=1)
    within = cluster_position - first_row
    placing = owners * bucket + within // leaves
    outgoing = jnp.zeros((leaves * bucket, columns), mesh_vector.dtype).at[placing].set(mesh_vector)
    targets = jnp.full((leaves * bucket,), capacity, jnp.int32).at[placing].set(within)
    arrived, slot_ids = (
        lax.all_to_all(
            outgoing.reshape(leaves, bucket, columns),
            ("group", "member"),
            split_axis=0,
            concat_axis=0,
            tiled=True,
        ),
        lax.all_to_all(
            targets.reshape(leaves, bucket),
            ("group", "member"),
            split_axis=0,
            concat_axis=0,
            tiled=True,
        ),
    )
    arrived = arrived.reshape(leaves * bucket, columns)
    slot_ids = slot_ids.reshape(leaves * bucket)
    cluster_field = (
        jnp.zeros((capacity, columns), mesh_vector.dtype).at[slot_ids].set(arrived, mode="drop")
    )
    paired = jnp.stack([cluster_field, rotate(cluster_field)])
    top_part = jnp.einsum("lprk,prn->lkn", top_right, paired, preferred_element_type=jnp.float32)
    low_part = jnp.einsum("lprk,prn->lkn", low_right, paired, preferred_element_type=jnp.float32)
    result = jnp.einsum("prc,pcn->rn", diag_block, paired, preferred_element_type=jnp.float32)
    low_coefs = []
    for low_pos in range(member_levels):
        sibling_bit = member_levels - 1 - low_pos
        running = low_part[low_pos]
        for lower_bit in range(sibling_bit):
            running = running + partner(running, "member", lower_bit)
        low_coefs.append(
            partner(running.astype(jnp.bfloat16), "member", sibling_bit).astype(running.dtype)
        )
    low_coef = jnp.stack(low_coefs)
    member_summed = lax.psum(top_part, "member")
    pending = [member_summed[group_levels - 1 - group_bit] for group_bit in range(group_levels)]
    gotten = []
    for group_bit in range(group_levels):
        received = partner(jnp.stack(pending[group_bit:]), "group", group_bit)
        gotten.append(received[0])
        for pending_bit in range(group_bit + 1, group_levels):
            pending[pending_bit] = pending[pending_bit] + received[pending_bit - group_bit]
    top_coef = jnp.stack(
        [gotten[group_levels - 1 - level_pos] for level_pos in range(group_levels)]
    )
    top_ranks = level_ranks(block_ranks, device, 1, group_levels, levels)
    low_ranks = level_ranks(block_ranks, device, group_levels + 1, member_levels, levels)
    result = result + jnp.einsum(
        "lprk,lpkn->rn",
        top_left,
        masked_pairs(top_coef, top_ranks),
        preferred_element_type=jnp.float32,
    )
    result = result + jnp.einsum(
        "lprk,lpkn->rn",
        low_left,
        masked_pairs(low_coef, low_ranks),
        preferred_element_type=jnp.float32,
    )
    leaving = result[jnp.minimum(slot_ids, capacity - 1)]
    returned = lax.all_to_all(
        leaving.reshape(leaves, bucket, columns),
        ("group", "member"),
        split_axis=0,
        concat_axis=0,
        tiled=True,
    )
    returned = returned.reshape(leaves * bucket, columns)
    return returned[placing]


def solution(mesh):
    return jax.shard_map(
        on_device,
        mesh=mesh,
        in_specs=(
            P(("group", "member"), None),
            P(("group", "member")),
            P(),
            P(),
            P(None, ("group", "member"), None),
            P(None, None, ("group", "member"), None),
            P(None, None, ("group", "member"), None),
            P(None, None, ("group", "member"), None),
            P(None, None, ("group", "member"), None),
        ),
        out_specs=P(("group", "member"), None),
        check_vma=False,
    )
```

profile of v0, /device:TPU:0, one launch (start us, length us, event | category | flops | bytes accessed | tf_op | source)
XLA Modules:
  0.0 179.9 jit_solution(9473059733891160169)
XLA Ops:
  6.5 0.9 copy.24
  8.2 0.8 convert_reduce_fusion
  9.1 0.7 broadcast_clamp_fusion
  9.8 4.3 %scatter_custom_fusion = s32[1792]{0:T(1024)S(1)} fusion(s32[1024]{0:T(1024)S(1)} %get-tuple-element.8, s32[1024]{0:T(1024)S(1)} %get-tuple-element.9, s32[]{:T(128)} %constant.25.clone.1), kind=kCustom, calls=%fused_computation.68 | custom fusion | bytes 7172 | tf_op jit(solution)/shard_map/scatter | solution.py:67
  14.1 0.7 all_to_all.12
  14.8 7.3 %all-to-all-start = ((s32[32,1,56]{2,1,0:T(1,128)}), s32[32,1,56]{2,1,0:T(1,128)S(1)}, u32[]{:S(2)}, u32[]{:S(2)}) async-start(s32[32,1,56]{2,1,0:T(1,128)} %all_to_all.12), calls=%async_computation | async-start | bytes 32768 | tf_op jit(solution)/shard_map/all_to_all | solution.py:76
  22.2 4.3 %scatter_custom_fusion.1 = bf16[1792,128]{1,0:T(8,128)(2,1)} fusion(s32[1024]{0:T(1024)S(1)} %get-tuple-element.8, bf16[1024,128]{1,0:T(8,128)(2,1)} %param.9, bf16[]{:T(256)} %constant.24.clone.1), kind=kCustom, calls=%fused_computation.20 | custom fusion | bytes 459264 | tf_op jit(solution)/shard_map/scatter | solution.py:66
  26.4 1.5 fusion.28
  27.9 1.3 all-to-all-done
  29.3 4.5 %all-to-all-start.1 = ((bf16[32,56,128]{2,1,0:T(8,128)(2,1)}), bf16[32,56,128]{2,1,0:T(8,128)(2,1)S(1)}, u32[]{:S(2)}, u32[]{:S(2)}) async-start(bf16[32,56,128]{2,1,0:T(8,128)(2,1)} %bitcast.1), calls=%async_computation.1 | async-start | bytes 917504 | tf_op jit(solution)/shard_map/all_to_all | solution.py:69
  33.8 1.3 pad_add_fusion
  35.1 1.9 %pad_add_fusion.1 = s32[3]{0:T(128)S(1)} fusion(s32[1]{0:T(128)} %get-tuple-element.28, s32[1]{0:T(128)} %get-tuple-element.29, s32[1]{0:T(128)} %get-tuple-element.26), kind=kLoop, calls=%fused_computation.75 | loop fusion | flops 6 | bytes 24 | tf_op jit(solution)/shard_map/stack | solution.py:28
  37.8 0.7 reduce.8
  38.7 10.1 %all-to-all-done.1 = bf16[32,56,128]{2,1,0:T(8,128)(2,1)S(1)} async-done(((bf16[32,56,128]{2,1,0:T(8,128)(2,1)}), bf16[32,56,128]{2,1,0:T(8,128)(2,1)S(1)}, u32[]{:S(2)}, u32[]{:S(2)}) %all-to-all-start.1) | async-done | bytes 458784 | tf_op jit(solution)/shard_map/all_to_all | solution.py:69
  48.7 8.2 %scatter_custom_fusion.2 = bf16[1792,128]{1,0:T(8,128)(2,1)S(1)} fusion(s32[1792]{0:T(1024)S(1)} %get-tuple-element.6, bf16[1792,128]{1,0:T(8,128)(2,1)S(1)} %bitcast.90, bf16[]{:T(256)} %constant.24.clone.1), kind=kCustom, calls=%fused_computation.18 | custom fusion | bytes 458754 | tf_op jit(solution)/shard_map/scatter | solution.py:87
  57.3 1.2 copy-done.2
  59.7 8.9 %convolution_bitcast_fusion.2 = f32[128,1792]{1,0:T(8,128)S(1)} fusion(bf16[2,1792,1792]{2,1,0:T(8,128)(2,1)} %param.13, bf16[1,1792,128]{1,2,0:T(8,128)(2,1)S(1)} %maximum_bitcast_fusion, bf16[1,1792,128]{1,2,0:T(8,128)(2,1)S(1)} %bitcast.87), kind=kOutput, calls=%fused_computation.7 | convolution fusion | flops 1644625920 | bytes 14680064 | tf_op jit(solution)/shard_map/prc,pcn->rn/dot_general | solution.py:92
  68.8 1.1 convolution_bitcast_fusion.3
  69.9 2.1 %collective-permute-start.6 = (bf16[64,128]{1,0:T(8,128)(2,1)S(1)}, bf16[64,128]{1,0:T(8,128)(2,1)S(1)}, u32[]{:S(2)}, u32[]{:S(2)}) collective-permute-start(bf16[64,128]{1,0:T(8,128)(2,1)S(1)} %get-tuple-element.18), channel_id=1, source_target_pairs={{0,2},{2,0},{1,3},{3,1},{4,6},{6,4},{5,7},{7,5},{8,10},{10,8},{9,1... | collective-permute-start | bytes 49160 | tf_op jit(solution)/shard_map/ppermute | solution.py:14
  72.0 0.7 collective-permute-done.3
  72.8 49.7 %all-reduce.2.cloned.1.call-done = f32[2,128,128]{1,2,0:T(8,128)} async-done(((f32[2,128,128]{1,2,0:T(8,128)}), f32[2,128,128]{1,2,0:T(8,128)}) %all-reduce.2.cloned.1.call-update) | async-done | bytes 131088 | tf_op jit(solution)/shard_map/psum | solution.py:103
  122.4 0.9 fusion.27
  123.3 1.5 collective-permute-start
  125.3 3.1 %collective-permute-done = f32[2,128,128]{1,2,0:T(8,128)S(1)} collective-permute-done((f32[2,128,128]{1,2,0:T(8,128)S(1)}, f32[2,128,128]{1,2,0:T(8,128)S(1)}, u32[]{:S(2)}, u32[]{:S(2)}) %collective-permute-start) | collective-permute-done | bytes 131104 | tf_op jit(solution)/shard_map/ppermute | solution.py:14
  128.4 0.9 slice_bitcast_fusion.2
  129.2 1.5 collective-permute-start.1
  130.8 1.8 convolution_bitcast_fusion
  133.3 1.7 fusion.2
  135.0 1.5 copy.31
  136.5 4.2 %gather_fusion = f32[1792,128]{1,0:T(8,128)} fusion(f32[1792,128]{1,0:T(8,128)S(1)} %copy.31, s32[2048]{0:T(1024)S(1)} %pad_clamp_fusion), kind=kCustom, calls=%fused_computation | custom fusion | bytes 1842176 | tf_op jit(solution)/shard_map/gather | solution.py:128
  140.7 28.4 %all_to_all.19 = f32[32,56,128]{2,1,0:T(8,128)S(1)} all-to-all(f32[32,56,128]{2,1,0:T(8,128)} %bitcast.89), channel_id=1, replica_groups=mesh['group'=4,'member'=8] {'group','member'}, dimensions={0} | all-to-all | bytes 1835008 | tf_op jit(solution)/shard_map/all_to_all | solution.py:129
  169.1 4.0 %gather_fusion.1 = f32[1024,128]{1,0:T(8,128)} fusion(f32[1792,128]{1,0:T(8,128)S(1)} %bitcast.85, s32[1024]{0:T(1024)S(1)} %get-tuple-element.7), kind=kCustom, calls=%fused_computation.1 | custom fusion | bytes 1052672 | tf_op jit(solution)/shard_map/gather | solution.py:137
  (45 shorter events, 4.6 us)
Async XLA Ops:
  6.5 126.8 %copy-start = (bf16[2,2,1792,128]{3,2,1,0:T(8,128)(2,1)S(1)}, bf16[2,2,1792,128]{3,2,1,0:T(8,128)(2,1)}, u32[]{:S(2)}) copy-start(bf16[2,2,1792,128]{3,2,1,0:T(8,128)(2,1)} %param.14) | copy-start | bytes 5505028
  14.8 14.4 %all-to-all-start = ((s32[32,1,56]{2,1,0:T(1,128)}), s32[32,1,56]{2,1,0:T(1,128)S(1)}, u32[]{:S(2)}, u32[]{:S(2)}) async-start(s32[32,1,56]{2,1,0:T(1,128)} %all_to_all.12), calls=%async_computation | async-start | bytes 32768 | tf_op jit(solution)/shard_map/all_to_all | solution.py:76
  29.3 19.5 %all-to-all-start.1 = ((bf16[32,56,128]{2,1,0:T(8,128)(2,1)}), bf16[32,56,128]{2,1,0:T(8,128)(2,1)S(1)}, u32[]{:S(2)}, u32[]{:S(2)}) async-start(bf16[32,56,128]{2,1,0:T(8,128)(2,1)} %bitcast.1), calls=%async_computation.1 | async-start | bytes 917504 | tf_op jit(solution)/shard_map/all_to_all | solution.py:69
  33.8 88.7 %all-reduce.2.cloned.1.call-start = ((), (), s32[]{:S(2)}) async-start(), calls=%async_computation.3 | async-start | bytes 262144 | tf_op jit(solution)/shard_map/psum | solution.py:103
  57.2 1.3 copy-start.2
  59.1 65.8 %collective-permute-start.7 = (bf16[64,128]{1,0:T(8,128)(2,1)S(1)}, bf16[64,128]{1,0:T(8,128)(2,1)S(1)}, u32[]{:S(2)}, u32[]{:S(2)}) collective-permute-start(bf16[64,128]{1,0:T(8,128)(2,1)S(1)} %fusion.15), channel_id=1, source_target_pairs={{0,1},{1,0},{2,3},{3,2},{4,5},{5,4},{6,7},{7,6},{8,9},{9,8},{10,11... | collective-permute-start | bytes 49160 | tf_op jit(solution)/shard_map/ppermute | solution.py:14
  59.2 9.5 %collective-permute-start.2 = (f32[64,128]{1,0:T(8,128)S(1)}, f32[64,128]{1,0:T(8,128)S(1)}, u32[]{:S(2)}, u32[]{:S(2)}) collective-permute-start(f32[64,128]{1,0:T(8,128)S(1)} %get-tuple-element.19), channel_id=1, source_target_pairs={{0,1},{1,0},{2,3},{3,2},{4,5},{5,4},{6,7},{7,6},{8,9},{9,8},{10,11... | collective-permute-start | bytes 98312 | tf_op jit(solution)/shard_map/ppermute | solution.py:14
  59.6 9.2 %copy-start.1 = (bf16[2,2,1792,128]{3,2,1,0:T(8,128)(2,1)S(1)}, bf16[2,2,1792,128]{3,2,1,0:T(8,128)(2,1)}, u32[]{:S(2)}) copy-start(bf16[2,2,1792,128]{3,2,1,0:T(8,128)(2,1)} %param.15) | copy-start | bytes 5505028
  59.6 9.1 %collective-permute-start.5 = (f32[64,128]{1,0:T(8,128)S(1)}, f32[64,128]{1,0:T(8,128)S(1)}, u32[]{:S(2)}, u32[]{:S(2)}) collective-permute-start(f32[64,128]{1,0:T(8,128)S(1)} %get-tuple-element.20), channel_id=1, source_target_pairs={{0,1},{1,0},{2,3},{3,2},{4,5},{5,4},{6,7},{7,6},{8,9},{9,8},{10,11... | collective-permute-start | bytes 98312 | tf_op jit(solution)/shard_map/ppermute | solution.py:14
  68.7 4.0 %collective-permute-start.3 = (f32[64,128]{1,0:T(8,128)S(1)}, f32[64,128]{1,0:T(8,128)S(1)}, u32[]{:S(2)}, u32[]{:S(2)}) collective-permute-start(f32[64,128]{1,0:T(8,128)S(1)} %get-tuple-element.17), channel_id=1, source_target_pairs={{0,2},{2,0},{1,3},{3,1},{4,6},{6,4},{5,7},{7,5},{8,10},{10,8},{9,1... | collective-permute-start | bytes 98312 | tf_op jit(solution)/shard_map/ppermute | solution.py:14
  69.9 55.0 %collective-permute-start.6 = (bf16[64,128]{1,0:T(8,128)(2,1)S(1)}, bf16[64,128]{1,0:T(8,128)(2,1)S(1)}, u32[]{:S(2)}, u32[]{:S(2)}) collective-permute-start(bf16[64,128]{1,0:T(8,128)(2,1)S(1)} %get-tuple-element.18), channel_id=1, source_target_pairs={{0,2},{2,0},{1,3},{3,1},{4,6},{6,4},{5,7},{7,5},{8,10},{10,8},{9,1... | collective-permute-start | bytes 49160 | tf_op jit(solution)/shard_map/ppermute | solution.py:14
  72.7 52.2 %collective-permute-start.4 = (bf16[64,128]{1,0:T(8,128)(2,1)S(1)}, bf16[64,128]{1,0:T(8,128)(2,1)S(1)}, u32[]{:S(2)}, u32[]{:S(2)}) collective-permute-start(bf16[64,128]{1,0:T(8,128)(2,1)S(1)} %add_convert_fusion.1), channel_id=1, source_target_pairs={{0,4},{4,0},{1,5},{5,1},{2,6},{6,2},{3,7},{7,3},{8,12},{12,8},{9,1... | collective-permute-start | bytes 49160 | tf_op jit(solution)/shard_map/ppermute | solution.py:14
  123.3 5.0 %collective-permute-start = (f32[2,128,128]{1,2,0:T(8,128)S(1)}, f32[2,128,128]{1,2,0:T(8,128)S(1)}, u32[]{:S(2)}, u32[]{:S(2)}) collective-permute-start(f32[2,128,128]{1,2,0:T(8,128)S(1)} %pad_maximum_fusion.4), channel_id=1, source_target_pairs={{0,8},{8,0},{16,24},{24,16},{1,9},{9,1},{17,25},{25,17},{2,10},{10... | collective-permute-start | bytes 393224 | tf_op jit(solution)/shard_map/ppermute | solution.py:14
  129.2 4.0 %collective-permute-start.1 = (bf16[1,128,128]{1,2,0:T(8,128)(2,1)S(1)}, bf16[1,128,128]{1,2,0:T(8,128)(2,1)S(1)}, u32[]{:S(2)}, u32[]{:S(2)}) collective-permute-start(bf16[1,128,128]{1,2,0:T(8,128)(2,1)S(1)} %get-tuple-element.14), channel_id=1, source_target_pairs={{0,16},{16,0},{8,24},{24,8},{1,17},{17,1},{9,25},{25,9},{2,18},{18... | collective-permute-start | bytes 98312 | tf_op jit(solution)/shard_map/ppermute | solution.py:14
Sparse Core Ops, SparseCore 0:
  70.0 52.3 all-reduce.1
where the time goes:
time: 181 us; the launch traced here: 180 us
  waiting for transfers between devices  65.6 us (36%)
  local copies, waits for them, and re-layouts  32.6 us (18%)
  blocking collectives  28.4 us (16%)
  starting transfers between devices  17.8 us (10%)
  matrix products  14 us (8%)
  between operations  13.7 us (8%)
  other arithmetic  7.9 us (4%)
    psum x1, waiting for transfers between devices, on_device(): member_summed = lax.psum(top_part, 'member')  49.7 us
    all_to_all x1, blocking collectives, on_device(): lax.all_to_all(leaving.reshape(leaves, bucket, columns), ('group', 'membe...  28.4 us
    all_to_all x1, waiting for transfers between devices, on_device(): lax.all_to_all(outgoing.reshape(leaves, bucket, columns), ('group', 'memb...  10.1 us
    dot_general x1, matrix products, on_device(): jnp.einsum('prc,pcn->rn', diag_block, paired, preferred_element_type=jnp....  8.93 us
    scatter x2, local copies, waits for them, and re-layouts, on_device(): jnp.zeros((capacity, columns), mesh_vector.dtype).at[slot_ids]  8.41 us
    all_to_all x1, starting transfers between devices, on_device(): lax.all_to_all(targets.reshape(leaves, bucket), ('group', 'member'), spli...  7.3 us
    ppermute x8, starting transfers between devices, partner(): return lax.ppermute(block, axis, route)  5.97 us
    all_to_all x1, starting transfers between devices, on_device(): lax.all_to_all(outgoing.reshape(leaves, bucket, columns), ('group', 'memb...  4.51 us
  transfers between devices with their start and end apart: 11, of which 6 were waited for; matrix products, arithmetic and copies ran while one was open for 13% of the time, Pallas kernels for 0%

commit v1 on v0

v1 whole, which is shorter than its diff:
```python
import functools

import jax
import jax.numpy as jnp
from jax import lax
from jax.experimental import pallas as pl
from jax.experimental.pallas import tpu as pltpu
from jax.sharding import PartitionSpec as P

F32 = jnp.float32
BF16 = jnp.bfloat16
I32 = jnp.int32
VMEM = pl.BlockSpec(memory_space=pltpu.VMEM)
SMEM = pl.BlockSpec(memory_space=pltpu.SMEM)
HBM = pl.BlockSpec(memory_space=pltpu.HBM)
DMA = pltpu.SemaphoreType.DMA


def iota(shape, dim):
    return lax.broadcasted_iota(I32, shape, dim)


def hot(mask):
    return jnp.where(mask, 1.0, 0.0).astype(BF16)


def dot(a, b, over=(1, 0)):
    return lax.dot_general(
        a, b, (((over[0],), (over[1],)), ((), ())), preferred_element_type=F32
    )


def call(kernel, outs, ins, args, flops, moved, limit, scratch=(), **more):
    return pl.pallas_call(
        kernel,
        out_shape=outs,
        in_specs=ins,
        out_specs=more.pop("out_specs", [VMEM] * len(outs)),
        scratch_shapes=scratch,
        cost_estimate=pl.CostEstimate(flops=flops, bytes_accessed=moved, transcendentals=0),
        compiler_params=pltpu.CompilerParams(vmem_limit_bytes=limit << 20),
        **more,
    )(*args)


def partner(block, axis, apart):
    count = lax.axis_size(axis)
    route = []
    for low in range(count):
        high = low | 1 << apart
        if high != low and high < count:
            route += [(low, high), (high, low)]
    return lax.ppermute(block, axis, route)


def far(*arrays):
    return [pltpu.with_memory_space_constraint(array, pltpu.HBM) for array in arrays]


def turn(block):
    half = block.shape[1] // 2
    return jnp.where(iota(block.shape, 1) < half, -1.0, 1.0) * pltpu.roll(block, half, 1)


def pack_kernel(leaves, bucket, sizes_in, position_in, rows_in, packed, windows, *scratch):
    sizes, position, rows, ordered, sems = scratch
    copies = [
        pltpu.make_async_copy(source, target, sems.at[i])
        for i, (source, target) in enumerate(
            [(sizes_in, sizes), (position_in, position), (rows_in, rows)]
        )
    ]
    for copy in copies:
        copy.start()
    for copy in copies[:2]:
        copy.wait()
    count = rows.shape[0]
    padded = packed.shape[1]
    shift = leaves.bit_length() - 1
    here = position[...]
    window = jnp.right_shift(here, shift)
    zero = jnp.zeros((1, count), I32)
    owner, first = zero, zero
    starts = [0]
    for c in range(leaves):
        starts.append(starts[-1] + jnp.right_shift(sizes[c], shift))
        beyond = window >= starts[-1]
        owner = owner + beyond.astype(I32)
        first = jnp.where(beyond, starts[-1], first)
    offset = jnp.bitwise_and(here, leaves - 1).astype(F32)
    picked = jnp.where(iota((leaves, count), 0) == owner, offset, 0.0).astype(BF16)
    offsets = dot(picked, hot(iota((128, count), 0) == window - first), (1, 1))
    windows[...] = jnp.transpose(jnp.broadcast_to(window, (128, count)))
    copies[2].wait()
    values = rows[...]
    block = 256
    for low in range(0, count, block):
        ordered[low : low + block, :] = dot(hot(iota((block, count), 0) + low == window), values)
    ordered[count:, :] = jnp.zeros((padded, 128), F32)
    line = iota((padded, 128), 0)
    for c in range(leaves):
        data = ordered[pl.ds(starts[c], padded), :]
        data = jnp.where(line < starts[c + 1] - starts[c], data, 0.0)
        data = jnp.where(line == bucket, offsets[c : c + 1, :], data)
        packed[c] = data.astype(BF16)


def stage_kernel(left_top_in, left_low_in, after, left_top, left_low, raw, sems):
    copies = [
        pltpu.make_async_copy(left_low_in, raw, sems.at[0]),
        pltpu.make_async_copy(left_top_in, left_top, sems.at[1]),
    ]
    for copy in copies:
        copy.start()
    copies[0].wait()
    levels, parts, width, capacity = raw.shape
    left_low[...] = jnp.transpose(raw[...].reshape(levels * parts * width, capacity))
    copies[1].wait()


def field_kernel(leaves, bucket, place, arrived, right_top_in, right_low_in, *rest):
    pair, targets, send, keep, whole, right_top, right_low, sems = rest
    copies = [
        pltpu.make_async_copy(right_low_in, right_low, sems.at[0]),
        pltpu.make_async_copy(right_top_in, right_top, sems.at[1]),
    ]
    for copy in copies:
        copy.start()
    capacity = leaves * bucket
    padded = arrived.shape[1]
    part = leaves * 8
    core = jnp.bitwise_and(place[0], 1)
    last = arrived[:, padded - 16 :, :].reshape(leaves * 16, 128)
    carrier = iota((leaves, leaves * 16), 1) == iota((leaves, leaves * 16), 0) * 16 + bucket % 16
    offsets = dot(hot(carrier), last).astype(BF16)
    spread = hot(jnp.right_shift(iota((leaves, part), 1), 3) == iota((leaves, part), 0))
    spread_offsets = dot(offsets, spread, (0, 0))
    lane_window = jnp.bitwise_and(iota((8, part), 1), 7)
    own = lane_window == iota((8, part), 0)
    for g in range(padded // 8):
        size = min(part, capacity - g * part)
        if size <= 0:
            continue
        rows = spread_offsets[g * 8 : g * 8 + 8, :]
        offset = jnp.sum(jnp.where(own, rows, 0.0), axis=0, keepdims=True).astype(I32)
        target = offset + lane_window[:1, :] * leaves
        targets[g * part : (g + 1) * part, :] = jnp.transpose(
            jnp.broadcast_to(target, (128, part))
        )
        if g % 2 == 0:
            both = arrived[:, g * 8 : g * 8 + 16, :].astype(F32)
        chunk = both[:, g % 2 * 8 : g % 2 * 8 + 8, :].reshape(part, 128).astype(BF16)
        placed = dot(hot(iota((part, part), 0) == target), chunk)
        pair[0, g * part : g * part + size, :] = placed[:size].astype(BF16)
        pair[1, g * part : g * part + size, :] = turn(placed)[:size].astype(BF16)
    for copy in copies:
        copy.wait()
    levels, _, width, _ = right_low.shape
    top_levels, _, _, top_width = right_top.shape
    total = jnp.zeros((levels * width, 128), F32)
    tops = jnp.zeros((128, top_levels * top_width), F32)
    for p in range(2):
        total += dot(right_low[:, p].reshape(levels * width, capacity), pair[p])
        factors = jnp.concatenate([right_top[level, p] for level in range(top_levels)], axis=1)
        tops += dot(jnp.transpose(pair[p]), factors)
    for level in range(top_levels):
        whole[level * 128 : (level + 1) * 128, :] = tops[:, level * top_width : (level + 1) * top_width]
    whole[top_levels * 128 :, :] = total
    at = 0
    for low, half in segments(top_levels, levels, width):
        mine = pl.multiple_of(low + core * half, 8)
        other = pl.multiple_of(low + (1 - core) * half, 8)
        keep[at : at + half, :] = whole[pl.ds(mine, half), :]
        send[at : at + half, :] = whole[pl.ds(other, half), :]
        at += half
    send[at:, :] = total[(levels - 1) * width :]


def segments(top_levels, levels, width):
    tops = [(level * 128, 64) for level in range(top_levels)]
    return tops + [(top_levels * 128 + level * width, width // 2) for level in range(levels - 1)]


def diag_kernel(block, pair, after, out):
    out[...] = dot(block[0], pair[0]) + dot(block[1], pair[1])


def out_kernel(leaves, bucket, pieces, place, *rest):
    bases = rest[:pieces]
    left_top, left_low, nearest, own, theirs, targets, packed, spare, ordered = rest[pieces:]
    capacity = leaves * bucket
    part = leaves * 8
    groups = spare.shape[0] // part
    top_levels = left_top.shape[0]
    width = nearest.shape[0]
    levels = left_low.shape[1] // (2 * width)
    core = jnp.bitwise_and(place[0], 1)
    coefs = []
    at = 0
    for _, half in segments(top_levels, levels, width):
        a, b = own[at : at + half, :].astype(F32), theirs[at : at + half, :].astype(F32)
        first, second = jnp.where(core == 0, a, b), jnp.where(core == 0, b, a)
        coefs.append(jnp.concatenate([first, second], axis=0))
        at += half
    coefs.append(nearest[...])
    tops, lows = [], []
    for level, coef in enumerate(coefs):
        lanes = level < top_levels
        coef = jnp.where(iota(coef.shape, 1 if lanes else 0) < place[1 + level], coef, 0.0)
        if lanes:
            half = coef.shape[0] // 2
            tops += [coef, jnp.concatenate([-coef[half:], coef[:half]], axis=0)]
        else:
            lows += [coef, turn(coef)]
    stacked = jnp.concatenate([jnp.transpose(coef) for coef in tops] + lows, axis=0).astype(BF16)
    cut = capacity // pieces
    for i in range(pieces):
        rows = slice(i * cut, (i + 1) * cut)
        factors = [left_top[level, p, rows, :] for level in range(top_levels) for p in range(2)]
        factors = jnp.concatenate(factors + [left_low[rows, :]], axis=1)
        spare[rows, :] = (bases[i][...] + dot(factors, stacked)).astype(BF16)
    if groups * part > capacity:
        spare[capacity:, :] = jnp.zeros((groups * part - capacity, 128), BF16)
    lanes = iota((part, 128), 1)
    for g in range(groups):
        target = targets[g * part : (g + 1) * part, :]
        picks = [hot(target == lanes + low) for low in range(0, part, 128)]
        moved = dot(jnp.concatenate(picks, axis=1), spare[g * part : (g + 1) * part, :])
        ordered[:, g * 8 : g * 8 + 8, :] = moved.reshape(leaves, 8, 128)
    packed[...] = ordered[:, :bucket, :].reshape(capacity, 128).astype(BF16)


def unpack_kernel(leaves, bucket, sizes, windows, returned, out, wide, ordered):
    count = windows.shape[0]
    shift = leaves.bit_length() - 1
    wide[...] = returned[...].astype(F32)
    start = 0
    for c in range(leaves):
        ordered[pl.ds(start, bucket), :] = wide[c * bucket : (c + 1) * bucket, :]
        start += jnp.right_shift(sizes[c], shift)
    values = ordered[:count, :].astype(BF16)
    block = 256
    lanes = iota((block, 128), 1)
    for low in range(0, count, block):
        window = windows[low : low + block, :]
        picks = [hot(window == lanes + at) for at in range(0, count, 128)]
        out[low : low + block, :] = dot(jnp.concatenate(picks, axis=1), values)


def on_device(
    mesh_vector,
    cluster_position,
    cluster_sizes,
    block_ranks,
    diag_block,
    top_left,
    top_right,
    low_left,
    low_right,
):
    groups = lax.axis_size("group")
    members = lax.axis_size("member")
    leaves = groups * members
    group_levels = groups.bit_length() - 1
    member_levels = members.bit_length() - 1
    levels = group_levels + member_levels
    device = lax.axis_index("group") * members + lax.axis_index("member")
    capacity = diag_block.shape[1]
    bucket = capacity // leaves
    padded = (bucket + 16) // 16 * 16
    filled = (bucket + 7) // 8 * 8
    count, columns = mesh_vector.shape
    everyone = ("group", "member")
    low_left = jnp.swapaxes(low_left, 2, 3)
    low_right = jnp.swapaxes(low_right, 2, 3)
    width = low_left.shape[2]
    top_width = top_left.shape[3]
    far_flops = 4 * capacity * columns * (group_levels * top_width + member_levels * width)

    level_ids = jnp.arange(1, levels + 1, dtype=I32)
    ranks = block_ranks[(1 << level_ids) - 2 + jnp.right_shift(device, levels - level_ids)]
    place = jnp.concatenate([device[None].astype(I32), ranks])

    packed, windows = call(
        functools.partial(pack_kernel, leaves, bucket),
        [
            jax.ShapeDtypeStruct((leaves, padded, columns), BF16),
            jax.ShapeDtypeStruct((count, 128), I32),
        ],
        [HBM] * 3,
        far(cluster_sizes, cluster_position.reshape(1, count), mesh_vector),
        2 * count * count * columns,
        4 << 20,
        16,
        scratch=[
            pltpu.SMEM((leaves,), I32),
            pltpu.VMEM((1, count), I32),
            pltpu.VMEM((count, columns), BF16),
            pltpu.VMEM((count + padded, columns), F32),
            DMA((3,)),
        ],
    )
    arrived = lax.all_to_all(packed, everyone, split_axis=0, concat_axis=0, tiled=True)
    shared = group_levels * columns // 2 + (member_levels - 1) * width // 2
    pair, targets, send, keep = call(
        functools.partial(field_kernel, leaves, bucket),
        [
            jax.ShapeDtypeStruct((2, capacity, columns), BF16),
            jax.ShapeDtypeStruct((leaves * filled, 128), I32),
            jax.ShapeDtypeStruct((shared + width, columns), F32),
            jax.ShapeDtypeStruct((shared, columns), F32),
        ],
        [SMEM, VMEM, HBM, HBM],
        (place, arrived, *far(top_right, low_right)),
        far_flops,
        6 << 20,
        24,
        scratch=[
            pltpu.VMEM((group_levels * columns + member_levels * width, columns), F32),
            pltpu.VMEM(top_right.shape, BF16),
            pltpu.VMEM(low_right.shape, BF16),
            DMA((2,)),
        ],
    )
    pieces = 2
    cut = capacity // pieces
    rows = cut // 4

    def diagonal(i, after):
        return call(
            diag_kernel,
            jax.ShapeDtypeStruct((cut, columns), F32),
            [
                pl.BlockSpec((2, rows, capacity), lambda j: (0, j + 4 * i, 0)),
                pl.BlockSpec((2, capacity, columns), lambda j: (0, 0, 0)),
                pl.BlockSpec(memory_space=pl.ANY),
            ],
            (*far(diag_block), pair, after),
            4 * cut * capacity * columns,
            4 * cut * capacity,
            16,
            grid=(4,),
            out_specs=pl.BlockSpec((rows, columns), lambda j: (j, 0)),
        )

    received = partner(send, "member", 0)
    nearest = received[shared:]
    running = keep + received[:shared]
    bases = []
    coefs = []
    for bit in range(1, member_levels):
        rest = running.shape[0] - width // 2
        received = partner(running, "member", bit)
        if len(bases) < pieces:
            bases.append(diagonal(len(bases), running))
            received, bases[-1] = lax.optimization_barrier((received, bases[-1]))
        coefs.insert(0, received[rest:].astype(BF16))
        running = running[:rest] + received[:rest]
    left_top, left_low = call(
        stage_kernel,
        [
            pltpu.VMEM(top_left.shape, BF16),
            pltpu.VMEM((capacity, member_levels * 2 * width), BF16),
        ],
        [HBM, HBM, pl.BlockSpec(memory_space=pl.ANY)],
        (*far(top_left, low_left), running),
        0,
        8 << 20,
        16,
        scratch=[pltpu.VMEM(low_left.shape, BF16), DMA((2,))],
    )
    half = columns // 2
    tops = [None] * group_levels
    for apart in range(1, groups):
        level = group_levels - apart.bit_length()
        sent = running[level * half : (level + 1) * half]
        if apart == 1:
            sent = sent.astype(BF16)
        route = [(low, low ^ apart) for low in range(groups)]
        heard = lax.ppermute(sent, "group", route)
        tops[level] = heard if tops[level] is None else tops[level] + heard
    left_top, left_low, tops = lax.optimization_barrier((left_top, left_low, tops))
    own = jnp.concatenate([top.astype(BF16) for top in tops] + coefs)
    theirs = partner(own, "member", 0)

    leaving = call(
        functools.partial(out_kernel, leaves, bucket, pieces),
        [jax.ShapeDtypeStruct((capacity, columns), BF16)],
        [SMEM] + [VMEM] * (pieces + 6),
        (place, *bases, left_top, left_low, nearest, own, theirs, targets),
        far_flops,
        6 << 20,
        24,
        scratch=[
            pltpu.VMEM((leaves * filled, 128), BF16),
            pltpu.VMEM((leaves, filled, 128), F32),
        ],
    )[0]
    returned = lax.all_to_all(
        leaving.reshape(leaves, bucket, columns), everyone, split_axis=0, concat_axis=0, tiled=True
    )
    return call(
        functools.partial(unpack_kernel, leaves, bucket),
        [jax.ShapeDtypeStruct((count, columns), F32)],
        [SMEM] + [VMEM] * 2,
        (cluster_sizes, windows, returned.reshape(capacity, columns)),
        2 * count * count * columns,
        2 << 20,
        16,
        scratch=[
            pltpu.VMEM((capacity, 128), F32),
            pltpu.VMEM((count + filled, 128), F32),
        ],
    )[0]


def solution(mesh):
    return jax.shard_map(
        on_device,
        mesh=mesh,
        in_specs=(
            P(("group", "member"), None),
            P(("group", "member")),
            P(),
            P(),
            P(None, ("group", "member"), None),
            P(None, None, ("group", "member"), None),
            P(None, None, ("group", "member"), None),
            P(None, None, ("group", "member"), None),
            P(None, None, ("group", "member"), None),
        ),
        out_specs=P(("group", "member"), None),
        check_vma=False,
    )
```

time: 181 us -> 73 us (0.40)
  waiting for transfers between devices: 65.6 us -> 20.2 us
  local copies, waits for them, and re-layouts: 32.6 us -> 0.67 us
  Pallas kernels: 0 us -> 21.9 us
  matrix products: 14 us -> 0 us
  between operations: 13.7 us -> 0.15 us
  blocking collectives: 28.4 us -> 17.8 us
  other arithmetic: 7.9 us -> 0.14 us
  starting transfers between devices: 17.8 us -> 11.9 us
    psum x1 -> x0, waiting for transfers between devices: 49.7 us -> none  [on_device(): member_summed = lax.psum(top_part, 'member')]
    pallas_call x0 -> x7, Pallas kernels: none -> 21.9 us  [call(): pl.pallas_call(kernel, out_shape=outs, in_specs=ins, out_specs=more.pop('...]
    scatter x4 -> x0, local copies, waits for them, and re-layouts: 17 us -> none  [the longest x2 8.41 us: on_device(): jnp.zeros((capacity, columns), mesh_vector.dtype).at[slot_ids]]
    dot_general x5 -> x0, matrix products: 14 us -> none  [the longest x1 8.93 us: on_device(): jnp.einsum('prc,pcn->rn', diag_block, paired, preferred_element_type=jnp....]
    all_to_all x1, blocking collectives: 28.4 us -> 17.8 us  [on_device(): lax.all_to_all(leaving.reshape(leaves, bucket, columns), everyone, split_...]
    gather x2 -> x1, local copies, waits for them, and re-layouts: 8.23 us -> 0.64 us  [on_device(): block_ranks[(1 << level_ids) - 2 + jnp.right_shift(device, levels - level...]
    ppermute x8 -> x4, starting transfers between devices: 5.97 us -> 1.04 us  [partner(): return lax.ppermute(block, axis, route)]
    all_to_all x2 -> x1, starting transfers between devices: 11.8 us -> 7.3 us  [on_device(): lax.all_to_all(packed, everyone, split_axis=0, concat_axis=0, tiled=True)]
  transfers between devices with their start and end apart: 11 -> 8, of which waited for: 6 -> 6; matrix products, arithmetic and copies ran while one was open for 13% -> 1% of each run, Pallas kernels for 0% -> 16%
where the time goes in v1:
time: 73 us; the launch traced here: 72.7 us
  Pallas kernels  21.9 us (30%)
  waiting for transfers between devices  20.2 us (28%)
  blocking collectives  17.8 us (24%)
  starting transfers between devices  11.9 us (16%)
    pallas_call x7, Pallas kernels, call(): pl.pallas_call(kernel, out_shape=outs, in_specs=ins, out_specs=more.pop('...  21.9 us
    all_to_all x1, blocking collectives, on_device(): lax.all_to_all(leaving.reshape(leaves, bucket, columns), everyone, split_...  17.8 us
    all_to_all x1, waiting for transfers between devices, on_device(): lax.all_to_all(packed, everyone, split_axis=0, concat_axis=0, tiled=True)  15.6 us
    all_to_all x1, starting transfers between devices, on_device(): lax.all_to_all(packed, everyone, split_axis=0, concat_axis=0, tiled=True)  7.3 us
    ppermute x4, waiting for transfers between devices, partner(): return lax.ppermute(block, axis, route)  4.17 us
    ppermute x3, starting transfers between devices, on_device(): heard = lax.ppermute(sent, 'group', route)  3.55 us
  transfers between devices with their start and end apart: 8, of which 6 were waited for; matrix products, arithmetic and copies ran while one was open for 1% of the time, Pallas kernels for 16%

profile of v1, /device:TPU:0, one launch (start us, length us, event | category | flops | bytes accessed | tf_op | source)
XLA Modules:
  0.0 72.7 jit_solution(14814179500305864779)
XLA Ops:
  0.0 0.0 copy-start
  0.0 2.8 %shard_map.91 = (bf16[32,64,128]{2,1,0:T(8,128)(2,1)}, s32[1024,128]{1,0:T(8,128)S(1)}) custom-call(s32[32]{0:T(128)} %sizes.1, s32[1,1024]{1,0:T(1,128)} %bitcast.12, bf16[1024,128]{1,0:T(8,128)(2,1)} %rows_in.1), custom_call_target="tpu_custom_call" | custom-call | flops 268435456 | bytes 4194304 | tf_op jit(solution)/shard_map/pallas_call | solution.py:34
  2.9 7.3 %all-to-all-start = ((bf16[32,64,128]{2,1,0:T(8,128)(2,1)}), bf16[32,64,128]{2,1,0:T(8,128)(2,1)S(1)}, u32[]{:S(2)}, u32[]{:S(2)}) async-start(bf16[32,64,128]{2,1,0:T(8,128)(2,1)} %get-tuple-element.22), calls=%async_computation | async-start | bytes 1048576 | tf_op jit(solution)/shard_map/all_to_all | solution.py:303
  10.2 0.0 copy-done
  10.2 0.6 gather_fusion
  10.9 0.1 pad_add_fusion.place
  10.9 15.6 %all-to-all-done.arrived = bf16[32,64,128]{2,1,0:T(8,128)(2,1)S(1)} async-done(((bf16[32,64,128]{2,1,0:T(8,128)(2,1)}), bf16[32,64,128]{2,1,0:T(8,128)(2,1)S(1)}, u32[]{:S(2)}, u32[]{:S(2)}) %all-to-all-start) | async-done | bytes 524320 | tf_op jit(solution)/shard_map/all_to_all | solution.py:303
  26.5 3.5 %shard_map.92 = (bf16[2,1792,128]{2,1,0:T(8,128)(2,1)S(1)}, s32[1792,128]{1,0:T(8,128)S(1)}, f32[256,128]{1,0:T(8,128)S(1)}, f32[192,128]{1,0:T(8,128)S(1)}) custom-call(s32[6]{0:T(128)S(1)} %pad_add_fusion.place, bf16[32,64,128]{2,1,0:T(8,128)(2,1)S(1)} %all-to-all-done.arrived, bf16[2,2,1792,128]{3,2,1,0:T(8,128)(2,1)} %right_top_in.1, ...), custom_call_target="tpu_custom_call" | custom-call | flops 411041792 | bytes 6291456 | tf_op jit(solution)/shard_map/pallas_call | solution.py:34
  30.1 0.1 collective-permute-start
  30.1 1.3 %collective-permute-done = f32[256,128]{1,0:T(8,128)S(1)} collective-permute-done((f32[256,128]{1,0:T(8,128)S(1)}, f32[256,128]{1,0:T(8,128)S(1)}, u32[]{:S(2)}, u32[]{:S(2)}) %collective-permute-start) | collective-permute-done | bytes 131104 | tf_op jit(solution)/shard_map/ppermute | solution.py:53
  31.5 0.1 collective-permute-start.1
  31.6 4.7 %shard_map.93.rest_0_ = f32[896,128]{1,0:T(8,128)S(1)} custom-call(bf16[2,1792,1792]{2,1,0:T(8,128)(2,1)} %block.3, bf16[2,1792,128]{2,1,0:T(8,128)(2,1)S(1)} %get-tuple-element.25.pair, f32[192,128]{1,0:T(8,128)S(1)} %slice_add_fusion.after), custom_call_target="tpu_custom_call" | custom-call | flops 822083584 | bytes 6422528 | tf_op jit(solution)/shard_map/pallas_call | solution.py:34
  36.3 0.1 collective-permute-done.1
  36.4 0.9 %collective-permute-start.2 = (f32[160,128]{1,0:T(8,128)S(1)}, f32[160,128]{1,0:T(8,128)S(1)}, u32[]{:S(2)}, u32[]{:S(2)}) collective-permute-start(f32[160,128]{1,0:T(8,128)S(1)} %slice_add_fusion.1.after), channel_id=1, source_target_pairs={{0,4},{4,0},{1,5},{5,1},{2,6},{6,2},{3,7},{7,3},{8,12},{12,8},{9,1... | collective-permute-start | bytes 245768 | tf_op jit(solution)/shard_map/ppermute | solution.py:53
  37.3 4.7 %shard_map.94.rest_1_ = f32[896,128]{1,0:T(8,128)S(1)} custom-call(bf16[2,1792,1792]{2,1,0:T(8,128)(2,1)} %block.3, bf16[2,1792,128]{2,1,0:T(8,128)(2,1)S(1)} %get-tuple-element.25.pair, f32[160,128]{1,0:T(8,128)S(1)} %slice_add_fusion.1.after), custom_call_target="tpu_custom_call" | custom-call | flops 822083584 | bytes 6422528 | tf_op jit(solution)/shard_map/pallas_call | solution.py:34
  42.0 1.5 %collective-permute-done.2 = f32[160,128]{1,0:T(8,128)S(1)} collective-permute-done((f32[160,128]{1,0:T(8,128)S(1)}, f32[160,128]{1,0:T(8,128)S(1)}, u32[]{:S(2)}, u32[]{:S(2)}) %collective-permute-start.2) | collective-permute-done | bytes 81952 | tf_op jit(solution)/shard_map/ppermute | solution.py:53
  43.6 0.7 %collective-permute-start.4 = (f32[64,128]{1,0:T(8,128)S(1)}, f32[64,128]{1,0:T(8,128)S(1)}, u32[]{:S(2)}, u32[]{:S(2)}) collective-permute-start(f32[64,128]{1,0:T(8,128)S(1)} %slice.49), channel_id=1, source_target_pairs={{0,24},{8,16},{16,8},{24,0},{1,25},{9,17},{17,9},{25,1},{2,26},{10... | collective-permute-start | bytes 98312 | tf_op jit(solution)/shard_map/ppermute | solution.py:380
  44.3 1.5 %collective-permute-start.3 = (f32[64,128]{1,0:T(8,128)S(1)}, f32[64,128]{1,0:T(8,128)S(1)}, u32[]{:S(2)}, u32[]{:S(2)}) collective-permute-start(f32[64,128]{1,0:T(8,128)S(1)} %slice.49), channel_id=1, source_target_pairs={{0,16},{8,24},{16,0},{24,8},{1,17},{9,25},{17,1},{25,9},{2,18},{10... | collective-permute-start | bytes 98312 | tf_op jit(solution)/shard_map/ppermute | solution.py:380
  45.8 1.3 %collective-permute-start.5 = (bf16[64,128]{1,0:T(8,128)(2,1)S(1)}, bf16[64,128]{1,0:T(8,128)(2,1)S(1)}, u32[]{:S(2)}, u32[]{:S(2)}) collective-permute-start(bf16[64,128]{1,0:T(8,128)(2,1)S(1)} %slice.62), channel_id=1, source_target_pairs={{0,8},{8,0},{16,24},{24,16},{1,9},{9,1},{17,25},{25,17},{2,10},{10... | collective-permute-start | bytes 49160 | tf_op jit(solution)/shard_map/ppermute | solution.py:380
  47.2 1.9 %shard_map.95 = (bf16[2,2,1792,128]{3,2,1,0:T(8,128)(2,1)S(1)}, bf16[1792,384]{1,0:T(8,128)(2,1)S(1)}) custom-call(bf16[2,2,1792,128]{3,2,1,0:T(8,128)(2,1)} %left_top_in.1, bf16[3,2,64,1792]{3,2,1,0:T(8,128)(2,1)} %bitcast.10, f32[128,128]{1,0:T(8,128)S(1)} %slice_add_fusion.2.after), custom_call_target="tpu_custom_call" | custom-call | bytes 8388608 | tf_op jit(solution)/shard_map/pallas_call | solution.py:34
  49.1 0.0 collective-permute-done.4
  49.1 0.0 collective-permute-done.3
  49.1 0.4 collective-permute-done.5
  49.6 0.0 collective-permute-start.6
  49.6 1.2 %collective-permute-done.6.rest_6_ = bf16[192,128]{1,0:T(8,128)(2,1)S(1)} collective-permute-done((bf16[192,128]{1,0:T(8,128)(2,1)S(1)}, bf16[192,128]{1,0:T(8,128)(2,1)S(1)}, u32[]{:S(2)}, u32[]{:S(2)}) %collective-permute-start.6) | collective-permute-done | bytes 49184 | tf_op jit(solution)/shard_map/ppermute | solution.py:53
  50.8 0.0 copy-start.1
  50.8 2.0 %shard_map.96 = bf16[1792,128]{1,0:T(8,128)(2,1)S(1)} custom-call(s32[6]{0:T(128)S(1)} %pad_add_fusion.place, f32[896,128]{1,0:T(8,128)S(1)} %shard_map.93.rest_0_, f32[896,128]{1,0:T(8,128)S(1)} %shard_map.94.rest_1_, bf16[2,2,1792,128]{3,2,1,0:T(8,128)(2,1)S(1)} %get-tuple-element.32.rest_2_, bf16[1792,384]{1,0:T(8,128)(2,1)S(1)} %get-tuple-element.33.rest_3_, ...), custom_call_target="tpu_custom_call" | custom-call | flops 411041792 | bytes 6291456 | tf_op jit(solution)/shard_map/pallas_call | solution.py:34
  52.8 17.8 %all_to_all.10 = bf16[32,56,128]{2,1,0:T(8,128)(2,1)S(1)} all-to-all(bf16[32,56,128]{2,1,0:T(8,128)(2,1)S(1)} %bitcast.8), channel_id=1, replica_groups=mesh['group'=4,'member'=8] {'group','member'}, dimensions={0} | all-to-all | bytes 917504 | tf_op jit(solution)/shard_map/all_to_all | solution.py:399
  70.6 0.0 copy-done.1
  70.6 2.1 %shard_map.97 = f32[1024,128]{1,0:T(8,128)} custom-call(s32[32]{0:T(128)S(1)} %copy-done.1, s32[1024,128]{1,0:T(8,128)S(1)} %get-tuple-element.21.windows, bf16[1792,128]{1,0:T(8,128)(2,1)S(1)} %bitcast.9), custom_call_target="tpu_custom_call" | custom-call | flops 268435456 | bytes 2097152 | tf_op jit(solution)/shard_map/pallas_call | solution.py:34
  (12 shorter events, 0.1 us)
Async XLA Ops:
  0.0 10.2 %copy-start = (s32[62]{0:T(128)S(1)}, s32[62]{0:T(128)}, u32[]{:S(2)}) copy-start(s32[62]{0:T(128)} %param.12) | copy-start | bytes 748
  2.9 23.7 %all-to-all-start = ((bf16[32,64,128]{2,1,0:T(8,128)(2,1)}), bf16[32,64,128]{2,1,0:T(8,128)(2,1)S(1)}, u32[]{:S(2)}, u32[]{:S(2)}) async-start(bf16[32,64,128]{2,1,0:T(8,128)(2,1)} %get-tuple-element.22), calls=%async_computation | async-start | bytes 1048576 | tf_op jit(solution)/shard_map/all_to_all | solution.py:303
  30.1 1.4 %collective-permute-start = (f32[256,128]{1,0:T(8,128)S(1)}, f32[256,128]{1,0:T(8,128)S(1)}, u32[]{:S(2)}, u32[]{:S(2)}) collective-permute-start(f32[256,128]{1,0:T(8,128)S(1)} %get-tuple-element.24), channel_id=1, source_target_pairs={{0,1},{1,0},{2,3},{3,2},{4,5},{5,4},{6,7},{7,6},{8,9},{9,8},{10,11... | collective-permute-start | bytes 393224 | tf_op jit(solution)/shard_map/ppermute | solution.py:53
  31.5 4.9 %collective-permute-start.1 = (f32[192,128]{1,0:T(8,128)S(1)}, f32[192,128]{1,0:T(8,128)S(1)}, u32[]{:S(2)}, u32[]{:S(2)}) collective-permute-start(f32[192,128]{1,0:T(8,128)S(1)} %slice_add_fusion.after), channel_id=1, source_target_pairs={{0,2},{2,0},{1,3},{3,1},{4,6},{6,4},{5,7},{7,5},{8,10},{10,8},{9,1... | collective-permute-start | bytes 294920 | tf_op jit(solution)/shard_map/ppermute | solution.py:53
  36.4 7.2 %collective-permute-start.2 = (f32[160,128]{1,0:T(8,128)S(1)}, f32[160,128]{1,0:T(8,128)S(1)}, u32[]{:S(2)}, u32[]{:S(2)}) collective-permute-start(f32[160,128]{1,0:T(8,128)S(1)} %slice_add_fusion.1.after), channel_id=1, source_target_pairs={{0,4},{4,0},{1,5},{5,1},{2,6},{6,2},{3,7},{7,3},{8,12},{12,8},{9,1... | collective-permute-start | bytes 245768 | tf_op jit(solution)/shard_map/ppermute | solution.py:53
  43.6 5.5 %collective-permute-start.4 = (f32[64,128]{1,0:T(8,128)S(1)}, f32[64,128]{1,0:T(8,128)S(1)}, u32[]{:S(2)}, u32[]{:S(2)}) collective-permute-start(f32[64,128]{1,0:T(8,128)S(1)} %slice.49), channel_id=1, source_target_pairs={{0,24},{8,16},{16,8},{24,0},{1,25},{9,17},{17,9},{25,1},{2,26},{10... | collective-permute-start | bytes 98312 | tf_op jit(solution)/shard_map/ppermute | solution.py:380
  44.3 4.8 %collective-permute-start.3 = (f32[64,128]{1,0:T(8,128)S(1)}, f32[64,128]{1,0:T(8,128)S(1)}, u32[]{:S(2)}, u32[]{:S(2)}) collective-permute-start(f32[64,128]{1,0:T(8,128)S(1)} %slice.49), channel_id=1, source_target_pairs={{0,16},{8,24},{16,0},{24,8},{1,17},{9,25},{17,1},{25,9},{2,18},{10... | collective-permute-start | bytes 98312 | tf_op jit(solution)/shard_map/ppermute | solution.py:380
  45.8 3.7 %collective-permute-start.5 = (bf16[64,128]{1,0:T(8,128)(2,1)S(1)}, bf16[64,128]{1,0:T(8,128)(2,1)S(1)}, u32[]{:S(2)}, u32[]{:S(2)}) collective-permute-start(bf16[64,128]{1,0:T(8,128)(2,1)S(1)} %slice.62), channel_id=1, source_target_pairs={{0,8},{8,0},{16,24},{24,16},{1,9},{9,1},{17,25},{25,17},{2,10},{10... | collective-permute-start | bytes 49160 | tf_op jit(solution)/shard_map/ppermute | solution.py:380
  49.6 1.2 %collective-permute-start.6 = (bf16[192,128]{1,0:T(8,128)(2,1)S(1)}, bf16[192,128]{1,0:T(8,128)(2,1)S(1)}, u32[]{:S(2)}, u32[]{:S(2)}) collective-permute-start(bf16[192,128]{1,0:T(8,128)(2,1)S(1)} %pad_maximum_fusion.rest_5_), channel_id=1, source_target_pairs={{0,1},{1,0},{2,3},{3,2},{4,5},{5,4},{6,7},{7,6},{8,9},{9,8},{10,11... | collective-permute-start | bytes 147464 | tf_op jit(solution)/shard_map/ppermute | solution.py:53
  50.8 19.8 %copy-start.1 = (s32[32]{0:T(128)S(1)}, s32[32]{0:T(128)}, u32[]{:S(2)}) copy-start(s32[32]{0:T(128)} %sizes.1) | copy-start | bytes 388

commit v2 on v1

--- a/solution.py
+++ b/solution.py
@@ -62,7 +62,7 @@
     return jnp.where(iota(block.shape, 1) < half, -1.0, 1.0) * pltpu.roll(block, half, 1)
 
 
-def pack_kernel(leaves, bucket, sizes_in, position_in, rows_in, packed, windows, *scratch):
+def pack_kernel(leaves, bucket, sizes_in, position_in, rows_in, packed, places, *scratch):
     sizes, position, rows, ordered, sems = scratch
     copies = [
         pltpu.make_async_copy(source, target, sems.at[i])
@@ -90,7 +90,7 @@
     offset = jnp.bitwise_and(here, leaves - 1).astype(F32)
     picked = jnp.where(iota((leaves, count), 0) == owner, offset, 0.0).astype(BF16)
     offsets = dot(picked, hot(iota((128, count), 0) == window - first), (1, 1))
-    windows[...] = jnp.transpose(jnp.broadcast_to(window, (128, count)))
+    places[...] = jnp.transpose(jnp.broadcast_to(owner * bucket + window - first, (128, count)))
     copies[2].wait()
     values = rows[...]
     block = 256
@@ -105,27 +105,43 @@
         packed[c] = data.astype(BF16)
 
 
-def stage_kernel(left_top_in, left_low_in, after, left_top, left_low, raw, sems):
+def near_kernel(source, target, sem):
+    copy = pltpu.make_async_copy(source, target, sem)
+    copy.start()
+    copy.wait()
+
+
+def stage_kernel(left_top_in, left_low_in, targets, places, after, *rest):
+    left_top, left_low, slots, order, raw, sems = rest
     copies = [
         pltpu.make_async_copy(left_low_in, raw, sems.at[0]),
         pltpu.make_async_copy(left_top_in, left_top, sems.at[1]),
     ]
     for copy in copies:
         copy.start()
+    groups, part = targets.shape
+    lanes = iota((part, 128), 1)
+    for g in range(groups):
+        target = jnp.transpose(jnp.broadcast_to(targets[g : g + 1, :], (128, part)))
+        for low in range(0, part, 128):
+            slots[g * part : (g + 1) * part, low : low + 128] = hot(target == lanes + low)
+    count, slots_out = order.shape
+    block = 256
+    lanes = iota((block, 128), 1)
+    for low in range(0, count, block):
+        place = places[low : low + block, :]
+        for at in range(0, slots_out, 128):
+            order[low : low + block, at : at + 128] = hot(place == lanes + at)
     copies[0].wait()
     levels, parts, width, capacity = raw.shape
     left_low[...] = jnp.transpose(raw[...].reshape(levels * parts * width, capacity))
     copies[1].wait()
 
 
-def field_kernel(leaves, bucket, place, arrived, right_top_in, right_low_in, *rest):
-    pair, targets, send, keep, whole, right_top, right_low, sems = rest
-    copies = [
-        pltpu.make_async_copy(right_low_in, right_low, sems.at[0]),
-        pltpu.make_async_copy(right_top_in, right_top, sems.at[1]),
-    ]
-    for copy in copies:
-        copy.start()
+def field_kernel(leaves, bucket, place, arrived, right_top, right_low_in, *rest):
+    pair, targets, send, keep, whole, right_low, sem = rest
+    copy = pltpu.make_async_copy(right_low_in, right_low, sem)
+    copy.start()
     capacity = leaves * bucket
     padded = arrived.shape[1]
     part = leaves * 8
@@ -144,17 +160,14 @@
         rows = spread_offsets[g * 8 : g * 8 + 8, :]
         offset = jnp.sum(jnp.where(own, rows, 0.0), axis=0, keepdims=True).astype(I32)
         target = offset + lane_window[:1, :] * leaves
-        targets[g * part : (g + 1) * part, :] = jnp.transpose(
-            jnp.broadcast_to(target, (128, part))
-        )
+        targets[g : g + 1, :] = target
         if g % 2 == 0:
             both = arrived[:, g * 8 : g * 8 + 16, :].astype(F32)
         chunk = both[:, g % 2 * 8 : g % 2 * 8 + 8, :].reshape(part, 128).astype(BF16)
         placed = dot(hot(iota((part, part), 0) == target), chunk)
         pair[0, g * part : g * part + size, :] = placed[:size].astype(BF16)
         pair[1, g * part : g * part + size, :] = turn(placed)[:size].astype(BF16)
-    for copy in copies:
-        copy.wait()
+    copy.wait()
     levels, _, width, _ = right_low.shape
     top_levels, _, _, top_width = right_top.shape
     total = jnp.zeros((levels * width, 128), F32)
@@ -181,70 +194,84 @@
     return tops + [(top_levels * 128 + level * width, width // 2) for level in range(levels - 1)]
 
 
-def diag_kernel(block, pair, after, out):
-    out[...] = dot(block[0], pair[0]) + dot(block[1], pair[1])
-
-
-def out_kernel(leaves, bucket, pieces, place, *rest):
+def diag_kernel(first, block_in, pair, after, out, block, sems):
+    count, _, height, _ = block.shape
+    copies = []
+    for j in range(count):
+        rows = pl.ds((first + j) * height, height)
+        copies.append(pltpu.make_async_copy(block_in.at[:, rows, :], block.at[j], sems.at[j]))
+        copies[j].start()
+    for j in range(count):
+        copies[j].wait()
+        out[j * height : (j + 1) * height, :] = dot(block[j, 0], pair[0]) + dot(block[j, 1], pair[1])
+
+
+def merged(core, own, theirs, at, half):
+    a, b = own[at : at + half, :].astype(F32), theirs[at : at + half, :].astype(F32)
+    return jnp.concatenate([jnp.where(core == 0, a, b), jnp.where(core == 0, b, a)], axis=0)
+
+
+def low_kernel(pieces, place, *rest):
     bases = rest[:pieces]
-    left_top, left_low, nearest, own, theirs, targets, packed, spare, ordered = rest[pieces:]
-    capacity = leaves * bucket
-    part = leaves * 8
-    groups = spare.shape[0] // part
-    top_levels = left_top.shape[0]
+    left_low, nearest, own, theirs, out = rest[pieces:]
     width = nearest.shape[0]
     levels = left_low.shape[1] // (2 * width)
+    tops = place.shape[0] - 1 - levels
     core = jnp.bitwise_and(place[0], 1)
-    coefs = []
-    at = 0
-    for _, half in segments(top_levels, levels, width):
-        a, b = own[at : at + half, :].astype(F32), theirs[at : at + half, :].astype(F32)
-        first, second = jnp.where(core == 0, a, b), jnp.where(core == 0, b, a)
-        coefs.append(jnp.concatenate([first, second], axis=0))
-        at += half
-    coefs.append(nearest[...])
-    tops, lows = [], []
-    for level, coef in enumerate(coefs):
-        lanes = level < top_levels
-        coef = jnp.where(iota(coef.shape, 1 if lanes else 0) < place[1 + level], coef, 0.0)
-        if lanes:
-            half = coef.shape[0] // 2
-            tops += [coef, jnp.concatenate([-coef[half:], coef[:half]], axis=0)]
+    half = width // 2
+    stacked = []
+    for level in range(levels):
+        if level < levels - 1:
+            coef = merged(core, own, theirs, level * half, half)
         else:
-            lows += [coef, turn(coef)]
-    stacked = jnp.concatenate([jnp.transpose(coef) for coef in tops] + lows, axis=0).astype(BF16)
-    cut = capacity // pieces
-    for i in range(pieces):
-        rows = slice(i * cut, (i + 1) * cut)
-        factors = [left_top[level, p, rows, :] for level in range(top_levels) for p in range(2)]
-        factors = jnp.concatenate(factors + [left_low[rows, :]], axis=1)
-        spare[rows, :] = (bases[i][...] + dot(factors, stacked)).astype(BF16)
+            coef = nearest[...]
+        coef = jnp.where(iota(coef.shape, 0) < place[1 + tops + level], coef, 0.0)
+        stacked += [coef, turn(coef)]
+    stacked = jnp.concatenate(stacked, axis=0).astype(BF16)
+    low = 0
+    for base in bases:
+        rows = slice(low, low + base.shape[0])
+        out[rows, :] = base[...] + dot(left_low[rows, :], stacked)
+        low += base.shape[0]
+
+
+def out_kernel(bucket, place, base, left_top, own, theirs, slots, packed, spare, ordered):
+    capacity = base.shape[0]
+    part = slots.shape[1]
+    groups = slots.shape[0] // part
+    leaves = part // 8
+    core = jnp.bitwise_and(place[0], 1)
+    levels = left_top.shape[0]
+    half = own.shape[0] // levels
+    stacked = []
+    for level in range(levels):
+        coef = merged(core, own, theirs, level * half, half)
+        coef = jnp.where(iota(coef.shape, 1) < place[1 + level], coef, 0.0)
+        turned = jnp.concatenate([-coef[half:], coef[:half]], axis=0)
+        stacked += [jnp.transpose(coef), jnp.transpose(turned)]
+    stacked = jnp.concatenate(stacked, axis=0).astype(BF16)
     if groups * part > capacity:
         spare[capacity:, :] = jnp.zeros((groups * part - capacity, 128), BF16)
-    lanes = iota((part, 128), 1)
+    factors = [left_top[level, p] for level in range(levels) for p in range(2)]
+    total = base[...] + dot(jnp.concatenate(factors, axis=1), stacked)
+    spare[:capacity, :] = total.astype(BF16)
     for g in range(groups):
-        target = targets[g * part : (g + 1) * part, :]
-        picks = [hot(target == lanes + low) for low in range(0, part, 128)]
-        moved = dot(jnp.concatenate(picks, axis=1), spare[g * part : (g + 1) * part, :])
+        moved = dot(slots[g * part : (g + 1) * part, :], spare[g * part : (g + 1) * part, :])
         ordered[:, g * 8 : g * 8 + 8, :] = moved.reshape(leaves, 8, 128)
     packed[...] = ordered[:, :bucket, :].reshape(capacity, 128).astype(BF16)
 
 
-def unpack_kernel(leaves, bucket, sizes, windows, returned, out, wide, ordered):
-    count = windows.shape[0]
-    shift = leaves.bit_length() - 1
-    wide[...] = returned[...].astype(F32)
-    start = 0
-    for c in range(leaves):
-        ordered[pl.ds(start, bucket), :] = wide[c * bucket : (c + 1) * bucket, :]
-        start += jnp.right_shift(sizes[c], shift)
-    values = ordered[:count, :].astype(BF16)
+def unpack_kernel(order, returned, out, near, sems):
+    count = order.shape[0]
     block = 256
-    lanes = iota((block, 128), 1)
+    copies = []
     for low in range(0, count, block):
-        window = windows[low : low + block, :]
-        picks = [hot(window == lanes + at) for at in range(0, count, 128)]
-        out[low : low + block, :] = dot(jnp.concatenate(picks, axis=1), values)
+        rows = pl.ds(low, block)
+        near[rows, :] = dot(order[low : low + block, :], returned[...])
+        copies.append(pltpu.make_async_copy(near.at[rows, :], out.at[rows, :], sems.at[low // block]))
+        copies[-1].start()
+    for copy in copies:
+        copy.wait()
 
 
 def on_device(
@@ -281,7 +308,7 @@
     ranks = block_ranks[(1 << level_ids) - 2 + jnp.right_shift(device, levels - level_ids)]
     place = jnp.concatenate([device[None].astype(I32), ranks])
 
-    packed, windows = call(
+    packed, places = call(
         functools.partial(pack_kernel, leaves, bucket),
         [
             jax.ShapeDtypeStruct((leaves, padded, columns), BF16),
@@ -301,47 +328,49 @@
         ],
     )
     arrived = lax.all_to_all(packed, everyone, split_axis=0, concat_axis=0, tiled=True)
+    right_top = call(
+        near_kernel,
+        [pltpu.VMEM(top_right.shape, BF16)],
+        [HBM],
+        far(top_right),
+        0,
+        4 << 20,
+        16,
+        scratch=[DMA],
+    )[0]
     shared = group_levels * columns // 2 + (member_levels - 1) * width // 2
     pair, targets, send, keep = call(
         functools.partial(field_kernel, leaves, bucket),
         [
             jax.ShapeDtypeStruct((2, capacity, columns), BF16),
-            jax.ShapeDtypeStruct((leaves * filled, 128), I32),
+            jax.ShapeDtypeStruct((filled // 8, leaves * 8), I32),
             jax.ShapeDtypeStruct((shared + width, columns), F32),
             jax.ShapeDtypeStruct((shared, columns), F32),
         ],
-        [SMEM, VMEM, HBM, HBM],
-        (place, arrived, *far(top_right, low_right)),
+        [SMEM, VMEM, VMEM, HBM],
+        (place, arrived, right_top, *far(low_right)),
         far_flops,
         6 << 20,
         24,
         scratch=[
             pltpu.VMEM((group_levels * columns + member_levels * width, columns), F32),
-            pltpu.VMEM(top_right.shape, BF16),
             pltpu.VMEM(low_right.shape, BF16),
-            DMA((2,)),
+            DMA,
         ],
     )
-    pieces = 2
-    cut = capacity // pieces
-    rows = cut // 4
-
-    def diagonal(i, after):
+    height = capacity // 8
+
+    def diagonal(first, chunks, after):
         return call(
-            diag_kernel,
-            jax.ShapeDtypeStruct((cut, columns), F32),
-            [
-                pl.BlockSpec((2, rows, capacity), lambda j: (0, j + 4 * i, 0)),
-                pl.BlockSpec((2, capacity, columns), lambda j: (0, 0, 0)),
-                pl.BlockSpec(memory_space=pl.ANY),
-            ],
+            functools.partial(diag_kernel, first),
+            [jax.ShapeDtypeStruct((chunks * height, columns), F32)],
+            [HBM, VMEM, pl.BlockSpec(memory_space=pl.ANY)],
             (*far(diag_block), pair, after),
-            4 * cut * capacity * columns,
-            4 * cut * capacity,
-            16,
-            grid=(4,),
-            out_specs=pl.BlockSpec((rows, columns), lambda j: (j, 0)),
-        )
+            4 * chunks * height * capacity * columns,
+            4 * chunks * height * capacity,
+            24,
+            scratch=[pltpu.VMEM((chunks, 2, height, capacity), BF16), DMA((chunks,))],
+        )[0]
 
     received = partner(send, "member", 0)
     nearest = received[shared:]
@@ -351,24 +380,31 @@
     for bit in range(1, member_levels):
         rest = running.shape[0] - width // 2
         received = partner(running, "member", bit)
-        if len(bases) < pieces:
-            bases.append(diagonal(len(bases), running))
-            received, bases[-1] = lax.optimization_barrier((received, bases[-1]))
+        if bit == 1:
+            bases.append(diagonal(0, 5, running))
+            received, bases[0] = lax.optimization_barrier((received, bases[0]))
+        if bit == member_levels - 1:
+            bases.append(diagonal(5, 3, running))
+            left_top, left_low, slots, order = call(
+                stage_kernel,
+                [
+                    pltpu.VMEM(top_left.shape, BF16),
+                    pltpu.VMEM((capacity, member_levels * 2 * width), BF16),
+                    jax.ShapeDtypeStruct((leaves * filled, leaves * 8), BF16),
+                    jax.ShapeDtypeStruct((count, capacity), BF16),
+                ],
+                [HBM, HBM, VMEM, VMEM, pl.BlockSpec(memory_space=pl.ANY)],
+                (*far(top_left, low_left), targets, places, running),
+                0,
+                8 << 20,
+                24,
+                scratch=[pltpu.VMEM(low_left.shape, BF16), DMA((2,))],
+            )
+            received, bases[1], left_top, left_low, slots, order = lax.optimization_barrier(
+                (received, bases[1], left_top, left_low, slots, order)
+            )
         coefs.insert(0, received[rest:].astype(BF16))
         running = running[:rest] + received[:rest]
-    left_top, left_low = call(
-        stage_kernel,
-        [
-            pltpu.VMEM(top_left.shape, BF16),
-            pltpu.VMEM((capacity, member_levels * 2 * width), BF16),
-        ],
-        [HBM, HBM, pl.BlockSpec(memory_space=pl.ANY)],
-        (*far(top_left, low_left), running),
-        0,
-        8 << 20,
-        16,
-        scratch=[pltpu.VMEM(low_left.shape, BF16), DMA((2,))],
-    )
     half = columns // 2
     tops = [None] * group_levels
     for apart in range(1, groups):
@@ -379,17 +415,27 @@
         route = [(low, low ^ apart) for low in range(groups)]
         heard = lax.ppermute(sent, "group", route)
         tops[level] = heard if tops[level] is None else tops[level] + heard
-    left_top, left_low, tops = lax.optimization_barrier((left_top, left_low, tops))
-    own = jnp.concatenate([top.astype(BF16) for top in tops] + coefs)
+    own_low = jnp.concatenate(coefs)
+    base = call(
+        functools.partial(low_kernel, len(bases)),
+        [jax.ShapeDtypeStruct((capacity, columns), F32)],
+        [SMEM] + [VMEM] * (len(bases) + 4),
+        (place, *bases, left_low, nearest, own_low, partner(own_low, "member", 0)),
+        4 * capacity * columns * member_levels * width,
+        3 << 20,
+        16,
+    )[0]
+    own = jnp.concatenate([top.astype(BF16) for top in tops])
+    own, base = lax.optimization_barrier((own, base))
     theirs = partner(own, "member", 0)
 
     leaving = call(
-        functools.partial(out_kernel, leaves, bucket, pieces),
+        functools.partial(out_kernel, bucket),
         [jax.ShapeDtypeStruct((capacity, columns), BF16)],
-        [SMEM] + [VMEM] * (pieces + 6),
-        (place, *bases, left_top, left_low, nearest, own, theirs, targets),
-        far_flops,
-        6 << 20,
+        [SMEM] + [VMEM] * 5,
+        (place, base, left_top, own, theirs, slots),
+        4 * capacity * columns * group_levels * top_width,
+        4 << 20,
         24,
         scratch=[
             pltpu.VMEM((leaves * filled, 128), BF16),
@@ -400,17 +446,15 @@
         leaving.reshape(leaves, bucket, columns), everyone, split_axis=0, concat_axis=0, tiled=True
     )
     return call(
-        functools.partial(unpack_kernel, leaves, bucket),
+        unpack_kernel,
         [jax.ShapeDtypeStruct((count, columns), F32)],
-        [SMEM] + [VMEM] * 2,
-        (cluster_sizes, windows, returned.reshape(capacity, columns)),
-        2 * count * count * columns,
-        2 << 20,
+        [VMEM] * 2,
+        (order, returned.reshape(capacity, columns)),
+        2 * capacity * count * columns,
+        4 << 20,
         16,
-        scratch=[
-            pltpu.VMEM((capacity, 128), F32),
-            pltpu.VMEM((count + filled, 128), F32),
-        ],
+        out_specs=[HBM],
+        scratch=[pltpu.VMEM((count, 128), F32), DMA((count // 256,))],
     )[0]
 
 

time: 73 us -> 72 us (0.986)
    all_to_all x1, waiting for transfers between devices: 15.6 us -> 14.1 us  [on_device(): lax.all_to_all(packed, everyone, split_axis=0, concat_axis=0, tiled=True)]
    ppermute x3, waiting for transfers between devices: 0.44 us -> 1.27 us  [on_device(): heard = lax.ppermute(sent, 'group', route)]
    pallas_call x7 -> x9, Pallas kernels: 21.9 us -> 21.4 us  [call(): pl.pallas_call(kernel, out_shape=outs, in_specs=ins, out_specs=more.pop('...]
    ppermute x4 -> x5, waiting for transfers between devices: 4.17 us -> 4.33 us  [partner(): return lax.ppermute(block, axis, route)]
  transfers between devices with their start and end apart: 8 -> 9, of which waited for: 6 -> 7; matrix products, arithmetic and copies ran while one was open for 1% -> 1% of each run, Pallas kernels for 16% -> 17%
where the time goes in v2:
time: 72 us; the launch traced here: 71.7 us
  Pallas kernels  21.4 us (30%)
  waiting for transfers between devices  19.7 us (27%)
  blocking collectives  18.1 us (25%)
  starting transfers between devices  11.6 us (16%)
    pallas_call x9, Pallas kernels, call(): pl.pallas_call(kernel, out_shape=outs, in_specs=ins, out_specs=more.pop('...  21.4 us
    all_to_all x1, blocking collectives, on_device(): lax.all_to_all(leaving.reshape(leaves, bucket, columns), everyone, split_...  18.1 us
    all_to_all x1, waiting for transfers between devices, on_device(): lax.all_to_all(packed, everyone, split_axis=0, concat_axis=0, tiled=True)  14.1 us
    all_to_all x1, starting transfers between devices, on_device(): lax.all_to_all(packed, everyone, split_axis=0, concat_axis=0, tiled=True)  7.3 us
    ppermute x5, waiting for transfers between devices, partner(): return lax.ppermute(block, axis, route)  4.33 us
    ppermute x3, starting transfers between devices, on_device(): heard = lax.ppermute(sent, 'group', route)  3.61 us
  transfers between devices with their start and end apart: 9, of which 7 were waited for; matrix products, arithmetic and copies ran while one was open for 1% of the time, Pallas kernels for 17%

profile of v2, /device:TPU:0, one launch (start us, length us, event | category | flops | bytes accessed | tf_op | source)
XLA Modules:
  0.0 71.7 jit_solution(11910324817097857747)
XLA Ops:
  0.0 0.0 copy-start
  0.0 2.8 %shard_map.91 = (bf16[32,64,128]{2,1,0:T(8,128)(2,1)}, s32[1024,128]{1,0:T(8,128)S(1)}) custom-call(s32[32]{0:T(128)} %sizes_in.1, s32[1,1024]{1,0:T(1,128)} %bitcast.12, bf16[1024,128]{1,0:T(8,128)(2,1)} %rows_in.1), custom_call_target="tpu_custom_call" | custom-call | flops 268435456 | bytes 4194304 | tf_op jit(solution)/shard_map/pallas_call | solution.py:34
  2.9 7.3 %all-to-all-start = ((bf16[32,64,128]{2,1,0:T(8,128)(2,1)}), bf16[32,64,128]{2,1,0:T(8,128)(2,1)S(1)}, u32[]{:S(2)}, u32[]{:S(2)}) async-start(bf16[32,64,128]{2,1,0:T(8,128)(2,1)} %get-tuple-element.25), calls=%async_computation | async-start | bytes 1048576 | tf_op jit(solution)/shard_map/all_to_all | solution.py:330
  10.2 1.5 %shard_map.92.right_top = bf16[2,2,1792,128]{3,2,1,0:T(8,128)(2,1)S(1)} custom-call(bf16[2,2,1792,128]{3,2,1,0:T(8,128)(2,1)} %source.1), custom_call_target="tpu_custom_call" | custom-call | bytes 4194304 | tf_op jit(solution)/shard_map/pallas_call | solution.py:34
  11.7 0.0 copy-done
  11.7 0.6 gather_fusion
  12.4 0.1 pad_add_fusion.place
  12.5 14.1 %all-to-all-done.arrived = bf16[32,64,128]{2,1,0:T(8,128)(2,1)S(1)} async-done(((bf16[32,64,128]{2,1,0:T(8,128)(2,1)}), bf16[32,64,128]{2,1,0:T(8,128)(2,1)S(1)}, u32[]{:S(2)}, u32[]{:S(2)}) %all-to-all-start) | async-done | bytes 524320 | tf_op jit(solution)/shard_map/all_to_all | solution.py:330
  26.5 2.9 %shard_map.93 = (bf16[2,1792,128]{2,1,0:T(8,128)(2,1)S(1)}, s32[7,256]{1,0:T(8,128)S(1)}, f32[256,128]{1,0:T(8,128)S(1)}, f32[192,128]{1,0:T(8,128)S(1)}) custom-call(s32[6]{0:T(128)S(1)} %pad_add_fusion.place, bf16[32,64,128]{2,1,0:T(8,128)(2,1)S(1)} %all-to-all-done.arrived, bf16[2,2,1792,128]{3,2,1,0:T(8,128)(2,1)S(1)} %shard_map.92.right_top, ...), custom_call_target="tpu_custom_call" | custom-call | flops 411041792 | bytes 6291456 | tf_op jit(solution)/shard_map/pallas_call | solution.py:34
  29.5 0.1 collective-permute-start
  29.5 1.3 %collective-permute-done = f32[256,128]{1,0:T(8,128)S(1)} collective-permute-done((f32[256,128]{1,0:T(8,128)S(1)}, f32[256,128]{1,0:T(8,128)S(1)}, u32[]{:S(2)}, u32[]{:S(2)}) %collective-permute-start) | collective-permute-done | bytes 131104 | tf_op jit(solution)/shard_map/ppermute | solution.py:53
  30.9 0.1 collective-permute-start.1
  31.0 4.4 %shard_map.94.rest_0_ = f32[1120,128]{1,0:T(8,128)S(1)} custom-call(bf16[2,1792,1792]{2,1,0:T(8,128)(2,1)} %block_in.3, bf16[2,1792,128]{2,1,0:T(8,128)(2,1)S(1)} %get-tuple-element.28.pair, f32[192,128]{1,0:T(8,128)S(1)} %slice_add_fusion.after), custom_call_target="tpu_custom_call" | custom-call | flops 1027604480 | bytes 8028160 | tf_op jit(solution)/shard_map/pallas_call | solution.py:34
  35.4 0.5 collective-permute-done.1
  35.8 0.5 collective-permute-start.2
  36.4 2.0 %shard_map.96 = (bf16[2,2,1792,128]{3,2,1,0:T(8,128)(2,1)S(1)}, bf16[1792,384]{1,0:T(8,128)(2,1)S(1)}, bf16[1792,256]{1,0:T(8,128)(2,1)S(1)}, bf16[1024,1792]{1,0:T(8,128)(2,1)S(1)}) custom-call(bf16[2,2,1792,128]{3,2,1,0:T(8,128)(2,1)} %left_top_in.1, bf16[3,2,64,1792]{3,2,1,0:T(8,128)(2,1)} %bitcast.11, s32[7,256]{1,0:T(8,128)S(1)} %get-tuple-element.30.targets, ...), custom_call_target="tpu_custom_call" | custom-call | bytes 8388608 | tf_op jit(solution)/shard_map/pallas_call | solution.py:34
  38.3 3.2 %shard_map.95.rest_1_ = f32[672,128]{1,0:T(8,128)S(1)} custom-call(bf16[2,1792,1792]{2,1,0:T(8,128)(2,1)} %block_in.3, bf16[2,1792,128]{2,1,0:T(8,128)(2,1)S(1)} %get-tuple-element.28.pair, f32[160,128]{1,0:T(8,128)S(1)} %slice_add_fusion.1.after), custom_call_target="tpu_custom_call" | custom-call | flops 616562688 | bytes 4816896 | tf_op jit(solution)/shard_map/pallas_call | solution.py:34
  41.5 1.3 %collective-permute-done.2 = f32[160,128]{1,0:T(8,128)S(1)} collective-permute-done((f32[160,128]{1,0:T(8,128)S(1)}, f32[160,128]{1,0:T(8,128)S(1)}, u32[]{:S(2)}, u32[]{:S(2)}) %collective-permute-start.2) | collective-permute-done | bytes 81952 | tf_op jit(solution)/shard_map/ppermute | solution.py:53
  42.9 0.0 collective-permute-start.6
  42.9 0.8 %collective-permute-start.3 = (f32[64,128]{1,0:T(8,128)S(1)}, f32[64,128]{1,0:T(8,128)S(1)}, u32[]{:S(2)}, u32[]{:S(2)}) collective-permute-start(f32[64,128]{1,0:T(8,128)S(1)} %slice.49), channel_id=1, source_target_pairs={{0,16},{8,24},{16,0},{24,8},{1,17},{9,25},{17,1},{25,9},{2,18},{10... | collective-permute-start | bytes 98312 | tf_op jit(solution)/shard_map/ppermute | solution.py:416
  43.7 1.5 %collective-permute-start.4 = (f32[64,128]{1,0:T(8,128)S(1)}, f32[64,128]{1,0:T(8,128)S(1)}, u32[]{:S(2)}, u32[]{:S(2)}) collective-permute-start(f32[64,128]{1,0:T(8,128)S(1)} %slice.49), channel_id=1, source_target_pairs={{0,24},{8,16},{16,8},{24,0},{1,25},{9,17},{17,9},{25,1},{2,26},{10... | collective-permute-start | bytes 98312 | tf_op jit(solution)/shard_map/ppermute | solution.py:416
  45.2 1.4 %collective-permute-start.5 = (bf16[64,128]{1,0:T(8,128)(2,1)S(1)}, bf16[64,128]{1,0:T(8,128)(2,1)S(1)}, u32[]{:S(2)}, u32[]{:S(2)}) collective-permute-start(bf16[64,128]{1,0:T(8,128)(2,1)S(1)} %slice.62), channel_id=1, source_target_pairs={{0,8},{8,0},{16,24},{24,16},{1,9},{9,1},{17,25},{25,17},{2,10},{10... | collective-permute-start | bytes 49160 | tf_op jit(solution)/shard_map/ppermute | solution.py:416
  46.6 0.0 collective-permute-done.6.rest_5_
  46.6 1.1 %shard_map.97.base = f32[1792,128]{1,0:T(8,128)S(1)} custom-call(s32[6]{0:T(128)S(1)} %pad_add_fusion.place, f32[1120,128]{1,0:T(8,128)S(1)} %shard_map.94.rest_0_, f32[672,128]{1,0:T(8,128)S(1)} %shard_map.95.rest_1_, bf16[1792,384]{1,0:T(8,128)(2,1)S(1)} %get-tuple-element.40.rest_2_, f32[64,128]{1,0:T(8,128)S(1)} %slice.51.rest_3_, ...), custom_call_target="tpu_custom_call" | custom-call | flops 176160768 | bytes 3145728 | tf_op jit(solution)/shard_map/pallas_call | solution.py:34
  47.7 0.0 collective-permute-done.3
  47.7 0.8 %collective-permute-done.4 = f32[64,128]{1,0:T(8,128)S(1)} collective-permute-done((f32[64,128]{1,0:T(8,128)S(1)}, f32[64,128]{1,0:T(8,128)S(1)}, u32[]{:S(2)}, u32[]{:S(2)}) %collective-permute-start.4) | collective-permute-done | bytes 32800 | tf_op jit(solution)/shard_map/ppermute | solution.py:416
  48.5 0.4 collective-permute-done.5
  49.0 0.0 collective-permute-start.7
  49.0 1.2 %collective-permute-done.7.theirs = bf16[128,128]{1,0:T(8,128)(2,1)S(1)} collective-permute-done((bf16[128,128]{1,0:T(8,128)(2,1)S(1)}, bf16[128,128]{1,0:T(8,128)(2,1)S(1)}, u32[]{:S(2)}, u32[]{:S(2)}) %collective-permute-start.7) | collective-permute-done | bytes 32800 | tf_op jit(solution)/shard_map/ppermute | solution.py:53
  50.2 1.6 %shard_map.98 = bf16[1792,128]{1,0:T(8,128)(2,1)S(1)} custom-call(s32[6]{0:T(128)S(1)} %pad_add_fusion.place, f32[1792,128]{1,0:T(8,128)S(1)} %shard_map.97.base, bf16[2,2,1792,128]{3,2,1,0:T(8,128)(2,1)S(1)} %get-tuple-element.42.left_top, bf16[128,128]{1,0:T(8,128)(2,1)S(1)} %pad_maximum_fusion.own, bf16[128,128]{1,0:T(8,128)(2,1)S(1)} %collective-permute-done.7.theirs, ...), custom_call_target="tpu_custom_call" | custom-call | flops 234881024 | bytes 4194304 | tf_op jit(solution)/shard_map/pallas_call | solution.py:34
  51.8 18.1 %all_to_all.10 = bf16[32,56,128]{2,1,0:T(8,128)(2,1)S(1)} all-to-all(bf16[32,56,128]{2,1,0:T(8,128)(2,1)S(1)} %bitcast.8), channel_id=1, replica_groups=mesh['group'=4,'member'=8] {'group','member'}, dimensions={0} | all-to-all | bytes 917504 | tf_op jit(solution)/shard_map/all_to_all | solution.py:445
  69.9 1.8 %shard_map.99 = f32[1024,128]{1,0:T(8,128)} custom-call(bf16[1024,1792]{1,0:T(8,128)(2,1)S(1)} %get-tuple-element.36.order, bf16[1792,128]{1,0:T(8,128)(2,1)S(1)} %bitcast.9), custom_call_target="tpu_custom_call" | custom-call | flops 469762048 | bytes 4194304 | tf_op jit(solution)/shard_map/pallas_call | solution.py:34
  (13 shorter events, 0.1 us)
Async XLA Ops:
  0.0 11.7 %copy-start = (s32[62]{0:T(128)S(1)}, s32[62]{0:T(128)}, u32[]{:S(2)}) copy-start(s32[62]{0:T(128)} %param.12) | copy-start | bytes 748
  2.9 23.7 %all-to-all-start = ((bf16[32,64,128]{2,1,0:T(8,128)(2,1)}), bf16[32,64,128]{2,1,0:T(8,128)(2,1)S(1)}, u32[]{:S(2)}, u32[]{:S(2)}) async-start(bf16[32,64,128]{2,1,0:T(8,128)(2,1)} %get-tuple-element.25), calls=%async_computation | async-start | bytes 1048576 | tf_op jit(solution)/shard_map/all_to_all | solution.py:330
  29.5 1.4 %collective-permute-start = (f32[256,128]{1,0:T(8,128)S(1)}, f32[256,128]{1,0:T(8,128)S(1)}, u32[]{:S(2)}, u32[]{:S(2)}) collective-permute-start(f32[256,128]{1,0:T(8,128)S(1)} %get-tuple-element.27), channel_id=1, source_target_pairs={{0,1},{1,0},{2,3},{3,2},{4,5},{5,4},{6,7},{7,6},{8,9},{9,8},{10,11... | collective-permute-start | bytes 393224 | tf_op jit(solution)/shard_map/ppermute | solution.py:53
  30.9 4.9 %collective-permute-start.1 = (f32[192,128]{1,0:T(8,128)S(1)}, f32[192,128]{1,0:T(8,128)S(1)}, u32[]{:S(2)}, u32[]{:S(2)}) collective-permute-start(f32[192,128]{1,0:T(8,128)S(1)} %slice_add_fusion.after), channel_id=1, source_target_pairs={{0,2},{2,0},{1,3},{3,1},{4,6},{6,4},{5,7},{7,5},{8,10},{10,8},{9,1... | collective-permute-start | bytes 294920 | tf_op jit(solution)/shard_map/ppermute | solution.py:53
  35.8 7.1 %collective-permute-start.2 = (f32[160,128]{1,0:T(8,128)S(1)}, f32[160,128]{1,0:T(8,128)S(1)}, u32[]{:S(2)}, u32[]{:S(2)}) collective-permute-start(f32[160,128]{1,0:T(8,128)S(1)} %slice_add_fusion.1.after), channel_id=1, source_target_pairs={{0,4},{4,0},{1,5},{5,1},{2,6},{6,2},{3,7},{7,3},{8,12},{12,8},{9,1... | collective-permute-start | bytes 245768 | tf_op jit(solution)/shard_map/ppermute | solution.py:53
  42.9 3.7 %collective-permute-start.6 = (bf16[64,128]{1,0:T(8,128)(2,1)S(1)}, bf16[64,128]{1,0:T(8,128)(2,1)S(1)}, u32[]{:S(2)}, u32[]{:S(2)}) collective-permute-start(bf16[64,128]{1,0:T(8,128)(2,1)S(1)} %pad_maximum_fusion.1.rest_4_), channel_id=1, source_target_pairs={{0,1},{1,0},{2,3},{3,2},{4,5},{5,4},{6,7},{7,6},{8,9},{9,8},{10,11... | collective-permute-start | bytes 49160 | tf_op jit(solution)/shard_map/ppermute | solution.py:53
  42.9 4.8 %collective-permute-start.3 = (f32[64,128]{1,0:T(8,128)S(1)}, f32[64,128]{1,0:T(8,128)S(1)}, u32[]{:S(2)}, u32[]{:S(2)}) collective-permute-start(f32[64,128]{1,0:T(8,128)S(1)} %slice.49), channel_id=1, source_target_pairs={{0,16},{8,24},{16,0},{24,8},{1,17},{9,25},{17,1},{25,9},{2,18},{10... | collective-permute-start | bytes 98312 | tf_op jit(solution)/shard_map/ppermute | solution.py:416
  43.7 4.8 %collective-permute-start.4 = (f32[64,128]{1,0:T(8,128)S(1)}, f32[64,128]{1,0:T(8,128)S(1)}, u32[]{:S(2)}, u32[]{:S(2)}) collective-permute-start(f32[64,128]{1,0:T(8,128)S(1)} %slice.49), channel_id=1, source_target_pairs={{0,24},{8,16},{16,8},{24,0},{1,25},{9,17},{17,9},{25,1},{2,26},{10... | collective-permute-start | bytes 98312 | tf_op jit(solution)/shard_map/ppermute | solution.py:416
  45.2 3.8 %collective-permute-start.5 = (bf16[64,128]{1,0:T(8,128)(2,1)S(1)}, bf16[64,128]{1,0:T(8,128)(2,1)S(1)}, u32[]{:S(2)}, u32[]{:S(2)}) collective-permute-start(bf16[64,128]{1,0:T(8,128)(2,1)S(1)} %slice.62), channel_id=1, source_target_pairs={{0,8},{8,0},{16,24},{24,16},{1,9},{9,1},{17,25},{25,17},{2,10},{10... | collective-permute-start | bytes 49160 | tf_op jit(solution)/shard_map/ppermute | solution.py:416
  49.0 1.2 %collective-permute-start.7 = (bf16[128,128]{1,0:T(8,128)(2,1)S(1)}, bf16[128,128]{1,0:T(8,128)(2,1)S(1)}, u32[]{:S(2)}, u32[]{:S(2)}) collective-permute-start(bf16[128,128]{1,0:T(8,128)(2,1)S(1)} %pad_maximum_fusion.own), channel_id=1, source_target_pairs={{0,1},{1,0},{2,3},{3,2},{4,5},{5,4},{6,7},{7,6},{8,9},{9,8},{10,11... | collective-permute-start | bytes 98312 | tf_op jit(solution)/shard_map/ppermute | solution.py:53

commit v3 on v2

--- a/solution.py
+++ b/solution.py
@@ -63,22 +63,28 @@
 
 
 def pack_kernel(leaves, bucket, sizes_in, position_in, rows_in, packed, places, *scratch):
-    sizes, position, rows, ordered, sems = scratch
+    sizes, position, rows, ordered, near, sems, out_sems = scratch
     copies = [
         pltpu.make_async_copy(source, target, sems.at[i])
         for i, (source, target) in enumerate(
-            [(sizes_in, sizes), (position_in, position), (rows_in, rows)]
+            [(position_in, position), (rows_in, rows), (sizes_in, sizes)]
         )
     ]
     for copy in copies:
         copy.start()
-    for copy in copies[:2]:
-        copy.wait()
+    copies[0].wait()
     count = rows.shape[0]
     padded = packed.shape[1]
     shift = leaves.bit_length() - 1
     here = position[...]
     window = jnp.right_shift(here, shift)
+    copies[1].wait()
+    values = rows[...]
+    block = 512
+    for low in range(0, count, block):
+        ordered[low : low + block, :] = dot(hot(iota((block, count), 0) + low == window), values)
+    ordered[count:, :] = jnp.zeros((padded, 128), F32)
+    copies[2].wait()
     zero = jnp.zeros((1, count), I32)
     owner, first = zero, zero
     starts = [0]
@@ -90,35 +96,44 @@
     offset = jnp.bitwise_and(here, leaves - 1).astype(F32)
     picked = jnp.where(iota((leaves, count), 0) == owner, offset, 0.0).astype(BF16)
     offsets = dot(picked, hot(iota((128, count), 0) == window - first), (1, 1))
-    places[...] = jnp.transpose(jnp.broadcast_to(owner * bucket + window - first, (128, count)))
-    copies[2].wait()
-    values = rows[...]
-    block = 256
-    for low in range(0, count, block):
-        ordered[low : low + block, :] = dot(hot(iota((block, count), 0) + low == window), values)
-    ordered[count:, :] = jnp.zeros((padded, 128), F32)
+    places[...] = owner * bucket + window - first
     line = iota((padded, 128), 0)
+    chunk = leaves // 4
+    out = []
     for c in range(leaves):
         data = ordered[pl.ds(starts[c], padded), :]
         data = jnp.where(line < starts[c + 1] - starts[c], data, 0.0)
         data = jnp.where(line == bucket, offsets[c : c + 1, :], data)
-        packed[c] = data.astype(BF16)
-
-
-def near_kernel(source, target, sem):
-    copy = pltpu.make_async_copy(source, target, sem)
-    copy.start()
-    copy.wait()
-
-
-def stage_kernel(left_top_in, left_low_in, targets, places, after, *rest):
-    left_top, left_low, slots, order, raw, sems = rest
-    copies = [
-        pltpu.make_async_copy(left_low_in, raw, sems.at[0]),
-        pltpu.make_async_copy(left_top_in, left_top, sems.at[1]),
-    ]
+        near[c] = data.astype(BF16)
+        if c % chunk == chunk - 1:
+            part = pl.ds(c + 1 - chunk, chunk)
+            out.append(pltpu.make_async_copy(near.at[part], packed.at[part], out_sems.at[c // chunk]))
+            out[-1].start()
+    for copy in out:
+        copy.wait()
+
+
+def near_kernel(right_top_in, right_low_in, right, raw, sems):
+    tops, _, _, top_width = right_top_in.shape
+    levels, _, width, _ = right_low_in.shape
+    copies = [pltpu.make_async_copy(right_top_in, raw, sems.at[0])]
+    for level in range(levels):
+        low = tops * top_width + level * width
+        for p in range(2):
+            target = right.at[p, pl.ds(low, width), :]
+            sem = sems.at[1 + 2 * level + p]
+            copies.append(pltpu.make_async_copy(right_low_in.at[level, p], target, sem))
     for copy in copies:
         copy.start()
+    copies[0].wait()
+    for level in range(tops):
+        for p in range(2):
+            right[p, level * top_width : (level + 1) * top_width, :] = jnp.transpose(raw[level, p])
+    for copy in copies[1:]:
+        copy.wait()
+
+
+def way_kernel(targets, places, after, slots, order):
     groups, part = targets.shape
     lanes = iota((part, 128), 1)
     for g in range(groups):
@@ -126,22 +141,29 @@
         for low in range(0, part, 128):
             slots[g * part : (g + 1) * part, low : low + 128] = hot(target == lanes + low)
     count, slots_out = order.shape
+    place = jnp.transpose(jnp.broadcast_to(places[...], (128, count)))
     block = 256
     lanes = iota((block, 128), 1)
     for low in range(0, count, block):
-        place = places[low : low + block, :]
         for at in range(0, slots_out, 128):
-            order[low : low + block, at : at + 128] = hot(place == lanes + at)
+            order[low : low + block, at : at + 128] = hot(place[low : low + block] == lanes + at)
+
+
+def stage_kernel(left_top_in, left_low_in, after, left_top, left_low, raw, sems):
+    copies = [
+        pltpu.make_async_copy(left_low_in, raw, sems.at[0]),
+        pltpu.make_async_copy(left_top_in, left_top, sems.at[1]),
+    ]
+    for copy in copies:
+        copy.start()
     copies[0].wait()
     levels, parts, width, capacity = raw.shape
     left_low[...] = jnp.transpose(raw[...].reshape(levels * parts * width, capacity))
     copies[1].wait()
 
 
-def field_kernel(leaves, bucket, place, arrived, right_top, right_low_in, *rest):
-    pair, targets, send, keep, whole, right_low, sem = rest
-    copy = pltpu.make_async_copy(right_low_in, right_low, sem)
-    copy.start()
+def field_kernel(leaves, bucket, tops, levels, place, arrived, right, *rest):
+    pair, targets, send, keep, whole = rest
     capacity = leaves * bucket
     padded = arrived.shape[1]
     part = leaves * 8
@@ -167,31 +189,24 @@
         placed = dot(hot(iota((part, part), 0) == target), chunk)
         pair[0, g * part : g * part + size, :] = placed[:size].astype(BF16)
         pair[1, g * part : g * part + size, :] = turn(placed)[:size].astype(BF16)
-    copy.wait()
-    levels, _, width, _ = right_low.shape
-    top_levels, _, _, top_width = right_top.shape
-    total = jnp.zeros((levels * width, 128), F32)
-    tops = jnp.zeros((128, top_levels * top_width), F32)
-    for p in range(2):
-        total += dot(right_low[:, p].reshape(levels * width, capacity), pair[p])
-        factors = jnp.concatenate([right_top[level, p] for level in range(top_levels)], axis=1)
-        tops += dot(jnp.transpose(pair[p]), factors)
-    for level in range(top_levels):
-        whole[level * 128 : (level + 1) * 128, :] = tops[:, level * top_width : (level + 1) * top_width]
-    whole[top_levels * 128 :, :] = total
+    whole[...] = dot(right[0], pair[0]) + dot(right[1], pair[1])
     at = 0
-    for low, half in segments(top_levels, levels, width):
+    for low, half in segments(tops, levels):
         mine = pl.multiple_of(low + core * half, 8)
         other = pl.multiple_of(low + (1 - core) * half, 8)
         keep[at : at + half, :] = whole[pl.ds(mine, half), :]
         send[at : at + half, :] = whole[pl.ds(other, half), :]
         at += half
-    send[at:, :] = total[(levels - 1) * width :]
-
-
-def segments(top_levels, levels, width):
-    tops = [(level * 128, 64) for level in range(top_levels)]
-    return tops + [(top_levels * 128 + level * width, width // 2) for level in range(levels - 1)]
+    send[at:, :] = whole[whole.shape[0] + at - send.shape[0] :, :]
+
+
+def segments(tops, lows):
+    found, low = [], 0
+    for count, width in (tops, (lows[0] - 1, lows[1])):
+        for _ in range(count):
+            found.append((low, width // 2))
+            low += width
+    return found
 
 
 def diag_kernel(first, block_in, pair, after, out, block, sems):
@@ -246,9 +261,8 @@
     stacked = []
     for level in range(levels):
         coef = merged(core, own, theirs, level * half, half)
-        coef = jnp.where(iota(coef.shape, 1) < place[1 + level], coef, 0.0)
-        turned = jnp.concatenate([-coef[half:], coef[:half]], axis=0)
-        stacked += [jnp.transpose(coef), jnp.transpose(turned)]
+        coef = jnp.where(iota(coef.shape, 0) < place[1 + level], coef, 0.0)
+        stacked += [coef, turn(coef)]
     stacked = jnp.concatenate(stacked, axis=0).astype(BF16)
     if groups * part > capacity:
         spare[capacity:, :] = jnp.zeros((groups * part - capacity, 128), BF16)
@@ -263,7 +277,7 @@
 
 def unpack_kernel(order, returned, out, near, sems):
     count = order.shape[0]
-    block = 256
+    block = 512
     copies = []
     for low in range(0, count, block):
         rows = pl.ds(low, block)
@@ -312,51 +326,53 @@
         functools.partial(pack_kernel, leaves, bucket),
         [
             jax.ShapeDtypeStruct((leaves, padded, columns), BF16),
-            jax.ShapeDtypeStruct((count, 128), I32),
+            jax.ShapeDtypeStruct((1, count), I32),
         ],
         [HBM] * 3,
         far(cluster_sizes, cluster_position.reshape(1, count), mesh_vector),
         2 * count * count * columns,
         4 << 20,
         16,
+        out_specs=[HBM, VMEM],
         scratch=[
             pltpu.SMEM((leaves,), I32),
             pltpu.VMEM((1, count), I32),
             pltpu.VMEM((count, columns), BF16),
             pltpu.VMEM((count + padded, columns), F32),
+            pltpu.VMEM((leaves, padded, columns), BF16),
             DMA((3,)),
+            DMA((4,)),
         ],
     )
     arrived = lax.all_to_all(packed, everyone, split_axis=0, concat_axis=0, tiled=True)
-    right_top = call(
+    tops = (group_levels, top_width)
+    lows = (member_levels, width)
+    ranked = group_levels * top_width + member_levels * width
+    right = call(
         near_kernel,
-        [pltpu.VMEM(top_right.shape, BF16)],
-        [HBM],
-        far(top_right),
+        [pltpu.VMEM((2, ranked, capacity), BF16)],
+        [HBM] * 2,
+        far(top_right, low_right),
         0,
-        4 << 20,
+        6 << 20,
         16,
-        scratch=[DMA],
+        scratch=[pltpu.VMEM(top_right.shape, BF16), DMA((1 + 2 * member_levels,))],
     )[0]
-    shared = group_levels * columns // 2 + (member_levels - 1) * width // 2
+    shared = (ranked - width) // 2
     pair, targets, send, keep = call(
-        functools.partial(field_kernel, leaves, bucket),
+        functools.partial(field_kernel, leaves, bucket, tops, lows),
         [
             jax.ShapeDtypeStruct((2, capacity, columns), BF16),
             jax.ShapeDtypeStruct((filled // 8, leaves * 8), I32),
             jax.ShapeDtypeStruct((shared + width, columns), F32),
             jax.ShapeDtypeStruct((shared, columns), F32),
         ],
-        [SMEM, VMEM, VMEM, HBM],
-        (place, arrived, right_top, *far(low_right)),
+        [SMEM, VMEM, VMEM],
+        (place, arrived, right),
         far_flops,
         6 << 20,
         24,
-        scratch=[
-            pltpu.VMEM((group_levels * columns + member_levels * width, columns), F32),
-            pltpu.VMEM(low_right.shape, BF16),
-            DMA,
-        ],
+        scratch=[pltpu.VMEM((ranked, columns), F32)],
     )
     height = capacity // 8
 
@@ -373,6 +389,19 @@
         )[0]
 
     received = partner(send, "member", 0)
+    slots, order = call(
+        way_kernel,
+        [
+            jax.ShapeDtypeStruct((leaves * filled, leaves * 8), BF16),
+            jax.ShapeDtypeStruct((count, capacity), BF16),
+        ],
+        [VMEM, VMEM, pl.BlockSpec(memory_space=pl.ANY)],
+        (targets, places, send),
+        0,
+        8 << 20,
+        16,
+    )
+    received, slots, order = lax.optimization_barrier((received, slots, order))
     nearest = received[shared:]
     running = keep + received[:shared]
     bases = []
@@ -385,27 +414,25 @@
             received, bases[0] = lax.optimization_barrier((received, bases[0]))
         if bit == member_levels - 1:
             bases.append(diagonal(5, 3, running))
-            left_top, left_low, slots, order = call(
+            left_top, left_low = call(
                 stage_kernel,
                 [
                     pltpu.VMEM(top_left.shape, BF16),
                     pltpu.VMEM((capacity, member_levels * 2 * width), BF16),
-                    jax.ShapeDtypeStruct((leaves * filled, leaves * 8), BF16),
-                    jax.ShapeDtypeStruct((count, capacity), BF16),
                 ],
-                [HBM, HBM, VMEM, VMEM, pl.BlockSpec(memory_space=pl.ANY)],
-                (*far(top_left, low_left), targets, places, running),
+                [HBM, HBM, pl.BlockSpec(memory_space=pl.ANY)],
+                (*far(top_left, low_left), running),
                 0,
                 8 << 20,
                 24,
                 scratch=[pltpu.VMEM(low_left.shape, BF16), DMA((2,))],
             )
-            received, bases[1], left_top, left_low, slots, order = lax.optimization_barrier(
-                (received, bases[1], left_top, left_low, slots, order)
+            received, bases[1], left_top, left_low = lax.optimization_barrier(
+                (received, bases[1], left_top, left_low)
             )
         coefs.insert(0, received[rest:].astype(BF16))
         running = running[:rest] + received[:rest]
-    half = columns // 2
+    half = top_width // 2
     tops = [None] * group_levels
     for apart in range(1, groups):
         level = group_levels - apart.bit_length()
@@ -454,7 +481,7 @@
         4 << 20,
         16,
         out_specs=[HBM],
-        scratch=[pltpu.VMEM((count, 128), F32), DMA((count // 256,))],
+        scratch=[pltpu.VMEM((count, 128), F32), DMA((count // 512,))],
     )[0]
 
 

time: 72 us -> 72.1 us (level)
  waiting for transfers between devices: 19.7 us -> 18.1 us
  Pallas kernels: 21.4 us -> 22.9 us
    pallas_call x9 -> x10, Pallas kernels: 21.4 us -> 22.9 us  [call(): pl.pallas_call(kernel, out_shape=outs, in_specs=ins, out_specs=more.pop('...]
    ppermute x5, waiting for transfers between devices: 4.33 us -> 3.46 us  [partner(): return lax.ppermute(block, axis, route)]
  transfers between devices with their start and end apart: 9 -> 9, of which waited for: 7 -> 7; matrix products, arithmetic and copies ran while one was open for 1% -> 1% of each run, Pallas kernels for 17% -> 19%
where the time goes in v3:
time: 72.1 us; the launch traced here: 71.8 us
  Pallas kernels  22.9 us (32%)
  waiting for transfers between devices  18.1 us (25%)
  blocking collectives  18 us (25%)
  starting transfers between devices  11.7 us (16%)
    pallas_call x10, Pallas kernels, call(): pl.pallas_call(kernel, out_shape=outs, in_specs=ins, out_specs=more.pop('...  22.9 us
    all_to_all x1, blocking collectives, on_device(): lax.all_to_all(leaving.reshape(leaves, bucket, columns), everyone, split_...  18 us
    all_to_all x1, waiting for transfers between devices, on_device(): lax.all_to_all(packed, everyone, split_axis=0, concat_axis=0, tiled=True)  13.5 us
    all_to_all x1, starting transfers between devices, on_device(): lax.all_to_all(packed, everyone, split_axis=0, concat_axis=0, tiled=True)  7.43 us
    ppermute x3, starting transfers between devices, on_device(): heard = lax.ppermute(sent, 'group', route)  3.61 us
    ppermute x5, waiting for transfers between devices, partner(): return lax.ppermute(block, axis, route)  3.46 us
  transfers between devices with their start and end apart: 9, of which 7 were waited for; matrix products, arithmetic and copies ran while one was open for 1% of the time, Pallas kernels for 19%

profile of v3, /device:TPU:0, one launch (start us, length us, event | category | flops | bytes accessed | tf_op | source)
XLA Modules:
  0.0 71.8 jit_solution(10495151811859270902)
XLA Ops:
  0.0 0.0 copy-start
  0.0 2.9 %shard_map.91 = (bf16[32,64,128]{2,1,0:T(8,128)(2,1)}, s32[1,1024]{1,0:T(1,128)S(1)}) custom-call(s32[32]{0:T(128)} %sizes_in.1, s32[1,1024]{1,0:T(1,128)} %bitcast.12, bf16[1024,128]{1,0:T(8,128)(2,1)} %rows_in.1), custom_call_target="tpu_custom_call" | custom-call | flops 268435456 | bytes 4194304 | tf_op jit(solution)/shard_map/pallas_call | solution.py:34
  2.9 7.4 %all-to-all-start = ((bf16[32,64,128]{2,1,0:T(8,128)(2,1)}), bf16[32,64,128]{2,1,0:T(8,128)(2,1)}, u32[]{:S(2)}, u32[]{:S(2)}) async-start(bf16[32,64,128]{2,1,0:T(8,128)(2,1)} %get-tuple-element.26), calls=%async_computation | async-start | bytes 1048576 | tf_op jit(solution)/shard_map/all_to_all | solution.py:347
  10.4 0.6 gather_fusion
  11.1 2.1 %shard_map.92.right = bf16[2,448,1792]{2,1,0:T(8,128)(2,1)S(1)} custom-call(bf16[2,2,1792,128]{3,2,1,0:T(8,128)(2,1)} %right_top_in.1, bf16[3,2,64,1792]{3,2,1,0:T(8,128)(2,1)} %bitcast.11), custom_call_target="tpu_custom_call" | custom-call | bytes 6291456 | tf_op jit(solution)/shard_map/pallas_call | solution.py:34
  13.2 0.1 pad_add_fusion.place
  13.2 13.5 %all-to-all-done.arrived = bf16[32,64,128]{2,1,0:T(8,128)(2,1)} async-done(((bf16[32,64,128]{2,1,0:T(8,128)(2,1)}), bf16[32,64,128]{2,1,0:T(8,128)(2,1)}, u32[]{:S(2)}, u32[]{:S(2)}) %all-to-all-start) | async-done | bytes 524320 | tf_op jit(solution)/shard_map/all_to_all | solution.py:347
  26.7 2.9 %shard_map.93 = (bf16[2,1792,128]{2,1,0:T(8,128)(2,1)S(1)}, s32[7,256]{1,0:T(8,128)S(1)}, f32[256,128]{1,0:T(8,128)S(1)}, f32[192,128]{1,0:T(8,128)S(1)}) custom-call(s32[6]{0:T(128)S(1)} %pad_add_fusion.place, bf16[32,64,128]{2,1,0:T(8,128)(2,1)} %all-to-all-done.arrived, bf16[2,448,1792]{2,1,0:T(8,128)(2,1)S(1)} %shard_map.92.right), custom_call_target="tpu_custom_call" | custom-call | flops 411041792 | bytes 6291456 | tf_op jit(solution)/shard_map/pallas_call | solution.py:34
  29.6 0.1 collective-permute-start
  29.7 1.0 %shard_map.94 = (bf16[1792,256]{1,0:T(8,128)(2,1)S(1)}, bf16[1024,1792]{1,0:T(8,128)(2,1)S(1)}) custom-call(s32[7,256]{1,0:T(8,128)S(1)} %get-tuple-element.28.targets, s32[1,1024]{1,0:T(1,128)S(1)} %get-tuple-element.29.places, f32[256,128]{1,0:T(8,128)S(1)} %get-tuple-element.27.after), custom_call_target="tpu_custom_call" | custom-call | bytes 8388608 | tf_op jit(solution)/shard_map/pallas_call | solution.py:34
  30.7 0.3 collective-permute-done
  31.0 0.1 collective-permute-start.1
  31.1 4.3 %shard_map.95.rest_0_ = f32[1120,128]{1,0:T(8,128)S(1)} custom-call(bf16[2,1792,1792]{2,1,0:T(8,128)(2,1)} %block_in.3, bf16[2,1792,128]{2,1,0:T(8,128)(2,1)S(1)} %get-tuple-element.35.pair, f32[192,128]{1,0:T(8,128)S(1)} %slice_add_fusion.after), custom_call_target="tpu_custom_call" | custom-call | flops 1027604480 | bytes 8028160 | tf_op jit(solution)/shard_map/pallas_call | solution.py:34
  35.4 0.5 collective-permute-done.1
  36.0 0.5 collective-permute-start.2
  36.5 1.9 %shard_map.97 = (bf16[2,2,1792,128]{3,2,1,0:T(8,128)(2,1)S(1)}, bf16[1792,384]{1,0:T(8,128)(2,1)S(1)}) custom-call(bf16[2,2,1792,128]{3,2,1,0:T(8,128)(2,1)} %left_top_in.1, bf16[3,2,64,1792]{3,2,1,0:T(8,128)(2,1)} %bitcast.10, f32[160,128]{1,0:T(8,128)S(1)} %slice_add_fusion.1.after), custom_call_target="tpu_custom_call" | custom-call | bytes 8388608 | tf_op jit(solution)/shard_map/pallas_call | solution.py:34
  38.4 3.2 %shard_map.96.rest_1_ = f32[672,128]{1,0:T(8,128)S(1)} custom-call(bf16[2,1792,1792]{2,1,0:T(8,128)(2,1)} %block_in.3, bf16[2,1792,128]{2,1,0:T(8,128)(2,1)S(1)} %get-tuple-element.35.pair, f32[160,128]{1,0:T(8,128)S(1)} %slice_add_fusion.1.after), custom_call_target="tpu_custom_call" | custom-call | flops 616562688 | bytes 4816896 | tf_op jit(solution)/shard_map/pallas_call | solution.py:34
  41.6 1.4 %collective-permute-done.2 = f32[160,128]{1,0:T(8,128)S(1)} collective-permute-done((f32[160,128]{1,0:T(8,128)S(1)}, f32[160,128]{1,0:T(8,128)S(1)}, u32[]{:S(2)}, u32[]{:S(2)}) %collective-permute-start.2) | collective-permute-done | bytes 81952 | tf_op jit(solution)/shard_map/ppermute | solution.py:53
  43.0 0.0 collective-permute-start.6
  43.1 0.7 %collective-permute-start.3 = (f32[64,128]{1,0:T(8,128)S(1)}, f32[64,128]{1,0:T(8,128)S(1)}, u32[]{:S(2)}, u32[]{:S(2)}) collective-permute-start(f32[64,128]{1,0:T(8,128)S(1)} %slice.48), channel_id=1, source_target_pairs={{0,16},{8,24},{16,0},{24,8},{1,17},{9,25},{17,1},{25,9},{2,18},{10... | collective-permute-start | bytes 98312 | tf_op jit(solution)/shard_map/ppermute | solution.py:443
  43.8 1.5 %collective-permute-start.4 = (f32[64,128]{1,0:T(8,128)S(1)}, f32[64,128]{1,0:T(8,128)S(1)}, u32[]{:S(2)}, u32[]{:S(2)}) collective-permute-start(f32[64,128]{1,0:T(8,128)S(1)} %slice.48), channel_id=1, source_target_pairs={{0,24},{8,16},{16,8},{24,0},{1,25},{9,17},{17,9},{25,1},{2,26},{10... | collective-permute-start | bytes 98312 | tf_op jit(solution)/shard_map/ppermute | solution.py:443
  45.3 1.4 %collective-permute-start.5 = (bf16[64,128]{1,0:T(8,128)(2,1)S(1)}, bf16[64,128]{1,0:T(8,128)(2,1)S(1)}, u32[]{:S(2)}, u32[]{:S(2)}) collective-permute-start(bf16[64,128]{1,0:T(8,128)(2,1)S(1)} %slice.60), channel_id=1, source_target_pairs={{0,8},{8,0},{16,24},{24,16},{1,9},{9,1},{17,25},{25,17},{2,10},{10... | collective-permute-start | bytes 49160 | tf_op jit(solution)/shard_map/ppermute | solution.py:443
  46.7 0.0 collective-permute-done.6.rest_5_
  46.7 1.1 %shard_map.98.base = f32[1792,128]{1,0:T(8,128)S(1)} custom-call(s32[6]{0:T(128)S(1)} %pad_add_fusion.place, f32[1120,128]{1,0:T(8,128)S(1)} %shard_map.95.rest_0_, f32[672,128]{1,0:T(8,128)S(1)} %shard_map.96.rest_1_, bf16[1792,384]{1,0:T(8,128)(2,1)S(1)} %get-tuple-element.42.rest_2_, f32[64,128]{1,0:T(8,128)S(1)} %slice.41.rest_3_, ...), custom_call_target="tpu_custom_call" | custom-call | flops 176160768 | bytes 3145728 | tf_op jit(solution)/shard_map/pallas_call | solution.py:34
  47.8 0.0 collective-permute-done.3
  47.8 0.8 %collective-permute-done.4 = f32[64,128]{1,0:T(8,128)S(1)} collective-permute-done((f32[64,128]{1,0:T(8,128)S(1)}, f32[64,128]{1,0:T(8,128)S(1)}, u32[]{:S(2)}, u32[]{:S(2)}) %collective-permute-start.4) | collective-permute-done | bytes 32800 | tf_op jit(solution)/shard_map/ppermute | solution.py:443
  48.6 0.5 collective-permute-done.5
  49.1 0.0 collective-permute-start.7
  49.1 1.2 %collective-permute-done.7.theirs = bf16[128,128]{1,0:T(8,128)(2,1)S(1)} collective-permute-done((bf16[128,128]{1,0:T(8,128)(2,1)S(1)}, bf16[128,128]{1,0:T(8,128)(2,1)S(1)}, u32[]{:S(2)}, u32[]{:S(2)}) %collective-permute-start.7) | collective-permute-done | bytes 32800 | tf_op jit(solution)/shard_map/ppermute | solution.py:53
  50.3 1.5 %shard_map.99 = bf16[1792,128]{1,0:T(8,128)(2,1)S(1)} custom-call(s32[6]{0:T(128)S(1)} %pad_add_fusion.place, f32[1792,128]{1,0:T(8,128)S(1)} %shard_map.98.base, bf16[2,2,1792,128]{3,2,1,0:T(8,128)(2,1)S(1)} %get-tuple-element.44.left_top, bf16[128,128]{1,0:T(8,128)(2,1)S(1)} %pad_maximum_fusion.own, bf16[128,128]{1,0:T(8,128)(2,1)S(1)} %collective-permute-done.7.theirs, ...), custom_call_target="tpu_custom_call" | custom-call | flops 234881024 | bytes 4194304 | tf_op jit(solution)/shard_map/pallas_call | solution.py:34
  51.8 18.0 %all_to_all.10 = bf16[32,56,128]{2,1,0:T(8,128)(2,1)S(1)} all-to-all(bf16[32,56,128]{2,1,0:T(8,128)(2,1)S(1)} %bitcast.8), channel_id=1, replica_groups=mesh['group'=4,'member'=8] {'group','member'}, dimensions={0} | all-to-all | bytes 917504 | tf_op jit(solution)/shard_map/all_to_all | solution.py:472
  69.9 1.9 %shard_map.100 = f32[1024,128]{1,0:T(8,128)} custom-call(bf16[1024,1792]{1,0:T(8,128)(2,1)S(1)} %get-tuple-element.32.order, bf16[1792,128]{1,0:T(8,128)(2,1)S(1)} %bitcast.9), custom_call_target="tpu_custom_call" | custom-call | flops 469762048 | bytes 4194304 | tf_op jit(solution)/shard_map/pallas_call | solution.py:34
  (14 shorter events, 0.1 us)
Async XLA Ops:
  0.0 10.4 %copy-start = (s32[62]{0:T(128)S(1)}, s32[62]{0:T(128)}, u32[]{:S(2)}) copy-start(s32[62]{0:T(128)} %param.12) | copy-start | bytes 748
  2.9 23.8 %all-to-all-start = ((bf16[32,64,128]{2,1,0:T(8,128)(2,1)}), bf16[32,64,128]{2,1,0:T(8,128)(2,1)}, u32[]{:S(2)}, u32[]{:S(2)}) async-start(bf16[32,64,128]{2,1,0:T(8,128)(2,1)} %get-tuple-element.26), calls=%async_computation | async-start | bytes 1048576 | tf_op jit(solution)/shard_map/all_to_all | solution.py:347
  29.6 1.4 %collective-permute-start = (f32[256,128]{1,0:T(8,128)S(1)}, f32[256,128]{1,0:T(8,128)S(1)}, u32[]{:S(2)}, u32[]{:S(2)}) collective-permute-start(f32[256,128]{1,0:T(8,128)S(1)} %get-tuple-element.27.after), channel_id=1, source_target_pairs={{0,1},{1,0},{2,3},{3,2},{4,5},{5,4},{6,7},{7,6},{8,9},{9,8},{10,11... | collective-permute-start | bytes 393224 | tf_op jit(solution)/shard_map/ppermute | solution.py:53
  31.0 5.0 %collective-permute-start.1 = (f32[192,128]{1,0:T(8,128)S(1)}, f32[192,128]{1,0:T(8,128)S(1)}, u32[]{:S(2)}, u32[]{:S(2)}) collective-permute-start(f32[192,128]{1,0:T(8,128)S(1)} %slice_add_fusion.after), channel_id=1, source_target_pairs={{0,2},{2,0},{1,3},{3,1},{4,6},{6,4},{5,7},{7,5},{8,10},{10,8},{9,1... | collective-permute-start | bytes 294920 | tf_op jit(solution)/shard_map/ppermute | solution.py:53
  36.0 7.0 %collective-permute-start.2 = (f32[160,128]{1,0:T(8,128)S(1)}, f32[160,128]{1,0:T(8,128)S(1)}, u32[]{:S(2)}, u32[]{:S(2)}) collective-permute-start(f32[160,128]{1,0:T(8,128)S(1)} %slice_add_fusion.1.after), channel_id=1, source_target_pairs={{0,4},{4,0},{1,5},{5,1},{2,6},{6,2},{3,7},{7,3},{8,12},{12,8},{9,1... | collective-permute-start | bytes 245768 | tf_op jit(solution)/shard_map/ppermute | solution.py:53
  43.0 3.7 %collective-permute-start.6 = (bf16[64,128]{1,0:T(8,128)(2,1)S(1)}, bf16[64,128]{1,0:T(8,128)(2,1)S(1)}, u32[]{:S(2)}, u32[]{:S(2)}) collective-permute-start(bf16[64,128]{1,0:T(8,128)(2,1)S(1)} %pad_maximum_fusion.1.rest_4_), channel_id=1, source_target_pairs={{0,1},{1,0},{2,3},{3,2},{4,5},{5,4},{6,7},{7,6},{8,9},{9,8},{10,11... | collective-permute-start | bytes 49160 | tf_op jit(solution)/shard_map/ppermute | solution.py:53
  43.1 4.8 %collective-permute-start.3 = (f32[64,128]{1,0:T(8,128)S(1)}, f32[64,128]{1,0:T(8,128)S(1)}, u32[]{:S(2)}, u32[]{:S(2)}) collective-permute-start(f32[64,128]{1,0:T(8,128)S(1)} %slice.48), channel_id=1, source_target_pairs={{0,16},{8,24},{16,0},{24,8},{1,17},{9,25},{17,1},{25,9},{2,18},{10... | collective-permute-start | bytes 98312 | tf_op jit(solution)/shard_map/ppermute | solution.py:443
  43.8 4.8 %collective-permute-start.4 = (f32[64,128]{1,0:T(8,128)S(1)}, f32[64,128]{1,0:T(8,128)S(1)}, u32[]{:S(2)}, u32[]{:S(2)}) collective-permute-start(f32[64,128]{1,0:T(8,128)S(1)} %slice.48), channel_id=1, source_target_pairs={{0,24},{8,16},{16,8},{24,0},{1,25},{9,17},{17,9},{25,1},{2,26},{10... | collective-permute-start | bytes 98312 | tf_op jit(solution)/shard_map/ppermute | solution.py:443
  45.3 3.8 %collective-permute-start.5 = (bf16[64,128]{1,0:T(8,128)(2,1)S(1)}, bf16[64,128]{1,0:T(8,128)(2,1)S(1)}, u32[]{:S(2)}, u32[]{:S(2)}) collective-permute-start(bf16[64,128]{1,0:T(8,128)(2,1)S(1)} %slice.60), channel_id=1, source_target_pairs={{0,8},{8,0},{16,24},{24,16},{1,9},{9,1},{17,25},{25,17},{2,10},{10... | collective-permute-start | bytes 49160 | tf_op jit(solution)/shard_map/ppermute | solution.py:443
  49.1 1.2 %collective-permute-start.7 = (bf16[128,128]{1,0:T(8,128)(2,1)S(1)}, bf16[128,128]{1,0:T(8,128)(2,1)S(1)}, u32[]{:S(2)}, u32[]{:S(2)}) collective-permute-start(bf16[128,128]{1,0:T(8,128)(2,1)S(1)} %pad_maximum_fusion.own), channel_id=1, source_target_pairs={{0,1},{1,0},{2,3},{3,2},{4,5},{5,4},{6,7},{7,6},{8,9},{9,8},{10,11... | collective-permute-start | bytes 98312 | tf_op jit(solution)/shard_map/ppermute | solution.py:53

commit v4 on v3

--- a/solution.py
+++ b/solution.py
@@ -133,19 +133,22 @@
         copy.wait()
 
 
-def way_kernel(targets, places, after, slots, order):
+def way_kernel(targets, places, after, slots, order, upper):
     groups, part = targets.shape
     lanes = iota((part, 128), 1)
     for g in range(groups):
         target = jnp.transpose(jnp.broadcast_to(targets[g : g + 1, :], (128, part)))
         for low in range(0, part, 128):
             slots[g * part : (g + 1) * part, low : low + 128] = hot(target == lanes + low)
-    count, slots_out = order.shape
+    count, folded = order.shape
     place = jnp.transpose(jnp.broadcast_to(places[...], (128, count)))
+    beyond = place >= folded
+    upper[...] = beyond.astype(I32)
+    place = jnp.where(beyond, place - folded, place)
     block = 256
     lanes = iota((block, 128), 1)
     for low in range(0, count, block):
-        for at in range(0, slots_out, 128):
+        for at in range(0, folded, 128):
             order[low : low + block, at : at + 128] = hot(place[low : low + block] == lanes + at)
 
 
@@ -167,46 +170,45 @@
     capacity = leaves * bucket
     padded = arrived.shape[1]
     part = leaves * 8
+    groups = targets.shape[0]
     core = jnp.bitwise_and(place[0], 1)
     last = arrived[:, padded - 16 :, :].reshape(leaves * 16, 128)
     carrier = iota((leaves, leaves * 16), 1) == iota((leaves, leaves * 16), 0) * 16 + bucket % 16
     offsets = dot(hot(carrier), last).astype(BF16)
     spread = hot(jnp.right_shift(iota((leaves, part), 1), 3) == iota((leaves, part), 0))
-    spread_offsets = dot(offsets, spread, (0, 0))
+    spread_offsets = dot(offsets, spread, (0, 0))[: groups * 8].reshape(groups, 8, part)
     lane_window = jnp.bitwise_and(iota((8, part), 1), 7)
-    own = lane_window == iota((8, part), 0)
-    for g in range(padded // 8):
+    own = (lane_window == iota((8, part), 0))[None]
+    target = jnp.sum(jnp.where(own, spread_offsets, 0.0), axis=1).astype(I32)
+    target = target + lane_window[:1, :] * leaves
+    targets[...] = target
+    for g in range(groups):
         size = min(part, capacity - g * part)
-        if size <= 0:
-            continue
-        rows = spread_offsets[g * 8 : g * 8 + 8, :]
-        offset = jnp.sum(jnp.where(own, rows, 0.0), axis=0, keepdims=True).astype(I32)
-        target = offset + lane_window[:1, :] * leaves
-        targets[g : g + 1, :] = target
         if g % 2 == 0:
             both = arrived[:, g * 8 : g * 8 + 16, :].astype(F32)
         chunk = both[:, g % 2 * 8 : g % 2 * 8 + 8, :].reshape(part, 128).astype(BF16)
-        placed = dot(hot(iota((part, part), 0) == target), chunk)
+        placed = dot(hot(iota((part, part), 0) == target[g : g + 1, :]), chunk)
         pair[0, g * part : g * part + size, :] = placed[:size].astype(BF16)
         pair[1, g * part : g * part + size, :] = turn(placed)[:size].astype(BF16)
-    whole[...] = dot(right[0], pair[0]) + dot(right[1], pair[1])
+    top_rows = tops * 128
+    width = (right.shape[1] - top_rows) // levels
+    plain = jnp.transpose(pair[0])
+    turned = jnp.concatenate([-plain[64:], plain[:64]], axis=0)
+    upper = dot(plain, right[0, :top_rows, :], (1, 1)) + dot(turned, right[1, :top_rows, :], (1, 1))
+    for level in range(tops):
+        whole[level * 128 : (level + 1) * 128, :] = upper[:, level * 128 : (level + 1) * 128]
+    lower = dot(right[0, top_rows:, :], pair[0]) + dot(right[1, top_rows:, :], pair[1])
+    whole[top_rows:, :] = lower
     at = 0
-    for low, half in segments(tops, levels):
+    low = 0
+    for half in [tops * 64] + [width // 2] * (levels - 1):
         mine = pl.multiple_of(low + core * half, 8)
         other = pl.multiple_of(low + (1 - core) * half, 8)
         keep[at : at + half, :] = whole[pl.ds(mine, half), :]
         send[at : at + half, :] = whole[pl.ds(other, half), :]
         at += half
-    send[at:, :] = whole[whole.shape[0] + at - send.shape[0] :, :]
-
-
-def segments(tops, lows):
-    found, low = [], 0
-    for count, width in (tops, (lows[0] - 1, lows[1])):
-        for _ in range(count):
-            found.append((low, width // 2))
-            low += width
-    return found
+        low += 2 * half
+    send[at:, :] = lower[(levels - 1) * width :]
 
 
 def diag_kernel(first, block_in, pair, after, out, block, sems):
@@ -257,12 +259,13 @@
     leaves = part // 8
     core = jnp.bitwise_and(place[0], 1)
     levels = left_top.shape[0]
-    half = own.shape[0] // levels
+    half = own.shape[0]
     stacked = []
     for level in range(levels):
-        coef = merged(core, own, theirs, level * half, half)
-        coef = jnp.where(iota(coef.shape, 0) < place[1 + level], coef, 0.0)
-        stacked += [coef, turn(coef)]
+        coef = jnp.where(core == level, own[...], theirs[...]).astype(F32)
+        coef = jnp.where(iota(coef.shape, 1) < place[1 + level], coef, 0.0)
+        turned = jnp.concatenate([-coef[half // 2 :], coef[: half // 2]], axis=0)
+        stacked += [jnp.transpose(coef), jnp.transpose(turned)]
     stacked = jnp.concatenate(stacked, axis=0).astype(BF16)
     if groups * part > capacity:
         spare[capacity:, :] = jnp.zeros((groups * part - capacity, 128), BF16)
@@ -275,13 +278,15 @@
     packed[...] = ordered[:, :bucket, :].reshape(capacity, 128).astype(BF16)
 
 
-def unpack_kernel(order, returned, out, near, sems):
-    count = order.shape[0]
+def unpack_kernel(order, upper, returned, out, near, sems):
+    count, folded = order.shape
+    wide = jnp.concatenate([returned[:folded, :], returned[folded:, :]], axis=1)
     block = 512
     copies = []
     for low in range(0, count, block):
         rows = pl.ds(low, block)
-        near[rows, :] = dot(order[low : low + block, :], returned[...])
+        both = dot(order[low : low + block, :], wide)
+        near[rows, :] = jnp.where(upper[low : low + block, :] != 0, both[:, 128:], both[:, :128])
         copies.append(pltpu.make_async_copy(near.at[rows, :], out.at[rows, :], sems.at[low // block]))
         copies[-1].start()
     for copy in copies:
@@ -345,8 +350,6 @@
         ],
     )
     arrived = lax.all_to_all(packed, everyone, split_axis=0, concat_axis=0, tiled=True)
-    tops = (group_levels, top_width)
-    lows = (member_levels, width)
     ranked = group_levels * top_width + member_levels * width
     right = call(
         near_kernel,
@@ -358,9 +361,10 @@
         16,
         scratch=[pltpu.VMEM(top_right.shape, BF16), DMA((1 + 2 * member_levels,))],
     )[0]
-    shared = (ranked - width) // 2
+    tops = group_levels * columns // 2
+    shared = tops + (member_levels - 1) * width // 2
     pair, targets, send, keep = call(
-        functools.partial(field_kernel, leaves, bucket, tops, lows),
+        functools.partial(field_kernel, leaves, bucket, group_levels, member_levels),
         [
             jax.ShapeDtypeStruct((2, capacity, columns), BF16),
             jax.ShapeDtypeStruct((filled // 8, leaves * 8), I32),
@@ -372,7 +376,7 @@
         far_flops,
         6 << 20,
         24,
-        scratch=[pltpu.VMEM((ranked, columns), F32)],
+        scratch=[pltpu.VMEM((2 * shared + width, columns), F32)],
     )
     height = capacity // 8
 
@@ -389,11 +393,12 @@
         )[0]
 
     received = partner(send, "member", 0)
-    slots, order = call(
+    slots, order, upper = call(
         way_kernel,
         [
             jax.ShapeDtypeStruct((leaves * filled, leaves * 8), BF16),
-            jax.ShapeDtypeStruct((count, capacity), BF16),
+            jax.ShapeDtypeStruct((count, capacity // 2), BF16),
+            jax.ShapeDtypeStruct((count, 128), I32),
         ],
         [VMEM, VMEM, pl.BlockSpec(memory_space=pl.ANY)],
         (targets, places, send),
@@ -401,7 +406,7 @@
         8 << 20,
         16,
     )
-    received, slots, order = lax.optimization_barrier((received, slots, order))
+    received, slots, order, upper = lax.optimization_barrier((received, slots, order, upper))
     nearest = received[shared:]
     running = keep + received[:shared]
     bases = []
@@ -432,16 +437,13 @@
             )
         coefs.insert(0, received[rest:].astype(BF16))
         running = running[:rest] + received[:rest]
-    half = top_width // 2
-    tops = [None] * group_levels
-    for apart in range(1, groups):
-        level = group_levels - apart.bit_length()
-        sent = running[level * half : (level + 1) * half]
-        if apart == 1:
-            sent = sent.astype(BF16)
-        route = [(low, low ^ apart) for low in range(groups)]
-        heard = lax.ppermute(sent, "group", route)
-        tops[level] = heard if tops[level] is None else tops[level] + heard
+    routes = [[], []]
+    for low in range(groups):
+        for near in range(0, members, 2):
+            at = low * members + near
+            routes[0] += [(at, (low ^ 2) * members + near), (at + 1, (low ^ 1) * members + near + 1)]
+            routes[1] += [(at + core, (low ^ 3) * members + near + core) for core in range(2)]
+    heard = [lax.ppermute(running, everyone, route) for route in routes]
     own_low = jnp.concatenate(coefs)
     base = call(
         functools.partial(low_kernel, len(bases)),
@@ -452,7 +454,8 @@
         3 << 20,
         16,
     )[0]
-    own = jnp.concatenate([top.astype(BF16) for top in tops])
+    second = jnp.where(jnp.bitwise_and(device, 1) == 0, heard[1], 0.0)
+    own = (heard[0] + second).astype(BF16)
     own, base = lax.optimization_barrier((own, base))
     theirs = partner(own, "member", 0)
 
@@ -475,8 +478,8 @@
     return call(
         unpack_kernel,
         [jax.ShapeDtypeStruct((count, columns), F32)],
-        [VMEM] * 2,
-        (order, returned.reshape(capacity, columns)),
+        [VMEM] * 3,
+        (order, upper, returned.reshape(capacity, columns)),
         2 * capacity * count * columns,
         4 << 20,
         16,

time: 72.1 us -> 75 us (1.040)
  local copies, waits for them, and re-layouts: 0.66 us -> 4.19 us
  waiting for transfers between devices: 18.1 us -> 16.5 us
  other arithmetic: 0.14 us -> 1.02 us
  blocking collectives: 18 us -> 18.8 us
    unnamed x2 -> x14, local copies, waits for them, and re-layouts: 0.01 us -> 3.53 us
    ppermute x3 -> x2, waiting for transfers between devices: 1.23 us -> 0.01 us  [on_device(): heard = [lax.ppermute(running, everyone, route) for route in routes]]
    convert_element_type x1, other arithmetic: 0.01 us -> 0.89 us  [on_device(): own = (heard[0] + second).astype(BF16)]
    ppermute x3 -> x2, starting transfers between devices: 3.61 us -> 2.79 us  [on_device(): heard = [lax.ppermute(running, everyone, route) for route in routes]]
    all_to_all x1, blocking collectives: 18 us -> 18.8 us  [on_device(): lax.all_to_all(leaving.reshape(leaves, bucket, columns), everyone, split_...]
  transfers between devices with their start and end apart: 9 -> 8, of which waited for: 7 -> 4; matrix products, arithmetic and copies ran while one was open for 1% -> 1% of each run, Pallas kernels for 19% -> 19%
where the time goes in v4:
time: 75 us; the launch traced here: 74.7 us
  Pallas kernels  22.8 us (30%)
  blocking collectives  18.8 us (25%)
  waiting for transfers between devices  16.5 us (22%)
  starting transfers between devices  11.1 us (15%)
  local copies, waits for them, and re-layouts  4.19 us (6%)
  other arithmetic  1.02 us (1%)
    pallas_call x10, Pallas kernels, call(): pl.pallas_call(kernel, out_shape=outs, in_specs=ins, out_specs=more.pop('...  22.8 us
    all_to_all x1, blocking collectives, on_device(): lax.all_to_all(leaving.reshape(leaves, bucket, columns), everyone, split_...  18.8 us
    all_to_all x1, waiting for transfers between devices, on_device(): lax.all_to_all(packed, everyone, split_axis=0, concat_axis=0, tiled=True)  13.5 us
    all_to_all x1, starting transfers between devices, on_device(): lax.all_to_all(packed, everyone, split_axis=0, concat_axis=0, tiled=True)  7.43 us
    unnamed x14, local copies, waits for them, and re-layouts  3.53 us
    ppermute x5, waiting for transfers between devices, partner(): return lax.ppermute(block, axis, route)  3.06 us
    ppermute x2, starting transfers between devices, on_device(): heard = [lax.ppermute(running, everyone, route) for route in routes]  2.79 us
  transfers between devices with their start and end apart: 8, of which 4 were waited for; matrix products, arithmetic and copies ran while one was open for 1% of the time, Pallas kernels for 19%

profile of v4, /device:TPU:0, one launch (start us, length us, event | category | flops | bytes accessed | tf_op | source)
XLA Modules:
  0.0 74.7 jit_solution(16368998699829314589)
XLA Ops:
  0.0 2.9 %shard_map.91 = (bf16[32,64,128]{2,1,0:T(8,128)(2,1)}, s32[1,1024]{1,0:T(1,128)S(1)}) custom-call(s32[32]{0:T(128)} %sizes_in.1, s32[1,1024]{1,0:T(1,128)} %bitcast.12, bf16[1024,128]{1,0:T(8,128)(2,1)} %rows_in.1), custom_call_target="tpu_custom_call" | custom-call | flops 268435456 | bytes 4194304 | tf_op jit(solution)/shard_map/pallas_call | solution.py:34
  2.9 7.4 %all-to-all-start = ((bf16[32,64,128]{2,1,0:T(8,128)(2,1)}), bf16[32,64,128]{2,1,0:T(8,128)(2,1)}, u32[]{:S(2)}, u32[]{:S(2)}) async-start(bf16[32,64,128]{2,1,0:T(8,128)(2,1)} %get-tuple-element.28), calls=%async_computation | async-start | bytes 1048576 | tf_op jit(solution)/shard_map/all_to_all | solution.py:352
  10.4 0.6 gather_fusion
  11.1 2.1 %shard_map.92.right = bf16[2,448,1792]{2,1,0:T(8,128)(2,1)S(1)} custom-call(bf16[2,2,1792,128]{3,2,1,0:T(8,128)(2,1)} %right_top_in.1, bf16[3,2,64,1792]{3,2,1,0:T(8,128)(2,1)} %bitcast.11), custom_call_target="tpu_custom_call" | custom-call | bytes 6291456 | tf_op jit(solution)/shard_map/pallas_call | solution.py:34
  13.2 0.1 pad_add_fusion.place
  13.2 13.5 %all-to-all-done.arrived = bf16[32,64,128]{2,1,0:T(8,128)(2,1)} async-done(((bf16[32,64,128]{2,1,0:T(8,128)(2,1)}), bf16[32,64,128]{2,1,0:T(8,128)(2,1)}, u32[]{:S(2)}, u32[]{:S(2)}) %all-to-all-start) | async-done | bytes 524320 | tf_op jit(solution)/shard_map/all_to_all | solution.py:352
  26.7 2.9 %shard_map.93 = (bf16[2,1792,128]{2,1,0:T(8,128)(2,1)S(1)}, s32[7,256]{1,0:T(8,128)S(1)}, f32[256,128]{1,0:T(8,128)S(1)}, f32[192,128]{1,0:T(8,128)S(1)}) custom-call(s32[6]{0:T(128)S(1)} %pad_add_fusion.place, bf16[32,64,128]{2,1,0:T(8,128)(2,1)} %all-to-all-done.arrived, bf16[2,448,1792]{2,1,0:T(8,128)(2,1)S(1)} %shard_map.92.right), custom_call_target="tpu_custom_call" | custom-call | flops 411041792 | bytes 6291456 | tf_op jit(solution)/shard_map/pallas_call | solution.py:34
  29.6 0.1 collective-permute-start
  29.7 0.7 shard_map.94
  30.5 0.9 %copy-done.5 = bf16[1792,256]{1,0:T(8,128)(2,1)} copy-done((bf16[1792,256]{1,0:T(8,128)(2,1)}, bf16[1792,256]{1,0:T(8,128)(2,1)S(1)}, u32[]{:S(2)}) %copy-start.5) | copy-done | bytes 917528
  31.4 0.0 collective-permute-done
  31.4 0.1 collective-permute-start.1
  31.5 4.3 %shard_map.95.rest_0_ = f32[1120,128]{1,0:T(8,128)S(1)} custom-call(bf16[2,1792,1792]{2,1,0:T(8,128)(2,1)} %block_in.3, bf16[2,1792,128]{2,1,0:T(8,128)(2,1)S(1)} %get-tuple-element.39.pair, f32[192,128]{1,0:T(8,128)S(1)} %slice_add_fusion.after), custom_call_target="tpu_custom_call" | custom-call | flops 1027604480 | bytes 8028160 | tf_op jit(solution)/shard_map/pallas_call | solution.py:34
  35.8 0.8 %collective-permute-done.1 = f32[192,128]{1,0:T(8,128)S(1)} collective-permute-done((f32[192,128]{1,0:T(8,128)S(1)}, f32[192,128]{1,0:T(8,128)S(1)}, u32[]{:S(2)}, u32[]{:S(2)}) %collective-permute-start.1) | collective-permute-done | bytes 98336 | tf_op jit(solution)/shard_map/ppermute | solution.py:53
  36.7 0.5 collective-permute-start.2
  37.2 1.9 %shard_map.97 = (bf16[2,2,1792,128]{3,2,1,0:T(8,128)(2,1)S(1)}, bf16[1792,384]{1,0:T(8,128)(2,1)S(1)}) custom-call(bf16[2,2,1792,128]{3,2,1,0:T(8,128)(2,1)} %left_top_in.1, bf16[3,2,64,1792]{3,2,1,0:T(8,128)(2,1)} %bitcast.10, f32[160,128]{1,0:T(8,128)S(1)} %slice_add_fusion.1.after), custom_call_target="tpu_custom_call" | custom-call | bytes 8388608 | tf_op jit(solution)/shard_map/pallas_call | solution.py:34
  39.1 1.2 %copy-done.1 = bf16[2,2,1792,128]{3,2,1,0:T(8,128)(2,1)} copy-done((bf16[2,2,1792,128]{3,2,1,0:T(8,128)(2,1)}, bf16[2,2,1792,128]{3,2,1,0:T(8,128)(2,1)S(1)}, u32[]{:S(2)}) %copy-start.1) | copy-done | bytes 1835032
  40.4 3.7 %shard_map.96.rest_1_ = f32[672,128]{1,0:T(8,128)S(1)} custom-call(bf16[2,1792,1792]{2,1,0:T(8,128)(2,1)} %block_in.3, bf16[2,1792,128]{2,1,0:T(8,128)(2,1)S(1)} %get-tuple-element.39.pair, f32[160,128]{1,0:T(8,128)S(1)} %slice_add_fusion.1.after), custom_call_target="tpu_custom_call" | custom-call | flops 616562688 | bytes 4816896 | tf_op jit(solution)/shard_map/pallas_call | solution.py:34
  44.1 0.9 %collective-permute-start.3 = (f32[128,128]{1,0:T(8,128)S(1)}, f32[128,128]{1,0:T(8,128)}, u32[]{:S(2)}, u32[]{:S(2)}) collective-permute-start(f32[128,128]{1,0:T(8,128)S(1)} %slice_add_fusion.2), channel_id=1, source_target_pairs={{0,16},{1,9},{2,18},{3,11},{4,20},{5,13},{6,22},{7,15},{8,24},{9,1... | collective-permute-start | bytes 196616 | tf_op jit(solution)/shard_map/ppermute | solution.py:446
  45.0 1.9 %collective-permute-start.4 = (f32[128,128]{1,0:T(8,128)S(1)}, f32[128,128]{1,0:T(8,128)}, u32[]{:S(2)}, u32[]{:S(2)}) collective-permute-start(f32[128,128]{1,0:T(8,128)S(1)} %slice_add_fusion.2), channel_id=1, source_target_pairs={{0,24},{1,25},{2,26},{3,27},{4,28},{5,29},{6,30},{7,31},{8,16},{9,... | collective-permute-start | bytes 196616 | tf_op jit(solution)/shard_map/ppermute | solution.py:446
  46.9 0.0 collective-permute-start.5
  46.9 1.2 %collective-permute-done.5.rest_5_ = bf16[64,128]{1,0:T(8,128)(2,1)S(1)} collective-permute-done((bf16[64,128]{1,0:T(8,128)(2,1)S(1)}, bf16[64,128]{1,0:T(8,128)(2,1)S(1)}, u32[]{:S(2)}, u32[]{:S(2)}) %collective-permute-start.5) | collective-permute-done | bytes 16416 | tf_op jit(solution)/shard_map/ppermute | solution.py:53
  48.1 1.3 %copy-done.4 = bf16[1792,384]{1,0:T(8,128)(2,1)S(1)} copy-done((bf16[1792,384]{1,0:T(8,128)(2,1)S(1)}, bf16[1792,384]{1,0:T(8,128)(2,1)}, u32[]{:S(2)}) %copy-start.4) | copy-done | bytes 1376280
  49.4 1.1 %shard_map.98.base = f32[1792,128]{1,0:T(8,128)S(1)} custom-call(s32[6]{0:T(128)S(1)} %pad_add_fusion.place, f32[1120,128]{1,0:T(8,128)S(1)} %shard_map.95.rest_0_, f32[672,128]{1,0:T(8,128)S(1)} %shard_map.96.rest_1_, bf16[1792,384]{1,0:T(8,128)(2,1)S(1)} %copy-done.4, f32[64,128]{1,0:T(8,128)S(1)} %slice.31.rest_3_, ...), custom_call_target="tpu_custom_call" | custom-call | flops 176160768 | bytes 3145728 | tf_op jit(solution)/shard_map/pallas_call | solution.py:34
  50.6 0.0 collective-permute-done.3
  50.6 0.0 collective-permute-done.4
  50.6 0.9 %add_convert_fusion.own = bf16[128,128]{1,0:T(8,128)(2,1)S(1)} fusion(f32[128,128]{1,0:T(8,128)} %collective-permute-done.3, f32[128,128]{1,0:T(8,128)} %collective-permute-done.4, pred[]{:T(512)S(6)} %eq.3), kind=kLoop, calls=%fused_computation.4 | loop fusion | flops 49152 | bytes 163841 | tf_op jit(solution)/shard_map/convert_element_type | solution.py:458
  51.5 0.2 collective-permute-start.6
  51.7 1.1 %collective-permute-done.6.theirs = bf16[128,128]{1,0:T(8,128)(2,1)S(1)} collective-permute-done((bf16[128,128]{1,0:T(8,128)(2,1)S(1)}, bf16[128,128]{1,0:T(8,128)(2,1)S(1)}, u32[]{:S(2)}, u32[]{:S(2)}) %collective-permute-start.6) | collective-permute-done | bytes 32800 | tf_op jit(solution)/shard_map/ppermute | solution.py:53
  52.8 1.6 %shard_map.99 = bf16[1792,128]{1,0:T(8,128)(2,1)S(1)} custom-call(s32[6]{0:T(128)S(1)} %pad_add_fusion.place, f32[1792,128]{1,0:T(8,128)S(1)} %shard_map.98.base, bf16[2,2,1792,128]{3,2,1,0:T(8,128)(2,1)S(1)} %copy-done.2, bf16[128,128]{1,0:T(8,128)(2,1)S(1)} %add_convert_fusion.own, bf16[128,128]{1,0:T(8,128)(2,1)S(1)} %collective-permute-done.6.theirs, ...), custom_call_target="tpu_custom_call" | custom-call | flops 234881024 | bytes 4194304 | tf_op jit(solution)/shard_map/pallas_call | solution.py:34
  54.3 18.8 %all_to_all.10 = bf16[32,56,128]{2,1,0:T(8,128)(2,1)S(1)} all-to-all(bf16[32,56,128]{2,1,0:T(8,128)(2,1)S(1)} %bitcast.8), channel_id=1, replica_groups=mesh['group'=4,'member'=8] {'group','member'}, dimensions={0} | all-to-all | bytes 917504 | tf_op jit(solution)/shard_map/all_to_all | solution.py:475
  73.2 1.5 %shard_map.100 = f32[1024,128]{1,0:T(8,128)} custom-call(bf16[1024,896]{1,0:T(8,128)(2,1)S(1)} %get-tuple-element.35.order, s32[1024,128]{1,0:T(8,128)S(1)} %get-tuple-element.36.upper, bf16[1792,128]{1,0:T(8,128)(2,1)S(1)} %bitcast.9), custom_call_target="tpu_custom_call" | custom-call | flops 469762048 | bytes 4194304 | tf_op jit(solution)/shard_map/pallas_call | solution.py:34
  (21 shorter events, 0.1 us)
Async XLA Ops:
  0.0 10.4 %copy-start = (s32[62]{0:T(128)S(1)}, s32[62]{0:T(128)}, u32[]{:S(2)}) copy-start(s32[62]{0:T(128)} %param.12) | copy-start | bytes 748
  2.9 23.8 %all-to-all-start = ((bf16[32,64,128]{2,1,0:T(8,128)(2,1)}), bf16[32,64,128]{2,1,0:T(8,128)(2,1)}, u32[]{:S(2)}, u32[]{:S(2)}) async-start(bf16[32,64,128]{2,1,0:T(8,128)(2,1)} %get-tuple-element.28), calls=%async_computation | async-start | bytes 1048576 | tf_op jit(solution)/shard_map/all_to_all | solution.py:352
  29.6 1.8 %collective-permute-start = (f32[256,128]{1,0:T(8,128)S(1)}, f32[256,128]{1,0:T(8,128)S(1)}, u32[]{:S(2)}, u32[]{:S(2)}) collective-permute-start(f32[256,128]{1,0:T(8,128)S(1)} %get-tuple-element.29.after), channel_id=1, source_target_pairs={{0,1},{1,0},{2,3},{3,2},{4,5},{5,4},{6,7},{7,6},{8,9},{9,8},{10,11... | collective-permute-start | bytes 393224 | tf_op jit(solution)/shard_map/ppermute | solution.py:53
  30.5 0.9 %copy-start.5 = (bf16[1792,256]{1,0:T(8,128)(2,1)}, bf16[1792,256]{1,0:T(8,128)(2,1)S(1)}, u32[]{:S(2)}) copy-start(bf16[1792,256]{1,0:T(8,128)(2,1)S(1)} %get-tuple-element.50.slots) | copy-start | bytes 2752516
  31.4 5.3 %collective-permute-start.1 = (f32[192,128]{1,0:T(8,128)S(1)}, f32[192,128]{1,0:T(8,128)S(1)}, u32[]{:S(2)}, u32[]{:S(2)}) collective-permute-start(f32[192,128]{1,0:T(8,128)S(1)} %slice_add_fusion.after), channel_id=1, source_target_pairs={{0,2},{2,0},{1,3},{3,1},{4,6},{6,4},{5,7},{7,5},{8,10},{10,8},{9,1... | collective-permute-start | bytes 294920 | tf_op jit(solution)/shard_map/ppermute | solution.py:53
  36.7 7.4 %collective-permute-start.2 = (f32[160,128]{1,0:T(8,128)S(1)}, f32[160,128]{1,0:T(8,128)S(1)}, u32[]{:S(2)}, u32[]{:S(2)}) collective-permute-start(f32[160,128]{1,0:T(8,128)S(1)} %slice_add_fusion.1.after), channel_id=1, source_target_pairs={{0,4},{4,0},{1,5},{5,1},{2,6},{6,2},{3,7},{7,3},{8,12},{12,8},{9,1... | collective-permute-start | bytes 245768 | tf_op jit(solution)/shard_map/ppermute | solution.py:53
  39.1 1.3 %copy-start.1 = (bf16[2,2,1792,128]{3,2,1,0:T(8,128)(2,1)}, bf16[2,2,1792,128]{3,2,1,0:T(8,128)(2,1)S(1)}, u32[]{:S(2)}) copy-start(bf16[2,2,1792,128]{3,2,1,0:T(8,128)(2,1)S(1)} %get-tuple-element.48.left_top) | copy-start | bytes 5505028
  40.4 3.7 %copy-start.3 = (bf16[1792,384]{1,0:T(8,128)(2,1)}, bf16[1792,384]{1,0:T(8,128)(2,1)S(1)}, u32[]{:S(2)}) copy-start(bf16[1792,384]{1,0:T(8,128)(2,1)S(1)} %get-tuple-element.46.rest_2_) | copy-start | bytes 4128772
  44.1 6.5 %collective-permute-start.3 = (f32[128,128]{1,0:T(8,128)S(1)}, f32[128,128]{1,0:T(8,128)}, u32[]{:S(2)}, u32[]{:S(2)}) collective-permute-start(f32[128,128]{1,0:T(8,128)S(1)} %slice_add_fusion.2), channel_id=1, source_target_pairs={{0,16},{1,9},{2,18},{3,11},{4,20},{5,13},{6,22},{7,15},{8,24},{9,1... | collective-permute-start | bytes 196616 | tf_op jit(solution)/shard_map/ppermute | solution.py:446
  45.0 5.6 %collective-permute-start.4 = (f32[128,128]{1,0:T(8,128)S(1)}, f32[128,128]{1,0:T(8,128)}, u32[]{:S(2)}, u32[]{:S(2)}) collective-permute-start(f32[128,128]{1,0:T(8,128)S(1)} %slice_add_fusion.2), channel_id=1, source_target_pairs={{0,24},{1,25},{2,26},{3,27},{4,28},{5,29},{6,30},{7,31},{8,16},{9,... | collective-permute-start | bytes 196616 | tf_op jit(solution)/shard_map/ppermute | solution.py:446
  46.9 1.2 %collective-permute-start.5 = (bf16[64,128]{1,0:T(8,128)(2,1)S(1)}, bf16[64,128]{1,0:T(8,128)(2,1)S(1)}, u32[]{:S(2)}, u32[]{:S(2)}) collective-permute-start(bf16[64,128]{1,0:T(8,128)(2,1)S(1)} %pad_maximum_fusion.rest_4_), channel_id=1, source_target_pairs={{0,1},{1,0},{2,3},{3,2},{4,5},{5,4},{6,7},{7,6},{8,9},{9,8},{10,11... | collective-permute-start | bytes 49160 | tf_op jit(solution)/shard_map/ppermute | solution.py:53
  46.9 5.8 %copy-start.2 = (bf16[2,2,1792,128]{3,2,1,0:T(8,128)(2,1)S(1)}, bf16[2,2,1792,128]{3,2,1,0:T(8,128)(2,1)}, u32[]{:S(2)}) copy-start(bf16[2,2,1792,128]{3,2,1,0:T(8,128)(2,1)} %copy-done.1) | copy-start | bytes 5505028
  48.1 1.3 %copy-start.4 = (bf16[1792,384]{1,0:T(8,128)(2,1)S(1)}, bf16[1792,384]{1,0:T(8,128)(2,1)}, u32[]{:S(2)}) copy-start(bf16[1792,384]{1,0:T(8,128)(2,1)} %copy-done.3) | copy-start | bytes 4128772
  49.4 3.3 %copy-start.6 = (bf16[1792,256]{1,0:T(8,128)(2,1)S(1)}, bf16[1792,256]{1,0:T(8,128)(2,1)}, u32[]{:S(2)}) copy-start(bf16[1792,256]{1,0:T(8,128)(2,1)} %copy-done.5) | copy-start | bytes 2752516
  51.5 1.3 %collective-permute-start.6 = (bf16[128,128]{1,0:T(8,128)(2,1)S(1)}, bf16[128,128]{1,0:T(8,128)(2,1)S(1)}, u32[]{:S(2)}, u32[]{:S(2)}) collective-permute-start(bf16[128,128]{1,0:T(8,128)(2,1)S(1)} %add_convert_fusion.own), channel_id=1, source_target_pairs={{0,1},{1,0},{2,3},{3,2},{4,5},{5,4},{6,7},{7,6},{8,9},{9,8},{10,11... | collective-permute-start | bytes 98312 | tf_op jit(solution)/shard_map/ppermute | solution.py:53

commit v5 on v4

--- a/solution.py
+++ b/solution.py
@@ -113,23 +113,25 @@
         copy.wait()
 
 
-def near_kernel(right_top_in, right_low_in, right, raw, sems):
-    tops, _, _, top_width = right_top_in.shape
-    levels, _, width, _ = right_low_in.shape
-    copies = [pltpu.make_async_copy(right_top_in, raw, sems.at[0])]
-    for level in range(levels):
-        low = tops * top_width + level * width
-        for p in range(2):
-            target = right.at[p, pl.ds(low, width), :]
-            sem = sems.at[1 + 2 * level + p]
-            copies.append(pltpu.make_async_copy(right_low_in.at[level, p], target, sem))
+def near_kernel(right_top_in, right_low_in, right, sems):
+    tops, parts, capacity, width = right_top_in.shape
+    levels, _, rows, _ = right_low_in.shape
+    pairs = []
+    for level in range(tops):
+        for p in range(parts):
+            place = (pl.ds(p * capacity, capacity), pl.ds(level * width, width))
+            pairs.append((right_top_in.at[level, p], right.at[place]))
+    at = parts * capacity
+    for low in range(0, capacity, 256):
+        for p in range(parts):
+            for level in range(levels):
+                source = right_low_in.at[level, p, :, pl.ds(low, 256)]
+                pairs.append((source, right.at[pl.ds(at, rows), :]))
+                at += rows
+    copies = [pltpu.make_async_copy(a, b, sems.at[i]) for i, (a, b) in enumerate(pairs)]
     for copy in copies:
         copy.start()
-    copies[0].wait()
-    for level in range(tops):
-        for p in range(2):
-            right[p, level * top_width : (level + 1) * top_width, :] = jnp.transpose(raw[level, p])
-    for copy in copies[1:]:
+    for copy in copies:
         copy.wait()
 
 
@@ -166,7 +168,7 @@
 
 
 def field_kernel(leaves, bucket, tops, levels, place, arrived, right, *rest):
-    pair, targets, send, keep, whole = rest
+    pair, targets, send, keep, gate, whole = rest
     capacity = leaves * bucket
     padded = arrived.shape[1]
     part = leaves * 8
@@ -190,15 +192,22 @@
         placed = dot(hot(iota((part, part), 0) == target[g : g + 1, :]), chunk)
         pair[0, g * part : g * part + size, :] = placed[:size].astype(BF16)
         pair[1, g * part : g * part + size, :] = turn(placed)[:size].astype(BF16)
-    top_rows = tops * 128
-    width = (right.shape[1] - top_rows) // levels
     plain = jnp.transpose(pair[0])
     turned = jnp.concatenate([-plain[64:], plain[:64]], axis=0)
-    upper = dot(plain, right[0, :top_rows, :], (1, 1)) + dot(turned, right[1, :top_rows, :], (1, 1))
+    upper = dot(plain, right[:capacity, :]) + dot(turned, right[capacity : 2 * capacity, :])
+    top_rows = tops * 128
     for level in range(tops):
         whole[level * 128 : (level + 1) * 128, :] = upper[:, level * 128 : (level + 1) * 128]
-    lower = dot(right[0, top_rows:, :], pair[0]) + dot(right[1, top_rows:, :], pair[1])
+    rows = whole.shape[0] - top_rows
+    width = rows // levels
+    lower = jnp.zeros((rows, 128), F32)
+    at = 2 * capacity
+    for low in range(0, capacity, 256):
+        for p in range(2):
+            lower += dot(right[at : at + rows, :], pair[p, low : low + 256, :])
+            at += rows
     whole[top_rows:, :] = lower
+    gate[...] = jnp.broadcast_to((1 - core).astype(F32), gate.shape)
     at = 0
     low = 0
     for half in [tops * 64] + [width // 2] * (levels - 1):
@@ -353,23 +362,24 @@
     ranked = group_levels * top_width + member_levels * width
     right = call(
         near_kernel,
-        [pltpu.VMEM((2, ranked, capacity), BF16)],
+        [pltpu.VMEM((2 * ranked * capacity // 256, 256), BF16)],
         [HBM] * 2,
         far(top_right, low_right),
         0,
         6 << 20,
         16,
-        scratch=[pltpu.VMEM(top_right.shape, BF16), DMA((1 + 2 * member_levels,))],
+        scratch=[DMA((2 * group_levels + 2 * member_levels * capacity // 256,))],
     )[0]
     tops = group_levels * columns // 2
     shared = tops + (member_levels - 1) * width // 2
-    pair, targets, send, keep = call(
+    pair, targets, send, keep, gate = call(
         functools.partial(field_kernel, leaves, bucket, group_levels, member_levels),
         [
             jax.ShapeDtypeStruct((2, capacity, columns), BF16),
             jax.ShapeDtypeStruct((filled // 8, leaves * 8), I32),
             jax.ShapeDtypeStruct((shared + width, columns), F32),
             jax.ShapeDtypeStruct((shared, columns), F32),
+            jax.ShapeDtypeStruct((1, columns), F32),
         ],
         [SMEM, VMEM, VMEM],
         (place, arrived, right),
@@ -419,22 +429,7 @@
             received, bases[0] = lax.optimization_barrier((received, bases[0]))
         if bit == member_levels - 1:
             bases.append(diagonal(5, 3, running))
-            left_top, left_low = call(
-                stage_kernel,
-                [
-                    pltpu.VMEM(top_left.shape, BF16),
-                    pltpu.VMEM((capacity, member_levels * 2 * width), BF16),
-                ],
-                [HBM, HBM, pl.BlockSpec(memory_space=pl.ANY)],
-                (*far(top_left, low_left), running),
-                0,
-                8 << 20,
-                24,
-                scratch=[pltpu.VMEM(low_left.shape, BF16), DMA((2,))],
-            )
-            received, bases[1], left_top, left_low = lax.optimization_barrier(
-                (received, bases[1], left_top, left_low)
-            )
+            received, bases[1] = lax.optimization_barrier((received, bases[1]))
         coefs.insert(0, received[rest:].astype(BF16))
         running = running[:rest] + received[:rest]
     routes = [[], []]
@@ -444,20 +439,33 @@
             routes[0] += [(at, (low ^ 2) * members + near), (at + 1, (low ^ 1) * members + near + 1)]
             routes[1] += [(at + core, (low ^ 3) * members + near + core) for core in range(2)]
     heard = [lax.ppermute(running, everyone, route) for route in routes]
+    left_top, left_low = call(
+        stage_kernel,
+        [
+            pltpu.VMEM(top_left.shape, BF16),
+            pltpu.VMEM((capacity, member_levels * 2 * width), BF16),
+        ],
+        [HBM, HBM, pl.BlockSpec(memory_space=pl.ANY)],
+        (*far(top_left, low_left), running),
+        0,
+        8 << 20,
+        24,
+        scratch=[pltpu.VMEM(low_left.shape, BF16), DMA((2,))],
+    )
+    heard, left_top, left_low = lax.optimization_barrier((heard, left_top, left_low))
+    own = (heard[0] + jnp.where(gate > 0, heard[1], 0.0)).astype(BF16)
     own_low = jnp.concatenate(coefs)
+    their_low, own = lax.optimization_barrier((partner(own_low, "member", 0), own))
+    theirs = partner(own, "member", 0)
     base = call(
         functools.partial(low_kernel, len(bases)),
         [jax.ShapeDtypeStruct((capacity, columns), F32)],
         [SMEM] + [VMEM] * (len(bases) + 4),
-        (place, *bases, left_low, nearest, own_low, partner(own_low, "member", 0)),
+        (place, *bases, left_low, nearest, own_low, their_low),
         4 * capacity * columns * member_levels * width,
         3 << 20,
         16,
     )[0]
-    second = jnp.where(jnp.bitwise_and(device, 1) == 0, heard[1], 0.0)
-    own = (heard[0] + second).astype(BF16)
-    own, base = lax.optimization_barrier((own, base))
-    theirs = partner(own, "member", 0)
 
     leaving = call(
         functools.partial(out_kernel, bucket),

time: 75 us -> 70.3 us (0.937)
  local copies, waits for them, and re-layouts: 4.19 us -> 0.66 us
  waiting for transfers between devices: 16.5 us -> 19.4 us
  blocking collectives: 18.8 us -> 17.3 us
  other arithmetic: 1.02 us -> 0.15 us
  Pallas kernels: 22.8 us -> 22 us
    unnamed x14 -> x2, local copies, waits for them, and re-layouts: 3.53 us -> 0.01 us
    ppermute x2, waiting for transfers between devices: 0.01 us -> 1.54 us  [on_device(): heard = [lax.ppermute(running, everyone, route) for route in routes]]
    all_to_all x1, blocking collectives: 18.8 us -> 17.3 us  [on_device(): lax.all_to_all(leaving.reshape(leaves, bucket, columns), everyone, split_...]
    ppermute x5, waiting for transfers between devices: 3.06 us -> 4.45 us  [partner(): return lax.ppermute(block, axis, route)]
    convert_element_type x1, other arithmetic: 0.89 us -> 0.01 us  [on_device(): own = (heard[0] + jnp.where(gate > 0, heard[1], 0.0)).astype(BF16)]
    pallas_call x10, Pallas kernels: 22.8 us -> 22 us  [call(): pl.pallas_call(kernel, out_shape=outs, in_specs=ins, out_specs=more.pop('...]
  transfers between devices with their start and end apart: 8 -> 8, of which waited for: 4 -> 6; matrix products, arithmetic and copies ran while one was open for 1% -> 1% of each run, Pallas kernels for 19% -> 19%
where the time goes in v5:
time: 70.3 us; the launch traced here: 70 us
  Pallas kernels  22 us (31%)
  waiting for transfers between devices  19.4 us (28%)
  blocking collectives  17.3 us (25%)
  starting transfers between devices  10.4 us (15%)
    pallas_call x10, Pallas kernels, call(): pl.pallas_call(kernel, out_shape=outs, in_specs=ins, out_specs=more.pop('...  22 us
    all_to_all x1, blocking collectives, on_device(): lax.all_to_all(leaving.reshape(leaves, bucket, columns), everyone, split_...  17.3 us
    all_to_all x1, waiting for transfers between devices, on_device(): lax.all_to_all(packed, everyone, split_axis=0, concat_axis=0, tiled=True)  13.4 us
    all_to_all x1, starting transfers between devices, on_device(): lax.all_to_all(packed, everyone, split_axis=0, concat_axis=0, tiled=True)  7.43 us
    ppermute x5, waiting for transfers between devices, partner(): return lax.ppermute(block, axis, route)  4.45 us
    ppermute x2, starting transfers between devices, on_device(): heard = [lax.ppermute(running, everyone, route) for route in routes]  2.23 us
    ppermute x2, waiting for transfers between devices, on_device(): heard = [lax.ppermute(running, everyone, route) for route in routes]  1.54 us
  transfers between devices with their start and end apart: 8, of which 6 were waited for; matrix products, arithmetic and copies ran while one was open for 1% of the time, Pallas kernels for 19%

profile of v5, /device:TPU:0, one launch (start us, length us, event | category | flops | bytes accessed | tf_op | source)
XLA Modules:
  0.0 70.0 jit_solution(18076169029946138501)
XLA Ops:
  0.0 0.0 copy-start
  0.0 2.9 %shard_map.91 = (bf16[32,64,128]{2,1,0:T(8,128)(2,1)}, s32[1,1024]{1,0:T(1,128)S(1)}) custom-call(s32[32]{0:T(128)} %sizes_in.1, s32[1,1024]{1,0:T(1,128)} %bitcast.14, bf16[1024,128]{1,0:T(8,128)(2,1)} %rows_in.1), custom_call_target="tpu_custom_call" | custom-call | flops 268435456 | bytes 4194304 | tf_op jit(solution)/shard_map/pallas_call | solution.py:34
  2.9 7.4 %all-to-all-start = ((bf16[32,64,128]{2,1,0:T(8,128)(2,1)}), bf16[32,64,128]{2,1,0:T(8,128)(2,1)}, u32[]{:S(2)}, u32[]{:S(2)}) async-start(bf16[32,64,128]{2,1,0:T(8,128)(2,1)} %get-tuple-element.31), calls=%async_computation | async-start | bytes 1048576 | tf_op jit(solution)/shard_map/all_to_all | solution.py:361
  10.4 0.0 copy-done
  10.4 0.6 gather_fusion
  11.1 2.2 %shard_map.92.right = bf16[6272,256]{1,0:T(8,128)(2,1)S(1)} custom-call(bf16[2,2,1792,128]{3,2,1,0:T(8,128)(2,1)} %right_top_in.1, bf16[3,2,64,1792]{3,2,1,0:T(8,128)(2,1)} %bitcast.13), custom_call_target="tpu_custom_call" | custom-call | bytes 6291456 | tf_op jit(solution)/shard_map/pallas_call | solution.py:34
  13.2 0.1 pad_add_fusion.place
  13.3 13.4 %all-to-all-done.arrived = bf16[32,64,128]{2,1,0:T(8,128)(2,1)} async-done(((bf16[32,64,128]{2,1,0:T(8,128)(2,1)}), bf16[32,64,128]{2,1,0:T(8,128)(2,1)}, u32[]{:S(2)}, u32[]{:S(2)}) %all-to-all-start) | async-done | bytes 524320 | tf_op jit(solution)/shard_map/all_to_all | solution.py:361
  26.7 2.5 %shard_map.93 = (bf16[2,1792,128]{2,1,0:T(8,128)(2,1)S(1)}, s32[7,256]{1,0:T(8,128)S(1)}, f32[256,128]{1,0:T(8,128)S(1)}, f32[192,128]{1,0:T(8,128)S(1)}, f32[1,128]{1,0:T(1,128)S(1)}) custom-call(s32[6]{0:T(128)S(1)} %pad_add_fusion.place, bf16[32,64,128]{2,1,0:T(8,128)(2,1)} %all-to-all-done.arrived, bf16[6272,256]{1,0:T(8,128)(2,1)S(1)} %shard_map.92.right), custom_call_target="tpu_custom_call" | custom-call | flops 411041792 | bytes 6291456 | tf_op jit(solution)/shard_map/pallas_call | solution.py:34
  29.2 0.1 collective-permute-start
  29.3 0.7 %shard_map.94 = (bf16[1792,256]{1,0:T(8,128)(2,1)S(1)}, bf16[1024,896]{1,0:T(8,128)(2,1)S(1)}, s32[1024,128]{1,0:T(8,128)S(1)}) custom-call(s32[7,256]{1,0:T(8,128)S(1)} %get-tuple-element.33.targets, s32[1,1024]{1,0:T(1,128)S(1)} %get-tuple-element.34.places, f32[256,128]{1,0:T(8,128)S(1)} %get-tuple-element.32.after), custom_call_target="tpu_custom_call" | custom-call | bytes 8388608 | tf_op jit(solution)/shard_map/pallas_call | solution.py:34
  30.0 0.6 collective-permute-done
  30.6 0.1 collective-permute-start.1
  30.7 4.3 %shard_map.95.rest_0_ = f32[1120,128]{1,0:T(8,128)S(1)} custom-call(bf16[2,1792,1792]{2,1,0:T(8,128)(2,1)} %block_in.3, bf16[2,1792,128]{2,1,0:T(8,128)(2,1)S(1)} %get-tuple-element.42.pair, f32[192,128]{1,0:T(8,128)S(1)} %slice_add_fusion.after), custom_call_target="tpu_custom_call" | custom-call | flops 1027604480 | bytes 8028160 | tf_op jit(solution)/shard_map/pallas_call | solution.py:34
  35.0 0.5 collective-permute-done.1
  35.5 0.5 collective-permute-start.2
  36.1 3.2 %shard_map.96.rest_1_ = f32[672,128]{1,0:T(8,128)S(1)} custom-call(bf16[2,1792,1792]{2,1,0:T(8,128)(2,1)} %block_in.3, bf16[2,1792,128]{2,1,0:T(8,128)(2,1)S(1)} %get-tuple-element.42.pair, f32[160,128]{1,0:T(8,128)S(1)} %slice_add_fusion.1.after), custom_call_target="tpu_custom_call" | custom-call | flops 616562688 | bytes 4816896 | tf_op jit(solution)/shard_map/pallas_call | solution.py:34
  39.2 3.3 %collective-permute-done.2 = f32[160,128]{1,0:T(8,128)S(1)} collective-permute-done((f32[160,128]{1,0:T(8,128)S(1)}, f32[160,128]{1,0:T(8,128)S(1)}, u32[]{:S(2)}, u32[]{:S(2)}) %collective-permute-start.2) | collective-permute-done | bytes 81952 | tf_op jit(solution)/shard_map/ppermute | solution.py:53
  42.6 0.8 %collective-permute-start.4 = (f32[128,128]{1,0:T(8,128)S(1)}, f32[128,128]{1,0:T(8,128)S(1)}, u32[]{:S(2)}, u32[]{:S(2)}) collective-permute-start(f32[128,128]{1,0:T(8,128)S(1)} %slice_add_fusion.2.after), channel_id=1, source_target_pairs={{0,24},{1,25},{2,26},{3,27},{4,28},{5,29},{6,30},{7,31},{8,16},{9,... | collective-permute-start | bytes 196616 | tf_op jit(solution)/shard_map/ppermute | solution.py:441
  43.4 1.5 %collective-permute-start.3 = (f32[128,128]{1,0:T(8,128)S(1)}, f32[128,128]{1,0:T(8,128)S(1)}, u32[]{:S(2)}, u32[]{:S(2)}) collective-permute-start(f32[128,128]{1,0:T(8,128)S(1)} %slice_add_fusion.2.after), channel_id=1, source_target_pairs={{0,16},{1,9},{2,18},{3,11},{4,20},{5,13},{6,22},{7,15},{8,24},{9,1... | collective-permute-start | bytes 196616 | tf_op jit(solution)/shard_map/ppermute | solution.py:441
  44.8 0.0 collective-permute-start.5
  44.8 1.9 %shard_map.97 = (bf16[2,2,1792,128]{3,2,1,0:T(8,128)(2,1)S(1)}, bf16[1792,384]{1,0:T(8,128)(2,1)S(1)}) custom-call(bf16[2,2,1792,128]{3,2,1,0:T(8,128)(2,1)} %left_top_in.1, bf16[3,2,64,1792]{3,2,1,0:T(8,128)(2,1)} %bitcast.12, f32[128,128]{1,0:T(8,128)S(1)} %slice_add_fusion.2.after), custom_call_target="tpu_custom_call" | custom-call | bytes 8388608 | tf_op jit(solution)/shard_map/pallas_call | solution.py:34
  46.8 1.2 %collective-permute-done.4 = f32[128,128]{1,0:T(8,128)S(1)} collective-permute-done((f32[128,128]{1,0:T(8,128)S(1)}, f32[128,128]{1,0:T(8,128)S(1)}, u32[]{:S(2)}, u32[]{:S(2)}) %collective-permute-start.4) | collective-permute-done | bytes 65568 | tf_op jit(solution)/shard_map/ppermute | solution.py:441
  47.9 0.4 collective-permute-done.3
  48.3 0.0 collective-permute-done.5.rest_5_
  48.4 0.1 collective-permute-start.6
  48.4 1.1 %shard_map.98.base = f32[1792,128]{1,0:T(8,128)S(1)} custom-call(s32[6]{0:T(128)S(1)} %pad_add_fusion.place, f32[1120,128]{1,0:T(8,128)S(1)} %shard_map.95.rest_0_, f32[672,128]{1,0:T(8,128)S(1)} %shard_map.96.rest_1_, bf16[1792,384]{1,0:T(8,128)(2,1)S(1)} %get-tuple-element.49.rest_2_, f32[64,128]{1,0:T(8,128)S(1)} %slice.31.rest_3_, ...), custom_call_target="tpu_custom_call" | custom-call | flops 176160768 | bytes 3145728 | tf_op jit(solution)/shard_map/pallas_call | solution.py:34
  49.6 0.0 collective-permute-done.6.theirs
  49.6 1.6 %shard_map.99 = bf16[1792,128]{1,0:T(8,128)(2,1)S(1)} custom-call(s32[6]{0:T(128)S(1)} %pad_add_fusion.place, f32[1792,128]{1,0:T(8,128)S(1)} %shard_map.98.base, bf16[2,2,1792,128]{3,2,1,0:T(8,128)(2,1)S(1)} %get-tuple-element.54.left_top, bf16[128,128]{1,0:T(8,128)(2,1)S(1)} %add_convert_fusion.own, bf16[128,128]{1,0:T(8,128)(2,1)S(1)} %collective-permute-done.6.theirs, ...), custom_call_target="tpu_custom_call" | custom-call | flops 234881024 | bytes 4194304 | tf_op jit(solution)/shard_map/pallas_call | solution.py:34
  51.2 17.3 %all_to_all.10 = bf16[32,56,128]{2,1,0:T(8,128)(2,1)S(1)} all-to-all(bf16[32,56,128]{2,1,0:T(8,128)(2,1)S(1)} %bitcast.10), channel_id=1, replica_groups=mesh['group'=4,'member'=8] {'group','member'}, dimensions={0} | all-to-all | bytes 917504 | tf_op jit(solution)/shard_map/all_to_all | solution.py:483
  68.5 1.5 %shard_map.100 = f32[1024,128]{1,0:T(8,128)} custom-call(bf16[1024,896]{1,0:T(8,128)(2,1)S(1)} %get-tuple-element.38.order, s32[1024,128]{1,0:T(8,128)S(1)} %get-tuple-element.39.upper, bf16[1792,128]{1,0:T(8,128)(2,1)S(1)} %bitcast.11), custom_call_target="tpu_custom_call" | custom-call | flops 469762048 | bytes 4194304 | tf_op jit(solution)/shard_map/pallas_call | solution.py:34
  (11 shorter events, 0.1 us)
Async XLA Ops:
  0.0 10.4 %copy-start = (s32[62]{0:T(128)S(1)}, s32[62]{0:T(128)}, u32[]{:S(2)}) copy-start(s32[62]{0:T(128)} %param.12) | copy-start | bytes 748
  2.9 23.8 %all-to-all-start = ((bf16[32,64,128]{2,1,0:T(8,128)(2,1)}), bf16[32,64,128]{2,1,0:T(8,128)(2,1)}, u32[]{:S(2)}, u32[]{:S(2)}) async-start(bf16[32,64,128]{2,1,0:T(8,128)(2,1)} %get-tuple-element.31), calls=%async_computation | async-start | bytes 1048576 | tf_op jit(solution)/shard_map/all_to_all | solution.py:361
  29.2 1.4 %collective-permute-start = (f32[256,128]{1,0:T(8,128)S(1)}, f32[256,128]{1,0:T(8,128)S(1)}, u32[]{:S(2)}, u32[]{:S(2)}) collective-permute-start(f32[256,128]{1,0:T(8,128)S(1)} %get-tuple-element.32.after), channel_id=1, source_target_pairs={{0,1},{1,0},{2,3},{3,2},{4,5},{5,4},{6,7},{7,6},{8,9},{9,8},{10,11... | collective-permute-start | bytes 393224 | tf_op jit(solution)/shard_map/ppermute | solution.py:53
  30.6 4.9 %collective-permute-start.1 = (f32[192,128]{1,0:T(8,128)S(1)}, f32[192,128]{1,0:T(8,128)S(1)}, u32[]{:S(2)}, u32[]{:S(2)}) collective-permute-start(f32[192,128]{1,0:T(8,128)S(1)} %slice_add_fusion.after), channel_id=1, source_target_pairs={{0,2},{2,0},{1,3},{3,1},{4,6},{6,4},{5,7},{7,5},{8,10},{10,8},{9,1... | collective-permute-start | bytes 294920 | tf_op jit(solution)/shard_map/ppermute | solution.py:53
  35.5 7.0 %collective-permute-start.2 = (f32[160,128]{1,0:T(8,128)S(1)}, f32[160,128]{1,0:T(8,128)S(1)}, u32[]{:S(2)}, u32[]{:S(2)}) collective-permute-start(f32[160,128]{1,0:T(8,128)S(1)} %slice_add_fusion.1.after), channel_id=1, source_target_pairs={{0,4},{4,0},{1,5},{5,1},{2,6},{6,2},{3,7},{7,3},{8,12},{12,8},{9,1... | collective-permute-start | bytes 245768 | tf_op jit(solution)/shard_map/ppermute | solution.py:53
  42.6 5.3 %collective-permute-start.4 = (f32[128,128]{1,0:T(8,128)S(1)}, f32[128,128]{1,0:T(8,128)S(1)}, u32[]{:S(2)}, u32[]{:S(2)}) collective-permute-start(f32[128,128]{1,0:T(8,128)S(1)} %slice_add_fusion.2.after), channel_id=1, source_target_pairs={{0,24},{1,25},{2,26},{3,27},{4,28},{5,29},{6,30},{7,31},{8,16},{9,... | collective-permute-start | bytes 196616 | tf_op jit(solution)/shard_map/ppermute | solution.py:441
  43.4 5.0 %collective-permute-start.3 = (f32[128,128]{1,0:T(8,128)S(1)}, f32[128,128]{1,0:T(8,128)S(1)}, u32[]{:S(2)}, u32[]{:S(2)}) collective-permute-start(f32[128,128]{1,0:T(8,128)S(1)} %slice_add_fusion.2.after), channel_id=1, source_target_pairs={{0,16},{1,9},{2,18},{3,11},{4,20},{5,13},{6,22},{7,15},{8,24},{9,1... | collective-permute-start | bytes 196616 | tf_op jit(solution)/shard_map/ppermute | solution.py:441
  44.8 3.5 %collective-permute-start.5 = (bf16[64,128]{1,0:T(8,128)(2,1)S(1)}, bf16[64,128]{1,0:T(8,128)(2,1)S(1)}, u32[]{:S(2)}, u32[]{:S(2)}) collective-permute-start(bf16[64,128]{1,0:T(8,128)(2,1)S(1)} %pad_maximum_fusion.rest_4_), channel_id=1, source_target_pairs={{0,1},{1,0},{2,3},{3,2},{4,5},{5,4},{6,7},{7,6},{8,9},{9,8},{10,11... | collective-permute-start | bytes 49160 | tf_op jit(solution)/shard_map/ppermute | solution.py:53
  48.4 1.3 %collective-permute-start.6 = (bf16[128,128]{1,0:T(8,128)(2,1)S(1)}, bf16[128,128]{1,0:T(8,128)(2,1)S(1)}, u32[]{:S(2)}, u32[]{:S(2)}) collective-permute-start(bf16[128,128]{1,0:T(8,128)(2,1)S(1)} %add_convert_fusion.own), channel_id=1, source_target_pairs={{0,1},{1,0},{2,3},{3,2},{4,5},{5,4},{6,7},{7,6},{8,9},{9,8},{10,11... | collective-permute-start | bytes 98312 | tf_op jit(solution)/shard_map/ppermute | solution.py:53

commit v6 on v5

--- a/solution.py
+++ b/solution.py
@@ -60,6 +60,11 @@
 def turn(block):
     half = block.shape[1] // 2
     return jnp.where(iota(block.shape, 1) < half, -1.0, 1.0) * pltpu.roll(block, half, 1)
+
+
+def rank_of(ranks, level, levels):
+    device = lax.axis_index("group") * lax.axis_size("member") + lax.axis_index("member")
+    return ranks[(1 << level) - 2 + jnp.right_shift(device, levels - level)]
 
 
 def pack_kernel(leaves, bucket, sizes_in, position_in, rows_in, packed, places, *scratch):
@@ -98,7 +103,7 @@
     offsets = dot(picked, hot(iota((128, count), 0) == window - first), (1, 1))
     places[...] = owner * bucket + window - first
     line = iota((padded, 128), 0)
-    chunk = leaves // 4
+    chunk = leaves // 8
     out = []
     for c in range(leaves):
         data = ordered[pl.ds(starts[c], padded), :]
@@ -113,7 +118,7 @@
         copy.wait()
 
 
-def near_kernel(right_top_in, right_low_in, right, sems):
+def near_kernel(ranks, right_top_in, right_low_in, right, flags, sems):
     tops, parts, capacity, width = right_top_in.shape
     levels, _, rows, _ = right_low_in.shape
     pairs = []
@@ -131,6 +136,12 @@
     copies = [pltpu.make_async_copy(a, b, sems.at[i]) for i, (a, b) in enumerate(pairs)]
     for copy in copies:
         copy.start()
+    row, lane = iota(flags.shape, 0), iota(flags.shape, 1)
+    marks = jnp.where(row == 0, 1 - jnp.bitwise_and(lax.axis_index("member"), 1), 0)
+    for level in range(1, tops + 1):
+        counts = (lane < rank_of(ranks, level, tops + levels)).astype(I32)
+        marks = jnp.where(row == level, counts, marks)
+    flags[...] = marks.astype(F32)
     for copy in copies:
         copy.wait()
 
@@ -167,18 +178,17 @@
     copies[1].wait()
 
 
-def field_kernel(leaves, bucket, tops, levels, place, arrived, right, *rest):
-    pair, targets, send, keep, gate, whole = rest
+def field_kernel(leaves, bucket, tops, levels, arrived, right, *rest):
+    pair, targets, send, keep, whole = rest
     capacity = leaves * bucket
     padded = arrived.shape[1]
     part = leaves * 8
     groups = targets.shape[0]
-    core = jnp.bitwise_and(place[0], 1)
+    core = jnp.bitwise_and(lax.axis_index("member"), 1)
     last = arrived[:, padded - 16 :, :].reshape(leaves * 16, 128)
-    carrier = iota((leaves, leaves * 16), 1) == iota((leaves, leaves * 16), 0) * 16 + bucket % 16
-    offsets = dot(hot(carrier), last).astype(BF16)
-    spread = hot(jnp.right_shift(iota((leaves, part), 1), 3) == iota((leaves, part), 0))
-    spread_offsets = dot(offsets, spread, (0, 0))[: groups * 8].reshape(groups, 8, part)
+    row = iota((leaves * 16, part), 0)
+    spread = jnp.right_shift(iota((leaves * 16, part), 1), 3) * 16 + bucket % 16 == row
+    spread_offsets = dot(last, hot(spread), (0, 0))[: groups * 8].reshape(groups, 8, part)
     lane_window = jnp.bitwise_and(iota((8, part), 1), 7)
     own = (lane_window == iota((8, part), 0))[None]
     target = jnp.sum(jnp.where(own, spread_offsets, 0.0), axis=1).astype(I32)
@@ -207,7 +217,6 @@
             lower += dot(right[at : at + rows, :], pair[p, low : low + 256, :])
             at += rows
     whole[top_rows:, :] = lower
-    gate[...] = jnp.broadcast_to((1 - core).astype(F32), gate.shape)
     at = 0
     low = 0
     for half in [tops * 64] + [width // 2] * (levels - 1):
@@ -237,13 +246,12 @@
     return jnp.concatenate([jnp.where(core == 0, a, b), jnp.where(core == 0, b, a)], axis=0)
 
 
-def low_kernel(pieces, place, *rest):
+def low_kernel(pieces, tops, ranks, *rest):
     bases = rest[:pieces]
     left_low, nearest, own, theirs, out = rest[pieces:]
     width = nearest.shape[0]
     levels = left_low.shape[1] // (2 * width)
-    tops = place.shape[0] - 1 - levels
-    core = jnp.bitwise_and(place[0], 1)
+    core = jnp.bitwise_and(lax.axis_index("member"), 1)
     half = width // 2
     stacked = []
     for level in range(levels):
@@ -251,7 +259,8 @@
             coef = merged(core, own, theirs, level * half, half)
         else:
             coef = nearest[...]
-        coef = jnp.where(iota(coef.shape, 0) < place[1 + tops + level], coef, 0.0)
+        rank = rank_of(ranks, 1 + tops + level, tops + levels)
+        coef = jnp.where(iota(coef.shape, 0) < rank, coef, 0.0)
         stacked += [coef, turn(coef)]
     stacked = jnp.concatenate(stacked, axis=0).astype(BF16)
     low = 0
@@ -261,18 +270,19 @@
         low += base.shape[0]
 
 
-def out_kernel(bucket, place, base, left_top, own, theirs, slots, packed, spare, ordered):
+def out_kernel(bucket, flags, base, left_top, own, theirs, slots, packed, spare, ordered):
     capacity = base.shape[0]
     part = slots.shape[1]
     groups = slots.shape[0] // part
     leaves = part // 8
-    core = jnp.bitwise_and(place[0], 1)
+    first = flags[:1, :] > 0
     levels = left_top.shape[0]
     half = own.shape[0]
     stacked = []
     for level in range(levels):
-        coef = jnp.where(core == level, own[...], theirs[...]).astype(F32)
-        coef = jnp.where(iota(coef.shape, 1) < place[1 + level], coef, 0.0)
+        pick = (own, theirs) if level == 0 else (theirs, own)
+        coef = jnp.where(first, pick[0][...].astype(F32), pick[1][...].astype(F32))
+        coef = jnp.where(flags[1 + level : 2 + level, :] > 0, coef, 0.0)
         turned = jnp.concatenate([-coef[half // 2 :], coef[: half // 2]], axis=0)
         stacked += [jnp.transpose(coef), jnp.transpose(turned)]
     stacked = jnp.concatenate(stacked, axis=0).astype(BF16)
@@ -290,7 +300,7 @@
 def unpack_kernel(order, upper, returned, out, near, sems):
     count, folded = order.shape
     wide = jnp.concatenate([returned[:folded, :], returned[folded:, :]], axis=1)
-    block = 512
+    block = 256
     copies = []
     for low in range(0, count, block):
         rows = pl.ds(low, block)
@@ -318,8 +328,6 @@
     leaves = groups * members
     group_levels = groups.bit_length() - 1
     member_levels = members.bit_length() - 1
-    levels = group_levels + member_levels
-    device = lax.axis_index("group") * members + lax.axis_index("member")
     capacity = diag_block.shape[1]
     bucket = capacity // leaves
     padded = (bucket + 16) // 16 * 16
@@ -331,10 +339,6 @@
     width = low_left.shape[2]
     top_width = top_left.shape[3]
     far_flops = 4 * capacity * columns * (group_levels * top_width + member_levels * width)
-
-    level_ids = jnp.arange(1, levels + 1, dtype=I32)
-    ranks = block_ranks[(1 << level_ids) - 2 + jnp.right_shift(device, levels - level_ids)]
-    place = jnp.concatenate([device[None].astype(I32), ranks])
 
     packed, places = call(
         functools.partial(pack_kernel, leaves, bucket),
@@ -355,34 +359,36 @@
             pltpu.VMEM((count + padded, columns), F32),
             pltpu.VMEM((leaves, padded, columns), BF16),
             DMA((3,)),
-            DMA((4,)),
+            DMA((8,)),
         ],
     )
     arrived = lax.all_to_all(packed, everyone, split_axis=0, concat_axis=0, tiled=True)
     ranked = group_levels * top_width + member_levels * width
-    right = call(
+    right, flags = call(
         near_kernel,
-        [pltpu.VMEM((2 * ranked * capacity // 256, 256), BF16)],
-        [HBM] * 2,
-        far(top_right, low_right),
+        [
+            pltpu.VMEM((2 * ranked * capacity // 256, 256), BF16),
+            jax.ShapeDtypeStruct((8, columns), F32),
+        ],
+        [SMEM, HBM, HBM],
+        (block_ranks, *far(top_right, low_right)),
         0,
         6 << 20,
         16,
         scratch=[DMA((2 * group_levels + 2 * member_levels * capacity // 256,))],
-    )[0]
+    )
     tops = group_levels * columns // 2
     shared = tops + (member_levels - 1) * width // 2
-    pair, targets, send, keep, gate = call(
+    pair, targets, send, keep = call(
         functools.partial(field_kernel, leaves, bucket, group_levels, member_levels),
         [
             jax.ShapeDtypeStruct((2, capacity, columns), BF16),
             jax.ShapeDtypeStruct((filled // 8, leaves * 8), I32),
             jax.ShapeDtypeStruct((shared + width, columns), F32),
             jax.ShapeDtypeStruct((shared, columns), F32),
-            jax.ShapeDtypeStruct((1, columns), F32),
-        ],
-        [SMEM, VMEM, VMEM],
-        (place, arrived, right),
+        ],
+        [VMEM, VMEM],
+        (arrived, right),
         far_flops,
         6 << 20,
         24,
@@ -453,15 +459,15 @@
         scratch=[pltpu.VMEM(low_left.shape, BF16), DMA((2,))],
     )
     heard, left_top, left_low = lax.optimization_barrier((heard, left_top, left_low))
-    own = (heard[0] + jnp.where(gate > 0, heard[1], 0.0)).astype(BF16)
+    own = (heard[0] + jnp.where(flags[:1] > 0, heard[1], 0.0)).astype(BF16)
     own_low = jnp.concatenate(coefs)
     their_low, own = lax.optimization_barrier((partner(own_low, "member", 0), own))
     theirs = partner(own, "member", 0)
     base = call(
-        functools.partial(low_kernel, len(bases)),
+        functools.partial(low_kernel, len(bases), group_levels),
         [jax.ShapeDtypeStruct((capacity, columns), F32)],
         [SMEM] + [VMEM] * (len(bases) + 4),
-        (place, *bases, left_low, nearest, own_low, their_low),
+        (block_ranks, *bases, left_low, nearest, own_low, their_low),
         4 * capacity * columns * member_levels * width,
         3 << 20,
         16,
@@ -470,8 +476,8 @@
     leaving = call(
         functools.partial(out_kernel, bucket),
         [jax.ShapeDtypeStruct((capacity, columns), BF16)],
-        [SMEM] + [VMEM] * 5,
-        (place, base, left_top, own, theirs, slots),
+        [VMEM] * 6,
+        (flags, base, left_top, own, theirs, slots),
         4 * capacity * columns * group_levels * top_width,
         4 << 20,
         24,
@@ -492,7 +498,7 @@
         4 << 20,
         16,
         out_specs=[HBM],
-        scratch=[pltpu.VMEM((count, 128), F32), DMA((count // 512,))],
+        scratch=[pltpu.VMEM((count, 128), F32), DMA((count // 256,))],
     )[0]
 
 

time: 70.3 us -> 69.6 us (0.990)
  transfers between devices with their start and end apart: 8 -> 8, of which waited for: 6 -> 6; matrix products, arithmetic and copies ran while one was open for 1% -> 0% of each run, Pallas kernels for 19% -> 20%
where the time goes in v6:
time: 69.6 us; the launch traced here: 69.3 us
  Pallas kernels  21.7 us (31%)
  waiting for transfers between devices  19.6 us (28%)
  blocking collectives  17.3 us (25%)
  starting transfers between devices  10.4 us (15%)
    pallas_call x10, Pallas kernels, call(): pl.pallas_call(kernel, out_shape=outs, in_specs=ins, out_specs=more.pop('...  21.7 us
    all_to_all x1, blocking collectives, on_device(): lax.all_to_all(leaving.reshape(leaves, bucket, columns), everyone, split_...  17.3 us
    all_to_all x1, waiting for transfers between devices, on_device(): lax.all_to_all(packed, everyone, split_axis=0, concat_axis=0, tiled=True)  13.6 us
    all_to_all x1, starting transfers between devices, on_device(): lax.all_to_all(packed, everyone, split_axis=0, concat_axis=0, tiled=True)  7.43 us
    ppermute x5, waiting for transfers between devices, partner(): return lax.ppermute(block, axis, route)  4.48 us
    ppermute x2, starting transfers between devices, on_device(): heard = [lax.ppermute(running, everyone, route) for route in routes]  2.24 us
    ppermute x2, waiting for transfers between devices, on_device(): heard = [lax.ppermute(running, everyone, route) for route in routes]  1.52 us
  transfers between devices with their start and end apart: 8, of which 6 were waited for; matrix products, arithmetic and copies ran while one was open for 0% of the time, Pallas kernels for 20%

profile of v6, /device:TPU:0, one launch (start us, length us, event | category | flops | bytes accessed | tf_op | source)
XLA Modules:
  0.0 69.3 jit_solution(15548924440322355789)
XLA Ops:
  0.0 0.0 copy-start
  0.0 2.9 %shard_map.91 = (bf16[32,64,128]{2,1,0:T(8,128)(2,1)}, s32[1,1024]{1,0:T(1,128)S(1)}) custom-call(s32[32]{0:T(128)} %sizes_in.1, s32[1,1024]{1,0:T(1,128)} %bitcast.11, bf16[1024,128]{1,0:T(8,128)(2,1)} %rows_in.1), custom_call_target="tpu_custom_call" | custom-call | flops 268435456 | bytes 4194304 | tf_op jit(solution)/shard_map/pallas_call | solution.py:34
  3.0 7.4 %all-to-all-start = ((bf16[32,64,128]{2,1,0:T(8,128)(2,1)}), bf16[32,64,128]{2,1,0:T(8,128)(2,1)}, u32[]{:S(2)}, u32[]{:S(2)}) async-start(bf16[32,64,128]{2,1,0:T(8,128)(2,1)} %get-tuple-element.32), calls=%async_computation | async-start | bytes 1048576 | tf_op jit(solution)/shard_map/all_to_all | solution.py:365
  10.4 0.0 copy-done
  10.4 2.7 %shard_map.92 = (bf16[6272,256]{1,0:T(8,128)(2,1)S(1)}, f32[8,128]{1,0:T(8,128)S(1)}) custom-call(s32[62]{0:T(128)S(1)} %copy-done, bf16[2,2,1792,128]{3,2,1,0:T(8,128)(2,1)} %right_top_in.1, bf16[3,2,64,1792]{3,2,1,0:T(8,128)(2,1)} %bitcast.10), custom_call_target="tpu_custom_call" | custom-call | bytes 6291456 | tf_op jit(solution)/shard_map/pallas_call | solution.py:34
  13.1 13.6 %all-to-all-done.arrived = bf16[32,64,128]{2,1,0:T(8,128)(2,1)} async-done(((bf16[32,64,128]{2,1,0:T(8,128)(2,1)}), bf16[32,64,128]{2,1,0:T(8,128)(2,1)}, u32[]{:S(2)}, u32[]{:S(2)}) %all-to-all-start) | async-done | bytes 524320 | tf_op jit(solution)/shard_map/all_to_all | solution.py:365
  26.7 2.4 %shard_map.93 = (bf16[2,1792,128]{2,1,0:T(8,128)(2,1)S(1)}, s32[7,256]{1,0:T(8,128)S(1)}, f32[256,128]{1,0:T(8,128)S(1)}, f32[192,128]{1,0:T(8,128)S(1)}) custom-call(bf16[32,64,128]{2,1,0:T(8,128)(2,1)} %all-to-all-done.arrived, bf16[6272,256]{1,0:T(8,128)(2,1)S(1)} %get-tuple-element.33.right), custom_call_target="tpu_custom_call" | custom-call | flops 411041792 | bytes 6291456 | tf_op jit(solution)/shard_map/pallas_call | solution.py:34
  29.1 0.1 collective-permute-start
  29.2 0.7 %shard_map.94 = (bf16[1792,256]{1,0:T(8,128)(2,1)S(1)}, bf16[1024,896]{1,0:T(8,128)(2,1)S(1)}, s32[1024,128]{1,0:T(8,128)S(1)}) custom-call(s32[7,256]{1,0:T(8,128)S(1)} %get-tuple-element.35.targets, s32[1,1024]{1,0:T(1,128)S(1)} %get-tuple-element.36.places, f32[256,128]{1,0:T(8,128)S(1)} %get-tuple-element.34.after), custom_call_target="tpu_custom_call" | custom-call | bytes 8388608 | tf_op jit(solution)/shard_map/pallas_call | solution.py:34
  29.9 0.6 collective-permute-done
  30.5 0.1 collective-permute-start.1
  30.6 4.3 %shard_map.95.rest_0_ = f32[1120,128]{1,0:T(8,128)S(1)} custom-call(bf16[2,1792,1792]{2,1,0:T(8,128)(2,1)} %block_in.3, bf16[2,1792,128]{2,1,0:T(8,128)(2,1)S(1)} %get-tuple-element.45.pair, f32[192,128]{1,0:T(8,128)S(1)} %slice_add_fusion.after), custom_call_target="tpu_custom_call" | custom-call | flops 1027604480 | bytes 8028160 | tf_op jit(solution)/shard_map/pallas_call | solution.py:34
  34.9 0.5 collective-permute-done.1
  35.4 0.5 collective-permute-start.2
  36.0 3.2 %shard_map.96.rest_1_ = f32[672,128]{1,0:T(8,128)S(1)} custom-call(bf16[2,1792,1792]{2,1,0:T(8,128)(2,1)} %block_in.3, bf16[2,1792,128]{2,1,0:T(8,128)(2,1)S(1)} %get-tuple-element.45.pair, f32[160,128]{1,0:T(8,128)S(1)} %slice_add_fusion.1.after), custom_call_target="tpu_custom_call" | custom-call | flops 616562688 | bytes 4816896 | tf_op jit(solution)/shard_map/pallas_call | solution.py:34
  39.1 3.3 %collective-permute-done.2 = f32[160,128]{1,0:T(8,128)S(1)} collective-permute-done((f32[160,128]{1,0:T(8,128)S(1)}, f32[160,128]{1,0:T(8,128)S(1)}, u32[]{:S(2)}, u32[]{:S(2)}) %collective-permute-start.2) | collective-permute-done | bytes 81952 | tf_op jit(solution)/shard_map/ppermute | solution.py:53
  42.5 0.7 %collective-permute-start.4 = (f32[128,128]{1,0:T(8,128)S(1)}, f32[128,128]{1,0:T(8,128)S(1)}, u32[]{:S(2)}, u32[]{:S(2)}) collective-permute-start(f32[128,128]{1,0:T(8,128)S(1)} %slice_add_fusion.2.after), channel_id=1, source_target_pairs={{0,24},{1,25},{2,26},{3,27},{4,28},{5,29},{6,30},{7,31},{8,16},{9,... | collective-permute-start | bytes 196616 | tf_op jit(solution)/shard_map/ppermute | solution.py:447
  43.2 1.5 %collective-permute-start.3 = (f32[128,128]{1,0:T(8,128)S(1)}, f32[128,128]{1,0:T(8,128)S(1)}, u32[]{:S(2)}, u32[]{:S(2)}) collective-permute-start(f32[128,128]{1,0:T(8,128)S(1)} %slice_add_fusion.2.after), channel_id=1, source_target_pairs={{0,16},{1,9},{2,18},{3,11},{4,20},{5,13},{6,22},{7,15},{8,24},{9,1... | collective-permute-start | bytes 196616 | tf_op jit(solution)/shard_map/ppermute | solution.py:447
  44.7 0.0 collective-permute-start.5
  44.7 1.9 %shard_map.97 = (bf16[2,2,1792,128]{3,2,1,0:T(8,128)(2,1)S(1)}, bf16[1792,384]{1,0:T(8,128)(2,1)S(1)}) custom-call(bf16[2,2,1792,128]{3,2,1,0:T(8,128)(2,1)} %left_top_in.1, bf16[3,2,64,1792]{3,2,1,0:T(8,128)(2,1)} %bitcast.9, f32[128,128]{1,0:T(8,128)S(1)} %slice_add_fusion.2.after), custom_call_target="tpu_custom_call" | custom-call | bytes 8388608 | tf_op jit(solution)/shard_map/pallas_call | solution.py:34
  46.7 1.1 %collective-permute-done.4 = f32[128,128]{1,0:T(8,128)S(1)} collective-permute-done((f32[128,128]{1,0:T(8,128)S(1)}, f32[128,128]{1,0:T(8,128)S(1)}, u32[]{:S(2)}, u32[]{:S(2)}) %collective-permute-start.4) | collective-permute-done | bytes 65568 | tf_op jit(solution)/shard_map/ppermute | solution.py:447
  47.8 0.4 collective-permute-done.3
  48.2 0.0 collective-permute-done.5.rest_5_
  48.2 0.1 collective-permute-start.6
  48.3 1.1 %shard_map.98.base = f32[1792,128]{1,0:T(8,128)S(1)} custom-call(s32[62]{0:T(128)S(1)} %copy-done, f32[1120,128]{1,0:T(8,128)S(1)} %shard_map.95.rest_0_, f32[672,128]{1,0:T(8,128)S(1)} %shard_map.96.rest_1_, bf16[1792,384]{1,0:T(8,128)(2,1)S(1)} %get-tuple-element.52.rest_2_, f32[64,128]{1,0:T(8,128)S(1)} %slice.34.rest_3_, ...), custom_call_target="tpu_custom_call" | custom-call | flops 176160768 | bytes 3145728 | tf_op jit(solution)/shard_map/pallas_call | solution.py:34
  49.5 0.0 collective-permute-done.6.theirs
  49.5 1.0 %shard_map.99 = bf16[1792,128]{1,0:T(8,128)(2,1)S(1)} custom-call(f32[8,128]{1,0:T(8,128)S(1)} %get-tuple-element.42.flags, f32[1792,128]{1,0:T(8,128)S(1)} %shard_map.98.base, bf16[2,2,1792,128]{3,2,1,0:T(8,128)(2,1)S(1)} %get-tuple-element.56.left_top, bf16[128,128]{1,0:T(8,128)(2,1)S(1)} %add_convert_fusion.own, ...), custom_call_target="tpu_custom_call" | custom-call | flops 234881024 | bytes 4194304 | tf_op jit(solution)/shard_map/pallas_call | solution.py:34
  50.5 17.3 %all_to_all.10 = bf16[32,56,128]{2,1,0:T(8,128)(2,1)S(1)} all-to-all(bf16[32,56,128]{2,1,0:T(8,128)(2,1)S(1)} %bitcast.7), channel_id=1, replica_groups=mesh['group'=4,'member'=8] {'group','member'}, dimensions={0} | all-to-all | bytes 917504 | tf_op jit(solution)/shard_map/all_to_all | solution.py:489
  67.9 1.4 %shard_map.100 = f32[1024,128]{1,0:T(8,128)} custom-call(bf16[1024,896]{1,0:T(8,128)(2,1)S(1)} %get-tuple-element.40.order, s32[1024,128]{1,0:T(8,128)S(1)} %get-tuple-element.41.upper, bf16[1792,128]{1,0:T(8,128)(2,1)S(1)} %bitcast.8), custom_call_target="tpu_custom_call" | custom-call | flops 469762048 | bytes 4194304 | tf_op jit(solution)/shard_map/pallas_call | solution.py:34
  (9 shorter events, 0.1 us)
Async XLA Ops:
  0.0 10.4 %copy-start = (s32[62]{0:T(128)S(1)}, s32[62]{0:T(128)}, u32[]{:S(2)}) copy-start(s32[62]{0:T(128)} %ranks.3) | copy-start | bytes 748
  3.0 23.8 %all-to-all-start = ((bf16[32,64,128]{2,1,0:T(8,128)(2,1)}), bf16[32,64,128]{2,1,0:T(8,128)(2,1)}, u32[]{:S(2)}, u32[]{:S(2)}) async-start(bf16[32,64,128]{2,1,0:T(8,128)(2,1)} %get-tuple-element.32), calls=%async_computation | async-start | bytes 1048576 | tf_op jit(solution)/shard_map/all_to_all | solution.py:365
  29.1 1.4 %collective-permute-start = (f32[256,128]{1,0:T(8,128)S(1)}, f32[256,128]{1,0:T(8,128)S(1)}, u32[]{:S(2)}, u32[]{:S(2)}) collective-permute-start(f32[256,128]{1,0:T(8,128)S(1)} %get-tuple-element.34.after), channel_id=1, source_target_pairs={{0,1},{1,0},{2,3},{3,2},{4,5},{5,4},{6,7},{7,6},{8,9},{9,8},{10,11... | collective-permute-start | bytes 393224 | tf_op jit(solution)/shard_map/ppermute | solution.py:53
  30.5 4.9 %collective-permute-start.1 = (f32[192,128]{1,0:T(8,128)S(1)}, f32[192,128]{1,0:T(8,128)S(1)}, u32[]{:S(2)}, u32[]{:S(2)}) collective-permute-start(f32[192,128]{1,0:T(8,128)S(1)} %slice_add_fusion.after), channel_id=1, source_target_pairs={{0,2},{2,0},{1,3},{3,1},{4,6},{6,4},{5,7},{7,5},{8,10},{10,8},{9,1... | collective-permute-start | bytes 294920 | tf_op jit(solution)/shard_map/ppermute | solution.py:53
  35.4 7.0 %collective-permute-start.2 = (f32[160,128]{1,0:T(8,128)S(1)}, f32[160,128]{1,0:T(8,128)S(1)}, u32[]{:S(2)}, u32[]{:S(2)}) collective-permute-start(f32[160,128]{1,0:T(8,128)S(1)} %slice_add_fusion.1.after), channel_id=1, source_target_pairs={{0,4},{4,0},{1,5},{5,1},{2,6},{6,2},{3,7},{7,3},{8,12},{12,8},{9,1... | collective-permute-start | bytes 245768 | tf_op jit(solution)/shard_map/ppermute | solution.py:53
  42.5 5.3 %collective-permute-start.4 = (f32[128,128]{1,0:T(8,128)S(1)}, f32[128,128]{1,0:T(8,128)S(1)}, u32[]{:S(2)}, u32[]{:S(2)}) collective-permute-start(f32[128,128]{1,0:T(8,128)S(1)} %slice_add_fusion.2.after), channel_id=1, source_target_pairs={{0,24},{1,25},{2,26},{3,27},{4,28},{5,29},{6,30},{7,31},{8,16},{9,... | collective-permute-start | bytes 196616 | tf_op jit(solution)/shard_map/ppermute | solution.py:447
  43.2 5.0 %collective-permute-start.3 = (f32[128,128]{1,0:T(8,128)S(1)}, f32[128,128]{1,0:T(8,128)S(1)}, u32[]{:S(2)}, u32[]{:S(2)}) collective-permute-start(f32[128,128]{1,0:T(8,128)S(1)} %slice_add_fusion.2.after), channel_id=1, source_target_pairs={{0,16},{1,9},{2,18},{3,11},{4,20},{5,13},{6,22},{7,15},{8,24},{9,1... | collective-permute-start | bytes 196616 | tf_op jit(solution)/shard_map/ppermute | solution.py:447
  44.7 3.5 %collective-permute-start.5 = (bf16[64,128]{1,0:T(8,128)(2,1)S(1)}, bf16[64,128]{1,0:T(8,128)(2,1)S(1)}, u32[]{:S(2)}, u32[]{:S(2)}) collective-permute-start(bf16[64,128]{1,0:T(8,128)(2,1)S(1)} %pad_maximum_fusion.rest_4_), channel_id=1, source_target_pairs={{0,1},{1,0},{2,3},{3,2},{4,5},{5,4},{6,7},{7,6},{8,9},{9,8},{10,11... | collective-permute-start | bytes 49160 | tf_op jit(solution)/shard_map/ppermute | solution.py:53
  48.2 1.3 %collective-permute-start.6 = (bf16[128,128]{1,0:T(8,128)(2,1)S(1)}, bf16[128,128]{1,0:T(8,128)(2,1)S(1)}, u32[]{:S(2)}, u32[]{:S(2)}) collective-permute-start(bf16[128,128]{1,0:T(8,128)(2,1)S(1)} %add_convert_fusion.own), channel_id=1, source_target_pairs={{0,1},{1,0},{2,3},{3,2},{4,5},{5,4},{6,7},{7,6},{8,9},{9,8},{10,11... | collective-permute-start | bytes 98312 | tf_op jit(solution)/shard_map/ppermute | solution.py:53

commit v7 on v6

--- a/solution.py
+++ b/solution.py
@@ -9,6 +9,7 @@
 
 F32 = jnp.float32
 BF16 = jnp.bfloat16
+F16 = jnp.float16
 I32 = jnp.int32
 VMEM = pl.BlockSpec(memory_space=pltpu.VMEM)
 SMEM = pl.BlockSpec(memory_space=pltpu.SMEM)
@@ -55,6 +56,19 @@
 
 def far(*arrays):
     return [pltpu.with_memory_space_constraint(array, pltpu.HBM) for array in arrays]
+
+
+def bound(mine, other):
+    return jnp.clip(jnp.maximum(mine, other) + 1.0, -100.0, 126.0)
+
+
+def narrow(rows, power):
+    return jnp.concatenate([rows * jnp.exp2(14.0 - power[:1]), power]).astype(F16)
+
+
+def widen(sent):
+    power = sent[-8:].astype(F32)
+    return sent[:-8].astype(F32) * jnp.exp2(power[:1] - 14.0), power
 
 
 def turn(block):
@@ -226,7 +240,11 @@
         send[at : at + half, :] = whole[pl.ds(other, half), :]
         at += half
         low += 2 * half
-    send[at:, :] = lower[(levels - 1) * width :]
+    send[at : at + width, :] = lower[(levels - 1) * width :]
+    largest = jnp.max(jnp.abs(whole[...]), axis=0, keepdims=True)
+    power = jnp.clip(jnp.ceil(jnp.log2(largest + 1e-30)) + 1.0, -100.0, 126.0)
+    send[at + width :, :] = jnp.broadcast_to(power, (8, 128))
+    keep[at:, :] = jnp.broadcast_to(power, (8, 128))
 
 
 def diag_kernel(first, block_in, pair, after, out, block, sems):
@@ -384,8 +402,8 @@
         [
             jax.ShapeDtypeStruct((2, capacity, columns), BF16),
             jax.ShapeDtypeStruct((filled // 8, leaves * 8), I32),
-            jax.ShapeDtypeStruct((shared + width, columns), F32),
-            jax.ShapeDtypeStruct((shared, columns), F32),
+            jax.ShapeDtypeStruct((shared + width + 8, columns), F32),
+            jax.ShapeDtypeStruct((shared + 8, columns), F32),
         ],
         [VMEM, VMEM],
         (arrived, right),
@@ -423,19 +441,22 @@
         16,
     )
     received, slots, order, upper = lax.optimization_barrier((received, slots, order, upper))
-    nearest = received[shared:]
-    running = keep + received[:shared]
+    nearest = received[shared : shared + width]
+    running = keep[:shared] + received[:shared]
+    power = bound(keep[shared:], received[shared + width :])
     bases = []
     coefs = []
     for bit in range(1, member_levels):
         rest = running.shape[0] - width // 2
-        received = partner(running, "member", bit)
+        received = partner(narrow(running, power), "member", bit)
         if bit == 1:
-            bases.append(diagonal(0, 5, running))
+            bases.append(diagonal(0, 4, running))
             received, bases[0] = lax.optimization_barrier((received, bases[0]))
         if bit == member_levels - 1:
-            bases.append(diagonal(5, 3, running))
+            bases.append(diagonal(4, 4, running))
             received, bases[1] = lax.optimization_barrier((received, bases[1]))
+        received, other = widen(received)
+        power = bound(power, other)
         coefs.insert(0, received[rest:].astype(BF16))
         running = running[:rest] + received[:rest]
     routes = [[], []]
@@ -443,8 +464,9 @@
         for near in range(0, members, 2):
             at = low * members + near
             routes[0] += [(at, (low ^ 2) * members + near), (at + 1, (low ^ 1) * members + near + 1)]
-            routes[1] += [(at + core, (low ^ 3) * members + near + core) for core in range(2)]
-    heard = [lax.ppermute(running, everyone, route) for route in routes]
+            routes[1] += [(at, (low ^ 3) * members + near), (at + 1, low * members + (near ^ 2) + 1)]
+    sums = narrow(running, power)
+    heard = [lax.ppermute(sums, everyone, route) for route in routes]
     left_top, left_low = call(
         stage_kernel,
         [
@@ -459,6 +481,7 @@
         scratch=[pltpu.VMEM(low_left.shape, BF16), DMA((2,))],
     )
     heard, left_top, left_low = lax.optimization_barrier((heard, left_top, left_low))
+    heard = [widen(block)[0] for block in heard]
     own = (heard[0] + jnp.where(flags[:1] > 0, heard[1], 0.0)).astype(BF16)
     own_low = jnp.concatenate(coefs)
     their_low, own = lax.optimization_barrier((partner(own_low, "member", 0), own))

time: 69.6 us -> 68.5 us (0.984)
  waiting for transfers between devices: 19.6 us -> 16.9 us
  blocking collectives: 17.3 us -> 18.7 us
    ppermute x5, waiting for transfers between devices: 4.48 us -> 2.02 us  [partner(): return lax.ppermute(block, axis, route)]
    all_to_all x1, blocking collectives: 17.3 us -> 18.7 us  [on_device(): lax.all_to_all(leaving.reshape(leaves, bucket, columns), everyone, split_...]
  transfers between devices with their start and end apart: 8 -> 8, of which waited for: 6 -> 6; matrix products, arithmetic and copies ran while one was open for 0% -> 0% of each run, Pallas kernels for 20% -> 21%
where the time goes in v7:
time: 68.5 us; the launch traced here: 68.2 us
  Pallas kernels  21.8 us (32%)
  blocking collectives  18.7 us (27%)
  waiting for transfers between devices  16.9 us (25%)
  starting transfers between devices  10.4 us (15%)
    pallas_call x10, Pallas kernels, call(): pl.pallas_call(kernel, out_shape=outs, in_specs=ins, out_specs=more.pop('...  21.8 us
    all_to_all x1, blocking collectives, on_device(): lax.all_to_all(leaving.reshape(leaves, bucket, columns), everyone, split_...  18.7 us
    all_to_all x1, waiting for transfers between devices, on_device(): lax.all_to_all(packed, everyone, split_axis=0, concat_axis=0, tiled=True)  13.6 us
    all_to_all x1, starting transfers between devices, on_device(): lax.all_to_all(packed, everyone, split_axis=0, concat_axis=0, tiled=True)  7.43 us
    ppermute x2, starting transfers between devices, on_device(): heard = [lax.ppermute(sums, everyone, route) for route in routes]  2.04 us
    ppermute x5, waiting for transfers between devices, partner(): return lax.ppermute(block, axis, route)  2.02 us
  transfers between devices with their start and end apart: 8, of which 6 were waited for; matrix products, arithmetic and copies ran while one was open for 0% of the time, Pallas kernels for 21%

profile of v7, /device:TPU:0, one launch (start us, length us, event | category | flops | bytes accessed | tf_op | source)
XLA Modules:
  0.0 68.2 jit_solution(663341732719974339)
XLA Ops:
  0.0 0.0 copy-start
  0.0 2.9 %shard_map.91 = (bf16[32,64,128]{2,1,0:T(8,128)(2,1)}, s32[1,1024]{1,0:T(1,128)S(1)}) custom-call(s32[32]{0:T(128)} %sizes_in.1, s32[1,1024]{1,0:T(1,128)} %bitcast.25, bf16[1024,128]{1,0:T(8,128)(2,1)} %rows_in.1), custom_call_target="tpu_custom_call" | custom-call | flops 268435456 | bytes 4194304 | tf_op jit(solution)/shard_map/pallas_call | solution.py:35
  3.0 7.4 %all-to-all-start = ((bf16[32,64,128]{2,1,0:T(8,128)(2,1)}), bf16[32,64,128]{2,1,0:T(8,128)(2,1)}, u32[]{:S(2)}, u32[]{:S(2)}) async-start(bf16[32,64,128]{2,1,0:T(8,128)(2,1)} %get-tuple-element.32), calls=%async_computation | async-start | bytes 1048576 | tf_op jit(solution)/shard_map/all_to_all | solution.py:383
  10.4 0.0 copy-done
  10.4 2.7 %shard_map.92 = (bf16[6272,256]{1,0:T(8,128)(2,1)S(1)}, f32[8,128]{1,0:T(8,128)S(1)}) custom-call(s32[62]{0:T(128)S(1)} %copy-done, bf16[2,2,1792,128]{3,2,1,0:T(8,128)(2,1)} %right_top_in.1, bf16[3,2,64,1792]{3,2,1,0:T(8,128)(2,1)} %bitcast.24), custom_call_target="tpu_custom_call" | custom-call | bytes 6291456 | tf_op jit(solution)/shard_map/pallas_call | solution.py:35
  13.1 13.6 %all-to-all-done.arrived = bf16[32,64,128]{2,1,0:T(8,128)(2,1)} async-done(((bf16[32,64,128]{2,1,0:T(8,128)(2,1)}), bf16[32,64,128]{2,1,0:T(8,128)(2,1)}, u32[]{:S(2)}, u32[]{:S(2)}) %all-to-all-start) | async-done | bytes 524320 | tf_op jit(solution)/shard_map/all_to_all | solution.py:383
  26.7 2.4 %shard_map.93 = (bf16[2,1792,128]{2,1,0:T(8,128)(2,1)S(1)}, s32[7,256]{1,0:T(8,128)S(1)}, f32[264,128]{1,0:T(8,128)S(1)}, f32[200,128]{1,0:T(8,128)S(1)}) custom-call(bf16[32,64,128]{2,1,0:T(8,128)(2,1)} %all-to-all-done.arrived, bf16[6272,256]{1,0:T(8,128)(2,1)S(1)} %get-tuple-element.33.right), custom_call_target="tpu_custom_call" | custom-call | flops 411041792 | bytes 6291456 | tf_op jit(solution)/shard_map/pallas_call | solution.py:35
  29.1 0.1 collective-permute-start
  29.2 0.7 %shard_map.94 = (bf16[1792,256]{1,0:T(8,128)(2,1)S(1)}, bf16[1024,896]{1,0:T(8,128)(2,1)S(1)}, s32[1024,128]{1,0:T(8,128)S(1)}) custom-call(s32[7,256]{1,0:T(8,128)S(1)} %get-tuple-element.35.targets, s32[1,1024]{1,0:T(1,128)S(1)} %get-tuple-element.36.places, f32[264,128]{1,0:T(8,128)S(1)} %get-tuple-element.34.after), custom_call_target="tpu_custom_call" | custom-call | bytes 8388608 | tf_op jit(solution)/shard_map/pallas_call | solution.py:35
  29.9 0.6 collective-permute-done
  30.6 0.1 collective-permute-start.1
  30.7 3.7 %shard_map.95.rest_0_ = f32[896,128]{1,0:T(8,128)S(1)} custom-call(bf16[2,1792,1792]{2,1,0:T(8,128)(2,1)} %block_in.3, bf16[2,1792,128]{2,1,0:T(8,128)(2,1)S(1)} %get-tuple-element.45.pair, f32[192,128]{1,0:T(8,128)S(1)} %get-tuple-element.68.after), custom_call_target="tpu_custom_call" | custom-call | flops 822083584 | bytes 6422528 | tf_op jit(solution)/shard_map/pallas_call | solution.py:35
  34.4 0.3 collective-permute-done.1
  34.9 0.7 collective-permute-start.2
  35.6 3.7 %shard_map.96.rest_1_ = f32[896,128]{1,0:T(8,128)S(1)} custom-call(bf16[2,1792,1792]{2,1,0:T(8,128)(2,1)} %block_in.3, bf16[2,1792,128]{2,1,0:T(8,128)(2,1)S(1)} %get-tuple-element.45.pair, f32[160,128]{1,0:T(8,128)S(1)} %get-tuple-element.64.after), custom_call_target="tpu_custom_call" | custom-call | flops 822083584 | bytes 6422528 | tf_op jit(solution)/shard_map/pallas_call | solution.py:35
  39.3 1.0 %collective-permute-done.2 = f16[168,128]{1,0:T(8,128)(2,1)S(1)} collective-permute-done((f16[168,128]{1,0:T(8,128)(2,1)S(1)}, f16[168,128]{1,0:T(8,128)(2,1)S(1)}, u32[]{:S(2)}, u32[]{:S(2)}) %collective-permute-start.2) | collective-permute-done | bytes 43040 | tf_op jit(solution)/shard_map/ppermute | solution.py:54
  40.5 1.1 %collective-permute-start.4 = (f16[136,128]{1,0:T(8,128)(2,1)S(1)}, f16[136,128]{1,0:T(8,128)(2,1)S(1)}, u32[]{:S(2)}, u32[]{:S(2)}) collective-permute-start(f16[136,128]{1,0:T(8,128)(2,1)S(1)} %pad_maximum_fusion.2), channel_id=1, source_target_pairs={{0,24},{1,3},{2,26},{3,1},{4,28},{5,7},{6,30},{7,5},{8,16},{9,11},... | collective-permute-start | bytes 104456 | tf_op jit(solution)/shard_map/ppermute | solution.py:469
  41.6 0.9 %collective-permute-start.3 = (f16[136,128]{1,0:T(8,128)(2,1)S(1)}, f16[136,128]{1,0:T(8,128)(2,1)S(1)}, u32[]{:S(2)}, u32[]{:S(2)}) collective-permute-start(f16[136,128]{1,0:T(8,128)(2,1)S(1)} %pad_maximum_fusion.2), channel_id=1, source_target_pairs={{0,16},{1,9},{2,18},{3,11},{4,20},{5,13},{6,22},{7,15},{8,24},{9,1... | collective-permute-start | bytes 104456 | tf_op jit(solution)/shard_map/ppermute | solution.py:469
  42.5 0.0 collective-permute-start.5
  42.5 1.9 %shard_map.97 = (bf16[2,2,1792,128]{3,2,1,0:T(8,128)(2,1)S(1)}, bf16[1792,384]{1,0:T(8,128)(2,1)S(1)}) custom-call(bf16[2,2,1792,128]{3,2,1,0:T(8,128)(2,1)} %left_top_in.1, bf16[3,2,64,1792]{3,2,1,0:T(8,128)(2,1)} %bitcast.23, f32[128,128]{1,0:T(8,128)S(1)} %get-tuple-element.60.after), custom_call_target="tpu_custom_call" | custom-call | bytes 8388608 | tf_op jit(solution)/shard_map/pallas_call | solution.py:35
  44.4 0.9 %collective-permute-done.4 = f16[136,128]{1,0:T(8,128)(2,1)S(1)} collective-permute-done((f16[136,128]{1,0:T(8,128)(2,1)S(1)}, f16[136,128]{1,0:T(8,128)(2,1)S(1)}, u32[]{:S(2)}, u32[]{:S(2)}) %collective-permute-start.4) | collective-permute-done | bytes 34848 | tf_op jit(solution)/shard_map/ppermute | solution.py:469
  45.4 0.4 collective-permute-done.3
  45.8 0.0 collective-permute-done.5.rest_5_
  45.8 0.1 collective-permute-start.6
  45.9 1.1 %shard_map.98.base = f32[1792,128]{1,0:T(8,128)S(1)} custom-call(s32[62]{0:T(128)S(1)} %copy-done, f32[896,128]{1,0:T(8,128)S(1)} %shard_map.95.rest_0_, f32[896,128]{1,0:T(8,128)S(1)} %shard_map.96.rest_1_, bf16[1792,384]{1,0:T(8,128)(2,1)S(1)} %get-tuple-element.52.rest_2_, f32[64,128]{1,0:T(8,128)S(1)} %slice.104.rest_3_, ...), custom_call_target="tpu_custom_call" | custom-call | flops 176160768 | bytes 3145728 | tf_op jit(solution)/shard_map/pallas_call | solution.py:35
  47.0 0.0 collective-permute-done.6.theirs
  47.1 1.0 %shard_map.99 = bf16[1792,128]{1,0:T(8,128)(2,1)S(1)} custom-call(f32[8,128]{1,0:T(8,128)S(1)} %get-tuple-element.42.flags, f32[1792,128]{1,0:T(8,128)S(1)} %shard_map.98.base, bf16[2,2,1792,128]{3,2,1,0:T(8,128)(2,1)S(1)} %get-tuple-element.56.left_top, bf16[128,128]{1,0:T(8,128)(2,1)S(1)} %add_convert_fusion.own, ...), custom_call_target="tpu_custom_call" | custom-call | flops 234881024 | bytes 4194304 | tf_op jit(solution)/shard_map/pallas_call | solution.py:35
  48.1 18.7 %all_to_all.10 = bf16[32,56,128]{2,1,0:T(8,128)(2,1)S(1)} all-to-all(bf16[32,56,128]{2,1,0:T(8,128)(2,1)S(1)} %bitcast.21), channel_id=1, replica_groups=mesh['group'=4,'member'=8] {'group','member'}, dimensions={0} | all-to-all | bytes 917504 | tf_op jit(solution)/shard_map/all_to_all | solution.py:512
  66.8 1.4 %shard_map.100 = f32[1024,128]{1,0:T(8,128)} custom-call(bf16[1024,896]{1,0:T(8,128)(2,1)S(1)} %get-tuple-element.40.order, s32[1024,128]{1,0:T(8,128)S(1)} %get-tuple-element.41.upper, bf16[1792,128]{1,0:T(8,128)(2,1)S(1)} %bitcast.22), custom_call_target="tpu_custom_call" | custom-call | flops 469762048 | bytes 4194304 | tf_op jit(solution)/shard_map/pallas_call | solution.py:35
  (25 shorter events, 0.2 us)
Async XLA Ops:
  0.0 10.4 %copy-start = (s32[62]{0:T(128)S(1)}, s32[62]{0:T(128)}, u32[]{:S(2)}) copy-start(s32[62]{0:T(128)} %ranks.3) | copy-start | bytes 748
  3.0 23.8 %all-to-all-start = ((bf16[32,64,128]{2,1,0:T(8,128)(2,1)}), bf16[32,64,128]{2,1,0:T(8,128)(2,1)}, u32[]{:S(2)}, u32[]{:S(2)}) async-start(bf16[32,64,128]{2,1,0:T(8,128)(2,1)} %get-tuple-element.32), calls=%async_computation | async-start | bytes 1048576 | tf_op jit(solution)/shard_map/all_to_all | solution.py:383
  29.1 1.4 %collective-permute-start = (f32[264,128]{1,0:T(8,128)S(1)}, f32[264,128]{1,0:T(8,128)S(1)}, u32[]{:S(2)}, u32[]{:S(2)}) collective-permute-start(f32[264,128]{1,0:T(8,128)S(1)} %get-tuple-element.34.after), channel_id=1, source_target_pairs={{0,1},{1,0},{2,3},{3,2},{4,5},{5,4},{6,7},{7,6},{8,9},{9,8},{10,11... | collective-permute-start | bytes 405512 | tf_op jit(solution)/shard_map/ppermute | solution.py:54
  30.6 4.2 %collective-permute-start.1 = (f16[200,128]{1,0:T(8,128)(2,1)S(1)}, f16[200,128]{1,0:T(8,128)(2,1)S(1)}, u32[]{:S(2)}, u32[]{:S(2)}) collective-permute-start(f16[200,128]{1,0:T(8,128)(2,1)S(1)} %pad_maximum_fusion), channel_id=1, source_target_pairs={{0,2},{2,0},{1,3},{3,1},{4,6},{6,4},{5,7},{7,5},{8,10},{10,8},{9,1... | collective-permute-start | bytes 153608 | tf_op jit(solution)/shard_map/ppermute | solution.py:54
  34.9 5.4 %collective-permute-start.2 = (f16[168,128]{1,0:T(8,128)(2,1)S(1)}, f16[168,128]{1,0:T(8,128)(2,1)S(1)}, u32[]{:S(2)}, u32[]{:S(2)}) collective-permute-start(f16[168,128]{1,0:T(8,128)(2,1)S(1)} %pad_maximum_fusion.1), channel_id=1, source_target_pairs={{0,4},{4,0},{1,5},{5,1},{2,6},{6,2},{3,7},{7,3},{8,12},{12,8},{9,1... | collective-permute-start | bytes 129032 | tf_op jit(solution)/shard_map/ppermute | solution.py:54
  40.5 4.9 %collective-permute-start.4 = (f16[136,128]{1,0:T(8,128)(2,1)S(1)}, f16[136,128]{1,0:T(8,128)(2,1)S(1)}, u32[]{:S(2)}, u32[]{:S(2)}) collective-permute-start(f16[136,128]{1,0:T(8,128)(2,1)S(1)} %pad_maximum_fusion.2), channel_id=1, source_target_pairs={{0,24},{1,3},{2,26},{3,1},{4,28},{5,7},{6,30},{7,5},{8,16},{9,11},... | collective-permute-start | bytes 104456 | tf_op jit(solution)/shard_map/ppermute | solution.py:469
  41.6 4.2 %collective-permute-start.3 = (f16[136,128]{1,0:T(8,128)(2,1)S(1)}, f16[136,128]{1,0:T(8,128)(2,1)S(1)}, u32[]{:S(2)}, u32[]{:S(2)}) collective-permute-start(f16[136,128]{1,0:T(8,128)(2,1)S(1)} %pad_maximum_fusion.2), channel_id=1, source_target_pairs={{0,16},{1,9},{2,18},{3,11},{4,20},{5,13},{6,22},{7,15},{8,24},{9,1... | collective-permute-start | bytes 104456 | tf_op jit(solution)/shard_map/ppermute | solution.py:469
  42.5 3.3 %collective-permute-start.5 = (bf16[64,128]{1,0:T(8,128)(2,1)S(1)}, bf16[64,128]{1,0:T(8,128)(2,1)S(1)}, u32[]{:S(2)}, u32[]{:S(2)}) collective-permute-start(bf16[64,128]{1,0:T(8,128)(2,1)S(1)} %pad_maximum_fusion.3.rest_4_), channel_id=1, source_target_pairs={{0,1},{1,0},{2,3},{3,2},{4,5},{5,4},{6,7},{7,6},{8,9},{9,8},{10,11... | collective-permute-start | bytes 49160 | tf_op jit(solution)/shard_map/ppermute | solution.py:54
  45.8 1.3 %collective-permute-start.6 = (bf16[128,128]{1,0:T(8,128)(2,1)S(1)}, bf16[128,128]{1,0:T(8,128)(2,1)S(1)}, u32[]{:S(2)}, u32[]{:S(2)}) collective-permute-start(bf16[128,128]{1,0:T(8,128)(2,1)S(1)} %add_convert_fusion.own), channel_id=1, source_target_pairs={{0,1},{1,0},{2,3},{3,2},{4,5},{5,4},{6,7},{7,6},{8,9},{9,8},{10,11... | collective-permute-start | bytes 98312 | tf_op jit(solution)/shard_map/ppermute | solution.py:54

commit v8 on v7

--- a/solution.py
+++ b/solution.py
@@ -247,16 +247,20 @@
     keep[at:, :] = jnp.broadcast_to(power, (8, 128))
 
 
-def diag_kernel(first, block_in, pair, after, out, block, sems):
-    count, _, height, _ = block.shape
+def diag_kernel(first, cuts, block_in, pair, after, out, block, sems):
+    low = 0
     copies = []
-    for j in range(count):
-        rows = pl.ds((first + j) * height, height)
-        copies.append(pltpu.make_async_copy(block_in.at[:, rows, :], block.at[j], sems.at[j]))
+    for j, rows in enumerate(cuts):
+        source = block_in.at[:, pl.ds(first + low, rows), :]
+        copies.append(pltpu.make_async_copy(source, block.at[:, pl.ds(low, rows), :], sems.at[j]))
         copies[j].start()
-    for j in range(count):
-        copies[j].wait()
-        out[j * height : (j + 1) * height, :] = dot(block[j, 0], pair[0]) + dot(block[j, 1], pair[1])
+        low += rows
+    low = 0
+    for copy, rows in zip(copies, cuts):
+        copy.wait()
+        part = slice(low, low + rows)
+        out[part, :] = dot(block[0, part, :], pair[0]) + dot(block[1, part, :], pair[1])
+        low += rows
 
 
 def merged(core, own, theirs, at, half):
@@ -288,26 +292,30 @@
         low += base.shape[0]
 
 
-def out_kernel(bucket, flags, base, left_top, own, theirs, slots, packed, spare, ordered):
+def upper(level, coef, flags, left_top):
+    half = coef.shape[0] // 2
+    mark = jnp.where(level == 0, flags[1:2, :], flags[2:3, :])
+    coef = jnp.where(mark > 0, coef.astype(F32), 0.0)
+    turned = jnp.concatenate([-coef[half:], coef[:half]], axis=0)
+    stacked = jnp.concatenate([jnp.transpose(coef), jnp.transpose(turned)], axis=0)
+    factors = jnp.concatenate([left_top[level, 0], left_top[level, 1]], axis=1)
+    return dot(factors, stacked.astype(BF16))
+
+
+def own_kernel(flags, base, left_top, own, out):
+    core = jnp.bitwise_and(lax.axis_index("member"), 1)
+    out[...] = base[...] + upper(core, own[...], flags, left_top)
+
+
+def out_kernel(bucket, flags, base, left_top, theirs, slots, packed, spare, ordered):
     capacity = base.shape[0]
     part = slots.shape[1]
     groups = slots.shape[0] // part
     leaves = part // 8
-    first = flags[:1, :] > 0
-    levels = left_top.shape[0]
-    half = own.shape[0]
-    stacked = []
-    for level in range(levels):
-        pick = (own, theirs) if level == 0 else (theirs, own)
-        coef = jnp.where(first, pick[0][...].astype(F32), pick[1][...].astype(F32))
-        coef = jnp.where(flags[1 + level : 2 + level, :] > 0, coef, 0.0)
-        turned = jnp.concatenate([-coef[half // 2 :], coef[: half // 2]], axis=0)
-        stacked += [jnp.transpose(coef), jnp.transpose(turned)]
-    stacked = jnp.concatenate(stacked, axis=0).astype(BF16)
+    core = jnp.bitwise_and(lax.axis_index("member"), 1)
     if groups * part > capacity:
         spare[capacity:, :] = jnp.zeros((groups * part - capacity, 128), BF16)
-    factors = [left_top[level, p] for level in range(levels) for p in range(2)]
-    total = base[...] + dot(jnp.concatenate(factors, axis=1), stacked)
+    total = base[...] + upper(1 - core, theirs[...], flags, left_top)
     spare[:capacity, :] = total.astype(BF16)
     for g in range(groups):
         moved = dot(slots[g * part : (g + 1) * part, :], spare[g * part : (g + 1) * part, :])
@@ -412,18 +420,20 @@
         24,
         scratch=[pltpu.VMEM((2 * shared + width, columns), F32)],
     )
-    height = capacity // 8
-
-    def diagonal(first, chunks, after):
+    unit = capacity // 28
+    cuts = [4 * unit, 4 * unit, 3 * unit, 2 * unit, unit]
+
+    def diagonal(first, cuts, after):
+        count = sum(cuts)
         return call(
-            functools.partial(diag_kernel, first),
-            [jax.ShapeDtypeStruct((chunks * height, columns), F32)],
+            functools.partial(diag_kernel, first, cuts),
+            [jax.ShapeDtypeStruct((count, columns), F32)],
             [HBM, VMEM, pl.BlockSpec(memory_space=pl.ANY)],
             (*far(diag_block), pair, after),
-            4 * chunks * height * capacity * columns,
-            4 * chunks * height * capacity,
+            4 * count * capacity * columns,
+            4 * count * capacity,
             24,
-            scratch=[pltpu.VMEM((chunks, 2, height, capacity), BF16), DMA((chunks,))],
+            scratch=[pltpu.VMEM((2, count, capacity), BF16), DMA((len(cuts),))],
         )[0]
 
     received = partner(send, "member", 0)
@@ -450,10 +460,10 @@
         rest = running.shape[0] - width // 2
         received = partner(narrow(running, power), "member", bit)
         if bit == 1:
-            bases.append(diagonal(0, 4, running))
+            bases.append(diagonal(0, cuts, running))
             received, bases[0] = lax.optimization_barrier((received, bases[0]))
         if bit == member_levels - 1:
-            bases.append(diagonal(4, 4, running))
+            bases.append(diagonal(sum(cuts), cuts, running))
             received, bases[1] = lax.optimization_barrier((received, bases[1]))
         received, other = widen(received)
         power = bound(power, other)
@@ -480,28 +490,37 @@
         24,
         scratch=[pltpu.VMEM(low_left.shape, BF16), DMA((2,))],
     )
-    heard, left_top, left_low = lax.optimization_barrier((heard, left_top, left_low))
-    heard = [widen(block)[0] for block in heard]
-    own = (heard[0] + jnp.where(flags[:1] > 0, heard[1], 0.0)).astype(BF16)
     own_low = jnp.concatenate(coefs)
-    their_low, own = lax.optimization_barrier((partner(own_low, "member", 0), own))
-    theirs = partner(own, "member", 0)
     base = call(
         functools.partial(low_kernel, len(bases), group_levels),
         [jax.ShapeDtypeStruct((capacity, columns), F32)],
         [SMEM] + [VMEM] * (len(bases) + 4),
-        (block_ranks, *bases, left_low, nearest, own_low, their_low),
+        (block_ranks, *bases, left_low, nearest, own_low, partner(own_low, "member", 0)),
         4 * capacity * columns * member_levels * width,
         3 << 20,
         16,
     )[0]
+    heard = [widen(block)[0] for block in heard]
+    own = (heard[0] + jnp.where(flags[:1] > 0, heard[1], 0.0)).astype(BF16)
+    own, base = lax.optimization_barrier((own, base))
+    theirs = partner(own, "member", 0)
+    base = call(
+        own_kernel,
+        [jax.ShapeDtypeStruct((capacity, columns), F32)],
+        [VMEM] * 4,
+        (flags, base, left_top, own),
+        4 * capacity * columns * top_width,
+        2 << 20,
+        16,
+    )[0]
+    theirs, base = lax.optimization_barrier((theirs, base))
 
     leaving = call(
         functools.partial(out_kernel, bucket),
         [jax.ShapeDtypeStruct((capacity, columns), BF16)],
-        [VMEM] * 6,
-        (flags, base, left_top, own, theirs, slots),
-        4 * capacity * columns * group_levels * top_width,
+        [VMEM] * 5,
+        (flags, base, left_top, theirs, slots),
+        4 * capacity * columns * top_width,
         4 << 20,
         24,
         scratch=[

time: 68.5 us -> 69.1 us (level)
  waiting for transfers between devices: 16.9 us -> 15.7 us
  Pallas kernels: 21.8 us -> 22.7 us
    ppermute x2, waiting for transfers between devices: 1.28 us -> 0.15 us  [on_device(): heard = [lax.ppermute(sums, everyone, route) for route in routes]]
    pallas_call x10 -> x11, Pallas kernels: 21.8 us -> 22.7 us  [call(): pl.pallas_call(kernel, out_shape=outs, in_specs=ins, out_specs=more.pop('...]
  transfers between devices with their start and end apart: 8 -> 8, of which waited for: 6 -> 6; matrix products, arithmetic and copies ran while one was open for 0% -> 0% of each run, Pallas kernels for 21% -> 22%
where the time goes in v8:
time: 69.1 us; the launch traced here: 68.8 us
  Pallas kernels  22.7 us (33%)
  blocking collectives  18.9 us (27%)
  waiting for transfers between devices  15.7 us (23%)
  starting transfers between devices  10.9 us (16%)
    pallas_call x11, Pallas kernels, call(): pl.pallas_call(kernel, out_shape=outs, in_specs=ins, out_specs=more.pop('...  22.7 us
    all_to_all x1, blocking collectives, on_device(): lax.all_to_all(leaving.reshape(leaves, bucket, columns), everyone, split_...  18.9 us
    all_to_all x1, waiting for transfers between devices, on_device(): lax.all_to_all(packed, everyone, split_axis=0, concat_axis=0, tiled=True)  13.6 us
    all_to_all x1, starting transfers between devices, on_device(): lax.all_to_all(packed, everyone, split_axis=0, concat_axis=0, tiled=True)  7.43 us
    ppermute x2, starting transfers between devices, on_device(): heard = [lax.ppermute(sums, everyone, route) for route in routes]  2.32 us
    ppermute x5, waiting for transfers between devices, partner(): return lax.ppermute(block, axis, route)  1.95 us
  transfers between devices with their start and end apart: 8, of which 6 were waited for; matrix products, arithmetic and copies ran while one was open for 0% of the time, Pallas kernels for 22%

profile of v8, /device:TPU:0, one launch (start us, length us, event | category | flops | bytes accessed | tf_op | source)
XLA Modules:
  0.0 68.8 jit_solution(5282598581297222852)
XLA Ops:
  0.0 0.0 copy-start
  0.0 2.9 %shard_map.91 = (bf16[32,64,128]{2,1,0:T(8,128)(2,1)}, s32[1,1024]{1,0:T(1,128)S(1)}) custom-call(s32[32]{0:T(128)} %sizes_in.1, s32[1,1024]{1,0:T(1,128)} %bitcast.25, bf16[1024,128]{1,0:T(8,128)(2,1)} %rows_in.1), custom_call_target="tpu_custom_call" | custom-call | flops 268435456 | bytes 4194304 | tf_op jit(solution)/shard_map/pallas_call | solution.py:35
  3.0 7.4 %all-to-all-start = ((bf16[32,64,128]{2,1,0:T(8,128)(2,1)}), bf16[32,64,128]{2,1,0:T(8,128)(2,1)}, u32[]{:S(2)}, u32[]{:S(2)}) async-start(bf16[32,64,128]{2,1,0:T(8,128)(2,1)} %get-tuple-element.30), calls=%async_computation | async-start | bytes 1048576 | tf_op jit(solution)/shard_map/all_to_all | solution.py:391
  10.4 0.0 copy-done
  10.4 2.7 %shard_map.92 = (bf16[6272,256]{1,0:T(8,128)(2,1)S(1)}, f32[8,128]{1,0:T(8,128)S(1)}) custom-call(s32[62]{0:T(128)S(1)} %copy-done, bf16[2,2,1792,128]{3,2,1,0:T(8,128)(2,1)} %right_top_in.1, bf16[3,2,64,1792]{3,2,1,0:T(8,128)(2,1)} %bitcast.24), custom_call_target="tpu_custom_call" | custom-call | bytes 6291456 | tf_op jit(solution)/shard_map/pallas_call | solution.py:35
  13.1 13.6 %all-to-all-done.arrived = bf16[32,64,128]{2,1,0:T(8,128)(2,1)} async-done(((bf16[32,64,128]{2,1,0:T(8,128)(2,1)}), bf16[32,64,128]{2,1,0:T(8,128)(2,1)}, u32[]{:S(2)}, u32[]{:S(2)}) %all-to-all-start) | async-done | bytes 524320 | tf_op jit(solution)/shard_map/all_to_all | solution.py:391
  26.7 2.4 %shard_map.93 = (bf16[2,1792,128]{2,1,0:T(8,128)(2,1)S(1)}, s32[7,256]{1,0:T(8,128)S(1)}, f32[264,128]{1,0:T(8,128)S(1)}, f32[200,128]{1,0:T(8,128)S(1)}) custom-call(bf16[32,64,128]{2,1,0:T(8,128)(2,1)} %all-to-all-done.arrived, bf16[6272,256]{1,0:T(8,128)(2,1)S(1)} %get-tuple-element.31.right), custom_call_target="tpu_custom_call" | custom-call | flops 411041792 | bytes 6291456 | tf_op jit(solution)/shard_map/pallas_call | solution.py:35
  29.1 0.1 collective-permute-start
  29.2 0.7 %shard_map.94 = (bf16[1792,256]{1,0:T(8,128)(2,1)S(1)}, bf16[1024,896]{1,0:T(8,128)(2,1)S(1)}, s32[1024,128]{1,0:T(8,128)S(1)}) custom-call(s32[7,256]{1,0:T(8,128)S(1)} %get-tuple-element.33.targets, s32[1,1024]{1,0:T(1,128)S(1)} %get-tuple-element.34.places, f32[264,128]{1,0:T(8,128)S(1)} %get-tuple-element.32.after), custom_call_target="tpu_custom_call" | custom-call | bytes 8388608 | tf_op jit(solution)/shard_map/pallas_call | solution.py:35
  29.9 0.6 collective-permute-done
  30.6 0.1 collective-permute-start.1
  30.7 4.0 %shard_map.95.rest_0_ = f32[896,128]{1,0:T(8,128)S(1)} custom-call(bf16[2,1792,1792]{2,1,0:T(8,128)(2,1)} %block_in.3, bf16[2,1792,128]{2,1,0:T(8,128)(2,1)S(1)} %get-tuple-element.43.pair, f32[192,128]{1,0:T(8,128)S(1)} %get-tuple-element.64.after), custom_call_target="tpu_custom_call" | custom-call | flops 822083584 | bytes 6422528 | tf_op jit(solution)/shard_map/pallas_call | solution.py:35
  34.7 0.1 collective-permute-done.1
  34.9 0.9 %collective-permute-start.2 = (f16[168,128]{1,0:T(8,128)(2,1)S(1)}, f16[168,128]{1,0:T(8,128)(2,1)S(1)}, u32[]{:S(2)}, u32[]{:S(2)}) collective-permute-start(f16[168,128]{1,0:T(8,128)(2,1)S(1)} %pad_maximum_fusion.1), channel_id=1, source_target_pairs={{0,4},{4,0},{1,5},{5,1},{2,6},{6,2},{3,7},{7,3},{8,12},{12,8},{9,1... | collective-permute-start | bytes 129032 | tf_op jit(solution)/shard_map/ppermute | solution.py:54
  35.8 4.0 %shard_map.96.rest_1_ = f32[896,128]{1,0:T(8,128)S(1)} custom-call(bf16[2,1792,1792]{2,1,0:T(8,128)(2,1)} %block_in.3, bf16[2,1792,128]{2,1,0:T(8,128)(2,1)S(1)} %get-tuple-element.43.pair, f32[160,128]{1,0:T(8,128)S(1)} %get-tuple-element.60.after), custom_call_target="tpu_custom_call" | custom-call | flops 822083584 | bytes 6422528 | tf_op jit(solution)/shard_map/pallas_call | solution.py:35
  39.8 0.6 collective-permute-done.2
  40.4 0.1 collective-permute-start.5
  40.5 1.6 %collective-permute-start.4 = (f16[136,128]{1,0:T(8,128)(2,1)S(1)}, f16[136,128]{1,0:T(8,128)(2,1)S(1)}, u32[]{:S(2)}, u32[]{:S(2)}) collective-permute-start(f16[136,128]{1,0:T(8,128)(2,1)S(1)} %pad_maximum_fusion.2), channel_id=1, source_target_pairs={{0,24},{1,3},{2,26},{3,1},{4,28},{5,7},{6,30},{7,5},{8,16},{9,11},... | collective-permute-start | bytes 104456 | tf_op jit(solution)/shard_map/ppermute | solution.py:479
  42.1 0.7 %collective-permute-start.3 = (f16[136,128]{1,0:T(8,128)(2,1)S(1)}, f16[136,128]{1,0:T(8,128)(2,1)S(1)}, u32[]{:S(2)}, u32[]{:S(2)}) collective-permute-start(f16[136,128]{1,0:T(8,128)(2,1)S(1)} %pad_maximum_fusion.2), channel_id=1, source_target_pairs={{0,16},{1,9},{2,18},{3,11},{4,20},{5,13},{6,22},{7,15},{8,24},{9,1... | collective-permute-start | bytes 104456 | tf_op jit(solution)/shard_map/ppermute | solution.py:479
  42.9 1.9 %shard_map.97 = (bf16[2,2,1792,128]{3,2,1,0:T(8,128)(2,1)S(1)}, bf16[1792,384]{1,0:T(8,128)(2,1)S(1)}) custom-call(bf16[2,2,1792,128]{3,2,1,0:T(8,128)(2,1)} %left_top_in.1, bf16[3,2,64,1792]{3,2,1,0:T(8,128)(2,1)} %bitcast.23, f32[128,128]{1,0:T(8,128)S(1)} %get-tuple-element.56.after), custom_call_target="tpu_custom_call" | custom-call | bytes 8388608 | tf_op jit(solution)/shard_map/pallas_call | solution.py:35
  44.8 0.0 collective-permute-done.5.rest_5_
  44.8 1.1 %shard_map.98.base = f32[1792,128]{1,0:T(8,128)S(1)} custom-call(s32[62]{0:T(128)S(1)} %copy-done, f32[896,128]{1,0:T(8,128)S(1)} %shard_map.95.rest_0_, f32[896,128]{1,0:T(8,128)S(1)} %shard_map.96.rest_1_, bf16[1792,384]{1,0:T(8,128)(2,1)S(1)} %get-tuple-element.48.rest_2_, f32[64,128]{1,0:T(8,128)S(1)} %slice.111.rest_3_, ...), custom_call_target="tpu_custom_call" | custom-call | flops 176160768 | bytes 3145728 | tf_op jit(solution)/shard_map/pallas_call | solution.py:35
  46.0 0.0 collective-permute-done.4
  46.0 0.2 collective-permute-done.3
  46.2 0.1 collective-permute-start.6
  46.3 0.5 shard_map.99.base
  46.8 0.7 %collective-permute-done.6.theirs = bf16[128,128]{1,0:T(8,128)(2,1)S(1)} collective-permute-done((bf16[128,128]{1,0:T(8,128)(2,1)S(1)}, bf16[128,128]{1,0:T(8,128)(2,1)S(1)}, u32[]{:S(2)}, u32[]{:S(2)}) %collective-permute-start.6) | collective-permute-done | bytes 32800 | tf_op jit(solution)/shard_map/ppermute | solution.py:54
  47.5 1.0 %shard_map.100 = bf16[1792,128]{1,0:T(8,128)(2,1)S(1)} custom-call(f32[8,128]{1,0:T(8,128)S(1)} %get-tuple-element.40.flags, f32[1792,128]{1,0:T(8,128)S(1)} %shard_map.99.base, bf16[2,2,1792,128]{3,2,1,0:T(8,128)(2,1)S(1)} %get-tuple-element.51.left_top, bf16[128,128]{1,0:T(8,128)(2,1)S(1)} %collective-permute-done.6.theirs, ...), custom_call_target="tpu_custom_call" | custom-call | flops 117440512 | bytes 4194304 | tf_op jit(solution)/shard_map/pallas_call | solution.py:35
  48.5 18.9 %all_to_all.10 = bf16[32,56,128]{2,1,0:T(8,128)(2,1)S(1)} all-to-all(bf16[32,56,128]{2,1,0:T(8,128)(2,1)S(1)} %bitcast.21), channel_id=1, replica_groups=mesh['group'=4,'member'=8] {'group','member'}, dimensions={0} | all-to-all | bytes 917504 | tf_op jit(solution)/shard_map/all_to_all | solution.py:531
  67.3 1.5 %shard_map.101 = f32[1024,128]{1,0:T(8,128)} custom-call(bf16[1024,896]{1,0:T(8,128)(2,1)S(1)} %get-tuple-element.38.order, s32[1024,128]{1,0:T(8,128)S(1)} %get-tuple-element.39.upper, bf16[1792,128]{1,0:T(8,128)(2,1)S(1)} %bitcast.22), custom_call_target="tpu_custom_call" | custom-call | flops 469762048 | bytes 4194304 | tf_op jit(solution)/shard_map/pallas_call | solution.py:35
  (26 shorter events, 0.3 us)
Async XLA Ops:
  0.0 10.4 %copy-start = (s32[62]{0:T(128)S(1)}, s32[62]{0:T(128)}, u32[]{:S(2)}) copy-start(s32[62]{0:T(128)} %ranks.3) | copy-start | bytes 748
  3.0 23.8 %all-to-all-start = ((bf16[32,64,128]{2,1,0:T(8,128)(2,1)}), bf16[32,64,128]{2,1,0:T(8,128)(2,1)}, u32[]{:S(2)}, u32[]{:S(2)}) async-start(bf16[32,64,128]{2,1,0:T(8,128)(2,1)} %get-tuple-element.30), calls=%async_computation | async-start | bytes 1048576 | tf_op jit(solution)/shard_map/all_to_all | solution.py:391
  29.1 1.4 %collective-permute-start = (f32[264,128]{1,0:T(8,128)S(1)}, f32[264,128]{1,0:T(8,128)S(1)}, u32[]{:S(2)}, u32[]{:S(2)}) collective-permute-start(f32[264,128]{1,0:T(8,128)S(1)} %get-tuple-element.32.after), channel_id=1, source_target_pairs={{0,1},{1,0},{2,3},{3,2},{4,5},{5,4},{6,7},{7,6},{8,9},{9,8},{10,11... | collective-permute-start | bytes 405512 | tf_op jit(solution)/shard_map/ppermute | solution.py:54
  30.6 4.2 %collective-permute-start.1 = (f16[200,128]{1,0:T(8,128)(2,1)S(1)}, f16[200,128]{1,0:T(8,128)(2,1)S(1)}, u32[]{:S(2)}, u32[]{:S(2)}) collective-permute-start(f16[200,128]{1,0:T(8,128)(2,1)S(1)} %pad_maximum_fusion), channel_id=1, source_target_pairs={{0,2},{2,0},{1,3},{3,1},{4,6},{6,4},{5,7},{7,5},{8,10},{10,8},{9,1... | collective-permute-start | bytes 153608 | tf_op jit(solution)/shard_map/ppermute | solution.py:54
  34.9 5.4 %collective-permute-start.2 = (f16[168,128]{1,0:T(8,128)(2,1)S(1)}, f16[168,128]{1,0:T(8,128)(2,1)S(1)}, u32[]{:S(2)}, u32[]{:S(2)}) collective-permute-start(f16[168,128]{1,0:T(8,128)(2,1)S(1)} %pad_maximum_fusion.1), channel_id=1, source_target_pairs={{0,4},{4,0},{1,5},{5,1},{2,6},{6,2},{3,7},{7,3},{8,12},{12,8},{9,1... | collective-permute-start | bytes 129032 | tf_op jit(solution)/shard_map/ppermute | solution.py:54
  40.4 4.4 %collective-permute-start.5 = (bf16[64,128]{1,0:T(8,128)(2,1)S(1)}, bf16[64,128]{1,0:T(8,128)(2,1)S(1)}, u32[]{:S(2)}, u32[]{:S(2)}) collective-permute-start(bf16[64,128]{1,0:T(8,128)(2,1)S(1)} %pad_maximum_fusion.3.rest_4_), channel_id=1, source_target_pairs={{0,1},{1,0},{2,3},{3,2},{4,5},{5,4},{6,7},{7,6},{8,9},{9,8},{10,11... | collective-permute-start | bytes 49160 | tf_op jit(solution)/shard_map/ppermute | solution.py:54
  40.5 5.4 %collective-permute-start.4 = (f16[136,128]{1,0:T(8,128)(2,1)S(1)}, f16[136,128]{1,0:T(8,128)(2,1)S(1)}, u32[]{:S(2)}, u32[]{:S(2)}) collective-permute-start(f16[136,128]{1,0:T(8,128)(2,1)S(1)} %pad_maximum_fusion.2), channel_id=1, source_target_pairs={{0,24},{1,3},{2,26},{3,1},{4,28},{5,7},{6,30},{7,5},{8,16},{9,11},... | collective-permute-start | bytes 104456 | tf_op jit(solution)/shard_map/ppermute | solution.py:479
  42.1 4.0 %collective-permute-start.3 = (f16[136,128]{1,0:T(8,128)(2,1)S(1)}, f16[136,128]{1,0:T(8,128)(2,1)S(1)}, u32[]{:S(2)}, u32[]{:S(2)}) collective-permute-start(f16[136,128]{1,0:T(8,128)(2,1)S(1)} %pad_maximum_fusion.2), channel_id=1, source_target_pairs={{0,16},{1,9},{2,18},{3,11},{4,20},{5,13},{6,22},{7,15},{8,24},{9,1... | collective-permute-start | bytes 104456 | tf_op jit(solution)/shard_map/ppermute | solution.py:479
  46.2 1.3 %collective-permute-start.6 = (bf16[128,128]{1,0:T(8,128)(2,1)S(1)}, bf16[128,128]{1,0:T(8,128)(2,1)S(1)}, u32[]{:S(2)}, u32[]{:S(2)}) collective-permute-start(bf16[128,128]{1,0:T(8,128)(2,1)S(1)} %add_convert_fusion.own), channel_id=1, source_target_pairs={{0,1},{1,0},{2,3},{3,2},{4,5},{5,4},{6,7},{7,6},{8,9},{9,8},{10,11... | collective-permute-start | bytes 98312 | tf_op jit(solution)/shard_map/ppermute | solution.py:54

commit v9 on v7

--- a/solution.py
+++ b/solution.py
@@ -179,17 +179,23 @@
             order[low : low + block, at : at + 128] = hot(place[low : low + block] == lanes + at)
 
 
-def stage_kernel(left_top_in, left_low_in, after, left_top, left_low, raw, sems):
-    copies = [
-        pltpu.make_async_copy(left_low_in, raw, sems.at[0]),
-        pltpu.make_async_copy(left_top_in, left_top, sems.at[1]),
-    ]
+def stage_kernel(first, left_top_in, left_low_in, block_in, pair, after, *rest):
+    left_top, left_low, out, raw, block, sems = rest
+    copies = [pltpu.make_async_copy(left_low_in, raw, sems.at[0])]
+    count, _, height, _ = block.shape
+    for j in range(count):
+        rows = pl.ds((first + j) * height, height)
+        copies.append(pltpu.make_async_copy(block_in.at[:, rows, :], block.at[j], sems.at[1 + j]))
+    copies.append(pltpu.make_async_copy(left_top_in, left_top, sems.at[1 + count]))
     for copy in copies:
         copy.start()
     copies[0].wait()
     levels, parts, width, capacity = raw.shape
     left_low[...] = jnp.transpose(raw[...].reshape(levels * parts * width, capacity))
-    copies[1].wait()
+    for j in range(count):
+        copies[1 + j].wait()
+        out[j * height : (j + 1) * height, :] = dot(block[j, 0], pair[0]) + dot(block[j, 1], pair[1])
+    copies[-1].wait()
 
 
 def field_kernel(leaves, bucket, tops, levels, arrived, right, *rest):
@@ -450,10 +456,10 @@
         rest = running.shape[0] - width // 2
         received = partner(narrow(running, power), "member", bit)
         if bit == 1:
-            bases.append(diagonal(0, 4, running))
+            bases.append(diagonal(0, 3, running))
             received, bases[0] = lax.optimization_barrier((received, bases[0]))
         if bit == member_levels - 1:
-            bases.append(diagonal(4, 4, running))
+            bases.append(diagonal(3, 3, running))
             received, bases[1] = lax.optimization_barrier((received, bases[1]))
         received, other = widen(received)
         power = bound(power, other)
@@ -467,19 +473,25 @@
             routes[1] += [(at, (low ^ 3) * members + near), (at + 1, low * members + (near ^ 2) + 1)]
     sums = narrow(running, power)
     heard = [lax.ppermute(sums, everyone, route) for route in routes]
-    left_top, left_low = call(
-        stage_kernel,
+    left_top, left_low, last = call(
+        functools.partial(stage_kernel, 6),
         [
             pltpu.VMEM(top_left.shape, BF16),
             pltpu.VMEM((capacity, member_levels * 2 * width), BF16),
-        ],
-        [HBM, HBM, pl.BlockSpec(memory_space=pl.ANY)],
-        (*far(top_left, low_left), running),
-        0,
-        8 << 20,
+            jax.ShapeDtypeStruct((2 * height, columns), F32),
+        ],
+        [HBM, HBM, HBM, VMEM, pl.BlockSpec(memory_space=pl.ANY)],
+        (*far(top_left, low_left, diag_block), pair, running),
+        8 * height * capacity * columns,
+        12 << 20,
         24,
-        scratch=[pltpu.VMEM(low_left.shape, BF16), DMA((2,))],
-    )
+        scratch=[
+            pltpu.VMEM(low_left.shape, BF16),
+            pltpu.VMEM((2, 2, height, capacity), BF16),
+            DMA((4,)),
+        ],
+    )
+    bases.append(last)
     heard, left_top, left_low = lax.optimization_barrier((heard, left_top, left_low))
     heard = [widen(block)[0] for block in heard]
     own = (heard[0] + jnp.where(flags[:1] > 0, heard[1], 0.0)).astype(BF16)

time: 68.5 us -> 67.4 us (0.984)
  blocking collectives: 18.7 us -> 17.2 us
    all_to_all x1, blocking collectives: 18.7 us -> 17.2 us  [on_device(): lax.all_to_all(leaving.reshape(leaves, bucket, columns), everyone, split_...]
    ppermute x2, waiting for transfers between devices: 1.28 us -> 0.01 us  [on_device(): heard = [lax.ppermute(sums, everyone, route) for route in routes]]
    ppermute x5, waiting for transfers between devices: 2.02 us -> 3.27 us  [partner(): return lax.ppermute(block, axis, route)]
  transfers between devices with their start and end apart: 8 -> 8, of which waited for: 6 -> 4; matrix products, arithmetic and copies ran while one was open for 0% -> 0% of each run, Pallas kernels for 21% -> 21%
where the time goes in v9:
time: 67.4 us; the launch traced here: 67.1 us
  Pallas kernels  21.7 us (32%)
  blocking collectives  17.2 us (26%)
  waiting for transfers between devices  16.9 us (25%)
  starting transfers between devices  10.8 us (16%)
    pallas_call x10, Pallas kernels, call(): pl.pallas_call(kernel, out_shape=outs, in_specs=ins, out_specs=more.pop('...  21.7 us
    all_to_all x1, blocking collectives, on_device(): lax.all_to_all(leaving.reshape(leaves, bucket, columns), everyone, split_...  17.2 us
    all_to_all x1, waiting for transfers between devices, on_device(): lax.all_to_all(packed, everyone, split_axis=0, concat_axis=0, tiled=True)  13.6 us
    all_to_all x1, starting transfers between devices, on_device(): lax.all_to_all(packed, everyone, split_axis=0, concat_axis=0, tiled=True)  7.43 us
    ppermute x5, waiting for transfers between devices, partner(): return lax.ppermute(block, axis, route)  3.27 us
    ppermute x2, starting transfers between devices, on_device(): heard = [lax.ppermute(sums, everyone, route) for route in routes]  2.6 us
  transfers between devices with their start and end apart: 8, of which 4 were waited for; matrix products, arithmetic and copies ran while one was open for 0% of the time, Pallas kernels for 21%

profile of v9, /device:TPU:0, one launch (start us, length us, event | category | flops | bytes accessed | tf_op | source)
XLA Modules:
  0.0 67.1 jit_solution(5795315911748176281)
XLA Ops:
  0.0 0.0 copy-start
  0.0 2.9 %shard_map.91 = (bf16[32,64,128]{2,1,0:T(8,128)(2,1)}, s32[1,1024]{1,0:T(1,128)S(1)}) custom-call(s32[32]{0:T(128)} %sizes_in.1, s32[1,1024]{1,0:T(1,128)} %bitcast.25, bf16[1024,128]{1,0:T(8,128)(2,1)} %rows_in.1), custom_call_target="tpu_custom_call" | custom-call | flops 268435456 | bytes 4194304 | tf_op jit(solution)/shard_map/pallas_call | solution.py:35
  3.0 7.4 %all-to-all-start = ((bf16[32,64,128]{2,1,0:T(8,128)(2,1)}), bf16[32,64,128]{2,1,0:T(8,128)(2,1)}, u32[]{:S(2)}, u32[]{:S(2)}) async-start(bf16[32,64,128]{2,1,0:T(8,128)(2,1)} %get-tuple-element.33), calls=%async_computation | async-start | bytes 1048576 | tf_op jit(solution)/shard_map/all_to_all | solution.py:389
  10.4 0.0 copy-done
  10.4 2.7 %shard_map.92 = (bf16[6272,256]{1,0:T(8,128)(2,1)S(1)}, f32[8,128]{1,0:T(8,128)S(1)}) custom-call(s32[62]{0:T(128)S(1)} %copy-done, bf16[2,2,1792,128]{3,2,1,0:T(8,128)(2,1)} %right_top_in.1, bf16[3,2,64,1792]{3,2,1,0:T(8,128)(2,1)} %bitcast.23), custom_call_target="tpu_custom_call" | custom-call | bytes 6291456 | tf_op jit(solution)/shard_map/pallas_call | solution.py:35
  13.1 13.6 %all-to-all-done.arrived = bf16[32,64,128]{2,1,0:T(8,128)(2,1)} async-done(((bf16[32,64,128]{2,1,0:T(8,128)(2,1)}), bf16[32,64,128]{2,1,0:T(8,128)(2,1)}, u32[]{:S(2)}, u32[]{:S(2)}) %all-to-all-start) | async-done | bytes 524320 | tf_op jit(solution)/shard_map/all_to_all | solution.py:389
  26.7 2.4 %shard_map.93 = (bf16[2,1792,128]{2,1,0:T(8,128)(2,1)S(1)}, s32[7,256]{1,0:T(8,128)S(1)}, f32[264,128]{1,0:T(8,128)S(1)}, f32[200,128]{1,0:T(8,128)S(1)}) custom-call(bf16[32,64,128]{2,1,0:T(8,128)(2,1)} %all-to-all-done.arrived, bf16[6272,256]{1,0:T(8,128)(2,1)S(1)} %get-tuple-element.34.right), custom_call_target="tpu_custom_call" | custom-call | flops 411041792 | bytes 6291456 | tf_op jit(solution)/shard_map/pallas_call | solution.py:35
  29.1 0.1 collective-permute-start
  29.2 0.7 %shard_map.94 = (bf16[1792,256]{1,0:T(8,128)(2,1)S(1)}, bf16[1024,896]{1,0:T(8,128)(2,1)S(1)}, s32[1024,128]{1,0:T(8,128)S(1)}) custom-call(s32[7,256]{1,0:T(8,128)S(1)} %get-tuple-element.36.targets, s32[1,1024]{1,0:T(1,128)S(1)} %get-tuple-element.37.places, f32[264,128]{1,0:T(8,128)S(1)} %get-tuple-element.35.after), custom_call_target="tpu_custom_call" | custom-call | bytes 8388608 | tf_op jit(solution)/shard_map/pallas_call | solution.py:35
  29.9 0.6 collective-permute-done
  30.6 0.1 collective-permute-start.1
  30.7 3.2 %shard_map.95.rest_0_ = f32[672,128]{1,0:T(8,128)S(1)} custom-call(bf16[2,1792,1792]{2,1,0:T(8,128)(2,1)} %block_in.5, bf16[2,1792,128]{2,1,0:T(8,128)(2,1)S(1)} %get-tuple-element.46.pair, f32[192,128]{1,0:T(8,128)S(1)} %get-tuple-element.70.after), custom_call_target="tpu_custom_call" | custom-call | flops 616562688 | bytes 4816896 | tf_op jit(solution)/shard_map/pallas_call | solution.py:35
  33.8 0.9 %collective-permute-done.1 = f16[200,128]{1,0:T(8,128)(2,1)S(1)} collective-permute-done((f16[200,128]{1,0:T(8,128)(2,1)S(1)}, f16[200,128]{1,0:T(8,128)(2,1)S(1)}, u32[]{:S(2)}, u32[]{:S(2)}) %collective-permute-start.1) | collective-permute-done | bytes 51232 | tf_op jit(solution)/shard_map/ppermute | solution.py:54
  34.9 0.1 collective-permute-start.2
  35.0 3.2 %shard_map.96.rest_1_ = f32[672,128]{1,0:T(8,128)S(1)} custom-call(bf16[2,1792,1792]{2,1,0:T(8,128)(2,1)} %block_in.5, bf16[2,1792,128]{2,1,0:T(8,128)(2,1)S(1)} %get-tuple-element.46.pair, f32[160,128]{1,0:T(8,128)S(1)} %get-tuple-element.66.after), custom_call_target="tpu_custom_call" | custom-call | flops 616562688 | bytes 4816896 | tf_op jit(solution)/shard_map/pallas_call | solution.py:35
  38.1 1.7 %collective-permute-done.2 = f16[168,128]{1,0:T(8,128)(2,1)S(1)} collective-permute-done((f16[168,128]{1,0:T(8,128)(2,1)S(1)}, f16[168,128]{1,0:T(8,128)(2,1)S(1)}, u32[]{:S(2)}, u32[]{:S(2)}) %collective-permute-start.2) | collective-permute-done | bytes 43040 | tf_op jit(solution)/shard_map/ppermute | solution.py:54
  40.0 0.6 collective-permute-start.4
  40.6 2.0 %collective-permute-start.3 = (f16[136,128]{1,0:T(8,128)(2,1)S(1)}, f16[136,128]{1,0:T(8,128)(2,1)S(1)}, u32[]{:S(2)}, u32[]{:S(2)}) collective-permute-start(f16[136,128]{1,0:T(8,128)(2,1)S(1)} %pad_maximum_fusion.2), channel_id=1, source_target_pairs={{0,16},{1,9},{2,18},{3,11},{4,20},{5,13},{6,22},{7,15},{8,24},{9,1... | collective-permute-start | bytes 104456 | tf_op jit(solution)/shard_map/ppermute | solution.py:475
  42.6 0.0 collective-permute-start.5
  42.6 3.0 %shard_map.97 = (bf16[2,2,1792,128]{3,2,1,0:T(8,128)(2,1)S(1)}, bf16[1792,384]{1,0:T(8,128)(2,1)S(1)}, f32[448,128]{1,0:T(8,128)S(1)}) custom-call(bf16[2,2,1792,128]{3,2,1,0:T(8,128)(2,1)} %left_top_in.1, bf16[3,2,64,1792]{3,2,1,0:T(8,128)(2,1)} %bitcast.24, bf16[2,1792,1792]{2,1,0:T(8,128)(2,1)} %block_in.5, ...), custom_call_target="tpu_custom_call" | custom-call | flops 411041792 | bytes 12582912 | tf_op jit(solution)/shard_map/pallas_call | solution.py:35
  45.6 0.0 collective-permute-done.4
  45.6 0.0 collective-permute-done.3
  45.7 0.0 collective-permute-done.5.rest_6_
  45.7 0.6 collective-permute-start.6
  46.3 1.1 %shard_map.98.base = f32[1792,128]{1,0:T(8,128)S(1)} custom-call(s32[62]{0:T(128)S(1)} %copy-done, f32[672,128]{1,0:T(8,128)S(1)} %shard_map.95.rest_0_, f32[672,128]{1,0:T(8,128)S(1)} %shard_map.96.rest_1_, f32[448,128]{1,0:T(8,128)S(1)} %get-tuple-element.51.rest_2_, bf16[1792,384]{1,0:T(8,128)(2,1)S(1)} %get-tuple-element.54.rest_3_, ...), custom_call_target="tpu_custom_call" | custom-call | flops 176160768 | bytes 3145728 | tf_op jit(solution)/shard_map/pallas_call | solution.py:35
  47.4 0.0 collective-permute-done.6.theirs
  47.4 1.0 %shard_map.99 = bf16[1792,128]{1,0:T(8,128)(2,1)S(1)} custom-call(f32[8,128]{1,0:T(8,128)S(1)} %get-tuple-element.43.flags, f32[1792,128]{1,0:T(8,128)S(1)} %shard_map.98.base, bf16[2,2,1792,128]{3,2,1,0:T(8,128)(2,1)S(1)} %get-tuple-element.58.left_top, bf16[128,128]{1,0:T(8,128)(2,1)S(1)} %add_convert_fusion.own, ...), custom_call_target="tpu_custom_call" | custom-call | flops 234881024 | bytes 4194304 | tf_op jit(solution)/shard_map/pallas_call | solution.py:35
  48.5 17.2 %all_to_all.10 = bf16[32,56,128]{2,1,0:T(8,128)(2,1)S(1)} all-to-all(bf16[32,56,128]{2,1,0:T(8,128)(2,1)S(1)} %bitcast.21), channel_id=1, replica_groups=mesh['group'=4,'member'=8] {'group','member'}, dimensions={0} | all-to-all | bytes 917504 | tf_op jit(solution)/shard_map/all_to_all | solution.py:524
  65.7 1.4 %shard_map.100 = f32[1024,128]{1,0:T(8,128)} custom-call(bf16[1024,896]{1,0:T(8,128)(2,1)S(1)} %get-tuple-element.41.order, s32[1024,128]{1,0:T(8,128)S(1)} %get-tuple-element.42.upper, bf16[1792,128]{1,0:T(8,128)(2,1)S(1)} %bitcast.22), custom_call_target="tpu_custom_call" | custom-call | flops 469762048 | bytes 4194304 | tf_op jit(solution)/shard_map/pallas_call | solution.py:35
  (25 shorter events, 0.2 us)
Async XLA Ops:
  0.0 10.4 %copy-start = (s32[62]{0:T(128)S(1)}, s32[62]{0:T(128)}, u32[]{:S(2)}) copy-start(s32[62]{0:T(128)} %ranks.3) | copy-start | bytes 748
  3.0 23.8 %all-to-all-start = ((bf16[32,64,128]{2,1,0:T(8,128)(2,1)}), bf16[32,64,128]{2,1,0:T(8,128)(2,1)}, u32[]{:S(2)}, u32[]{:S(2)}) async-start(bf16[32,64,128]{2,1,0:T(8,128)(2,1)} %get-tuple-element.33), calls=%async_computation | async-start | bytes 1048576 | tf_op jit(solution)/shard_map/all_to_all | solution.py:389
  29.1 1.4 %collective-permute-start = (f32[264,128]{1,0:T(8,128)S(1)}, f32[264,128]{1,0:T(8,128)S(1)}, u32[]{:S(2)}, u32[]{:S(2)}) collective-permute-start(f32[264,128]{1,0:T(8,128)S(1)} %get-tuple-element.35.after), channel_id=1, source_target_pairs={{0,1},{1,0},{2,3},{3,2},{4,5},{5,4},{6,7},{7,6},{8,9},{9,8},{10,11... | collective-permute-start | bytes 405512 | tf_op jit(solution)/shard_map/ppermute | solution.py:54
  30.6 4.2 %collective-permute-start.1 = (f16[200,128]{1,0:T(8,128)(2,1)S(1)}, f16[200,128]{1,0:T(8,128)(2,1)S(1)}, u32[]{:S(2)}, u32[]{:S(2)}) collective-permute-start(f16[200,128]{1,0:T(8,128)(2,1)S(1)} %pad_maximum_fusion), channel_id=1, source_target_pairs={{0,2},{2,0},{1,3},{3,1},{4,6},{6,4},{5,7},{7,5},{8,10},{10,8},{9,1... | collective-permute-start | bytes 153608 | tf_op jit(solution)/shard_map/ppermute | solution.py:54
  34.9 5.0 %collective-permute-start.2 = (f16[168,128]{1,0:T(8,128)(2,1)S(1)}, f16[168,128]{1,0:T(8,128)(2,1)S(1)}, u32[]{:S(2)}, u32[]{:S(2)}) collective-permute-start(f16[168,128]{1,0:T(8,128)(2,1)S(1)} %pad_maximum_fusion.1), channel_id=1, source_target_pairs={{0,4},{4,0},{1,5},{5,1},{2,6},{6,2},{3,7},{7,3},{8,12},{12,8},{9,1... | collective-permute-start | bytes 129032 | tf_op jit(solution)/shard_map/ppermute | solution.py:54
  40.0 5.6 %collective-permute-start.4 = (f16[136,128]{1,0:T(8,128)(2,1)S(1)}, f16[136,128]{1,0:T(8,128)(2,1)S(1)}, u32[]{:S(2)}, u32[]{:S(2)}) collective-permute-start(f16[136,128]{1,0:T(8,128)(2,1)S(1)} %pad_maximum_fusion.2), channel_id=1, source_target_pairs={{0,24},{1,3},{2,26},{3,1},{4,28},{5,7},{6,30},{7,5},{8,16},{9,11},... | collective-permute-start | bytes 104456 | tf_op jit(solution)/shard_map/ppermute | solution.py:475
  40.6 5.0 %collective-permute-start.3 = (f16[136,128]{1,0:T(8,128)(2,1)S(1)}, f16[136,128]{1,0:T(8,128)(2,1)S(1)}, u32[]{:S(2)}, u32[]{:S(2)}) collective-permute-start(f16[136,128]{1,0:T(8,128)(2,1)S(1)} %pad_maximum_fusion.2), channel_id=1, source_target_pairs={{0,16},{1,9},{2,18},{3,11},{4,20},{5,13},{6,22},{7,15},{8,24},{9,1... | collective-permute-start | bytes 104456 | tf_op jit(solution)/shard_map/ppermute | solution.py:475
  42.6 3.1 %collective-permute-start.5 = (bf16[64,128]{1,0:T(8,128)(2,1)S(1)}, bf16[64,128]{1,0:T(8,128)(2,1)S(1)}, u32[]{:S(2)}, u32[]{:S(2)}) collective-permute-start(bf16[64,128]{1,0:T(8,128)(2,1)S(1)} %pad_maximum_fusion.3.rest_5_), channel_id=1, source_target_pairs={{0,1},{1,0},{2,3},{3,2},{4,5},{5,4},{6,7},{7,6},{8,9},{9,8},{10,11... | collective-permute-start | bytes 49160 | tf_op jit(solution)/shard_map/ppermute | solution.py:54
  45.7 1.7 %collective-permute-start.6 = (bf16[128,128]{1,0:T(8,128)(2,1)S(1)}, bf16[128,128]{1,0:T(8,128)(2,1)S(1)}, u32[]{:S(2)}, u32[]{:S(2)}) collective-permute-start(bf16[128,128]{1,0:T(8,128)(2,1)S(1)} %add_convert_fusion.own), channel_id=1, source_target_pairs={{0,1},{1,0},{2,3},{3,2},{4,5},{5,4},{6,7},{7,6},{8,9},{9,8},{10,11... | collective-permute-start | bytes 98312 | tf_op jit(solution)/shard_map/ppermute | solution.py:54

commit v10 on v9

--- a/solution.py
+++ b/solution.py
@@ -459,7 +459,7 @@
             bases.append(diagonal(0, 3, running))
             received, bases[0] = lax.optimization_barrier((received, bases[0]))
         if bit == member_levels - 1:
-            bases.append(diagonal(3, 3, running))
+            bases.append(diagonal(3, 4, running))
             received, bases[1] = lax.optimization_barrier((received, bases[1]))
         received, other = widen(received)
         power = bound(power, other)
@@ -474,21 +474,21 @@
     sums = narrow(running, power)
     heard = [lax.ppermute(sums, everyone, route) for route in routes]
     left_top, left_low, last = call(
-        functools.partial(stage_kernel, 6),
+        functools.partial(stage_kernel, 7),
         [
             pltpu.VMEM(top_left.shape, BF16),
             pltpu.VMEM((capacity, member_levels * 2 * width), BF16),
-            jax.ShapeDtypeStruct((2 * height, columns), F32),
+            jax.ShapeDtypeStruct((height, columns), F32),
         ],
         [HBM, HBM, HBM, VMEM, pl.BlockSpec(memory_space=pl.ANY)],
         (*far(top_left, low_left, diag_block), pair, running),
-        8 * height * capacity * columns,
-        12 << 20,
+        4 * height * capacity * columns,
+        10 << 20,
         24,
         scratch=[
             pltpu.VMEM(low_left.shape, BF16),
-            pltpu.VMEM((2, 2, height, capacity), BF16),
-            DMA((4,)),
+            pltpu.VMEM((1, 2, height, capacity), BF16),
+            DMA((3,)),
         ],
     )
     bases.append(last)

time: 67.4 us -> 68 us (level)
  blocking collectives: 17.2 us -> 18.3 us
    all_to_all x1, blocking collectives: 17.2 us -> 18.3 us  [on_device(): lax.all_to_all(leaving.reshape(leaves, bucket, columns), everyone, split_...]
  transfers between devices with their start and end apart: 8 -> 8, of which waited for: 4 -> 5; matrix products, arithmetic and copies ran while one was open for 0% -> 0% of each run, Pallas kernels for 21% -> 21%
where the time goes in v10:
time: 68 us; the launch traced here: 67.7 us
  Pallas kernels  21.7 us (32%)
  blocking collectives  18.3 us (27%)
  waiting for transfers between devices  16.5 us (24%)
  starting transfers between devices  10.6 us (16%)
    pallas_call x10, Pallas kernels, call(): pl.pallas_call(kernel, out_shape=outs, in_specs=ins, out_specs=more.pop('...  21.7 us
    all_to_all x1, blocking collectives, on_device(): lax.all_to_all(leaving.reshape(leaves, bucket, columns), everyone, split_...  18.3 us
    all_to_all x1, waiting for transfers between devices, on_device(): lax.all_to_all(packed, everyone, split_axis=0, concat_axis=0, tiled=True)  13.6 us
    all_to_all x1, starting transfers between devices, on_device(): lax.all_to_all(packed, everyone, split_axis=0, concat_axis=0, tiled=True)  7.43 us
    ppermute x5, waiting for transfers between devices, partner(): return lax.ppermute(block, axis, route)  2.67 us
    ppermute x2, starting transfers between devices, on_device(): heard = [lax.ppermute(sums, everyone, route) for route in routes]  2.6 us
  transfers between devices with their start and end apart: 8, of which 5 were waited for; matrix products, arithmetic and copies ran while one was open for 0% of the time, Pallas kernels for 21%

profile of v10, /device:TPU:0, one launch (start us, length us, event | category | flops | bytes accessed | tf_op | source)
XLA Modules:
  0.0 67.7 jit_solution(1097016320168254014)
XLA Ops:
  0.0 0.0 copy-start
  0.0 2.9 %shard_map.91 = (bf16[32,64,128]{2,1,0:T(8,128)(2,1)}, s32[1,1024]{1,0:T(1,128)S(1)}) custom-call(s32[32]{0:T(128)} %sizes_in.1, s32[1,1024]{1,0:T(1,128)} %bitcast.25, bf16[1024,128]{1,0:T(8,128)(2,1)} %rows_in.1), custom_call_target="tpu_custom_call" | custom-call | flops 268435456 | bytes 4194304 | tf_op jit(solution)/shard_map/pallas_call | solution.py:35
  3.0 7.4 %all-to-all-start = ((bf16[32,64,128]{2,1,0:T(8,128)(2,1)}), bf16[32,64,128]{2,1,0:T(8,128)(2,1)}, u32[]{:S(2)}, u32[]{:S(2)}) async-start(bf16[32,64,128]{2,1,0:T(8,128)(2,1)} %get-tuple-element.33), calls=%async_computation | async-start | bytes 1048576 | tf_op jit(solution)/shard_map/all_to_all | solution.py:389
  10.4 0.0 copy-done
  10.4 2.7 %shard_map.92 = (bf16[6272,256]{1,0:T(8,128)(2,1)S(1)}, f32[8,128]{1,0:T(8,128)S(1)}) custom-call(s32[62]{0:T(128)S(1)} %copy-done, bf16[2,2,1792,128]{3,2,1,0:T(8,128)(2,1)} %right_top_in.1, bf16[3,2,64,1792]{3,2,1,0:T(8,128)(2,1)} %bitcast.23), custom_call_target="tpu_custom_call" | custom-call | bytes 6291456 | tf_op jit(solution)/shard_map/pallas_call | solution.py:35
  13.1 13.6 %all-to-all-done.arrived = bf16[32,64,128]{2,1,0:T(8,128)(2,1)} async-done(((bf16[32,64,128]{2,1,0:T(8,128)(2,1)}), bf16[32,64,128]{2,1,0:T(8,128)(2,1)}, u32[]{:S(2)}, u32[]{:S(2)}) %all-to-all-start) | async-done | bytes 524320 | tf_op jit(solution)/shard_map/all_to_all | solution.py:389
  26.7 2.4 %shard_map.93 = (bf16[2,1792,128]{2,1,0:T(8,128)(2,1)S(1)}, s32[7,256]{1,0:T(8,128)S(1)}, f32[264,128]{1,0:T(8,128)S(1)}, f32[200,128]{1,0:T(8,128)S(1)}) custom-call(bf16[32,64,128]{2,1,0:T(8,128)(2,1)} %all-to-all-done.arrived, bf16[6272,256]{1,0:T(8,128)(2,1)S(1)} %get-tuple-element.34.right), custom_call_target="tpu_custom_call" | custom-call | flops 411041792 | bytes 6291456 | tf_op jit(solution)/shard_map/pallas_call | solution.py:35
  29.1 0.1 collective-permute-start
  29.2 0.7 %shard_map.94 = (bf16[1792,256]{1,0:T(8,128)(2,1)S(1)}, bf16[1024,896]{1,0:T(8,128)(2,1)S(1)}, s32[1024,128]{1,0:T(8,128)S(1)}) custom-call(s32[7,256]{1,0:T(8,128)S(1)} %get-tuple-element.36.targets, s32[1,1024]{1,0:T(1,128)S(1)} %get-tuple-element.37.places, f32[264,128]{1,0:T(8,128)S(1)} %get-tuple-element.35.after), custom_call_target="tpu_custom_call" | custom-call | bytes 8388608 | tf_op jit(solution)/shard_map/pallas_call | solution.py:35
  29.9 0.6 collective-permute-done
  30.6 0.1 collective-permute-start.1
  30.7 3.2 %shard_map.95.rest_0_ = f32[672,128]{1,0:T(8,128)S(1)} custom-call(bf16[2,1792,1792]{2,1,0:T(8,128)(2,1)} %block_in.5, bf16[2,1792,128]{2,1,0:T(8,128)(2,1)S(1)} %get-tuple-element.46.pair, f32[192,128]{1,0:T(8,128)S(1)} %get-tuple-element.70.after), custom_call_target="tpu_custom_call" | custom-call | flops 616562688 | bytes 4816896 | tf_op jit(solution)/shard_map/pallas_call | solution.py:35
  33.8 0.9 %collective-permute-done.1 = f16[200,128]{1,0:T(8,128)(2,1)S(1)} collective-permute-done((f16[200,128]{1,0:T(8,128)(2,1)S(1)}, f16[200,128]{1,0:T(8,128)(2,1)S(1)}, u32[]{:S(2)}, u32[]{:S(2)}) %collective-permute-start.1) | collective-permute-done | bytes 51232 | tf_op jit(solution)/shard_map/ppermute | solution.py:54
  34.9 0.1 collective-permute-start.2
  35.0 3.7 %shard_map.96.rest_1_ = f32[896,128]{1,0:T(8,128)S(1)} custom-call(bf16[2,1792,1792]{2,1,0:T(8,128)(2,1)} %block_in.5, bf16[2,1792,128]{2,1,0:T(8,128)(2,1)S(1)} %get-tuple-element.46.pair, f32[160,128]{1,0:T(8,128)S(1)} %get-tuple-element.66.after), custom_call_target="tpu_custom_call" | custom-call | flops 822083584 | bytes 6422528 | tf_op jit(solution)/shard_map/pallas_call | solution.py:35
  38.7 1.2 %collective-permute-done.2 = f16[168,128]{1,0:T(8,128)(2,1)S(1)} collective-permute-done((f16[168,128]{1,0:T(8,128)(2,1)S(1)}, f16[168,128]{1,0:T(8,128)(2,1)S(1)}, u32[]{:S(2)}, u32[]{:S(2)}) %collective-permute-start.2) | collective-permute-done | bytes 43040 | tf_op jit(solution)/shard_map/ppermute | solution.py:54
  40.0 1.0 %collective-permute-start.4 = (f16[136,128]{1,0:T(8,128)(2,1)S(1)}, f16[136,128]{1,0:T(8,128)(2,1)S(1)}, u32[]{:S(2)}, u32[]{:S(2)}) collective-permute-start(f16[136,128]{1,0:T(8,128)(2,1)S(1)} %pad_maximum_fusion.2), channel_id=1, source_target_pairs={{0,24},{1,3},{2,26},{3,1},{4,28},{5,7},{6,30},{7,5},{8,16},{9,11},... | collective-permute-start | bytes 104456 | tf_op jit(solution)/shard_map/ppermute | solution.py:475
  41.0 1.6 %collective-permute-start.3 = (f16[136,128]{1,0:T(8,128)(2,1)S(1)}, f16[136,128]{1,0:T(8,128)(2,1)S(1)}, u32[]{:S(2)}, u32[]{:S(2)}) collective-permute-start(f16[136,128]{1,0:T(8,128)(2,1)S(1)} %pad_maximum_fusion.2), channel_id=1, source_target_pairs={{0,16},{1,9},{2,18},{3,11},{4,20},{5,13},{6,22},{7,15},{8,24},{9,1... | collective-permute-start | bytes 104456 | tf_op jit(solution)/shard_map/ppermute | solution.py:475
  42.6 0.0 collective-permute-start.5
  42.6 2.4 %shard_map.97 = (bf16[2,2,1792,128]{3,2,1,0:T(8,128)(2,1)S(1)}, bf16[1792,384]{1,0:T(8,128)(2,1)S(1)}, f32[224,128]{1,0:T(8,128)S(1)}) custom-call(bf16[2,2,1792,128]{3,2,1,0:T(8,128)(2,1)} %left_top_in.1, bf16[3,2,64,1792]{3,2,1,0:T(8,128)(2,1)} %bitcast.24, bf16[2,1792,1792]{2,1,0:T(8,128)(2,1)} %block_in.5, ...), custom_call_target="tpu_custom_call" | custom-call | flops 205520896 | bytes 10485760 | tf_op jit(solution)/shard_map/pallas_call | solution.py:35
  45.0 0.0 collective-permute-done.4
  45.1 0.2 collective-permute-done.3
  45.3 0.0 collective-permute-done.5.rest_6_
  45.3 0.4 collective-permute-start.6
  45.7 1.1 %shard_map.98.base = f32[1792,128]{1,0:T(8,128)S(1)} custom-call(s32[62]{0:T(128)S(1)} %copy-done, f32[672,128]{1,0:T(8,128)S(1)} %shard_map.95.rest_0_, f32[896,128]{1,0:T(8,128)S(1)} %shard_map.96.rest_1_, f32[224,128]{1,0:T(8,128)S(1)} %get-tuple-element.51.rest_2_, bf16[1792,384]{1,0:T(8,128)(2,1)S(1)} %get-tuple-element.54.rest_3_, ...), custom_call_target="tpu_custom_call" | custom-call | flops 176160768 | bytes 3145728 | tf_op jit(solution)/shard_map/pallas_call | solution.py:35
  46.8 0.0 collective-permute-done.6.theirs
  46.8 1.0 %shard_map.99 = bf16[1792,128]{1,0:T(8,128)(2,1)S(1)} custom-call(f32[8,128]{1,0:T(8,128)S(1)} %get-tuple-element.43.flags, f32[1792,128]{1,0:T(8,128)S(1)} %shard_map.98.base, bf16[2,2,1792,128]{3,2,1,0:T(8,128)(2,1)S(1)} %get-tuple-element.58.left_top, bf16[128,128]{1,0:T(8,128)(2,1)S(1)} %add_convert_fusion.own, ...), custom_call_target="tpu_custom_call" | custom-call | flops 234881024 | bytes 4194304 | tf_op jit(solution)/shard_map/pallas_call | solution.py:35
  47.9 18.3 %all_to_all.10 = bf16[32,56,128]{2,1,0:T(8,128)(2,1)S(1)} all-to-all(bf16[32,56,128]{2,1,0:T(8,128)(2,1)S(1)} %bitcast.21), channel_id=1, replica_groups=mesh['group'=4,'member'=8] {'group','member'}, dimensions={0} | all-to-all | bytes 917504 | tf_op jit(solution)/shard_map/all_to_all | solution.py:524
  66.2 1.4 %shard_map.100 = f32[1024,128]{1,0:T(8,128)} custom-call(bf16[1024,896]{1,0:T(8,128)(2,1)S(1)} %get-tuple-element.41.order, s32[1024,128]{1,0:T(8,128)S(1)} %get-tuple-element.42.upper, bf16[1792,128]{1,0:T(8,128)(2,1)S(1)} %bitcast.22), custom_call_target="tpu_custom_call" | custom-call | flops 469762048 | bytes 4194304 | tf_op jit(solution)/shard_map/pallas_call | solution.py:35
  (25 shorter events, 0.2 us)
Async XLA Ops:
  0.0 10.4 %copy-start = (s32[62]{0:T(128)S(1)}, s32[62]{0:T(128)}, u32[]{:S(2)}) copy-start(s32[62]{0:T(128)} %ranks.3) | copy-start | bytes 748
  3.0 23.8 %all-to-all-start = ((bf16[32,64,128]{2,1,0:T(8,128)(2,1)}), bf16[32,64,128]{2,1,0:T(8,128)(2,1)}, u32[]{:S(2)}, u32[]{:S(2)}) async-start(bf16[32,64,128]{2,1,0:T(8,128)(2,1)} %get-tuple-element.33), calls=%async_computation | async-start | bytes 1048576 | tf_op jit(solution)/shard_map/all_to_all | solution.py:389
  29.1 1.4 %collective-permute-start = (f32[264,128]{1,0:T(8,128)S(1)}, f32[264,128]{1,0:T(8,128)S(1)}, u32[]{:S(2)}, u32[]{:S(2)}) collective-permute-start(f32[264,128]{1,0:T(8,128)S(1)} %get-tuple-element.35.after), channel_id=1, source_target_pairs={{0,1},{1,0},{2,3},{3,2},{4,5},{5,4},{6,7},{7,6},{8,9},{9,8},{10,11... | collective-permute-start | bytes 405512 | tf_op jit(solution)/shard_map/ppermute | solution.py:54
  30.6 4.2 %collective-permute-start.1 = (f16[200,128]{1,0:T(8,128)(2,1)S(1)}, f16[200,128]{1,0:T(8,128)(2,1)S(1)}, u32[]{:S(2)}, u32[]{:S(2)}) collective-permute-start(f16[200,128]{1,0:T(8,128)(2,1)S(1)} %pad_maximum_fusion), channel_id=1, source_target_pairs={{0,2},{2,0},{1,3},{3,1},{4,6},{6,4},{5,7},{7,5},{8,10},{10,8},{9,1... | collective-permute-start | bytes 153608 | tf_op jit(solution)/shard_map/ppermute | solution.py:54
  34.9 5.0 %collective-permute-start.2 = (f16[168,128]{1,0:T(8,128)(2,1)S(1)}, f16[168,128]{1,0:T(8,128)(2,1)S(1)}, u32[]{:S(2)}, u32[]{:S(2)}) collective-permute-start(f16[168,128]{1,0:T(8,128)(2,1)S(1)} %pad_maximum_fusion.1), channel_id=1, source_target_pairs={{0,4},{4,0},{1,5},{5,1},{2,6},{6,2},{3,7},{7,3},{8,12},{12,8},{9,1... | collective-permute-start | bytes 129032 | tf_op jit(solution)/shard_map/ppermute | solution.py:54
  40.0 5.1 %collective-permute-start.4 = (f16[136,128]{1,0:T(8,128)(2,1)S(1)}, f16[136,128]{1,0:T(8,128)(2,1)S(1)}, u32[]{:S(2)}, u32[]{:S(2)}) collective-permute-start(f16[136,128]{1,0:T(8,128)(2,1)S(1)} %pad_maximum_fusion.2), channel_id=1, source_target_pairs={{0,24},{1,3},{2,26},{3,1},{4,28},{5,7},{6,30},{7,5},{8,16},{9,11},... | collective-permute-start | bytes 104456 | tf_op jit(solution)/shard_map/ppermute | solution.py:475
  41.0 4.3 %collective-permute-start.3 = (f16[136,128]{1,0:T(8,128)(2,1)S(1)}, f16[136,128]{1,0:T(8,128)(2,1)S(1)}, u32[]{:S(2)}, u32[]{:S(2)}) collective-permute-start(f16[136,128]{1,0:T(8,128)(2,1)S(1)} %pad_maximum_fusion.2), channel_id=1, source_target_pairs={{0,16},{1,9},{2,18},{3,11},{4,20},{5,13},{6,22},{7,15},{8,24},{9,1... | collective-permute-start | bytes 104456 | tf_op jit(solution)/shard_map/ppermute | solution.py:475
  42.6 2.7 %collective-permute-start.5 = (bf16[64,128]{1,0:T(8,128)(2,1)S(1)}, bf16[64,128]{1,0:T(8,128)(2,1)S(1)}, u32[]{:S(2)}, u32[]{:S(2)}) collective-permute-start(bf16[64,128]{1,0:T(8,128)(2,1)S(1)} %pad_maximum_fusion.3.rest_5_), channel_id=1, source_target_pairs={{0,1},{1,0},{2,3},{3,2},{4,5},{5,4},{6,7},{7,6},{8,9},{9,8},{10,11... | collective-permute-start | bytes 49160 | tf_op jit(solution)/shard_map/ppermute | solution.py:54
  45.3 1.5 %collective-permute-start.6 = (bf16[128,128]{1,0:T(8,128)(2,1)S(1)}, bf16[128,128]{1,0:T(8,128)(2,1)S(1)}, u32[]{:S(2)}, u32[]{:S(2)}) collective-permute-start(bf16[128,128]{1,0:T(8,128)(2,1)S(1)} %add_convert_fusion.own), channel_id=1, source_target_pairs={{0,1},{1,0},{2,3},{3,2},{4,5},{5,4},{6,7},{7,6},{8,9},{9,8},{10,11... | collective-permute-start | bytes 98312 | tf_op jit(solution)/shard_map/ppermute | solution.py:54

commit v11 on v9

--- a/solution.py
+++ b/solution.py
@@ -81,7 +81,7 @@
     return ranks[(1 << level) - 2 + jnp.right_shift(device, levels - level)]
 
 
-def pack_kernel(leaves, bucket, sizes_in, position_in, rows_in, packed, places, *scratch):
+def pack_kernel(leaves, groups, bucket, sizes_in, position_in, rows_in, packed, places, *scratch):
     sizes, position, rows, ordered, near, sems, out_sems = scratch
     copies = [
         pltpu.make_async_copy(source, target, sems.at[i])
@@ -115,18 +115,20 @@
     offset = jnp.bitwise_and(here, leaves - 1).astype(F32)
     picked = jnp.where(iota((leaves, count), 0) == owner, offset, 0.0).astype(BF16)
     offsets = dot(picked, hot(iota((128, count), 0) == window - first), (1, 1))
-    places[...] = owner * bucket + window - first
+    members = leaves // groups
+    places[...] = (owner % members * groups + owner // members) * bucket + window - first
     line = iota((padded, 128), 0)
     chunk = leaves // 8
     out = []
-    for c in range(leaves):
+    for at in range(leaves):
+        c = at % groups * members + at // groups
         data = ordered[pl.ds(starts[c], padded), :]
         data = jnp.where(line < starts[c + 1] - starts[c], data, 0.0)
         data = jnp.where(line == bucket, offsets[c : c + 1, :], data)
-        near[c] = data.astype(BF16)
-        if c % chunk == chunk - 1:
-            part = pl.ds(c + 1 - chunk, chunk)
-            out.append(pltpu.make_async_copy(near.at[part], packed.at[part], out_sems.at[c // chunk]))
+        near[at] = data.astype(BF16)
+        if at % chunk == chunk - 1:
+            part = pl.ds(at + 1 - chunk, chunk)
+            out.append(pltpu.make_async_copy(near.at[part], packed.at[part], out_sems.at[at // chunk]))
             out[-1].start()
     for copy in out:
         copy.wait()
@@ -365,7 +367,7 @@
     far_flops = 4 * capacity * columns * (group_levels * top_width + member_levels * width)
 
     packed, places = call(
-        functools.partial(pack_kernel, leaves, bucket),
+        functools.partial(pack_kernel, leaves, groups, bucket),
         [
             jax.ShapeDtypeStruct((leaves, padded, columns), BF16),
             jax.ShapeDtypeStruct((1, count), I32),
@@ -386,7 +388,7 @@
             DMA((8,)),
         ],
     )
-    arrived = lax.all_to_all(packed, everyone, split_axis=0, concat_axis=0, tiled=True)
+    arrived = lax.all_to_all(packed, ("member", "group"), split_axis=0, concat_axis=0, tiled=True)
     ranked = group_levels * top_width + member_levels * width
     right, flags = call(
         near_kernel,
@@ -522,7 +524,7 @@
         ],
     )[0]
     returned = lax.all_to_all(
-        leaving.reshape(leaves, bucket, columns), everyone, split_axis=0, concat_axis=0, tiled=True
+        leaving.reshape(leaves, bucket, columns), ("member", "group"), split_axis=0, concat_axis=0, tiled=True
     )
     return call(
         unpack_kernel,

time: 67.4 us -> 67.5 us (level)
  waiting for transfers between devices: 16.9 us -> 15.4 us
  blocking collectives: 17.2 us -> 18.2 us
    ppermute x5, waiting for transfers between devices: 3.27 us -> 1.31 us  [partner(): return lax.ppermute(block, axis, route)]
    ppermute x5, starting transfers between devices: 0.79 us -> 2.32 us  [partner(): return lax.ppermute(block, axis, route)]
    all_to_all x1, blocking collectives: 17.2 us -> 18.2 us  [on_device(): lax.all_to_all(leaving.reshape(leaves, bucket, columns), ('member', 'grou...]
    ppermute x2, starting transfers between devices: 2.6 us -> 1.7 us  [on_device(): heard = [lax.ppermute(sums, everyone, route) for route in routes]]
  transfers between devices with their start and end apart: 8 -> 8, of which waited for: 4 -> 5; matrix products, arithmetic and copies ran while one was open for 0% -> 0% of each run, Pallas kernels for 21% -> 21%
where the time goes in v11:
time: 67.5 us; the launch traced here: 67.2 us
  Pallas kernels  21.7 us (32%)
  blocking collectives  18.2 us (27%)
  waiting for transfers between devices  15.4 us (23%)
  starting transfers between devices  11.4 us (17%)
    pallas_call x10, Pallas kernels, call(): pl.pallas_call(kernel, out_shape=outs, in_specs=ins, out_specs=more.pop('...  21.7 us
    all_to_all x1, blocking collectives, on_device(): lax.all_to_all(leaving.reshape(leaves, bucket, columns), ('member', 'grou...  18.2 us
    all_to_all x1, waiting for transfers between devices, on_device(): lax.all_to_all(packed, ('member', 'group'), split_axis=0, concat_axis=0,...  13.5 us
    all_to_all x1, starting transfers between devices, on_device(): lax.all_to_all(packed, ('member', 'group'), split_axis=0, concat_axis=0,...  7.43 us
    ppermute x5, starting transfers between devices, partner(): return lax.ppermute(block, axis, route)  2.32 us
    ppermute x2, starting transfers between devices, on_device(): heard = [lax.ppermute(sums, everyone, route) for route in routes]  1.7 us
  transfers between devices with their start and end apart: 8, of which 5 were waited for; matrix products, arithmetic and copies ran while one was open for 0% of the time, Pallas kernels for 21%

profile of v11, /device:TPU:0, one launch (start us, length us, event | category | flops | bytes accessed | tf_op | source)
XLA Modules:
  0.0 67.2 jit_solution(11883305349887001480)
XLA Ops:
  0.0 0.0 copy-start
  0.0 3.0 %shard_map.91 = (bf16[32,64,128]{2,1,0:T(8,128)(2,1)}, s32[1,1024]{1,0:T(1,128)S(1)}) custom-call(s32[32]{0:T(128)} %sizes_in.1, s32[1,1024]{1,0:T(1,128)} %bitcast.25, bf16[1024,128]{1,0:T(8,128)(2,1)} %rows_in.1), custom_call_target="tpu_custom_call" | custom-call | flops 268435456 | bytes 4194304 | tf_op jit(solution)/shard_map/pallas_call | solution.py:35
  3.0 7.4 %all-to-all-start = ((bf16[32,64,128]{2,1,0:T(8,128)(2,1)}), bf16[32,64,128]{2,1,0:T(8,128)(2,1)}, u32[]{:S(2)}, u32[]{:S(2)}) async-start(bf16[32,64,128]{2,1,0:T(8,128)(2,1)} %get-tuple-element.33), calls=%async_computation | async-start | bytes 1048576 | tf_op jit(solution)/shard_map/all_to_all | solution.py:391
  10.4 0.0 copy-done
  10.4 2.7 %shard_map.92 = (bf16[6272,256]{1,0:T(8,128)(2,1)S(1)}, f32[8,128]{1,0:T(8,128)S(1)}) custom-call(s32[62]{0:T(128)S(1)} %copy-done, bf16[2,2,1792,128]{3,2,1,0:T(8,128)(2,1)} %right_top_in.1, bf16[3,2,64,1792]{3,2,1,0:T(8,128)(2,1)} %bitcast.23), custom_call_target="tpu_custom_call" | custom-call | bytes 6291456 | tf_op jit(solution)/shard_map/pallas_call | solution.py:35
  13.1 13.5 %all-to-all-done.arrived = bf16[32,64,128]{2,1,0:T(8,128)(2,1)} async-done(((bf16[32,64,128]{2,1,0:T(8,128)(2,1)}), bf16[32,64,128]{2,1,0:T(8,128)(2,1)}, u32[]{:S(2)}, u32[]{:S(2)}) %all-to-all-start) | async-done | bytes 524320 | tf_op jit(solution)/shard_map/all_to_all | solution.py:391
  26.7 2.4 %shard_map.93 = (bf16[2,1792,128]{2,1,0:T(8,128)(2,1)S(1)}, s32[7,256]{1,0:T(8,128)S(1)}, f32[264,128]{1,0:T(8,128)S(1)}, f32[200,128]{1,0:T(8,128)S(1)}) custom-call(bf16[32,64,128]{2,1,0:T(8,128)(2,1)} %all-to-all-done.arrived, bf16[6272,256]{1,0:T(8,128)(2,1)S(1)} %get-tuple-element.34.right), custom_call_target="tpu_custom_call" | custom-call | flops 411041792 | bytes 6291456 | tf_op jit(solution)/shard_map/pallas_call | solution.py:35
  29.0 0.1 collective-permute-start
  29.1 0.7 %shard_map.94 = (bf16[1792,256]{1,0:T(8,128)(2,1)S(1)}, bf16[1024,896]{1,0:T(8,128)(2,1)S(1)}, s32[1024,128]{1,0:T(8,128)S(1)}) custom-call(s32[7,256]{1,0:T(8,128)S(1)} %get-tuple-element.36.targets, s32[1,1024]{1,0:T(1,128)S(1)} %get-tuple-element.37.places, f32[264,128]{1,0:T(8,128)S(1)} %get-tuple-element.35.after), custom_call_target="tpu_custom_call" | custom-call | bytes 8388608 | tf_op jit(solution)/shard_map/pallas_call | solution.py:35
  29.9 0.6 collective-permute-done
  30.5 1.0 %collective-permute-start.1 = (f16[200,128]{1,0:T(8,128)(2,1)S(1)}, f16[200,128]{1,0:T(8,128)(2,1)S(1)}, u32[]{:S(2)}, u32[]{:S(2)}) collective-permute-start(f16[200,128]{1,0:T(8,128)(2,1)S(1)} %pad_maximum_fusion), channel_id=1, source_target_pairs={{0,2},{2,0},{1,3},{3,1},{4,6},{6,4},{5,7},{7,5},{8,10},{10,8},{9,1... | collective-permute-start | bytes 153608 | tf_op jit(solution)/shard_map/ppermute | solution.py:54
  31.6 3.2 %shard_map.95.rest_0_ = f32[672,128]{1,0:T(8,128)S(1)} custom-call(bf16[2,1792,1792]{2,1,0:T(8,128)(2,1)} %block_in.5, bf16[2,1792,128]{2,1,0:T(8,128)(2,1)S(1)} %get-tuple-element.46.pair, f32[192,128]{1,0:T(8,128)S(1)} %get-tuple-element.70.after), custom_call_target="tpu_custom_call" | custom-call | flops 616562688 | bytes 4816896 | tf_op jit(solution)/shard_map/pallas_call | solution.py:35
  34.7 0.0 collective-permute-done.1
  34.9 1.1 %collective-permute-start.2 = (f16[168,128]{1,0:T(8,128)(2,1)S(1)}, f16[168,128]{1,0:T(8,128)(2,1)S(1)}, u32[]{:S(2)}, u32[]{:S(2)}) collective-permute-start(f16[168,128]{1,0:T(8,128)(2,1)S(1)} %pad_maximum_fusion.1), channel_id=1, source_target_pairs={{0,4},{4,0},{1,5},{5,1},{2,6},{6,2},{3,7},{7,3},{8,12},{12,8},{9,1... | collective-permute-start | bytes 129032 | tf_op jit(solution)/shard_map/ppermute | solution.py:54
  36.0 3.2 %shard_map.96.rest_1_ = f32[672,128]{1,0:T(8,128)S(1)} custom-call(bf16[2,1792,1792]{2,1,0:T(8,128)(2,1)} %block_in.5, bf16[2,1792,128]{2,1,0:T(8,128)(2,1)S(1)} %get-tuple-element.46.pair, f32[160,128]{1,0:T(8,128)S(1)} %get-tuple-element.66.after), custom_call_target="tpu_custom_call" | custom-call | flops 616562688 | bytes 4816896 | tf_op jit(solution)/shard_map/pallas_call | solution.py:35
  39.2 0.7 %collective-permute-done.2 = f16[168,128]{1,0:T(8,128)(2,1)S(1)} collective-permute-done((f16[168,128]{1,0:T(8,128)(2,1)S(1)}, f16[168,128]{1,0:T(8,128)(2,1)S(1)}, u32[]{:S(2)}, u32[]{:S(2)}) %collective-permute-start.2) | collective-permute-done | bytes 43040 | tf_op jit(solution)/shard_map/ppermute | solution.py:54
  40.0 1.2 %collective-permute-start.4 = (f16[136,128]{1,0:T(8,128)(2,1)S(1)}, f16[136,128]{1,0:T(8,128)(2,1)S(1)}, u32[]{:S(2)}, u32[]{:S(2)}) collective-permute-start(f16[136,128]{1,0:T(8,128)(2,1)S(1)} %pad_maximum_fusion.2), channel_id=1, source_target_pairs={{0,24},{1,3},{2,26},{3,1},{4,28},{5,7},{6,30},{7,5},{8,16},{9,11},... | collective-permute-start | bytes 104456 | tf_op jit(solution)/shard_map/ppermute | solution.py:477
  41.1 0.5 collective-permute-start.3
  41.7 0.0 collective-permute-start.5
  41.7 3.0 %shard_map.97 = (bf16[2,2,1792,128]{3,2,1,0:T(8,128)(2,1)S(1)}, bf16[1792,384]{1,0:T(8,128)(2,1)S(1)}, f32[448,128]{1,0:T(8,128)S(1)}) custom-call(bf16[2,2,1792,128]{3,2,1,0:T(8,128)(2,1)} %left_top_in.1, bf16[3,2,64,1792]{3,2,1,0:T(8,128)(2,1)} %bitcast.24, bf16[2,1792,1792]{2,1,0:T(8,128)(2,1)} %block_in.5, ...), custom_call_target="tpu_custom_call" | custom-call | flops 411041792 | bytes 12582912 | tf_op jit(solution)/shard_map/pallas_call | solution.py:35
  44.7 0.2 collective-permute-done.4
  44.9 0.4 collective-permute-done.3
  45.3 0.0 collective-permute-done.5.rest_6_
  45.3 0.1 collective-permute-start.6
  45.4 1.1 %shard_map.98.base = f32[1792,128]{1,0:T(8,128)S(1)} custom-call(s32[62]{0:T(128)S(1)} %copy-done, f32[672,128]{1,0:T(8,128)S(1)} %shard_map.95.rest_0_, f32[672,128]{1,0:T(8,128)S(1)} %shard_map.96.rest_1_, f32[448,128]{1,0:T(8,128)S(1)} %get-tuple-element.51.rest_2_, bf16[1792,384]{1,0:T(8,128)(2,1)S(1)} %get-tuple-element.54.rest_3_, ...), custom_call_target="tpu_custom_call" | custom-call | flops 176160768 | bytes 3145728 | tf_op jit(solution)/shard_map/pallas_call | solution.py:35
  46.5 0.0 collective-permute-done.6.theirs
  46.6 1.0 %shard_map.99 = bf16[1792,128]{1,0:T(8,128)(2,1)S(1)} custom-call(f32[8,128]{1,0:T(8,128)S(1)} %get-tuple-element.43.flags, f32[1792,128]{1,0:T(8,128)S(1)} %shard_map.98.base, bf16[2,2,1792,128]{3,2,1,0:T(8,128)(2,1)S(1)} %get-tuple-element.58.left_top, bf16[128,128]{1,0:T(8,128)(2,1)S(1)} %add_convert_fusion.own, ...), custom_call_target="tpu_custom_call" | custom-call | flops 234881024 | bytes 4194304 | tf_op jit(solution)/shard_map/pallas_call | solution.py:35
  47.6 18.2 %all_to_all.10 = bf16[32,56,128]{2,1,0:T(8,128)(2,1)S(1)} all-to-all(bf16[32,56,128]{2,1,0:T(8,128)(2,1)S(1)} %bitcast.21), channel_id=1, replica_groups=mesh['group'=4,'member'=8] {'member','group'}, dimensions={0} | all-to-all | bytes 917504 | tf_op jit(solution)/shard_map/all_to_all | solution.py:526
  65.8 1.4 %shard_map.100 = f32[1024,128]{1,0:T(8,128)} custom-call(bf16[1024,896]{1,0:T(8,128)(2,1)S(1)} %get-tuple-element.41.order, s32[1024,128]{1,0:T(8,128)S(1)} %get-tuple-element.42.upper, bf16[1792,128]{1,0:T(8,128)(2,1)S(1)} %bitcast.22), custom_call_target="tpu_custom_call" | custom-call | flops 469762048 | bytes 4194304 | tf_op jit(solution)/shard_map/pallas_call | solution.py:35
  (25 shorter events, 0.2 us)
Async XLA Ops:
  0.0 10.4 %copy-start = (s32[62]{0:T(128)S(1)}, s32[62]{0:T(128)}, u32[]{:S(2)}) copy-start(s32[62]{0:T(128)} %ranks.3) | copy-start | bytes 748
  3.0 23.7 %all-to-all-start = ((bf16[32,64,128]{2,1,0:T(8,128)(2,1)}), bf16[32,64,128]{2,1,0:T(8,128)(2,1)}, u32[]{:S(2)}, u32[]{:S(2)}) async-start(bf16[32,64,128]{2,1,0:T(8,128)(2,1)} %get-tuple-element.33), calls=%async_computation | async-start | bytes 1048576 | tf_op jit(solution)/shard_map/all_to_all | solution.py:391
  29.0 1.4 %collective-permute-start = (f32[264,128]{1,0:T(8,128)S(1)}, f32[264,128]{1,0:T(8,128)S(1)}, u32[]{:S(2)}, u32[]{:S(2)}) collective-permute-start(f32[264,128]{1,0:T(8,128)S(1)} %get-tuple-element.35.after), channel_id=1, source_target_pairs={{0,1},{1,0},{2,3},{3,2},{4,5},{5,4},{6,7},{7,6},{8,9},{9,8},{10,11... | collective-permute-start | bytes 405512 | tf_op jit(solution)/shard_map/ppermute | solution.py:54
  30.5 4.2 %collective-permute-start.1 = (f16[200,128]{1,0:T(8,128)(2,1)S(1)}, f16[200,128]{1,0:T(8,128)(2,1)S(1)}, u32[]{:S(2)}, u32[]{:S(2)}) collective-permute-start(f16[200,128]{1,0:T(8,128)(2,1)S(1)} %pad_maximum_fusion), channel_id=1, source_target_pairs={{0,2},{2,0},{1,3},{3,1},{4,6},{6,4},{5,7},{7,5},{8,10},{10,8},{9,1... | collective-permute-start | bytes 153608 | tf_op jit(solution)/shard_map/ppermute | solution.py:54
  34.9 5.0 %collective-permute-start.2 = (f16[168,128]{1,0:T(8,128)(2,1)S(1)}, f16[168,128]{1,0:T(8,128)(2,1)S(1)}, u32[]{:S(2)}, u32[]{:S(2)}) collective-permute-start(f16[168,128]{1,0:T(8,128)(2,1)S(1)} %pad_maximum_fusion.1), channel_id=1, source_target_pairs={{0,4},{4,0},{1,5},{5,1},{2,6},{6,2},{3,7},{7,3},{8,12},{12,8},{9,1... | collective-permute-start | bytes 129032 | tf_op jit(solution)/shard_map/ppermute | solution.py:54
  40.0 4.9 %collective-permute-start.4 = (f16[136,128]{1,0:T(8,128)(2,1)S(1)}, f16[136,128]{1,0:T(8,128)(2,1)S(1)}, u32[]{:S(2)}, u32[]{:S(2)}) collective-permute-start(f16[136,128]{1,0:T(8,128)(2,1)S(1)} %pad_maximum_fusion.2), channel_id=1, source_target_pairs={{0,24},{1,3},{2,26},{3,1},{4,28},{5,7},{6,30},{7,5},{8,16},{9,11},... | collective-permute-start | bytes 104456 | tf_op jit(solution)/shard_map/ppermute | solution.py:477
  41.1 4.1 %collective-permute-start.3 = (f16[136,128]{1,0:T(8,128)(2,1)S(1)}, f16[136,128]{1,0:T(8,128)(2,1)S(1)}, u32[]{:S(2)}, u32[]{:S(2)}) collective-permute-start(f16[136,128]{1,0:T(8,128)(2,1)S(1)} %pad_maximum_fusion.2), channel_id=1, source_target_pairs={{0,16},{1,9},{2,18},{3,11},{4,20},{5,13},{6,22},{7,15},{8,24},{9,1... | collective-permute-start | bytes 104456 | tf_op jit(solution)/shard_map/ppermute | solution.py:477
  41.7 3.6 %collective-permute-start.5 = (bf16[64,128]{1,0:T(8,128)(2,1)S(1)}, bf16[64,128]{1,0:T(8,128)(2,1)S(1)}, u32[]{:S(2)}, u32[]{:S(2)}) collective-permute-start(bf16[64,128]{1,0:T(8,128)(2,1)S(1)} %pad_maximum_fusion.3.rest_5_), channel_id=1, source_target_pairs={{0,1},{1,0},{2,3},{3,2},{4,5},{5,4},{6,7},{7,6},{8,9},{9,8},{10,11... | collective-permute-start | bytes 49160 | tf_op jit(solution)/shard_map/ppermute | solution.py:54
  45.3 1.3 %collective-permute-start.6 = (bf16[128,128]{1,0:T(8,128)(2,1)S(1)}, bf16[128,128]{1,0:T(8,128)(2,1)S(1)}, u32[]{:S(2)}, u32[]{:S(2)}) collective-permute-start(bf16[128,128]{1,0:T(8,128)(2,1)S(1)} %add_convert_fusion.own), channel_id=1, source_target_pairs={{0,1},{1,0},{2,3},{3,2},{4,5},{5,4},{6,7},{7,6},{8,9},{9,8},{10,11... | collective-permute-start | bytes 98312 | tf_op jit(solution)/shard_map/ppermute | solution.py:54

commit v12 on v9

--- a/solution.py
+++ b/solution.py
@@ -99,7 +99,7 @@
     window = jnp.right_shift(here, shift)
     copies[1].wait()
     values = rows[...]
-    block = 512
+    block = 256
     for low in range(0, count, block):
         ordered[low : low + block, :] = dot(hot(iota((block, count), 0) + low == window), values)
     ordered[count:, :] = jnp.zeros((padded, 128), F32)
@@ -155,12 +155,15 @@
     for level in range(1, tops + 1):
         counts = (lane < rank_of(ranks, level, tops + levels)).astype(I32)
         marks = jnp.where(row == level, counts, marks)
-    flags[...] = marks.astype(F32)
+    last = rank_of(ranks, tops + levels, tops + levels)
+    flags[...] = jnp.where(row < 8, marks, (row - 8 < last).astype(I32)).astype(F32)
     for copy in copies:
         copy.wait()
 
 
-def way_kernel(targets, places, after, slots, order, upper):
+def way_kernel(targets, places, left_low_in, after, slots, order, upper, left_last, raw, sem):
+    copy = pltpu.make_async_copy(left_low_in.at[left_low_in.shape[0] - 1], raw, sem)
+    copy.start()
     groups, part = targets.shape
     lanes = iota((part, 128), 1)
     for g in range(groups):
@@ -177,11 +180,18 @@
     for low in range(0, count, block):
         for at in range(0, folded, 128):
             order[low : low + block, at : at + 128] = hot(place[low : low + block] == lanes + at)
-
-
-def stage_kernel(first, left_top_in, left_low_in, block_in, pair, after, *rest):
+    copy.wait()
+    left_last[...] = jnp.transpose(raw[...].reshape(-1, raw.shape[2]))
+
+
+def last_level(flags, nearest):
+    coef = jnp.where(flags[8:, :] > 0, nearest[...], 0.0)
+    return jnp.concatenate([coef, turn(coef)], axis=0).astype(BF16)
+
+
+def stage_kernel(first, left_top_in, left_low_in, block_in, pair, flags, nearest, left_last, after, *rest):
     left_top, left_low, out, raw, block, sems = rest
-    copies = [pltpu.make_async_copy(left_low_in, raw, sems.at[0])]
+    copies = [pltpu.make_async_copy(left_low_in.at[pl.ds(0, raw.shape[0])], raw, sems.at[0])]
     count, _, height, _ = block.shape
     for j in range(count):
         rows = pl.ds((first + j) * height, height)
@@ -192,9 +202,12 @@
     copies[0].wait()
     levels, parts, width, capacity = raw.shape
     left_low[...] = jnp.transpose(raw[...].reshape(levels * parts * width, capacity))
+    stacked = last_level(flags, nearest)
     for j in range(count):
         copies[1 + j].wait()
-        out[j * height : (j + 1) * height, :] = dot(block[j, 0], pair[0]) + dot(block[j, 1], pair[1])
+        far_part = dot(left_last[(first + j) * height : (first + j + 1) * height, :], stacked)
+        near_part = dot(block[j, 0], pair[0]) + dot(block[j, 1], pair[1])
+        out[j * height : (j + 1) * height, :] = near_part + far_part
     copies[-1].wait()
 
 
@@ -253,16 +266,19 @@
     keep[at:, :] = jnp.broadcast_to(power, (8, 128))
 
 
-def diag_kernel(first, block_in, pair, after, out, block, sems):
+def diag_kernel(first, block_in, pair, flags, nearest, left_last, after, out, block, sems):
     count, _, height, _ = block.shape
     copies = []
     for j in range(count):
         rows = pl.ds((first + j) * height, height)
         copies.append(pltpu.make_async_copy(block_in.at[:, rows, :], block.at[j], sems.at[j]))
         copies[j].start()
+    stacked = last_level(flags, nearest)
     for j in range(count):
+        far_part = dot(left_last[(first + j) * height : (first + j + 1) * height, :], stacked)
         copies[j].wait()
-        out[j * height : (j + 1) * height, :] = dot(block[j, 0], pair[0]) + dot(block[j, 1], pair[1])
+        near_part = dot(block[j, 0], pair[0]) + dot(block[j, 1], pair[1])
+        out[j * height : (j + 1) * height, :] = near_part + far_part
 
 
 def merged(core, own, theirs, at, half):
@@ -272,18 +288,14 @@
 
 def low_kernel(pieces, tops, ranks, *rest):
     bases = rest[:pieces]
-    left_low, nearest, own, theirs, out = rest[pieces:]
-    width = nearest.shape[0]
-    levels = left_low.shape[1] // (2 * width)
+    left_low, own, theirs, out = rest[pieces:]
     core = jnp.bitwise_and(lax.axis_index("member"), 1)
-    half = width // 2
+    half = own.shape[0] // (left_low.shape[1] // 128)
+    levels = own.shape[0] // half
     stacked = []
     for level in range(levels):
-        if level < levels - 1:
-            coef = merged(core, own, theirs, level * half, half)
-        else:
-            coef = nearest[...]
-        rank = rank_of(ranks, 1 + tops + level, tops + levels)
+        coef = merged(core, own, theirs, level * half, half)
+        rank = rank_of(ranks, 1 + tops + level, tops + levels + 1)
         coef = jnp.where(iota(coef.shape, 0) < rank, coef, 0.0)
         stacked += [coef, turn(coef)]
     stacked = jnp.concatenate(stacked, axis=0).astype(BF16)
@@ -392,7 +404,7 @@
         near_kernel,
         [
             pltpu.VMEM((2 * ranked * capacity // 256, 256), BF16),
-            jax.ShapeDtypeStruct((8, columns), F32),
+            jax.ShapeDtypeStruct((8 + width, columns), F32),
         ],
         [SMEM, HBM, HBM],
         (block_ranks, *far(top_right, low_right)),
@@ -424,8 +436,8 @@
         return call(
             functools.partial(diag_kernel, first),
             [jax.ShapeDtypeStruct((chunks * height, columns), F32)],
-            [HBM, VMEM, pl.BlockSpec(memory_space=pl.ANY)],
-            (*far(diag_block), pair, after),
+            [HBM] + [VMEM] * 4 + [pl.BlockSpec(memory_space=pl.ANY)],
+            (*far(diag_block), pair, flags, nearest, left_last, after),
             4 * chunks * height * capacity * columns,
             4 * chunks * height * capacity,
             24,
@@ -433,20 +445,24 @@
         )[0]
 
     received = partner(send, "member", 0)
-    slots, order, upper = call(
+    slots, order, upper, left_last = call(
         way_kernel,
         [
             jax.ShapeDtypeStruct((leaves * filled, leaves * 8), BF16),
             jax.ShapeDtypeStruct((count, capacity // 2), BF16),
             jax.ShapeDtypeStruct((count, 128), I32),
-        ],
-        [VMEM, VMEM, pl.BlockSpec(memory_space=pl.ANY)],
-        (targets, places, send),
+            jax.ShapeDtypeStruct((capacity, 2 * width), BF16),
+        ],
+        [VMEM, VMEM, HBM, pl.BlockSpec(memory_space=pl.ANY)],
+        (targets, places, *far(low_left), send),
         0,
         8 << 20,
         16,
-    )
-    received, slots, order, upper = lax.optimization_barrier((received, slots, order, upper))
+        scratch=[pltpu.VMEM(low_left.shape[1:], BF16), DMA],
+    )
+    received, slots, order, upper, left_last = lax.optimization_barrier(
+        (received, slots, order, upper, left_last)
+    )
     nearest = received[shared : shared + width]
     running = keep[:shared] + received[:shared]
     power = bound(keep[shared:], received[shared + width :])
@@ -477,16 +493,16 @@
         functools.partial(stage_kernel, 6),
         [
             pltpu.VMEM(top_left.shape, BF16),
-            pltpu.VMEM((capacity, member_levels * 2 * width), BF16),
+            pltpu.VMEM((capacity, (member_levels - 1) * 2 * width), BF16),
             jax.ShapeDtypeStruct((2 * height, columns), F32),
         ],
-        [HBM, HBM, HBM, VMEM, pl.BlockSpec(memory_space=pl.ANY)],
-        (*far(top_left, low_left, diag_block), pair, running),
+        [HBM] * 3 + [VMEM] * 4 + [pl.BlockSpec(memory_space=pl.ANY)],
+        (*far(top_left, low_left, diag_block), pair, flags, nearest, left_last, running),
         8 * height * capacity * columns,
         12 << 20,
         24,
         scratch=[
-            pltpu.VMEM(low_left.shape, BF16),
+            pltpu.VMEM((member_levels - 1,) + low_left.shape[1:], BF16),
             pltpu.VMEM((2, 2, height, capacity), BF16),
             DMA((4,)),
         ],
@@ -501,8 +517,8 @@
     base = call(
         functools.partial(low_kernel, len(bases), group_levels),
         [jax.ShapeDtypeStruct((capacity, columns), F32)],
-        [SMEM] + [VMEM] * (len(bases) + 4),
-        (block_ranks, *bases, left_low, nearest, own_low, their_low),
+        [SMEM] + [VMEM] * (len(bases) + 3),
+        (block_ranks, *bases, left_low, own_low, their_low),
         4 * capacity * columns * member_levels * width,
         3 << 20,
         16,

time: 67.4 us -> 67.9 us (level)
  starting transfers between devices: 10.8 us -> 9.86 us
  Pallas kernels: 21.7 us -> 22.4 us
  blocking collectives: 17.2 us -> 17.9 us
    ppermute x2, starting transfers between devices: 2.6 us -> 1.61 us  [on_device(): heard = [lax.ppermute(sums, everyone, route) for route in routes]]
    pallas_call x10, Pallas kernels: 21.7 us -> 22.4 us  [call(): pl.pallas_call(kernel, out_shape=outs, in_specs=ins, out_specs=more.pop('...]
  transfers between devices with their start and end apart: 8 -> 8, of which waited for: 4 -> 4; matrix products, arithmetic and copies ran while one was open for 0% -> 0% of each run, Pallas kernels for 21% -> 22%
where the time goes in v12:
time: 67.9 us; the launch traced here: 67.6 us
  Pallas kernels  22.4 us (33%)
  blocking collectives  17.9 us (26%)
  waiting for transfers between devices  16.9 us (25%)
  starting transfers between devices  9.86 us (15%)
    pallas_call x10, Pallas kernels, call(): pl.pallas_call(kernel, out_shape=outs, in_specs=ins, out_specs=more.pop('...  22.4 us
    all_to_all x1, blocking collectives, on_device(): lax.all_to_all(leaving.reshape(leaves, bucket, columns), everyone, split_...  17.9 us
    all_to_all x1, waiting for transfers between devices, on_device(): lax.all_to_all(packed, everyone, split_axis=0, concat_axis=0, tiled=True)  13.6 us
    all_to_all x1, starting transfers between devices, on_device(): lax.all_to_all(packed, everyone, split_axis=0, concat_axis=0, tiled=True)  7.43 us
    ppermute x5, waiting for transfers between devices, partner(): return lax.ppermute(block, axis, route)  2.99 us
    ppermute x2, starting transfers between devices, on_device(): heard = [lax.ppermute(sums, everyone, route) for route in routes]  1.61 us
  transfers between devices with their start and end apart: 8, of which 4 were waited for; matrix products, arithmetic and copies ran while one was open for 0% of the time, Pallas kernels for 22%

profile of v12, /device:TPU:0, one launch (start us, length us, event | category | flops | bytes accessed | tf_op | source)
XLA Modules:
  0.0 67.6 jit_solution(2781919828166537989)
XLA Ops:
  0.0 0.0 copy-start
  0.0 2.9 %shard_map.91 = (bf16[32,64,128]{2,1,0:T(8,128)(2,1)}, s32[1,1024]{1,0:T(1,128)S(1)}) custom-call(s32[32]{0:T(128)} %sizes_in.1, s32[1,1024]{1,0:T(1,128)} %bitcast.26, bf16[1024,128]{1,0:T(8,128)(2,1)} %rows_in.1), custom_call_target="tpu_custom_call" | custom-call | flops 268435456 | bytes 4194304 | tf_op jit(solution)/shard_map/pallas_call | solution.py:35
  2.9 7.4 %all-to-all-start = ((bf16[32,64,128]{2,1,0:T(8,128)(2,1)}), bf16[32,64,128]{2,1,0:T(8,128)(2,1)}, u32[]{:S(2)}, u32[]{:S(2)}) async-start(bf16[32,64,128]{2,1,0:T(8,128)(2,1)} %get-tuple-element.35), calls=%async_computation | async-start | bytes 1048576 | tf_op jit(solution)/shard_map/all_to_all | solution.py:401
  10.4 0.0 copy-done
  10.4 2.7 %shard_map.92 = (bf16[6272,256]{1,0:T(8,128)(2,1)S(1)}, f32[72,128]{1,0:T(8,128)S(1)}) custom-call(s32[62]{0:T(128)S(1)} %copy-done, bf16[2,2,1792,128]{3,2,1,0:T(8,128)(2,1)} %right_top_in.1, bf16[3,2,64,1792]{3,2,1,0:T(8,128)(2,1)} %bitcast.25), custom_call_target="tpu_custom_call" | custom-call | bytes 6291456 | tf_op jit(solution)/shard_map/pallas_call | solution.py:35
  13.1 13.6 %all-to-all-done.arrived = bf16[32,64,128]{2,1,0:T(8,128)(2,1)} async-done(((bf16[32,64,128]{2,1,0:T(8,128)(2,1)}), bf16[32,64,128]{2,1,0:T(8,128)(2,1)}, u32[]{:S(2)}, u32[]{:S(2)}) %all-to-all-start) | async-done | bytes 524320 | tf_op jit(solution)/shard_map/all_to_all | solution.py:401
  26.7 2.4 %shard_map.93 = (bf16[2,1792,128]{2,1,0:T(8,128)(2,1)S(1)}, s32[7,256]{1,0:T(8,128)S(1)}, f32[264,128]{1,0:T(8,128)S(1)}, f32[200,128]{1,0:T(8,128)S(1)}) custom-call(bf16[32,64,128]{2,1,0:T(8,128)(2,1)} %all-to-all-done.arrived, bf16[6272,256]{1,0:T(8,128)(2,1)S(1)} %get-tuple-element.36.right), custom_call_target="tpu_custom_call" | custom-call | flops 411041792 | bytes 6291456 | tf_op jit(solution)/shard_map/pallas_call | solution.py:35
  29.1 0.1 collective-permute-start
  29.2 1.5 %shard_map.94 = (bf16[1792,256]{1,0:T(8,128)(2,1)S(1)}, bf16[1024,896]{1,0:T(8,128)(2,1)S(1)}, s32[1024,128]{1,0:T(8,128)S(1)}, bf16[1792,128]{1,0:T(8,128)(2,1)S(1)}) custom-call(s32[7,256]{1,0:T(8,128)S(1)} %get-tuple-element.38.targets, s32[1,1024]{1,0:T(1,128)S(1)} %get-tuple-element.39.places, bf16[3,2,64,1792]{3,2,1,0:T(8,128)(2,1)} %bitcast.23, ...), custom_call_target="tpu_custom_call" | custom-call | bytes 8388608 | tf_op jit(solution)/shard_map/pallas_call | solution.py:35
  30.7 0.0 collective-permute-done
  30.8 0.1 collective-permute-start.1
  30.9 3.2 %shard_map.95.rest_0_ = f32[672,128]{1,0:T(8,128)S(1)} custom-call(bf16[2,1792,1792]{2,1,0:T(8,128)(2,1)} %block_in.5, bf16[2,1792,128]{2,1,0:T(8,128)(2,1)S(1)} %get-tuple-element.49.pair, f32[72,128]{1,0:T(8,128)S(1)} %get-tuple-element.46.flags, f32[64,128]{1,0:T(8,128)S(1)} %slice.92.nearest, bf16[1792,128]{1,0:T(8,128)(2,1)S(1)} %get-tuple-element.50.left_last, ...), custom_call_target="tpu_custom_call" | custom-call | flops 616562688 | bytes 4816896 | tf_op jit(solution)/shard_map/pallas_call | solution.py:35
  34.1 0.9 %collective-permute-done.1 = f16[200,128]{1,0:T(8,128)(2,1)S(1)} collective-permute-done((f16[200,128]{1,0:T(8,128)(2,1)S(1)}, f16[200,128]{1,0:T(8,128)(2,1)S(1)}, u32[]{:S(2)}, u32[]{:S(2)}) %collective-permute-start.1) | collective-permute-done | bytes 51232 | tf_op jit(solution)/shard_map/ppermute | solution.py:54
  35.1 0.4 collective-permute-start.2
  35.6 3.2 %shard_map.96.rest_1_ = f32[672,128]{1,0:T(8,128)S(1)} custom-call(bf16[2,1792,1792]{2,1,0:T(8,128)(2,1)} %block_in.5, bf16[2,1792,128]{2,1,0:T(8,128)(2,1)S(1)} %get-tuple-element.49.pair, f32[72,128]{1,0:T(8,128)S(1)} %get-tuple-element.46.flags, f32[64,128]{1,0:T(8,128)S(1)} %slice.92.nearest, bf16[1792,128]{1,0:T(8,128)(2,1)S(1)} %get-tuple-element.50.left_last, ...), custom_call_target="tpu_custom_call" | custom-call | flops 616562688 | bytes 4816896 | tf_op jit(solution)/shard_map/pallas_call | solution.py:35
  38.8 2.1 %collective-permute-done.2 = f16[168,128]{1,0:T(8,128)(2,1)S(1)} collective-permute-done((f16[168,128]{1,0:T(8,128)(2,1)S(1)}, f16[168,128]{1,0:T(8,128)(2,1)S(1)}, u32[]{:S(2)}, u32[]{:S(2)}) %collective-permute-start.2) | collective-permute-done | bytes 43040 | tf_op jit(solution)/shard_map/ppermute | solution.py:54
  40.9 0.2 collective-permute-start.4
  41.1 1.5 %collective-permute-start.3 = (f16[136,128]{1,0:T(8,128)(2,1)S(1)}, f16[136,128]{1,0:T(8,128)(2,1)S(1)}, u32[]{:S(2)}, u32[]{:S(2)}) collective-permute-start(f16[136,128]{1,0:T(8,128)(2,1)S(1)} %pad_maximum_fusion.2), channel_id=1, source_target_pairs={{0,16},{1,9},{2,18},{3,11},{4,20},{5,13},{6,22},{7,15},{8,24},{9,1... | collective-permute-start | bytes 104456 | tf_op jit(solution)/shard_map/ppermute | solution.py:491
  42.6 0.0 collective-permute-start.5
  42.6 3.0 %shard_map.97 = (bf16[2,2,1792,128]{3,2,1,0:T(8,128)(2,1)S(1)}, bf16[1792,256]{1,0:T(8,128)(2,1)S(1)}, f32[448,128]{1,0:T(8,128)S(1)}) custom-call(bf16[2,2,1792,128]{3,2,1,0:T(8,128)(2,1)} %left_top_in.1, bf16[3,2,64,1792]{3,2,1,0:T(8,128)(2,1)} %bitcast.24, bf16[2,1792,1792]{2,1,0:T(8,128)(2,1)} %block_in.5, ...), custom_call_target="tpu_custom_call" | custom-call | flops 411041792 | bytes 12582912 | tf_op jit(solution)/shard_map/pallas_call | solution.py:35
  45.5 0.3 collective-permute-done.4
  45.8 0.0 collective-permute-done.3
  45.9 0.0 collective-permute-done.5.rest_5_
  45.9 0.3 collective-permute-start.6
  46.2 1.0 %shard_map.98.base = f32[1792,128]{1,0:T(8,128)S(1)} custom-call(s32[62]{0:T(128)S(1)} %copy-done, f32[672,128]{1,0:T(8,128)S(1)} %shard_map.95.rest_0_, f32[672,128]{1,0:T(8,128)S(1)} %shard_map.96.rest_1_, f32[448,128]{1,0:T(8,128)S(1)} %get-tuple-element.55.rest_2_, bf16[1792,256]{1,0:T(8,128)(2,1)S(1)} %get-tuple-element.58.rest_3_, ...), custom_call_target="tpu_custom_call" | custom-call | flops 176160768 | bytes 3145728 | tf_op jit(solution)/shard_map/pallas_call | solution.py:35
  47.2 0.0 collective-permute-done.6.theirs
  47.2 1.0 %shard_map.99 = bf16[1792,128]{1,0:T(8,128)(2,1)S(1)} custom-call(f32[72,128]{1,0:T(8,128)S(1)} %get-tuple-element.46.flags, f32[1792,128]{1,0:T(8,128)S(1)} %shard_map.98.base, bf16[2,2,1792,128]{3,2,1,0:T(8,128)(2,1)S(1)} %get-tuple-element.62.left_top, bf16[128,128]{1,0:T(8,128)(2,1)S(1)} %add_convert_fusion.own, ...), custom_call_target="tpu_custom_call" | custom-call | flops 234881024 | bytes 4194304 | tf_op jit(solution)/shard_map/pallas_call | solution.py:35
  48.2 17.9 %all_to_all.10 = bf16[32,56,128]{2,1,0:T(8,128)(2,1)S(1)} all-to-all(bf16[32,56,128]{2,1,0:T(8,128)(2,1)S(1)} %bitcast.21), channel_id=1, replica_groups=mesh['group'=4,'member'=8] {'group','member'}, dimensions={0} | all-to-all | bytes 917504 | tf_op jit(solution)/shard_map/all_to_all | solution.py:540
  66.1 1.4 %shard_map.100 = f32[1024,128]{1,0:T(8,128)} custom-call(bf16[1024,896]{1,0:T(8,128)(2,1)S(1)} %get-tuple-element.44.order, s32[1024,128]{1,0:T(8,128)S(1)} %get-tuple-element.45.upper, bf16[1792,128]{1,0:T(8,128)(2,1)S(1)} %bitcast.22), custom_call_target="tpu_custom_call" | custom-call | flops 469762048 | bytes 4194304 | tf_op jit(solution)/shard_map/pallas_call | solution.py:35
  (25 shorter events, 0.2 us)
Async XLA Ops:
  0.0 10.4 %copy-start = (s32[62]{0:T(128)S(1)}, s32[62]{0:T(128)}, u32[]{:S(2)}) copy-start(s32[62]{0:T(128)} %ranks.3) | copy-start | bytes 748
  2.9 23.8 %all-to-all-start = ((bf16[32,64,128]{2,1,0:T(8,128)(2,1)}), bf16[32,64,128]{2,1,0:T(8,128)(2,1)}, u32[]{:S(2)}, u32[]{:S(2)}) async-start(bf16[32,64,128]{2,1,0:T(8,128)(2,1)} %get-tuple-element.35), calls=%async_computation | async-start | bytes 1048576 | tf_op jit(solution)/shard_map/all_to_all | solution.py:401
  29.1 1.6 %collective-permute-start = (f32[264,128]{1,0:T(8,128)S(1)}, f32[264,128]{1,0:T(8,128)S(1)}, u32[]{:S(2)}, u32[]{:S(2)}) collective-permute-start(f32[264,128]{1,0:T(8,128)S(1)} %get-tuple-element.37.after), channel_id=1, source_target_pairs={{0,1},{1,0},{2,3},{3,2},{4,5},{5,4},{6,7},{7,6},{8,9},{9,8},{10,11... | collective-permute-start | bytes 405512 | tf_op jit(solution)/shard_map/ppermute | solution.py:54
  30.8 4.2 %collective-permute-start.1 = (f16[200,128]{1,0:T(8,128)(2,1)S(1)}, f16[200,128]{1,0:T(8,128)(2,1)S(1)}, u32[]{:S(2)}, u32[]{:S(2)}) collective-permute-start(f16[200,128]{1,0:T(8,128)(2,1)S(1)} %pad_maximum_fusion), channel_id=1, source_target_pairs={{0,2},{2,0},{1,3},{3,1},{4,6},{6,4},{5,7},{7,5},{8,10},{10,8},{9,1... | collective-permute-start | bytes 153608 | tf_op jit(solution)/shard_map/ppermute | solution.py:54
  35.1 5.7 %collective-permute-start.2 = (f16[168,128]{1,0:T(8,128)(2,1)S(1)}, f16[168,128]{1,0:T(8,128)(2,1)S(1)}, u32[]{:S(2)}, u32[]{:S(2)}) collective-permute-start(f16[168,128]{1,0:T(8,128)(2,1)S(1)} %pad_maximum_fusion.1), channel_id=1, source_target_pairs={{0,4},{4,0},{1,5},{5,1},{2,6},{6,2},{3,7},{7,3},{8,12},{12,8},{9,1... | collective-permute-start | bytes 129032 | tf_op jit(solution)/shard_map/ppermute | solution.py:54
  40.9 4.9 %collective-permute-start.4 = (f16[136,128]{1,0:T(8,128)(2,1)S(1)}, f16[136,128]{1,0:T(8,128)(2,1)S(1)}, u32[]{:S(2)}, u32[]{:S(2)}) collective-permute-start(f16[136,128]{1,0:T(8,128)(2,1)S(1)} %pad_maximum_fusion.2), channel_id=1, source_target_pairs={{0,24},{1,3},{2,26},{3,1},{4,28},{5,7},{6,30},{7,5},{8,16},{9,11},... | collective-permute-start | bytes 104456 | tf_op jit(solution)/shard_map/ppermute | solution.py:491
  41.1 4.7 %collective-permute-start.3 = (f16[136,128]{1,0:T(8,128)(2,1)S(1)}, f16[136,128]{1,0:T(8,128)(2,1)S(1)}, u32[]{:S(2)}, u32[]{:S(2)}) collective-permute-start(f16[136,128]{1,0:T(8,128)(2,1)S(1)} %pad_maximum_fusion.2), channel_id=1, source_target_pairs={{0,16},{1,9},{2,18},{3,11},{4,20},{5,13},{6,22},{7,15},{8,24},{9,1... | collective-permute-start | bytes 104456 | tf_op jit(solution)/shard_map/ppermute | solution.py:491
  42.6 3.3 %collective-permute-start.5 = (bf16[64,128]{1,0:T(8,128)(2,1)S(1)}, bf16[64,128]{1,0:T(8,128)(2,1)S(1)}, u32[]{:S(2)}, u32[]{:S(2)}) collective-permute-start(bf16[64,128]{1,0:T(8,128)(2,1)S(1)} %pad_maximum_fusion.3.rest_4_), channel_id=1, source_target_pairs={{0,1},{1,0},{2,3},{3,2},{4,5},{5,4},{6,7},{7,6},{8,9},{9,8},{10,11... | collective-permute-start | bytes 49160 | tf_op jit(solution)/shard_map/ppermute | solution.py:54
  45.9 1.3 %collective-permute-start.6 = (bf16[128,128]{1,0:T(8,128)(2,1)S(1)}, bf16[128,128]{1,0:T(8,128)(2,1)S(1)}, u32[]{:S(2)}, u32[]{:S(2)}) collective-permute-start(bf16[128,128]{1,0:T(8,128)(2,1)S(1)} %add_convert_fusion.own), channel_id=1, source_target_pairs={{0,1},{1,0},{2,3},{3,2},{4,5},{5,4},{6,7},{7,6},{8,9},{9,8},{10,11... | collective-permute-start | bytes 98312 | tf_op jit(solution)/shard_map/ppermute | solution.py:54

commit v13 on v9

--- a/solution.py
+++ b/solution.py
@@ -99,7 +99,7 @@
     window = jnp.right_shift(here, shift)
     copies[1].wait()
     values = rows[...]
-    block = 512
+    block = 256
     for low in range(0, count, block):
         ordered[low : low + block, :] = dot(hot(iota((block, count), 0) + low == window), values)
     ordered[count:, :] = jnp.zeros((padded, 128), F32)
@@ -155,6 +155,10 @@
     for level in range(1, tops + 1):
         counts = (lane < rank_of(ranks, level, tops + levels)).astype(I32)
         marks = jnp.where(row == level, counts, marks)
+    for level in range(levels):
+        inside = row - 8 - level * rows
+        counts = (inside < rank_of(ranks, 1 + tops + level, tops + levels)).astype(I32)
+        marks = jnp.where(inside >= 0, counts, marks)
     flags[...] = marks.astype(F32)
     for copy in copies:
         copy.wait()
@@ -270,7 +274,7 @@
     return jnp.concatenate([jnp.where(core == 0, a, b), jnp.where(core == 0, b, a)], axis=0)
 
 
-def low_kernel(pieces, tops, ranks, *rest):
+def low_kernel(pieces, flags, *rest):
     bases = rest[:pieces]
     left_low, nearest, own, theirs, out = rest[pieces:]
     width = nearest.shape[0]
@@ -283,8 +287,7 @@
             coef = merged(core, own, theirs, level * half, half)
         else:
             coef = nearest[...]
-        rank = rank_of(ranks, 1 + tops + level, tops + levels)
-        coef = jnp.where(iota(coef.shape, 0) < rank, coef, 0.0)
+        coef = jnp.where(flags[8 + level * width : 8 + (level + 1) * width, :] > 0, coef, 0.0)
         stacked += [coef, turn(coef)]
     stacked = jnp.concatenate(stacked, axis=0).astype(BF16)
     low = 0
@@ -392,7 +395,7 @@
         near_kernel,
         [
             pltpu.VMEM((2 * ranked * capacity // 256, 256), BF16),
-            jax.ShapeDtypeStruct((8, columns), F32),
+            jax.ShapeDtypeStruct((8 + member_levels * width, columns), F32),
         ],
         [SMEM, HBM, HBM],
         (block_ranks, *far(top_right, low_right)),
@@ -499,10 +502,10 @@
     their_low, own = lax.optimization_barrier((partner(own_low, "member", 0), own))
     theirs = partner(own, "member", 0)
     base = call(
-        functools.partial(low_kernel, len(bases), group_levels),
+        functools.partial(low_kernel, len(bases)),
         [jax.ShapeDtypeStruct((capacity, columns), F32)],
-        [SMEM] + [VMEM] * (len(bases) + 4),
-        (block_ranks, *bases, left_low, nearest, own_low, their_low),
+        [VMEM] * (len(bases) + 5),
+        (flags, *bases, left_low, nearest, own_low, their_low),
         4 * capacity * columns * member_levels * width,
         3 << 20,
         16,

time: 67.4 us -> 67.3 us (level)
  transfers between devices with their start and end apart: 8 -> 8, of which waited for: 4 -> 5; matrix products, arithmetic and copies ran while one was open for 0% -> 0% of each run, Pallas kernels for 21% -> 20%
where the time goes in v13:
time: 67.3 us; the launch traced here: 67 us
  Pallas kernels  21.1 us (31%)
  blocking collectives  17.4 us (26%)
  waiting for transfers between devices  17.2 us (26%)
  starting transfers between devices  10.8 us (16%)
    pallas_call x10, Pallas kernels, call(): pl.pallas_call(kernel, out_shape=outs, in_specs=ins, out_specs=more.pop('...  21.1 us
    all_to_all x1, blocking collectives, on_device(): lax.all_to_all(leaving.reshape(leaves, bucket, columns), everyone, split_...  17.4 us
    all_to_all x1, waiting for transfers between devices, on_device(): lax.all_to_all(packed, everyone, split_axis=0, concat_axis=0, tiled=True)  13.6 us
    all_to_all x1, starting transfers between devices, on_device(): lax.all_to_all(packed, everyone, split_axis=0, concat_axis=0, tiled=True)  7.43 us
    ppermute x5, waiting for transfers between devices, partner(): return lax.ppermute(block, axis, route)  3.54 us
    ppermute x2, starting transfers between devices, on_device(): heard = [lax.ppermute(sums, everyone, route) for route in routes]  2.6 us
  transfers between devices with their start and end apart: 8, of which 5 were waited for; matrix products, arithmetic and copies ran while one was open for 0% of the time, Pallas kernels for 20%

profile of v13, /device:TPU:0, one launch (start us, length us, event | category | flops | bytes accessed | tf_op | source)
XLA Modules:
  0.0 67.0 jit_solution(8622054297331095597)
XLA Ops:
  0.0 0.0 copy-start
  0.0 2.9 %shard_map.91 = (bf16[32,64,128]{2,1,0:T(8,128)(2,1)}, s32[1,1024]{1,0:T(1,128)S(1)}) custom-call(s32[32]{0:T(128)} %sizes_in.1, s32[1,1024]{1,0:T(1,128)} %bitcast.25, bf16[1024,128]{1,0:T(8,128)(2,1)} %rows_in.1), custom_call_target="tpu_custom_call" | custom-call | flops 268435456 | bytes 4194304 | tf_op jit(solution)/shard_map/pallas_call | solution.py:35
  2.9 7.4 %all-to-all-start = ((bf16[32,64,128]{2,1,0:T(8,128)(2,1)}), bf16[32,64,128]{2,1,0:T(8,128)(2,1)}, u32[]{:S(2)}, u32[]{:S(2)}) async-start(bf16[32,64,128]{2,1,0:T(8,128)(2,1)} %get-tuple-element.33), calls=%async_computation | async-start | bytes 1048576 | tf_op jit(solution)/shard_map/all_to_all | solution.py:392
  10.4 0.0 copy-done
  10.4 2.7 %shard_map.92 = (bf16[6272,256]{1,0:T(8,128)(2,1)S(1)}, f32[200,128]{1,0:T(8,128)S(1)}) custom-call(s32[62]{0:T(128)S(1)} %copy-done, bf16[2,2,1792,128]{3,2,1,0:T(8,128)(2,1)} %right_top_in.1, bf16[3,2,64,1792]{3,2,1,0:T(8,128)(2,1)} %bitcast.23), custom_call_target="tpu_custom_call" | custom-call | bytes 6291456 | tf_op jit(solution)/shard_map/pallas_call | solution.py:35
  13.1 13.6 %all-to-all-done.arrived = bf16[32,64,128]{2,1,0:T(8,128)(2,1)} async-done(((bf16[32,64,128]{2,1,0:T(8,128)(2,1)}), bf16[32,64,128]{2,1,0:T(8,128)(2,1)}, u32[]{:S(2)}, u32[]{:S(2)}) %all-to-all-start) | async-done | bytes 524320 | tf_op jit(solution)/shard_map/all_to_all | solution.py:392
  26.7 2.4 %shard_map.93 = (bf16[2,1792,128]{2,1,0:T(8,128)(2,1)S(1)}, s32[7,256]{1,0:T(8,128)S(1)}, f32[264,128]{1,0:T(8,128)S(1)}, f32[200,128]{1,0:T(8,128)S(1)}) custom-call(bf16[32,64,128]{2,1,0:T(8,128)(2,1)} %all-to-all-done.arrived, bf16[6272,256]{1,0:T(8,128)(2,1)S(1)} %get-tuple-element.34.right), custom_call_target="tpu_custom_call" | custom-call | flops 411041792 | bytes 6291456 | tf_op jit(solution)/shard_map/pallas_call | solution.py:35
  29.1 0.1 collective-permute-start
  29.2 0.7 %shard_map.94 = (bf16[1792,256]{1,0:T(8,128)(2,1)S(1)}, bf16[1024,896]{1,0:T(8,128)(2,1)S(1)}, s32[1024,128]{1,0:T(8,128)S(1)}) custom-call(s32[7,256]{1,0:T(8,128)S(1)} %get-tuple-element.36.targets, s32[1,1024]{1,0:T(1,128)S(1)} %get-tuple-element.37.places, f32[264,128]{1,0:T(8,128)S(1)} %get-tuple-element.35.after), custom_call_target="tpu_custom_call" | custom-call | bytes 8388608 | tf_op jit(solution)/shard_map/pallas_call | solution.py:35
  29.9 0.6 collective-permute-done
  30.6 0.1 collective-permute-start.1
  30.7 3.2 %shard_map.95.rest_0_ = f32[672,128]{1,0:T(8,128)S(1)} custom-call(bf16[2,1792,1792]{2,1,0:T(8,128)(2,1)} %block_in.5, bf16[2,1792,128]{2,1,0:T(8,128)(2,1)S(1)} %get-tuple-element.46.pair, f32[192,128]{1,0:T(8,128)S(1)} %get-tuple-element.70.after), custom_call_target="tpu_custom_call" | custom-call | flops 616562688 | bytes 4816896 | tf_op jit(solution)/shard_map/pallas_call | solution.py:35
  33.8 0.9 %collective-permute-done.1 = f16[200,128]{1,0:T(8,128)(2,1)S(1)} collective-permute-done((f16[200,128]{1,0:T(8,128)(2,1)S(1)}, f16[200,128]{1,0:T(8,128)(2,1)S(1)}, u32[]{:S(2)}, u32[]{:S(2)}) %collective-permute-start.1) | collective-permute-done | bytes 51232 | tf_op jit(solution)/shard_map/ppermute | solution.py:54
  34.9 0.1 collective-permute-start.2
  35.0 3.2 %shard_map.96.rest_1_ = f32[672,128]{1,0:T(8,128)S(1)} custom-call(bf16[2,1792,1792]{2,1,0:T(8,128)(2,1)} %block_in.5, bf16[2,1792,128]{2,1,0:T(8,128)(2,1)S(1)} %get-tuple-element.46.pair, f32[160,128]{1,0:T(8,128)S(1)} %get-tuple-element.66.after), custom_call_target="tpu_custom_call" | custom-call | flops 616562688 | bytes 4816896 | tf_op jit(solution)/shard_map/pallas_call | solution.py:35
  38.1 1.7 %collective-permute-done.2 = f16[168,128]{1,0:T(8,128)(2,1)S(1)} collective-permute-done((f16[168,128]{1,0:T(8,128)(2,1)S(1)}, f16[168,128]{1,0:T(8,128)(2,1)S(1)}, u32[]{:S(2)}, u32[]{:S(2)}) %collective-permute-start.2) | collective-permute-done | bytes 43040 | tf_op jit(solution)/shard_map/ppermute | solution.py:54
  40.0 0.6 collective-permute-start.4
  40.6 2.0 %collective-permute-start.3 = (f16[136,128]{1,0:T(8,128)(2,1)S(1)}, f16[136,128]{1,0:T(8,128)(2,1)S(1)}, u32[]{:S(2)}, u32[]{:S(2)}) collective-permute-start(f16[136,128]{1,0:T(8,128)(2,1)S(1)} %pad_maximum_fusion.2), channel_id=1, source_target_pairs={{0,16},{1,9},{2,18},{3,11},{4,20},{5,13},{6,22},{7,15},{8,24},{9,1... | collective-permute-start | bytes 104456 | tf_op jit(solution)/shard_map/ppermute | solution.py:478
  42.6 0.0 collective-permute-start.5
  42.6 3.0 %shard_map.97 = (bf16[2,2,1792,128]{3,2,1,0:T(8,128)(2,1)S(1)}, bf16[1792,384]{1,0:T(8,128)(2,1)S(1)}, f32[448,128]{1,0:T(8,128)S(1)}) custom-call(bf16[2,2,1792,128]{3,2,1,0:T(8,128)(2,1)} %left_top_in.1, bf16[3,2,64,1792]{3,2,1,0:T(8,128)(2,1)} %bitcast.24, bf16[2,1792,1792]{2,1,0:T(8,128)(2,1)} %block_in.5, ...), custom_call_target="tpu_custom_call" | custom-call | flops 411041792 | bytes 12582912 | tf_op jit(solution)/shard_map/pallas_call | solution.py:35
  45.6 0.0 collective-permute-done.4
  45.6 0.0 collective-permute-done.3
  45.7 0.0 collective-permute-done.5.rest_6_
  45.7 0.6 collective-permute-start.6
  46.2 0.6 shard_map.98.base
  46.8 0.3 collective-permute-done.6.theirs
  47.1 1.0 %shard_map.99 = bf16[1792,128]{1,0:T(8,128)(2,1)S(1)} custom-call(f32[200,128]{1,0:T(8,128)S(1)} %get-tuple-element.43.flags, f32[1792,128]{1,0:T(8,128)S(1)} %shard_map.98.base, bf16[2,2,1792,128]{3,2,1,0:T(8,128)(2,1)S(1)} %get-tuple-element.58.left_top, bf16[128,128]{1,0:T(8,128)(2,1)S(1)} %add_convert_fusion.own, ...), custom_call_target="tpu_custom_call" | custom-call | flops 234881024 | bytes 4194304 | tf_op jit(solution)/shard_map/pallas_call | solution.py:35
  48.1 17.4 %all_to_all.10 = bf16[32,56,128]{2,1,0:T(8,128)(2,1)S(1)} all-to-all(bf16[32,56,128]{2,1,0:T(8,128)(2,1)S(1)} %bitcast.21), channel_id=1, replica_groups=mesh['group'=4,'member'=8] {'group','member'}, dimensions={0} | all-to-all | bytes 917504 | tf_op jit(solution)/shard_map/all_to_all | solution.py:527
  65.5 1.4 %shard_map.100 = f32[1024,128]{1,0:T(8,128)} custom-call(bf16[1024,896]{1,0:T(8,128)(2,1)S(1)} %get-tuple-element.41.order, s32[1024,128]{1,0:T(8,128)S(1)} %get-tuple-element.42.upper, bf16[1792,128]{1,0:T(8,128)(2,1)S(1)} %bitcast.22), custom_call_target="tpu_custom_call" | custom-call | flops 469762048 | bytes 4194304 | tf_op jit(solution)/shard_map/pallas_call | solution.py:35
  (25 shorter events, 0.2 us)
Async XLA Ops:
  0.0 10.4 %copy-start = (s32[62]{0:T(128)S(1)}, s32[62]{0:T(128)}, u32[]{:S(2)}) copy-start(s32[62]{0:T(128)} %ranks.1) | copy-start | bytes 748
  2.9 23.8 %all-to-all-start = ((bf16[32,64,128]{2,1,0:T(8,128)(2,1)}), bf16[32,64,128]{2,1,0:T(8,128)(2,1)}, u32[]{:S(2)}, u32[]{:S(2)}) async-start(bf16[32,64,128]{2,1,0:T(8,128)(2,1)} %get-tuple-element.33), calls=%async_computation | async-start | bytes 1048576 | tf_op jit(solution)/shard_map/all_to_all | solution.py:392
  29.1 1.4 %collective-permute-start = (f32[264,128]{1,0:T(8,128)S(1)}, f32[264,128]{1,0:T(8,128)S(1)}, u32[]{:S(2)}, u32[]{:S(2)}) collective-permute-start(f32[264,128]{1,0:T(8,128)S(1)} %get-tuple-element.35.after), channel_id=1, source_target_pairs={{0,1},{1,0},{2,3},{3,2},{4,5},{5,4},{6,7},{7,6},{8,9},{9,8},{10,11... | collective-permute-start | bytes 405512 | tf_op jit(solution)/shard_map/ppermute | solution.py:54
  30.6 4.2 %collective-permute-start.1 = (f16[200,128]{1,0:T(8,128)(2,1)S(1)}, f16[200,128]{1,0:T(8,128)(2,1)S(1)}, u32[]{:S(2)}, u32[]{:S(2)}) collective-permute-start(f16[200,128]{1,0:T(8,128)(2,1)S(1)} %pad_maximum_fusion), channel_id=1, source_target_pairs={{0,2},{2,0},{1,3},{3,1},{4,6},{6,4},{5,7},{7,5},{8,10},{10,8},{9,1... | collective-permute-start | bytes 153608 | tf_op jit(solution)/shard_map/ppermute | solution.py:54
  34.9 5.0 %collective-permute-start.2 = (f16[168,128]{1,0:T(8,128)(2,1)S(1)}, f16[168,128]{1,0:T(8,128)(2,1)S(1)}, u32[]{:S(2)}, u32[]{:S(2)}) collective-permute-start(f16[168,128]{1,0:T(8,128)(2,1)S(1)} %pad_maximum_fusion.1), channel_id=1, source_target_pairs={{0,4},{4,0},{1,5},{5,1},{2,6},{6,2},{3,7},{7,3},{8,12},{12,8},{9,1... | collective-permute-start | bytes 129032 | tf_op jit(solution)/shard_map/ppermute | solution.py:54
  40.0 5.6 %collective-permute-start.4 = (f16[136,128]{1,0:T(8,128)(2,1)S(1)}, f16[136,128]{1,0:T(8,128)(2,1)S(1)}, u32[]{:S(2)}, u32[]{:S(2)}) collective-permute-start(f16[136,128]{1,0:T(8,128)(2,1)S(1)} %pad_maximum_fusion.2), channel_id=1, source_target_pairs={{0,24},{1,3},{2,26},{3,1},{4,28},{5,7},{6,30},{7,5},{8,16},{9,11},... | collective-permute-start | bytes 104456 | tf_op jit(solution)/shard_map/ppermute | solution.py:478
  40.6 5.0 %collective-permute-start.3 = (f16[136,128]{1,0:T(8,128)(2,1)S(1)}, f16[136,128]{1,0:T(8,128)(2,1)S(1)}, u32[]{:S(2)}, u32[]{:S(2)}) collective-permute-start(f16[136,128]{1,0:T(8,128)(2,1)S(1)} %pad_maximum_fusion.2), channel_id=1, source_target_pairs={{0,16},{1,9},{2,18},{3,11},{4,20},{5,13},{6,22},{7,15},{8,24},{9,1... | collective-permute-start | bytes 104456 | tf_op jit(solution)/shard_map/ppermute | solution.py:478
  42.6 3.1 %collective-permute-start.5 = (bf16[64,128]{1,0:T(8,128)(2,1)S(1)}, bf16[64,128]{1,0:T(8,128)(2,1)S(1)}, u32[]{:S(2)}, u32[]{:S(2)}) collective-permute-start(bf16[64,128]{1,0:T(8,128)(2,1)S(1)} %pad_maximum_fusion.3.rest_5_), channel_id=1, source_target_pairs={{0,1},{1,0},{2,3},{3,2},{4,5},{5,4},{6,7},{7,6},{8,9},{9,8},{10,11... | collective-permute-start | bytes 49160 | tf_op jit(solution)/shard_map/ppermute | solution.py:54
  45.7 1.4 %collective-permute-start.6 = (bf16[128,128]{1,0:T(8,128)(2,1)S(1)}, bf16[128,128]{1,0:T(8,128)(2,1)S(1)}, u32[]{:S(2)}, u32[]{:S(2)}) collective-permute-start(bf16[128,128]{1,0:T(8,128)(2,1)S(1)} %add_convert_fusion.own), channel_id=1, source_target_pairs={{0,1},{1,0},{2,3},{3,2},{4,5},{5,4},{6,7},{7,6},{8,9},{9,8},{10,11... | collective-permute-start | bytes 98312 | tf_op jit(solution)/shard_map/ppermute | solution.py:54

commit v14 on v13

--- a/solution.py
+++ b/solution.py
@@ -62,13 +62,18 @@
     return jnp.clip(jnp.maximum(mine, other) + 1.0, -100.0, 126.0)
 
 
-def narrow(rows, power):
-    return jnp.concatenate([rows * jnp.exp2(14.0 - power[:1]), power]).astype(F16)
-
-
-def widen(sent):
+def stretch(power, heights):
+    parts = [jnp.broadcast_to(power[i : i + 1], (h, power.shape[1])) for i, h in enumerate(heights)]
+    return jnp.concatenate(parts)
+
+
+def narrow(rows, power, heights):
+    return jnp.concatenate([rows * jnp.exp2(14.0 - stretch(power, heights)), power]).astype(F16)
+
+
+def widen(sent, heights):
     power = sent[-8:].astype(F32)
-    return sent[:-8].astype(F32) * jnp.exp2(power[:1] - 14.0), power
+    return sent[:-8].astype(F32) * jnp.exp2(stretch(power, heights) - 14.0), power
 
 
 def turn(block):
@@ -76,9 +81,10 @@
     return jnp.where(iota(block.shape, 1) < half, -1.0, 1.0) * pltpu.roll(block, half, 1)
 
 
-def rank_of(ranks, level, levels):
+def rank_of(ranks, level, levels, other=0):
     device = lax.axis_index("group") * lax.axis_size("member") + lax.axis_index("member")
-    return ranks[(1 << level) - 2 + jnp.right_shift(device, levels - level)]
+    node = jnp.bitwise_xor(jnp.right_shift(device, levels - level), other)
+    return ranks[(1 << level) - 2 + node]
 
 
 def pack_kernel(leaves, bucket, sizes_in, position_in, rows_in, packed, places, *scratch):
@@ -157,7 +163,7 @@
         marks = jnp.where(row == level, counts, marks)
     for level in range(levels):
         inside = row - 8 - level * rows
-        counts = (inside < rank_of(ranks, 1 + tops + level, tops + levels)).astype(I32)
+        counts = (inside < rank_of(ranks, 1 + tops + level, tops + levels, 1)).astype(I32)
         marks = jnp.where(inside >= 0, counts, marks)
     flags[...] = marks.astype(F32)
     for copy in copies:
@@ -202,7 +208,7 @@
     copies[-1].wait()
 
 
-def field_kernel(leaves, bucket, tops, levels, arrived, right, *rest):
+def field_kernel(leaves, bucket, tops, levels, arrived, right, flags, *rest):
     pair, targets, send, keep, whole = rest
     capacity = leaves * bucket
     padded = arrived.shape[1]
@@ -240,7 +246,7 @@
         for p in range(2):
             lower += dot(right[at : at + rows, :], pair[p, low : low + 256, :])
             at += rows
-    whole[top_rows:, :] = lower
+    whole[top_rows:, :] = jnp.where(flags[8:, :] > 0, lower, 0.0)
     at = 0
     low = 0
     for half in [tops * 64] + [width // 2] * (levels - 1):
@@ -250,11 +256,19 @@
         send[at : at + half, :] = whole[pl.ds(other, half), :]
         at += half
         low += 2 * half
-    send[at : at + width, :] = lower[(levels - 1) * width :]
-    largest = jnp.max(jnp.abs(whole[...]), axis=0, keepdims=True)
-    power = jnp.clip(jnp.ceil(jnp.log2(largest + 1e-30)) + 1.0, -100.0, 126.0)
-    send[at + width :, :] = jnp.broadcast_to(power, (8, 128))
-    keep[at:, :] = jnp.broadcast_to(power, (8, 128))
+    send[at : at + width, :] = whole[whole.shape[0] - width :, :]
+    power = []
+    for low, high in [(level * 128, level * 128 + 128) for level in range(tops)] + [
+        (top_rows + level * width, top_rows + (level + 1) * width) for level in range(levels - 1)
+    ]:
+        largest = jnp.max(jnp.abs(whole[low:high, :]), axis=0, keepdims=True)
+        power.append(jnp.clip(jnp.ceil(jnp.log2(largest + 1e-30)) + 1.0, -100.0, 126.0))
+    line = iota((8, 128), 0)
+    shared = jnp.zeros((8, 128), F32)
+    for i, row in enumerate(power[tops:]):
+        shared = jnp.where(line == 1 + i, row, shared)
+    send[at + width :, :] = jnp.where(line == 0, jnp.where(core == 0, power[1], power[0]), shared)
+    keep[at:, :] = jnp.where(line == 0, jnp.where(core == 0, power[0], power[1]), shared)
 
 
 def diag_kernel(first, block_in, pair, after, out, block, sems):
@@ -274,7 +288,7 @@
     return jnp.concatenate([jnp.where(core == 0, a, b), jnp.where(core == 0, b, a)], axis=0)
 
 
-def low_kernel(pieces, flags, *rest):
+def low_kernel(pieces, *rest):
     bases = rest[:pieces]
     left_low, nearest, own, theirs, out = rest[pieces:]
     width = nearest.shape[0]
@@ -287,7 +301,6 @@
             coef = merged(core, own, theirs, level * half, half)
         else:
             coef = nearest[...]
-        coef = jnp.where(flags[8 + level * width : 8 + (level + 1) * width, :] > 0, coef, 0.0)
         stacked += [coef, turn(coef)]
     stacked = jnp.concatenate(stacked, axis=0).astype(BF16)
     low = 0
@@ -414,8 +427,8 @@
             jax.ShapeDtypeStruct((shared + width + 8, columns), F32),
             jax.ShapeDtypeStruct((shared + 8, columns), F32),
         ],
-        [VMEM, VMEM],
-        (arrived, right),
+        [VMEM] * 3,
+        (arrived, right, flags),
         far_flops,
         6 << 20,
         24,
@@ -453,19 +466,21 @@
     nearest = received[shared : shared + width]
     running = keep[:shared] + received[:shared]
     power = bound(keep[shared:], received[shared + width :])
+    heights = [columns] + [width // 2] * (member_levels - 1)
     bases = []
     coefs = []
     for bit in range(1, member_levels):
         rest = running.shape[0] - width // 2
-        received = partner(narrow(running, power), "member", bit)
+        received = partner(narrow(running, power, heights), "member", bit)
         if bit == 1:
             bases.append(diagonal(0, 3, running))
             received, bases[0] = lax.optimization_barrier((received, bases[0]))
         if bit == member_levels - 1:
             bases.append(diagonal(3, 3, running))
             received, bases[1] = lax.optimization_barrier((received, bases[1]))
-        received, other = widen(received)
+        received, other = widen(received, heights)
         power = bound(power, other)
+        heights = heights[:-1]
         coefs.insert(0, received[rest:].astype(BF16))
         running = running[:rest] + received[:rest]
     routes = [[], []]
@@ -474,7 +489,7 @@
             at = low * members + near
             routes[0] += [(at, (low ^ 2) * members + near), (at + 1, (low ^ 1) * members + near + 1)]
             routes[1] += [(at, (low ^ 3) * members + near), (at + 1, low * members + (near ^ 2) + 1)]
-    sums = narrow(running, power)
+    sums = narrow(running, power, heights)
     heard = [lax.ppermute(sums, everyone, route) for route in routes]
     left_top, left_low, last = call(
         functools.partial(stage_kernel, 6),
@@ -496,7 +511,7 @@
     )
     bases.append(last)
     heard, left_top, left_low = lax.optimization_barrier((heard, left_top, left_low))
-    heard = [widen(block)[0] for block in heard]
+    heard = [widen(block, heights)[0] for block in heard]
     own = (heard[0] + jnp.where(flags[:1] > 0, heard[1], 0.0)).astype(BF16)
     own_low = jnp.concatenate(coefs)
     their_low, own = lax.optimization_barrier((partner(own_low, "member", 0), own))
@@ -504,8 +519,8 @@
     base = call(
         functools.partial(low_kernel, len(bases)),
         [jax.ShapeDtypeStruct((capacity, columns), F32)],
-        [VMEM] * (len(bases) + 5),
-        (flags, *bases, left_low, nearest, own_low, their_low),
+        [VMEM] * (len(bases) + 4),
+        (*bases, left_low, nearest, own_low, their_low),
         4 * capacity * columns * member_levels * width,
         3 << 20,
         16,

time: 67.3 us -> 67.5 us (level)
  no operation moved by 1% of the time
where the time goes in v14:
time: 67.5 us; the launch traced here: 67.2 us
  Pallas kernels  21.1 us (31%)
  blocking collectives  17.4 us (26%)
  waiting for transfers between devices  17.1 us (25%)
  starting transfers between devices  10.9 us (16%)
    pallas_call x10, Pallas kernels, call(): pl.pallas_call(kernel, out_shape=outs, in_specs=ins, out_specs=more.pop('...  21.1 us
    all_to_all x1, blocking collectives, on_device(): lax.all_to_all(leaving.reshape(leaves, bucket, columns), everyone, split_...  17.4 us
    all_to_all x1, waiting for transfers between devices, on_device(): lax.all_to_all(packed, everyone, split_axis=0, concat_axis=0, tiled=True)  13.6 us
    all_to_all x1, starting transfers between devices, on_device(): lax.all_to_all(packed, everyone, split_axis=0, concat_axis=0, tiled=True)  7.43 us
    ppermute x5, waiting for transfers between devices, partner(): return lax.ppermute(block, axis, route)  3.51 us
    ppermute x2, starting transfers between devices, on_device(): heard = [lax.ppermute(sums, everyone, route) for route in routes]  2.62 us
  transfers between devices with their start and end apart: 8, of which 5 were waited for; matrix products, arithmetic and copies ran while one was open for 0% of the time, Pallas kernels for 20%

profile of v14, /device:TPU:0, one launch (start us, length us, event | category | flops | bytes accessed | tf_op | source)
XLA Modules:
  0.0 67.2 jit_solution(16112058728203863644)
XLA Ops:
  0.0 0.0 copy-start
  0.0 2.9 %shard_map.91 = (bf16[32,64,128]{2,1,0:T(8,128)(2,1)}, s32[1,1024]{1,0:T(1,128)S(1)}) custom-call(s32[32]{0:T(128)} %sizes_in.1, s32[1,1024]{1,0:T(1,128)} %bitcast.37, bf16[1024,128]{1,0:T(8,128)(2,1)} %rows_in.1), custom_call_target="tpu_custom_call" | custom-call | flops 268435456 | bytes 4194304 | tf_op jit(solution)/shard_map/pallas_call | solution.py:35
  2.9 7.4 %all-to-all-start = ((bf16[32,64,128]{2,1,0:T(8,128)(2,1)}), bf16[32,64,128]{2,1,0:T(8,128)(2,1)}, u32[]{:S(2)}, u32[]{:S(2)}) async-start(bf16[32,64,128]{2,1,0:T(8,128)(2,1)} %get-tuple-element.33), calls=%async_computation | async-start | bytes 1048576 | tf_op jit(solution)/shard_map/all_to_all | solution.py:405
  10.4 0.0 copy-done
  10.4 2.7 %shard_map.92 = (bf16[6272,256]{1,0:T(8,128)(2,1)S(1)}, f32[200,128]{1,0:T(8,128)S(1)}) custom-call(s32[62]{0:T(128)S(1)} %copy-done, bf16[2,2,1792,128]{3,2,1,0:T(8,128)(2,1)} %right_top_in.1, bf16[3,2,64,1792]{3,2,1,0:T(8,128)(2,1)} %bitcast.35), custom_call_target="tpu_custom_call" | custom-call | bytes 6291456 | tf_op jit(solution)/shard_map/pallas_call | solution.py:35
  13.1 13.6 %all-to-all-done.arrived = bf16[32,64,128]{2,1,0:T(8,128)(2,1)} async-done(((bf16[32,64,128]{2,1,0:T(8,128)(2,1)}), bf16[32,64,128]{2,1,0:T(8,128)(2,1)}, u32[]{:S(2)}, u32[]{:S(2)}) %all-to-all-start) | async-done | bytes 524320 | tf_op jit(solution)/shard_map/all_to_all | solution.py:405
  26.7 2.4 %shard_map.93 = (bf16[2,1792,128]{2,1,0:T(8,128)(2,1)S(1)}, s32[7,256]{1,0:T(8,128)S(1)}, f32[264,128]{1,0:T(8,128)S(1)}, f32[200,128]{1,0:T(8,128)S(1)}) custom-call(bf16[32,64,128]{2,1,0:T(8,128)(2,1)} %all-to-all-done.arrived, bf16[6272,256]{1,0:T(8,128)(2,1)S(1)} %get-tuple-element.34.right, f32[200,128]{1,0:T(8,128)S(1)} %get-tuple-element.35.flags), custom_call_target="tpu_custom_call" | custom-call | flops 411041792 | bytes 6291456 | tf_op jit(solution)/shard_map/pallas_call | solution.py:35
  29.1 0.1 collective-permute-start
  29.2 0.7 %shard_map.94 = (bf16[1792,256]{1,0:T(8,128)(2,1)S(1)}, bf16[1024,896]{1,0:T(8,128)(2,1)S(1)}, s32[1024,128]{1,0:T(8,128)S(1)}) custom-call(s32[7,256]{1,0:T(8,128)S(1)} %get-tuple-element.37.targets, s32[1,1024]{1,0:T(1,128)S(1)} %get-tuple-element.38.places, f32[264,128]{1,0:T(8,128)S(1)} %get-tuple-element.36.after), custom_call_target="tpu_custom_call" | custom-call | bytes 8388608 | tf_op jit(solution)/shard_map/pallas_call | solution.py:35
  29.9 0.6 collective-permute-done
  30.6 0.1 collective-permute-start.1
  30.7 3.2 %shard_map.95.rest_0_ = f32[672,128]{1,0:T(8,128)S(1)} custom-call(bf16[2,1792,1792]{2,1,0:T(8,128)(2,1)} %block_in.5, bf16[2,1792,128]{2,1,0:T(8,128)(2,1)S(1)} %get-tuple-element.46.pair, f32[192,128]{1,0:T(8,128)S(1)} %get-tuple-element.70.after), custom_call_target="tpu_custom_call" | custom-call | flops 616562688 | bytes 4816896 | tf_op jit(solution)/shard_map/pallas_call | solution.py:35
  33.9 0.9 %collective-permute-done.1 = f16[200,128]{1,0:T(8,128)(2,1)S(1)} collective-permute-done((f16[200,128]{1,0:T(8,128)(2,1)S(1)}, f16[200,128]{1,0:T(8,128)(2,1)S(1)}, u32[]{:S(2)}, u32[]{:S(2)}) %collective-permute-start.1) | collective-permute-done | bytes 51232 | tf_op jit(solution)/shard_map/ppermute | solution.py:54
  35.0 0.1 collective-permute-start.2
  35.1 3.2 %shard_map.96.rest_1_ = f32[672,128]{1,0:T(8,128)S(1)} custom-call(bf16[2,1792,1792]{2,1,0:T(8,128)(2,1)} %block_in.5, bf16[2,1792,128]{2,1,0:T(8,128)(2,1)S(1)} %get-tuple-element.46.pair, f32[160,128]{1,0:T(8,128)S(1)} %get-tuple-element.66.after), custom_call_target="tpu_custom_call" | custom-call | flops 616562688 | bytes 4816896 | tf_op jit(solution)/shard_map/pallas_call | solution.py:35
  38.3 1.7 %collective-permute-done.2 = f16[168,128]{1,0:T(8,128)(2,1)S(1)} collective-permute-done((f16[168,128]{1,0:T(8,128)(2,1)S(1)}, f16[168,128]{1,0:T(8,128)(2,1)S(1)}, u32[]{:S(2)}, u32[]{:S(2)}) %collective-permute-start.2) | collective-permute-done | bytes 43040 | tf_op jit(solution)/shard_map/ppermute | solution.py:54
  40.2 0.7 collective-permute-start.4
  40.8 2.0 %collective-permute-start.3 = (f16[136,128]{1,0:T(8,128)(2,1)S(1)}, f16[136,128]{1,0:T(8,128)(2,1)S(1)}, u32[]{:S(2)}, u32[]{:S(2)}) collective-permute-start(f16[136,128]{1,0:T(8,128)(2,1)S(1)} %pad_maximum_fusion.2), channel_id=1, source_target_pairs={{0,16},{1,9},{2,18},{3,11},{4,20},{5,13},{6,22},{7,15},{8,24},{9,1... | collective-permute-start | bytes 104456 | tf_op jit(solution)/shard_map/ppermute | solution.py:493
  42.8 0.0 collective-permute-start.5
  42.8 3.0 %shard_map.97 = (bf16[2,2,1792,128]{3,2,1,0:T(8,128)(2,1)S(1)}, bf16[1792,384]{1,0:T(8,128)(2,1)S(1)}, f32[448,128]{1,0:T(8,128)S(1)}) custom-call(bf16[2,2,1792,128]{3,2,1,0:T(8,128)(2,1)} %left_top_in.1, bf16[3,2,64,1792]{3,2,1,0:T(8,128)(2,1)} %bitcast.36, bf16[2,1792,1792]{2,1,0:T(8,128)(2,1)} %block_in.5, ...), custom_call_target="tpu_custom_call" | custom-call | flops 411041792 | bytes 12582912 | tf_op jit(solution)/shard_map/pallas_call | solution.py:35
  45.8 0.0 collective-permute-done.4
  45.8 0.0 collective-permute-done.3
  45.9 0.0 collective-permute-done.5.rest_6_
  45.9 0.6 collective-permute-start.6
  46.5 0.6 shard_map.98.base
  47.1 0.3 collective-permute-done.6.theirs
  47.3 1.0 %shard_map.99 = bf16[1792,128]{1,0:T(8,128)(2,1)S(1)} custom-call(f32[200,128]{1,0:T(8,128)S(1)} %get-tuple-element.35.flags, f32[1792,128]{1,0:T(8,128)S(1)} %shard_map.98.base, bf16[2,2,1792,128]{3,2,1,0:T(8,128)(2,1)S(1)} %get-tuple-element.58.left_top, bf16[128,128]{1,0:T(8,128)(2,1)S(1)} %add_convert_fusion.own, ...), custom_call_target="tpu_custom_call" | custom-call | flops 234881024 | bytes 4194304 | tf_op jit(solution)/shard_map/pallas_call | solution.py:35
  48.4 17.4 %all_to_all.10 = bf16[32,56,128]{2,1,0:T(8,128)(2,1)S(1)} all-to-all(bf16[32,56,128]{2,1,0:T(8,128)(2,1)S(1)} %bitcast.33), channel_id=1, replica_groups=mesh['group'=4,'member'=8] {'group','member'}, dimensions={0} | all-to-all | bytes 917504 | tf_op jit(solution)/shard_map/all_to_all | solution.py:542
  65.8 1.5 %shard_map.100 = f32[1024,128]{1,0:T(8,128)} custom-call(bf16[1024,896]{1,0:T(8,128)(2,1)S(1)} %get-tuple-element.42.order, s32[1024,128]{1,0:T(8,128)S(1)} %get-tuple-element.43.upper, bf16[1792,128]{1,0:T(8,128)(2,1)S(1)} %bitcast.34), custom_call_target="tpu_custom_call" | custom-call | flops 469762048 | bytes 4194304 | tf_op jit(solution)/shard_map/pallas_call | solution.py:35
  (35 shorter events, 0.4 us)
Async XLA Ops:
  0.0 10.4 %copy-start = (s32[62]{0:T(128)S(1)}, s32[62]{0:T(128)}, u32[]{:S(2)}) copy-start(s32[62]{0:T(128)} %ranks.1) | copy-start | bytes 748
  2.9 23.8 %all-to-all-start = ((bf16[32,64,128]{2,1,0:T(8,128)(2,1)}), bf16[32,64,128]{2,1,0:T(8,128)(2,1)}, u32[]{:S(2)}, u32[]{:S(2)}) async-start(bf16[32,64,128]{2,1,0:T(8,128)(2,1)} %get-tuple-element.33), calls=%async_computation | async-start | bytes 1048576 | tf_op jit(solution)/shard_map/all_to_all | solution.py:405
  29.1 1.4 %collective-permute-start = (f32[264,128]{1,0:T(8,128)S(1)}, f32[264,128]{1,0:T(8,128)S(1)}, u32[]{:S(2)}, u32[]{:S(2)}) collective-permute-start(f32[264,128]{1,0:T(8,128)S(1)} %get-tuple-element.36.after), channel_id=1, source_target_pairs={{0,1},{1,0},{2,3},{3,2},{4,5},{5,4},{6,7},{7,6},{8,9},{9,8},{10,11... | collective-permute-start | bytes 405512 | tf_op jit(solution)/shard_map/ppermute | solution.py:54
  30.6 4.2 %collective-permute-start.1 = (f16[200,128]{1,0:T(8,128)(2,1)S(1)}, f16[200,128]{1,0:T(8,128)(2,1)S(1)}, u32[]{:S(2)}, u32[]{:S(2)}) collective-permute-start(f16[200,128]{1,0:T(8,128)(2,1)S(1)} %pad_maximum_fusion), channel_id=1, source_target_pairs={{0,2},{2,0},{1,3},{3,1},{4,6},{6,4},{5,7},{7,5},{8,10},{10,8},{9,1... | collective-permute-start | bytes 153608 | tf_op jit(solution)/shard_map/ppermute | solution.py:54
  35.0 5.0 %collective-permute-start.2 = (f16[168,128]{1,0:T(8,128)(2,1)S(1)}, f16[168,128]{1,0:T(8,128)(2,1)S(1)}, u32[]{:S(2)}, u32[]{:S(2)}) collective-permute-start(f16[168,128]{1,0:T(8,128)(2,1)S(1)} %pad_maximum_fusion.1), channel_id=1, source_target_pairs={{0,4},{4,0},{1,5},{5,1},{2,6},{6,2},{3,7},{7,3},{8,12},{12,8},{9,1... | collective-permute-start | bytes 129032 | tf_op jit(solution)/shard_map/ppermute | solution.py:54
  40.2 5.7 %collective-permute-start.4 = (f16[136,128]{1,0:T(8,128)(2,1)S(1)}, f16[136,128]{1,0:T(8,128)(2,1)S(1)}, u32[]{:S(2)}, u32[]{:S(2)}) collective-permute-start(f16[136,128]{1,0:T(8,128)(2,1)S(1)} %pad_maximum_fusion.2), channel_id=1, source_target_pairs={{0,24},{1,3},{2,26},{3,1},{4,28},{5,7},{6,30},{7,5},{8,16},{9,11},... | collective-permute-start | bytes 104456 | tf_op jit(solution)/shard_map/ppermute | solution.py:493
  40.8 5.0 %collective-permute-start.3 = (f16[136,128]{1,0:T(8,128)(2,1)S(1)}, f16[136,128]{1,0:T(8,128)(2,1)S(1)}, u32[]{:S(2)}, u32[]{:S(2)}) collective-permute-start(f16[136,128]{1,0:T(8,128)(2,1)S(1)} %pad_maximum_fusion.2), channel_id=1, source_target_pairs={{0,16},{1,9},{2,18},{3,11},{4,20},{5,13},{6,22},{7,15},{8,24},{9,1... | collective-permute-start | bytes 104456 | tf_op jit(solution)/shard_map/ppermute | solution.py:493
  42.8 3.1 %collective-permute-start.5 = (bf16[64,128]{1,0:T(8,128)(2,1)S(1)}, bf16[64,128]{1,0:T(8,128)(2,1)S(1)}, u32[]{:S(2)}, u32[]{:S(2)}) collective-permute-start(bf16[64,128]{1,0:T(8,128)(2,1)S(1)} %pad_maximum_fusion.3.rest_5_), channel_id=1, source_target_pairs={{0,1},{1,0},{2,3},{3,2},{4,5},{5,4},{6,7},{7,6},{8,9},{9,8},{10,11... | collective-permute-start | bytes 49160 | tf_op jit(solution)/shard_map/ppermute | solution.py:54
  45.9 1.4 %collective-permute-start.6 = (bf16[128,128]{1,0:T(8,128)(2,1)S(1)}, bf16[128,128]{1,0:T(8,128)(2,1)S(1)}, u32[]{:S(2)}, u32[]{:S(2)}) collective-permute-start(bf16[128,128]{1,0:T(8,128)(2,1)S(1)} %add_convert_fusion.own), channel_id=1, source_target_pairs={{0,1},{1,0},{2,3},{3,2},{4,5},{5,4},{6,7},{7,6},{8,9},{9,8},{10,11... | collective-permute-start | bytes 98312 | tf_op jit(solution)/shard_map/ppermute | solution.py:54

commit v15 on v14

--- a/solution.py
+++ b/solution.py
@@ -483,6 +483,8 @@
         heights = heights[:-1]
         coefs.insert(0, received[rest:].astype(BF16))
         running = running[:rest] + received[:rest]
+    own_low = jnp.concatenate(coefs)
+    their_low = partner(own_low, "member", 0)
     routes = [[], []]
     for low in range(groups):
         for near in range(0, members, 2):
@@ -499,7 +501,7 @@
             jax.ShapeDtypeStruct((2 * height, columns), F32),
         ],
         [HBM, HBM, HBM, VMEM, pl.BlockSpec(memory_space=pl.ANY)],
-        (*far(top_left, low_left, diag_block), pair, running),
+        (*far(top_left, low_left, diag_block), pair, their_low),
         8 * height * capacity * columns,
         12 << 20,
         24,
@@ -513,8 +515,7 @@
     heard, left_top, left_low = lax.optimization_barrier((heard, left_top, left_low))
     heard = [widen(block, heights)[0] for block in heard]
     own = (heard[0] + jnp.where(flags[:1] > 0, heard[1], 0.0)).astype(BF16)
-    own_low = jnp.concatenate(coefs)
-    their_low, own = lax.optimization_barrier((partner(own_low, "member", 0), own))
+    their_low, own = lax.optimization_barrier((their_low, own))
     theirs = partner(own, "member", 0)
     base = call(
         functools.partial(low_kernel, len(bases)),

time: 67.5 us -> 67.6 us (level)
  no operation moved by 1% of the time
where the time goes in v15:
time: 67.6 us; the launch traced here: 67.3 us
  Pallas kernels  21.2 us (31%)
  blocking collectives  17.6 us (26%)
  waiting for transfers between devices  17.4 us (26%)
  starting transfers between devices  10.4 us (15%)
    pallas_call x10, Pallas kernels, call(): pl.pallas_call(kernel, out_shape=outs, in_specs=ins, out_specs=more.pop('...  21.2 us
    all_to_all x1, blocking collectives, on_device(): lax.all_to_all(leaving.reshape(leaves, bucket, columns), everyone, split_...  17.6 us
    all_to_all x1, waiting for transfers between devices, on_device(): lax.all_to_all(packed, everyone, split_axis=0, concat_axis=0, tiled=True)  13.6 us
    all_to_all x1, starting transfers between devices, on_device(): lax.all_to_all(packed, everyone, split_axis=0, concat_axis=0, tiled=True)  7.43 us
    ppermute x5, waiting for transfers between devices, partner(): return lax.ppermute(block, axis, route)  3.82 us
    ppermute x2, starting transfers between devices, on_device(): heard = [lax.ppermute(sums, everyone, route) for route in routes]  2.61 us
  transfers between devices with their start and end apart: 8, of which 5 were waited for; matrix products, arithmetic and copies ran while one was open for 0% of the time, Pallas kernels for 20%

profile of v15, /device:TPU:0, one launch (start us, length us, event | category | flops | bytes accessed | tf_op | source)
XLA Modules:
  0.0 67.3 jit_solution(11396460642254814173)
XLA Ops:
  0.0 0.0 copy-start
  0.0 2.9 %shard_map.91 = (bf16[32,64,128]{2,1,0:T(8,128)(2,1)}, s32[1,1024]{1,0:T(1,128)S(1)}) custom-call(s32[32]{0:T(128)} %sizes_in.1, s32[1,1024]{1,0:T(1,128)} %bitcast.37, bf16[1024,128]{1,0:T(8,128)(2,1)} %rows_in.1), custom_call_target="tpu_custom_call" | custom-call | flops 268435456 | bytes 4194304 | tf_op jit(solution)/shard_map/pallas_call | solution.py:35
  2.9 7.4 %all-to-all-start = ((bf16[32,64,128]{2,1,0:T(8,128)(2,1)}), bf16[32,64,128]{2,1,0:T(8,128)(2,1)}, u32[]{:S(2)}, u32[]{:S(2)}) async-start(bf16[32,64,128]{2,1,0:T(8,128)(2,1)} %get-tuple-element.33), calls=%async_computation | async-start | bytes 1048576 | tf_op jit(solution)/shard_map/all_to_all | solution.py:405
  10.4 0.0 copy-done
  10.4 2.7 %shard_map.92 = (bf16[6272,256]{1,0:T(8,128)(2,1)S(1)}, f32[200,128]{1,0:T(8,128)S(1)}) custom-call(s32[62]{0:T(128)S(1)} %copy-done, bf16[2,2,1792,128]{3,2,1,0:T(8,128)(2,1)} %right_top_in.1, bf16[3,2,64,1792]{3,2,1,0:T(8,128)(2,1)} %bitcast.35), custom_call_target="tpu_custom_call" | custom-call | bytes 6291456 | tf_op jit(solution)/shard_map/pallas_call | solution.py:35
  13.1 13.6 %all-to-all-done.arrived = bf16[32,64,128]{2,1,0:T(8,128)(2,1)} async-done(((bf16[32,64,128]{2,1,0:T(8,128)(2,1)}), bf16[32,64,128]{2,1,0:T(8,128)(2,1)}, u32[]{:S(2)}, u32[]{:S(2)}) %all-to-all-start) | async-done | bytes 524320 | tf_op jit(solution)/shard_map/all_to_all | solution.py:405
  26.7 2.4 %shard_map.93 = (bf16[2,1792,128]{2,1,0:T(8,128)(2,1)S(1)}, s32[7,256]{1,0:T(8,128)S(1)}, f32[264,128]{1,0:T(8,128)S(1)}, f32[200,128]{1,0:T(8,128)S(1)}) custom-call(bf16[32,64,128]{2,1,0:T(8,128)(2,1)} %all-to-all-done.arrived, bf16[6272,256]{1,0:T(8,128)(2,1)S(1)} %get-tuple-element.34.right, f32[200,128]{1,0:T(8,128)S(1)} %get-tuple-element.35.flags), custom_call_target="tpu_custom_call" | custom-call | flops 411041792 | bytes 6291456 | tf_op jit(solution)/shard_map/pallas_call | solution.py:35
  29.1 0.1 collective-permute-start
  29.2 0.7 %shard_map.94 = (bf16[1792,256]{1,0:T(8,128)(2,1)S(1)}, bf16[1024,896]{1,0:T(8,128)(2,1)S(1)}, s32[1024,128]{1,0:T(8,128)S(1)}) custom-call(s32[7,256]{1,0:T(8,128)S(1)} %get-tuple-element.37.targets, s32[1,1024]{1,0:T(1,128)S(1)} %get-tuple-element.38.places, f32[264,128]{1,0:T(8,128)S(1)} %get-tuple-element.36.after), custom_call_target="tpu_custom_call" | custom-call | bytes 8388608 | tf_op jit(solution)/shard_map/pallas_call | solution.py:35
  29.9 0.6 collective-permute-done
  30.6 0.1 collective-permute-start.1
  30.7 3.2 %shard_map.95.rest_0_ = f32[672,128]{1,0:T(8,128)S(1)} custom-call(bf16[2,1792,1792]{2,1,0:T(8,128)(2,1)} %block_in.5, bf16[2,1792,128]{2,1,0:T(8,128)(2,1)S(1)} %get-tuple-element.46.pair, f32[192,128]{1,0:T(8,128)S(1)} %get-tuple-element.68.after), custom_call_target="tpu_custom_call" | custom-call | flops 616562688 | bytes 4816896 | tf_op jit(solution)/shard_map/pallas_call | solution.py:35
  33.9 0.9 %collective-permute-done.1 = f16[200,128]{1,0:T(8,128)(2,1)S(1)} collective-permute-done((f16[200,128]{1,0:T(8,128)(2,1)S(1)}, f16[200,128]{1,0:T(8,128)(2,1)S(1)}, u32[]{:S(2)}, u32[]{:S(2)}) %collective-permute-start.1) | collective-permute-done | bytes 51232 | tf_op jit(solution)/shard_map/ppermute | solution.py:54
  35.0 0.1 collective-permute-start.2
  35.1 3.2 %shard_map.96.rest_1_ = f32[672,128]{1,0:T(8,128)S(1)} custom-call(bf16[2,1792,1792]{2,1,0:T(8,128)(2,1)} %block_in.5, bf16[2,1792,128]{2,1,0:T(8,128)(2,1)S(1)} %get-tuple-element.46.pair, f32[160,128]{1,0:T(8,128)S(1)} %get-tuple-element.64.after), custom_call_target="tpu_custom_call" | custom-call | flops 616562688 | bytes 4816896 | tf_op jit(solution)/shard_map/pallas_call | solution.py:35
  38.3 1.7 %collective-permute-done.2 = f16[168,128]{1,0:T(8,128)(2,1)S(1)} collective-permute-done((f16[168,128]{1,0:T(8,128)(2,1)S(1)}, f16[168,128]{1,0:T(8,128)(2,1)S(1)}, u32[]{:S(2)}, u32[]{:S(2)}) %collective-permute-start.2) | collective-permute-done | bytes 43040 | tf_op jit(solution)/shard_map/ppermute | solution.py:54
  40.2 0.1 collective-permute-start.3
  40.3 0.7 collective-permute-start.5
  40.9 1.9 %collective-permute-start.4 = (f16[136,128]{1,0:T(8,128)(2,1)S(1)}, f16[136,128]{1,0:T(8,128)(2,1)S(1)}, u32[]{:S(2)}, u32[]{:S(2)}) collective-permute-start(f16[136,128]{1,0:T(8,128)(2,1)S(1)} %pad_maximum_fusion.2), channel_id=1, source_target_pairs={{0,16},{1,9},{2,18},{3,11},{4,20},{5,13},{6,22},{7,15},{8,24},{9,1... | collective-permute-start | bytes 104456 | tf_op jit(solution)/shard_map/ppermute | solution.py:495
  42.9 0.0 collective-permute-done.3.after.rest_6_
  42.9 3.0 %shard_map.97 = (bf16[2,2,1792,128]{3,2,1,0:T(8,128)(2,1)S(1)}, bf16[1792,384]{1,0:T(8,128)(2,1)S(1)}, f32[448,128]{1,0:T(8,128)S(1)}) custom-call(bf16[2,2,1792,128]{3,2,1,0:T(8,128)(2,1)} %left_top_in.1, bf16[3,2,64,1792]{3,2,1,0:T(8,128)(2,1)} %bitcast.36, bf16[2,1792,1792]{2,1,0:T(8,128)(2,1)} %block_in.5, ...), custom_call_target="tpu_custom_call" | custom-call | flops 411041792 | bytes 12582912 | tf_op jit(solution)/shard_map/pallas_call | solution.py:35
  45.9 0.0 collective-permute-done.5
  45.9 0.0 collective-permute-done.4
  46.0 0.1 collective-permute-start.6
  46.1 0.6 shard_map.98.base
  46.6 0.6 collective-permute-done.6.theirs
  47.2 1.0 %shard_map.99 = bf16[1792,128]{1,0:T(8,128)(2,1)S(1)} custom-call(f32[200,128]{1,0:T(8,128)S(1)} %get-tuple-element.35.flags, f32[1792,128]{1,0:T(8,128)S(1)} %shard_map.98.base, bf16[2,2,1792,128]{3,2,1,0:T(8,128)(2,1)S(1)} %get-tuple-element.58.left_top, bf16[128,128]{1,0:T(8,128)(2,1)S(1)} %add_convert_fusion.own, ...), custom_call_target="tpu_custom_call" | custom-call | flops 234881024 | bytes 4194304 | tf_op jit(solution)/shard_map/pallas_call | solution.py:35
  48.3 17.6 %all_to_all.10 = bf16[32,56,128]{2,1,0:T(8,128)(2,1)S(1)} all-to-all(bf16[32,56,128]{2,1,0:T(8,128)(2,1)S(1)} %bitcast.33), channel_id=1, replica_groups=mesh['group'=4,'member'=8] {'group','member'}, dimensions={0} | all-to-all | bytes 917504 | tf_op jit(solution)/shard_map/all_to_all | solution.py:543
  65.8 1.5 %shard_map.100 = f32[1024,128]{1,0:T(8,128)} custom-call(bf16[1024,896]{1,0:T(8,128)(2,1)S(1)} %get-tuple-element.42.order, s32[1024,128]{1,0:T(8,128)S(1)} %get-tuple-element.43.upper, bf16[1792,128]{1,0:T(8,128)(2,1)S(1)} %bitcast.34), custom_call_target="tpu_custom_call" | custom-call | flops 469762048 | bytes 4194304 | tf_op jit(solution)/shard_map/pallas_call | solution.py:35
  (35 shorter events, 0.4 us)
Async XLA Ops:
  0.0 10.4 %copy-start = (s32[62]{0:T(128)S(1)}, s32[62]{0:T(128)}, u32[]{:S(2)}) copy-start(s32[62]{0:T(128)} %ranks.1) | copy-start | bytes 748
  2.9 23.8 %all-to-all-start = ((bf16[32,64,128]{2,1,0:T(8,128)(2,1)}), bf16[32,64,128]{2,1,0:T(8,128)(2,1)}, u32[]{:S(2)}, u32[]{:S(2)}) async-start(bf16[32,64,128]{2,1,0:T(8,128)(2,1)} %get-tuple-element.33), calls=%async_computation | async-start | bytes 1048576 | tf_op jit(solution)/shard_map/all_to_all | solution.py:405
  29.1 1.4 %collective-permute-start = (f32[264,128]{1,0:T(8,128)S(1)}, f32[264,128]{1,0:T(8,128)S(1)}, u32[]{:S(2)}, u32[]{:S(2)}) collective-permute-start(f32[264,128]{1,0:T(8,128)S(1)} %get-tuple-element.36.after), channel_id=1, source_target_pairs={{0,1},{1,0},{2,3},{3,2},{4,5},{5,4},{6,7},{7,6},{8,9},{9,8},{10,11... | collective-permute-start | bytes 405512 | tf_op jit(solution)/shard_map/ppermute | solution.py:54
  30.6 4.2 %collective-permute-start.1 = (f16[200,128]{1,0:T(8,128)(2,1)S(1)}, f16[200,128]{1,0:T(8,128)(2,1)S(1)}, u32[]{:S(2)}, u32[]{:S(2)}) collective-permute-start(f16[200,128]{1,0:T(8,128)(2,1)S(1)} %pad_maximum_fusion), channel_id=1, source_target_pairs={{0,2},{2,0},{1,3},{3,1},{4,6},{6,4},{5,7},{7,5},{8,10},{10,8},{9,1... | collective-permute-start | bytes 153608 | tf_op jit(solution)/shard_map/ppermute | solution.py:54
  35.0 5.0 %collective-permute-start.2 = (f16[168,128]{1,0:T(8,128)(2,1)S(1)}, f16[168,128]{1,0:T(8,128)(2,1)S(1)}, u32[]{:S(2)}, u32[]{:S(2)}) collective-permute-start(f16[168,128]{1,0:T(8,128)(2,1)S(1)} %pad_maximum_fusion.1), channel_id=1, source_target_pairs={{0,4},{4,0},{1,5},{5,1},{2,6},{6,2},{3,7},{7,3},{8,12},{12,8},{9,1... | collective-permute-start | bytes 129032 | tf_op jit(solution)/shard_map/ppermute | solution.py:54
  40.2 2.7 %collective-permute-start.3 = (bf16[64,128]{1,0:T(8,128)(2,1)S(1)}, bf16[64,128]{1,0:T(8,128)(2,1)S(1)}, u32[]{:S(2)}, u32[]{:S(2)}) collective-permute-start(bf16[64,128]{1,0:T(8,128)(2,1)S(1)} %pad_maximum_fusion.3.rest_5_), channel_id=1, source_target_pairs={{0,1},{1,0},{2,3},{3,2},{4,5},{5,4},{6,7},{7,6},{8,9},{9,8},{10,11... | collective-permute-start | bytes 49160 | tf_op jit(solution)/shard_map/ppermute | solution.py:54
  40.3 5.6 %collective-permute-start.5 = (f16[136,128]{1,0:T(8,128)(2,1)S(1)}, f16[136,128]{1,0:T(8,128)(2,1)S(1)}, u32[]{:S(2)}, u32[]{:S(2)}) collective-permute-start(f16[136,128]{1,0:T(8,128)(2,1)S(1)} %pad_maximum_fusion.2), channel_id=1, source_target_pairs={{0,24},{1,3},{2,26},{3,1},{4,28},{5,7},{6,30},{7,5},{8,16},{9,11},... | collective-permute-start | bytes 104456 | tf_op jit(solution)/shard_map/ppermute | solution.py:495
  40.9 5.0 %collective-permute-start.4 = (f16[136,128]{1,0:T(8,128)(2,1)S(1)}, f16[136,128]{1,0:T(8,128)(2,1)S(1)}, u32[]{:S(2)}, u32[]{:S(2)}) collective-permute-start(f16[136,128]{1,0:T(8,128)(2,1)S(1)} %pad_maximum_fusion.2), channel_id=1, source_target_pairs={{0,16},{1,9},{2,18},{3,11},{4,20},{5,13},{6,22},{7,15},{8,24},{9,1... | collective-permute-start | bytes 104456 | tf_op jit(solution)/shard_map/ppermute | solution.py:495
  46.0 1.3 %collective-permute-start.6 = (bf16[128,128]{1,0:T(8,128)(2,1)S(1)}, bf16[128,128]{1,0:T(8,128)(2,1)S(1)}, u32[]{:S(2)}, u32[]{:S(2)}) collective-permute-start(bf16[128,128]{1,0:T(8,128)(2,1)S(1)} %add_convert_fusion.own), channel_id=1, source_target_pairs={{0,1},{1,0},{2,3},{3,2},{4,5},{5,4},{6,7},{7,6},{8,9},{9,8},{10,11... | collective-permute-start | bytes 98312 | tf_op jit(solution)/shard_map/ppermute | solution.py:54

commit v16 on v15

--- a/solution.py
+++ b/solution.py
@@ -476,7 +476,7 @@
             bases.append(diagonal(0, 3, running))
             received, bases[0] = lax.optimization_barrier((received, bases[0]))
         if bit == member_levels - 1:
-            bases.append(diagonal(3, 3, running))
+            bases.append(diagonal(3, 4, running))
             received, bases[1] = lax.optimization_barrier((received, bases[1]))
         received, other = widen(received, heights)
         power = bound(power, other)
@@ -494,21 +494,21 @@
     sums = narrow(running, power, heights)
     heard = [lax.ppermute(sums, everyone, route) for route in routes]
     left_top, left_low, last = call(
-        functools.partial(stage_kernel, 6),
+        functools.partial(stage_kernel, 7),
         [
             pltpu.VMEM(top_left.shape, BF16),
             pltpu.VMEM((capacity, member_levels * 2 * width), BF16),
-            jax.ShapeDtypeStruct((2 * height, columns), F32),
+            jax.ShapeDtypeStruct((height, columns), F32),
         ],
         [HBM, HBM, HBM, VMEM, pl.BlockSpec(memory_space=pl.ANY)],
         (*far(top_left, low_left, diag_block), pair, their_low),
-        8 * height * capacity * columns,
-        12 << 20,
+        4 * height * capacity * columns,
+        10 << 20,
         24,
         scratch=[
             pltpu.VMEM(low_left.shape, BF16),
-            pltpu.VMEM((2, 2, height, capacity), BF16),
-            DMA((4,)),
+            pltpu.VMEM((1, 2, height, capacity), BF16),
+            DMA((3,)),
         ],
     )
     bases.append(last)

time: 67.6 us -> 68.4 us (1.012)
  transfers between devices with their start and end apart: 8 -> 8, of which waited for: 5 -> 6; matrix products, arithmetic and copies ran while one was open for 0% -> 0% of each run, Pallas kernels for 20% -> 20%
where the time goes in v16:
time: 68.4 us; the launch traced here: 68.1 us
  Pallas kernels  21.2 us (31%)
  waiting for transfers between devices  17.9 us (26%)
  blocking collectives  17.8 us (26%)
  starting transfers between devices  10.5 us (15%)
    pallas_call x10, Pallas kernels, call(): pl.pallas_call(kernel, out_shape=outs, in_specs=ins, out_specs=more.pop('...  21.2 us
    all_to_all x1, blocking collectives, on_device(): lax.all_to_all(leaving.reshape(leaves, bucket, columns), everyone, split_...  17.8 us
    all_to_all x1, waiting for transfers between devices, on_device(): lax.all_to_all(packed, everyone, split_axis=0, concat_axis=0, tiled=True)  13.6 us
    all_to_all x1, starting transfers between devices, on_device(): lax.all_to_all(packed, everyone, split_axis=0, concat_axis=0, tiled=True)  7.43 us
    ppermute x5, waiting for transfers between devices, partner(): return lax.ppermute(block, axis, route)  4.27 us
    ppermute x2, starting transfers between devices, on_device(): heard = [lax.ppermute(sums, everyone, route) for route in routes]  2.61 us
  transfers between devices with their start and end apart: 8, of which 6 were waited for; matrix products, arithmetic and copies ran while one was open for 0% of the time, Pallas kernels for 20%

profile of v16, /device:TPU:0, one launch (start us, length us, event | category | flops | bytes accessed | tf_op | source)
XLA Modules:
  0.0 68.1 jit_solution(12361506562292963963)
XLA Ops:
  0.0 0.0 copy-start
  0.0 2.9 %shard_map.91 = (bf16[32,64,128]{2,1,0:T(8,128)(2,1)}, s32[1,1024]{1,0:T(1,128)S(1)}) custom-call(s32[32]{0:T(128)} %sizes_in.1, s32[1,1024]{1,0:T(1,128)} %bitcast.37, bf16[1024,128]{1,0:T(8,128)(2,1)} %rows_in.1), custom_call_target="tpu_custom_call" | custom-call | flops 268435456 | bytes 4194304 | tf_op jit(solution)/shard_map/pallas_call | solution.py:35
  2.9 7.4 %all-to-all-start = ((bf16[32,64,128]{2,1,0:T(8,128)(2,1)}), bf16[32,64,128]{2,1,0:T(8,128)(2,1)}, u32[]{:S(2)}, u32[]{:S(2)}) async-start(bf16[32,64,128]{2,1,0:T(8,128)(2,1)} %get-tuple-element.33), calls=%async_computation | async-start | bytes 1048576 | tf_op jit(solution)/shard_map/all_to_all | solution.py:405
  10.4 0.0 copy-done
  10.4 2.7 %shard_map.92 = (bf16[6272,256]{1,0:T(8,128)(2,1)S(1)}, f32[200,128]{1,0:T(8,128)S(1)}) custom-call(s32[62]{0:T(128)S(1)} %copy-done, bf16[2,2,1792,128]{3,2,1,0:T(8,128)(2,1)} %right_top_in.1, bf16[3,2,64,1792]{3,2,1,0:T(8,128)(2,1)} %bitcast.35), custom_call_target="tpu_custom_call" | custom-call | bytes 6291456 | tf_op jit(solution)/shard_map/pallas_call | solution.py:35
  13.1 13.6 %all-to-all-done.arrived = bf16[32,64,128]{2,1,0:T(8,128)(2,1)} async-done(((bf16[32,64,128]{2,1,0:T(8,128)(2,1)}), bf16[32,64,128]{2,1,0:T(8,128)(2,1)}, u32[]{:S(2)}, u32[]{:S(2)}) %all-to-all-start) | async-done | bytes 524320 | tf_op jit(solution)/shard_map/all_to_all | solution.py:405
  26.7 2.4 %shard_map.93 = (bf16[2,1792,128]{2,1,0:T(8,128)(2,1)S(1)}, s32[7,256]{1,0:T(8,128)S(1)}, f32[264,128]{1,0:T(8,128)S(1)}, f32[200,128]{1,0:T(8,128)S(1)}) custom-call(bf16[32,64,128]{2,1,0:T(8,128)(2,1)} %all-to-all-done.arrived, bf16[6272,256]{1,0:T(8,128)(2,1)S(1)} %get-tuple-element.34.right, f32[200,128]{1,0:T(8,128)S(1)} %get-tuple-element.35.flags), custom_call_target="tpu_custom_call" | custom-call | flops 411041792 | bytes 6291456 | tf_op jit(solution)/shard_map/pallas_call | solution.py:35
  29.1 0.1 collective-permute-start
  29.2 0.7 %shard_map.94 = (bf16[1792,256]{1,0:T(8,128)(2,1)S(1)}, bf16[1024,896]{1,0:T(8,128)(2,1)S(1)}, s32[1024,128]{1,0:T(8,128)S(1)}) custom-call(s32[7,256]{1,0:T(8,128)S(1)} %get-tuple-element.37.targets, s32[1,1024]{1,0:T(1,128)S(1)} %get-tuple-element.38.places, f32[264,128]{1,0:T(8,128)S(1)} %get-tuple-element.36.after), custom_call_target="tpu_custom_call" | custom-call | bytes 8388608 | tf_op jit(solution)/shard_map/pallas_call | solution.py:35
  29.9 0.6 collective-permute-done
  30.6 0.1 collective-permute-start.1
  30.7 3.2 %shard_map.95.rest_0_ = f32[672,128]{1,0:T(8,128)S(1)} custom-call(bf16[2,1792,1792]{2,1,0:T(8,128)(2,1)} %block_in.5, bf16[2,1792,128]{2,1,0:T(8,128)(2,1)S(1)} %get-tuple-element.46.pair, f32[192,128]{1,0:T(8,128)S(1)} %get-tuple-element.68.after), custom_call_target="tpu_custom_call" | custom-call | flops 616562688 | bytes 4816896 | tf_op jit(solution)/shard_map/pallas_call | solution.py:35
  33.9 0.9 %collective-permute-done.1 = f16[200,128]{1,0:T(8,128)(2,1)S(1)} collective-permute-done((f16[200,128]{1,0:T(8,128)(2,1)S(1)}, f16[200,128]{1,0:T(8,128)(2,1)S(1)}, u32[]{:S(2)}, u32[]{:S(2)}) %collective-permute-start.1) | collective-permute-done | bytes 51232 | tf_op jit(solution)/shard_map/ppermute | solution.py:54
  35.0 0.1 collective-permute-start.2
  35.1 3.8 %shard_map.96.rest_1_ = f32[896,128]{1,0:T(8,128)S(1)} custom-call(bf16[2,1792,1792]{2,1,0:T(8,128)(2,1)} %block_in.5, bf16[2,1792,128]{2,1,0:T(8,128)(2,1)S(1)} %get-tuple-element.46.pair, f32[160,128]{1,0:T(8,128)S(1)} %get-tuple-element.64.after), custom_call_target="tpu_custom_call" | custom-call | flops 822083584 | bytes 6422528 | tf_op jit(solution)/shard_map/pallas_call | solution.py:35
  38.9 1.1 %collective-permute-done.2 = f16[168,128]{1,0:T(8,128)(2,1)S(1)} collective-permute-done((f16[168,128]{1,0:T(8,128)(2,1)S(1)}, f16[168,128]{1,0:T(8,128)(2,1)S(1)}, u32[]{:S(2)}, u32[]{:S(2)}) %collective-permute-start.2) | collective-permute-done | bytes 43040 | tf_op jit(solution)/shard_map/ppermute | solution.py:54
  40.2 1.0 %collective-permute-start.5 = (f16[136,128]{1,0:T(8,128)(2,1)S(1)}, f16[136,128]{1,0:T(8,128)(2,1)S(1)}, u32[]{:S(2)}, u32[]{:S(2)}) collective-permute-start(f16[136,128]{1,0:T(8,128)(2,1)S(1)} %pad_maximum_fusion.2), channel_id=1, source_target_pairs={{0,24},{1,3},{2,26},{3,1},{4,28},{5,7},{6,30},{7,5},{8,16},{9,11},... | collective-permute-start | bytes 104456 | tf_op jit(solution)/shard_map/ppermute | solution.py:495
  41.2 1.6 %collective-permute-start.4 = (f16[136,128]{1,0:T(8,128)(2,1)S(1)}, f16[136,128]{1,0:T(8,128)(2,1)S(1)}, u32[]{:S(2)}, u32[]{:S(2)}) collective-permute-start(f16[136,128]{1,0:T(8,128)(2,1)S(1)} %pad_maximum_fusion.2), channel_id=1, source_target_pairs={{0,16},{1,9},{2,18},{3,11},{4,20},{5,13},{6,22},{7,15},{8,24},{9,1... | collective-permute-start | bytes 104456 | tf_op jit(solution)/shard_map/ppermute | solution.py:495
  42.8 0.0 collective-permute-start.3
  42.8 1.2 %collective-permute-done.3.after.rest_6_ = bf16[64,128]{1,0:T(8,128)(2,1)S(1)} collective-permute-done((bf16[64,128]{1,0:T(8,128)(2,1)S(1)}, bf16[64,128]{1,0:T(8,128)(2,1)S(1)}, u32[]{:S(2)}, u32[]{:S(2)}) %collective-permute-start.3) | collective-permute-done | bytes 16416 | tf_op jit(solution)/shard_map/ppermute | solution.py:54
  44.0 2.4 %shard_map.97 = (bf16[2,2,1792,128]{3,2,1,0:T(8,128)(2,1)S(1)}, bf16[1792,384]{1,0:T(8,128)(2,1)S(1)}, f32[224,128]{1,0:T(8,128)S(1)}) custom-call(bf16[2,2,1792,128]{3,2,1,0:T(8,128)(2,1)} %left_top_in.1, bf16[3,2,64,1792]{3,2,1,0:T(8,128)(2,1)} %bitcast.36, bf16[2,1792,1792]{2,1,0:T(8,128)(2,1)} %block_in.5, ...), custom_call_target="tpu_custom_call" | custom-call | flops 205520896 | bytes 10485760 | tf_op jit(solution)/shard_map/pallas_call | solution.py:35
  46.4 0.0 collective-permute-done.5
  46.4 0.0 collective-permute-done.4
  46.5 0.2 collective-permute-start.6
  46.7 0.6 shard_map.98.base
  47.3 0.4 collective-permute-done.6.theirs
  47.8 1.0 %shard_map.99 = bf16[1792,128]{1,0:T(8,128)(2,1)S(1)} custom-call(f32[200,128]{1,0:T(8,128)S(1)} %get-tuple-element.35.flags, f32[1792,128]{1,0:T(8,128)S(1)} %shard_map.98.base, bf16[2,2,1792,128]{3,2,1,0:T(8,128)(2,1)S(1)} %get-tuple-element.58.left_top, bf16[128,128]{1,0:T(8,128)(2,1)S(1)} %add_convert_fusion.own, ...), custom_call_target="tpu_custom_call" | custom-call | flops 234881024 | bytes 4194304 | tf_op jit(solution)/shard_map/pallas_call | solution.py:35
  48.8 17.8 %all_to_all.10 = bf16[32,56,128]{2,1,0:T(8,128)(2,1)S(1)} all-to-all(bf16[32,56,128]{2,1,0:T(8,128)(2,1)S(1)} %bitcast.33), channel_id=1, replica_groups=mesh['group'=4,'member'=8] {'group','member'}, dimensions={0} | all-to-all | bytes 917504 | tf_op jit(solution)/shard_map/all_to_all | solution.py:543
  66.6 1.5 %shard_map.100 = f32[1024,128]{1,0:T(8,128)} custom-call(bf16[1024,896]{1,0:T(8,128)(2,1)S(1)} %get-tuple-element.42.order, s32[1024,128]{1,0:T(8,128)S(1)} %get-tuple-element.43.upper, bf16[1792,128]{1,0:T(8,128)(2,1)S(1)} %bitcast.34), custom_call_target="tpu_custom_call" | custom-call | flops 469762048 | bytes 4194304 | tf_op jit(solution)/shard_map/pallas_call | solution.py:35
  (35 shorter events, 0.4 us)
Async XLA Ops:
  0.0 10.4 %copy-start = (s32[62]{0:T(128)S(1)}, s32[62]{0:T(128)}, u32[]{:S(2)}) copy-start(s32[62]{0:T(128)} %ranks.1) | copy-start | bytes 748
  2.9 23.8 %all-to-all-start = ((bf16[32,64,128]{2,1,0:T(8,128)(2,1)}), bf16[32,64,128]{2,1,0:T(8,128)(2,1)}, u32[]{:S(2)}, u32[]{:S(2)}) async-start(bf16[32,64,128]{2,1,0:T(8,128)(2,1)} %get-tuple-element.33), calls=%async_computation | async-start | bytes 1048576 | tf_op jit(solution)/shard_map/all_to_all | solution.py:405
  29.1 1.4 %collective-permute-start = (f32[264,128]{1,0:T(8,128)S(1)}, f32[264,128]{1,0:T(8,128)S(1)}, u32[]{:S(2)}, u32[]{:S(2)}) collective-permute-start(f32[264,128]{1,0:T(8,128)S(1)} %get-tuple-element.36.after), channel_id=1, source_target_pairs={{0,1},{1,0},{2,3},{3,2},{4,5},{5,4},{6,7},{7,6},{8,9},{9,8},{10,11... | collective-permute-start | bytes 405512 | tf_op jit(solution)/shard_map/ppermute | solution.py:54
  30.6 4.2 %collective-permute-start.1 = (f16[200,128]{1,0:T(8,128)(2,1)S(1)}, f16[200,128]{1,0:T(8,128)(2,1)S(1)}, u32[]{:S(2)}, u32[]{:S(2)}) collective-permute-start(f16[200,128]{1,0:T(8,128)(2,1)S(1)} %pad_maximum_fusion), channel_id=1, source_target_pairs={{0,2},{2,0},{1,3},{3,1},{4,6},{6,4},{5,7},{7,5},{8,10},{10,8},{9,1... | collective-permute-start | bytes 153608 | tf_op jit(solution)/shard_map/ppermute | solution.py:54
  35.0 5.0 %collective-permute-start.2 = (f16[168,128]{1,0:T(8,128)(2,1)S(1)}, f16[168,128]{1,0:T(8,128)(2,1)S(1)}, u32[]{:S(2)}, u32[]{:S(2)}) collective-permute-start(f16[168,128]{1,0:T(8,128)(2,1)S(1)} %pad_maximum_fusion.1), channel_id=1, source_target_pairs={{0,4},{4,0},{1,5},{5,1},{2,6},{6,2},{3,7},{7,3},{8,12},{12,8},{9,1... | collective-permute-start | bytes 129032 | tf_op jit(solution)/shard_map/ppermute | solution.py:54
  40.2 6.3 %collective-permute-start.5 = (f16[136,128]{1,0:T(8,128)(2,1)S(1)}, f16[136,128]{1,0:T(8,128)(2,1)S(1)}, u32[]{:S(2)}, u32[]{:S(2)}) collective-permute-start(f16[136,128]{1,0:T(8,128)(2,1)S(1)} %pad_maximum_fusion.2), channel_id=1, source_target_pairs={{0,24},{1,3},{2,26},{3,1},{4,28},{5,7},{6,30},{7,5},{8,16},{9,11},... | collective-permute-start | bytes 104456 | tf_op jit(solution)/shard_map/ppermute | solution.py:495
  41.2 5.3 %collective-permute-start.4 = (f16[136,128]{1,0:T(8,128)(2,1)S(1)}, f16[136,128]{1,0:T(8,128)(2,1)S(1)}, u32[]{:S(2)}, u32[]{:S(2)}) collective-permute-start(f16[136,128]{1,0:T(8,128)(2,1)S(1)} %pad_maximum_fusion.2), channel_id=1, source_target_pairs={{0,16},{1,9},{2,18},{3,11},{4,20},{5,13},{6,22},{7,15},{8,24},{9,1... | collective-permute-start | bytes 104456 | tf_op jit(solution)/shard_map/ppermute | solution.py:495
  42.8 1.2 %collective-permute-start.3 = (bf16[64,128]{1,0:T(8,128)(2,1)S(1)}, bf16[64,128]{1,0:T(8,128)(2,1)S(1)}, u32[]{:S(2)}, u32[]{:S(2)}) collective-permute-start(bf16[64,128]{1,0:T(8,128)(2,1)S(1)} %pad_maximum_fusion.3.rest_5_), channel_id=1, source_target_pairs={{0,1},{1,0},{2,3},{3,2},{4,5},{5,4},{6,7},{7,6},{8,9},{9,8},{10,11... | collective-permute-start | bytes 49160 | tf_op jit(solution)/shard_map/ppermute | solution.py:54
  46.5 1.3 %collective-permute-start.6 = (bf16[128,128]{1,0:T(8,128)(2,1)S(1)}, bf16[128,128]{1,0:T(8,128)(2,1)S(1)}, u32[]{:S(2)}, u32[]{:S(2)}) collective-permute-start(bf16[128,128]{1,0:T(8,128)(2,1)S(1)} %add_convert_fusion.own), channel_id=1, source_target_pairs={{0,1},{1,0},{2,3},{3,2},{4,5},{5,4},{6,7},{7,6},{8,9},{9,8},{10,11... | collective-permute-start | bytes 98312 | tf_op jit(solution)/shard_map/ppermute | solution.py:54

commit v17 on v14

--- a/solution.py
+++ b/solution.py
@@ -276,11 +276,15 @@
     copies = []
     for j in range(count):
         rows = pl.ds((first + j) * height, height)
-        copies.append(pltpu.make_async_copy(block_in.at[:, rows, :], block.at[j], sems.at[j]))
-        copies[j].start()
+        for p in range(2):
+            source = block_in.at[p, rows, :]
+            copies.append(pltpu.make_async_copy(source, block.at[j, p], sems.at[2 * j + p]))
+            copies[-1].start()
     for j in range(count):
-        copies[j].wait()
-        out[j * height : (j + 1) * height, :] = dot(block[j, 0], pair[0]) + dot(block[j, 1], pair[1])
+        copies[2 * j].wait()
+        real = dot(block[j, 0], pair[0])
+        copies[2 * j + 1].wait()
+        out[j * height : (j + 1) * height, :] = real + dot(block[j, 1], pair[1])
 
 
 def merged(core, own, theirs, at, half):
@@ -445,7 +449,7 @@
             4 * chunks * height * capacity * columns,
             4 * chunks * height * capacity,
             24,
-            scratch=[pltpu.VMEM((chunks, 2, height, capacity), BF16), DMA((chunks,))],
+            scratch=[pltpu.VMEM((chunks, 2, height, capacity), BF16), DMA((2 * chunks,))],
         )[0]
 
     received = partner(send, "member", 0)

time: 67.5 us -> 67.9 us (level)
  no operation moved by 1% of the time
where the time goes in v17:
time: 67.9 us; the launch traced here: 67.6 us
  Pallas kernels  21.6 us (32%)
  blocking collectives  17.6 us (26%)
  waiting for transfers between devices  16.6 us (24%)
  starting transfers between devices  11.2 us (16%)
    pallas_call x10, Pallas kernels, call(): pl.pallas_call(kernel, out_shape=outs, in_specs=ins, out_specs=more.pop('...  21.6 us
    all_to_all x1, blocking collectives, on_device(): lax.all_to_all(leaving.reshape(leaves, bucket, columns), everyone, split_...  17.6 us
    all_to_all x1, waiting for transfers between devices, on_device(): lax.all_to_all(packed, everyone, split_axis=0, concat_axis=0, tiled=True)  13.6 us
    all_to_all x1, starting transfers between devices, on_device(): lax.all_to_all(packed, everyone, split_axis=0, concat_axis=0, tiled=True)  7.43 us
    ppermute x5, waiting for transfers between devices, partner(): return lax.ppermute(block, axis, route)  2.98 us
    ppermute x2, starting transfers between devices, on_device(): heard = [lax.ppermute(sums, everyone, route) for route in routes]  2.7 us
  transfers between devices with their start and end apart: 8, of which 5 were waited for; matrix products, arithmetic and copies ran while one was open for 0% of the time, Pallas kernels for 20%

profile of v17, /device:TPU:0, one launch (start us, length us, event | category | flops | bytes accessed | tf_op | source)
XLA Modules:
  0.0 67.6 jit_solution(9620336438891020366)
XLA Ops:
  0.0 0.0 copy-start
  0.0 2.9 %shard_map.91 = (bf16[32,64,128]{2,1,0:T(8,128)(2,1)}, s32[1,1024]{1,0:T(1,128)S(1)}) custom-call(s32[32]{0:T(128)} %sizes_in.1, s32[1,1024]{1,0:T(1,128)} %bitcast.37, bf16[1024,128]{1,0:T(8,128)(2,1)} %rows_in.1), custom_call_target="tpu_custom_call" | custom-call | flops 268435456 | bytes 4194304 | tf_op jit(solution)/shard_map/pallas_call | solution.py:35
  2.9 7.4 %all-to-all-start = ((bf16[32,64,128]{2,1,0:T(8,128)(2,1)}), bf16[32,64,128]{2,1,0:T(8,128)(2,1)}, u32[]{:S(2)}, u32[]{:S(2)}) async-start(bf16[32,64,128]{2,1,0:T(8,128)(2,1)} %get-tuple-element.33), calls=%async_computation | async-start | bytes 1048576 | tf_op jit(solution)/shard_map/all_to_all | solution.py:409
  10.4 0.0 copy-done
  10.4 2.7 %shard_map.92 = (bf16[6272,256]{1,0:T(8,128)(2,1)S(1)}, f32[200,128]{1,0:T(8,128)S(1)}) custom-call(s32[62]{0:T(128)S(1)} %copy-done, bf16[2,2,1792,128]{3,2,1,0:T(8,128)(2,1)} %right_top_in.1, bf16[3,2,64,1792]{3,2,1,0:T(8,128)(2,1)} %bitcast.35), custom_call_target="tpu_custom_call" | custom-call | bytes 6291456 | tf_op jit(solution)/shard_map/pallas_call | solution.py:35
  13.1 13.6 %all-to-all-done.arrived = bf16[32,64,128]{2,1,0:T(8,128)(2,1)} async-done(((bf16[32,64,128]{2,1,0:T(8,128)(2,1)}), bf16[32,64,128]{2,1,0:T(8,128)(2,1)}, u32[]{:S(2)}, u32[]{:S(2)}) %all-to-all-start) | async-done | bytes 524320 | tf_op jit(solution)/shard_map/all_to_all | solution.py:409
  26.7 2.4 %shard_map.93 = (bf16[2,1792,128]{2,1,0:T(8,128)(2,1)S(1)}, s32[7,256]{1,0:T(8,128)S(1)}, f32[264,128]{1,0:T(8,128)S(1)}, f32[200,128]{1,0:T(8,128)S(1)}) custom-call(bf16[32,64,128]{2,1,0:T(8,128)(2,1)} %all-to-all-done.arrived, bf16[6272,256]{1,0:T(8,128)(2,1)S(1)} %get-tuple-element.34.right, f32[200,128]{1,0:T(8,128)S(1)} %get-tuple-element.35.flags), custom_call_target="tpu_custom_call" | custom-call | flops 411041792 | bytes 6291456 | tf_op jit(solution)/shard_map/pallas_call | solution.py:35
  29.1 0.1 collective-permute-start
  29.2 0.7 %shard_map.94 = (bf16[1792,256]{1,0:T(8,128)(2,1)S(1)}, bf16[1024,896]{1,0:T(8,128)(2,1)S(1)}, s32[1024,128]{1,0:T(8,128)S(1)}) custom-call(s32[7,256]{1,0:T(8,128)S(1)} %get-tuple-element.37.targets, s32[1,1024]{1,0:T(1,128)S(1)} %get-tuple-element.38.places, f32[264,128]{1,0:T(8,128)S(1)} %get-tuple-element.36.after), custom_call_target="tpu_custom_call" | custom-call | bytes 8388608 | tf_op jit(solution)/shard_map/pallas_call | solution.py:35
  29.9 0.6 collective-permute-done
  30.6 0.1 collective-permute-start.1
  30.7 3.4 %shard_map.95.rest_0_ = f32[672,128]{1,0:T(8,128)S(1)} custom-call(bf16[2,1792,1792]{2,1,0:T(8,128)(2,1)} %block_in.5, bf16[2,1792,128]{2,1,0:T(8,128)(2,1)S(1)} %get-tuple-element.46.pair, f32[192,128]{1,0:T(8,128)S(1)} %get-tuple-element.70.after), custom_call_target="tpu_custom_call" | custom-call | flops 616562688 | bytes 4816896 | tf_op jit(solution)/shard_map/pallas_call | solution.py:35
  34.1 0.7 %collective-permute-done.1 = f16[200,128]{1,0:T(8,128)(2,1)S(1)} collective-permute-done((f16[200,128]{1,0:T(8,128)(2,1)S(1)}, f16[200,128]{1,0:T(8,128)(2,1)S(1)}, u32[]{:S(2)}, u32[]{:S(2)}) %collective-permute-start.1) | collective-permute-done | bytes 51232 | tf_op jit(solution)/shard_map/ppermute | solution.py:54
  35.0 0.3 collective-permute-start.2
  35.3 3.4 %shard_map.96.rest_1_ = f32[672,128]{1,0:T(8,128)S(1)} custom-call(bf16[2,1792,1792]{2,1,0:T(8,128)(2,1)} %block_in.5, bf16[2,1792,128]{2,1,0:T(8,128)(2,1)S(1)} %get-tuple-element.46.pair, f32[160,128]{1,0:T(8,128)S(1)} %get-tuple-element.66.after), custom_call_target="tpu_custom_call" | custom-call | flops 616562688 | bytes 4816896 | tf_op jit(solution)/shard_map/pallas_call | solution.py:35
  38.7 1.4 %collective-permute-done.2 = f16[168,128]{1,0:T(8,128)(2,1)S(1)} collective-permute-done((f16[168,128]{1,0:T(8,128)(2,1)S(1)}, f16[168,128]{1,0:T(8,128)(2,1)S(1)}, u32[]{:S(2)}, u32[]{:S(2)}) %collective-permute-start.2) | collective-permute-done | bytes 43040 | tf_op jit(solution)/shard_map/ppermute | solution.py:54
  40.3 0.7 %collective-permute-start.4 = (f16[136,128]{1,0:T(8,128)(2,1)S(1)}, f16[136,128]{1,0:T(8,128)(2,1)S(1)}, u32[]{:S(2)}, u32[]{:S(2)}) collective-permute-start(f16[136,128]{1,0:T(8,128)(2,1)S(1)} %pad_maximum_fusion.2), channel_id=1, source_target_pairs={{0,24},{1,3},{2,26},{3,1},{4,28},{5,7},{6,30},{7,5},{8,16},{9,11},... | collective-permute-start | bytes 104456 | tf_op jit(solution)/shard_map/ppermute | solution.py:497
  41.0 2.0 %collective-permute-start.3 = (f16[136,128]{1,0:T(8,128)(2,1)S(1)}, f16[136,128]{1,0:T(8,128)(2,1)S(1)}, u32[]{:S(2)}, u32[]{:S(2)}) collective-permute-start(f16[136,128]{1,0:T(8,128)(2,1)S(1)} %pad_maximum_fusion.2), channel_id=1, source_target_pairs={{0,16},{1,9},{2,18},{3,11},{4,20},{5,13},{6,22},{7,15},{8,24},{9,1... | collective-permute-start | bytes 104456 | tf_op jit(solution)/shard_map/ppermute | solution.py:497
  43.0 0.0 collective-permute-start.5
  43.0 3.0 %shard_map.97 = (bf16[2,2,1792,128]{3,2,1,0:T(8,128)(2,1)S(1)}, bf16[1792,384]{1,0:T(8,128)(2,1)S(1)}, f32[448,128]{1,0:T(8,128)S(1)}) custom-call(bf16[2,2,1792,128]{3,2,1,0:T(8,128)(2,1)} %left_top_in.1, bf16[3,2,64,1792]{3,2,1,0:T(8,128)(2,1)} %bitcast.36, bf16[2,1792,1792]{2,1,0:T(8,128)(2,1)} %block_in.5, ...), custom_call_target="tpu_custom_call" | custom-call | flops 411041792 | bytes 12582912 | tf_op jit(solution)/shard_map/pallas_call | solution.py:35
  46.0 0.0 collective-permute-done.4
  46.0 0.0 collective-permute-done.3
  46.1 0.0 collective-permute-done.5.rest_6_
  46.1 0.6 collective-permute-start.6
  46.7 0.6 shard_map.98.base
  47.3 0.3 collective-permute-done.6.theirs
  47.5 1.0 %shard_map.99 = bf16[1792,128]{1,0:T(8,128)(2,1)S(1)} custom-call(f32[200,128]{1,0:T(8,128)S(1)} %get-tuple-element.35.flags, f32[1792,128]{1,0:T(8,128)S(1)} %shard_map.98.base, bf16[2,2,1792,128]{3,2,1,0:T(8,128)(2,1)S(1)} %get-tuple-element.58.left_top, bf16[128,128]{1,0:T(8,128)(2,1)S(1)} %add_convert_fusion.own, ...), custom_call_target="tpu_custom_call" | custom-call | flops 234881024 | bytes 4194304 | tf_op jit(solution)/shard_map/pallas_call | solution.py:35
  48.6 17.6 %all_to_all.10 = bf16[32,56,128]{2,1,0:T(8,128)(2,1)S(1)} all-to-all(bf16[32,56,128]{2,1,0:T(8,128)(2,1)S(1)} %bitcast.33), channel_id=1, replica_groups=mesh['group'=4,'member'=8] {'group','member'}, dimensions={0} | all-to-all | bytes 917504 | tf_op jit(solution)/shard_map/all_to_all | solution.py:546
  66.2 1.5 %shard_map.100 = f32[1024,128]{1,0:T(8,128)} custom-call(bf16[1024,896]{1,0:T(8,128)(2,1)S(1)} %get-tuple-element.42.order, s32[1024,128]{1,0:T(8,128)S(1)} %get-tuple-element.43.upper, bf16[1792,128]{1,0:T(8,128)(2,1)S(1)} %bitcast.34), custom_call_target="tpu_custom_call" | custom-call | flops 469762048 | bytes 4194304 | tf_op jit(solution)/shard_map/pallas_call | solution.py:35
  (35 shorter events, 0.4 us)
Async XLA Ops:
  0.0 10.4 %copy-start = (s32[62]{0:T(128)S(1)}, s32[62]{0:T(128)}, u32[]{:S(2)}) copy-start(s32[62]{0:T(128)} %ranks.1) | copy-start | bytes 748
  2.9 23.8 %all-to-all-start = ((bf16[32,64,128]{2,1,0:T(8,128)(2,1)}), bf16[32,64,128]{2,1,0:T(8,128)(2,1)}, u32[]{:S(2)}, u32[]{:S(2)}) async-start(bf16[32,64,128]{2,1,0:T(8,128)(2,1)} %get-tuple-element.33), calls=%async_computation | async-start | bytes 1048576 | tf_op jit(solution)/shard_map/all_to_all | solution.py:409
  29.1 1.4 %collective-permute-start = (f32[264,128]{1,0:T(8,128)S(1)}, f32[264,128]{1,0:T(8,128)S(1)}, u32[]{:S(2)}, u32[]{:S(2)}) collective-permute-start(f32[264,128]{1,0:T(8,128)S(1)} %get-tuple-element.36.after), channel_id=1, source_target_pairs={{0,1},{1,0},{2,3},{3,2},{4,5},{5,4},{6,7},{7,6},{8,9},{9,8},{10,11... | collective-permute-start | bytes 405512 | tf_op jit(solution)/shard_map/ppermute | solution.py:54
  30.6 4.2 %collective-permute-start.1 = (f16[200,128]{1,0:T(8,128)(2,1)S(1)}, f16[200,128]{1,0:T(8,128)(2,1)S(1)}, u32[]{:S(2)}, u32[]{:S(2)}) collective-permute-start(f16[200,128]{1,0:T(8,128)(2,1)S(1)} %pad_maximum_fusion), channel_id=1, source_target_pairs={{0,2},{2,0},{1,3},{3,1},{4,6},{6,4},{5,7},{7,5},{8,10},{10,8},{9,1... | collective-permute-start | bytes 153608 | tf_op jit(solution)/shard_map/ppermute | solution.py:54
  35.0 5.1 %collective-permute-start.2 = (f16[168,128]{1,0:T(8,128)(2,1)S(1)}, f16[168,128]{1,0:T(8,128)(2,1)S(1)}, u32[]{:S(2)}, u32[]{:S(2)}) collective-permute-start(f16[168,128]{1,0:T(8,128)(2,1)S(1)} %pad_maximum_fusion.1), channel_id=1, source_target_pairs={{0,4},{4,0},{1,5},{5,1},{2,6},{6,2},{3,7},{7,3},{8,12},{12,8},{9,1... | collective-permute-start | bytes 129032 | tf_op jit(solution)/shard_map/ppermute | solution.py:54
  40.3 5.7 %collective-permute-start.4 = (f16[136,128]{1,0:T(8,128)(2,1)S(1)}, f16[136,128]{1,0:T(8,128)(2,1)S(1)}, u32[]{:S(2)}, u32[]{:S(2)}) collective-permute-start(f16[136,128]{1,0:T(8,128)(2,1)S(1)} %pad_maximum_fusion.2), channel_id=1, source_target_pairs={{0,24},{1,3},{2,26},{3,1},{4,28},{5,7},{6,30},{7,5},{8,16},{9,11},... | collective-permute-start | bytes 104456 | tf_op jit(solution)/shard_map/ppermute | solution.py:497
  41.0 5.0 %collective-permute-start.3 = (f16[136,128]{1,0:T(8,128)(2,1)S(1)}, f16[136,128]{1,0:T(8,128)(2,1)S(1)}, u32[]{:S(2)}, u32[]{:S(2)}) collective-permute-start(f16[136,128]{1,0:T(8,128)(2,1)S(1)} %pad_maximum_fusion.2), channel_id=1, source_target_pairs={{0,16},{1,9},{2,18},{3,11},{4,20},{5,13},{6,22},{7,15},{8,24},{9,1... | collective-permute-start | bytes 104456 | tf_op jit(solution)/shard_map/ppermute | solution.py:497
  43.0 3.1 %collective-permute-start.5 = (bf16[64,128]{1,0:T(8,128)(2,1)S(1)}, bf16[64,128]{1,0:T(8,128)(2,1)S(1)}, u32[]{:S(2)}, u32[]{:S(2)}) collective-permute-start(bf16[64,128]{1,0:T(8,128)(2,1)S(1)} %pad_maximum_fusion.3.rest_5_), channel_id=1, source_target_pairs={{0,1},{1,0},{2,3},{3,2},{4,5},{5,4},{6,7},{7,6},{8,9},{9,8},{10,11... | collective-permute-start | bytes 49160 | tf_op jit(solution)/shard_map/ppermute | solution.py:54
  46.1 1.4 %collective-permute-start.6 = (bf16[128,128]{1,0:T(8,128)(2,1)S(1)}, bf16[128,128]{1,0:T(8,128)(2,1)S(1)}, u32[]{:S(2)}, u32[]{:S(2)}) collective-permute-start(bf16[128,128]{1,0:T(8,128)(2,1)S(1)} %add_convert_fusion.own), channel_id=1, source_target_pairs={{0,1},{1,0},{2,3},{3,2},{4,5},{5,4},{6,7},{7,6},{8,9},{9,8},{10,11... | collective-permute-start | bytes 98312 | tf_op jit(solution)/shard_map/ppermute | solution.py:54
